TPU v7x, 32 devices: a whole 2x2x4 slice. The times are simulated.
32 devices in a mesh: dp: 8 (over y, x, core), head: 4 (over z).
Axes of the slice: x: 2, y: 2, z: 4, core: 2. Of those that a mesh axis runs over, the one named last changes fastest.
Arguments:
- tokens: bfloat16 [12288, 1024], P(('dp', 'head')), may hold values from -6 to 6
- cotangent: bfloat16 [12288, 1024], P(('dp', 'head')), may hold values from -6 to 6
- class_table: bfloat16 [1000, 1024], replicated, may hold values from -5 to 5
- ada_weight: bfloat16 [1024, 6144], replicated, may hold values from -0.1875 to 0.1875
- ada_bias: bfloat16 [6144], replicated, may hold values from -2 to 2
- qkv_weight: bfloat16 [3, 1024, 1024], replicated, may hold values from -0.1875 to 0.1875
- q_bias: bfloat16 [1024], replicated, may hold values from -3 to 3
- v_bias: bfloat16 [1024], replicated, may hold values from -3 to 3
- log_scale: float32 [16], replicated, may hold values from 2.3 to 3
- proj_weight: bfloat16 [1024, 1024], replicated, may hold values from -1 to 1
- proj_bias: bfloat16 [1024], replicated, may hold values from -3 to 3
- fc1_weight: bfloat16 [1024, 4096], P(None, 'head'), may hold values from -0.1875 to 0.1875
- fc1_bias: bfloat16 [4096], P('head'), may hold values from -3 to 3
- fc2_weight: bfloat16 [4096, 1024], P('head'), may hold values from -0.09375 to 0.09375
- fc2_bias: bfloat16 [1024], replicated, may hold values from -3 to 3
- item_lens: int32 [8, 4], replicated, may hold values from 1 to 680, as said below
- class_ids: int32 [8, 4], replicated, may hold values from 0 to 999
- section_ids: int32 [8, 1536], P('dp'), may hold values from 0 to 39, never falling along the last dimension, each value on 1 to 256 neighbouring positions
- destination: int32 [12288], P(('dp', 'head')), may hold values from 0 to 12287, as said below
Outputs:
- output: bfloat16 [12288, 1024], P(('dp', 'head'))
- tokens_grad: float32 [12288, 1024], P(('dp', 'head'))
- ada_weight_grad: float32 [1024, 6144], P(None, ('dp', 'head'))
- ada_bias_grad: float32 [6144], P(('dp', 'head'))
- qkv_weight_grad: float32 [3, 1024, 1024], P(None, 'head', 'dp')
- q_bias_grad: float32 [1024], replicated
- v_bias_grad: float32 [1024], replicated
- log_scale_grad: float32 [16], replicated
- proj_weight_grad: float32 [1024, 1024], P('head', 'dp')
- proj_bias_grad: float32 [1024], replicated
- fc1_weight_grad: float32 [1024, 4096], P('dp', 'head')
- fc1_bias_grad: float32 [4096], P('head')
- fc2_weight_grad: float32 [4096, 1024], P('head', 'dp')
- fc2_bias_grad: float32 [1024], replicated
Inputs may be any that keep to these rules, and one draw needn't show every extreme that they name: destination is a permutation of 0 to 12287; row r of the data layout goes to pack destination[r] // 1536, and the 384 rows of each device of the data layout (devices along dp+head, dp slowest) send exactly 48 rows to each pack. Within a pack, the positions are ranked by the class of their item, then item, then position, and device d takes the d-th run of 48 of that order, so that a device's rows come from items of nearby classes; a device's rows stand in order of class, then pack, then position. `item_lens`: each row sums to 1536, and each pack has an item of exactly 680 positions.
All inputs are finite; a program needn't handle non-finite values.
Results may differ from a plain program's by a relative error of at most 0.018.
Values may be sent and summed in bfloat16 or wider, within the bound.
No kernel may reach another device: no remote copies, remote signals or barrier semaphores. Data moves between devices by JAX's collectives and lax.ppermute only.
A program may use at most 192 MiB of HBM per device.

v0:
```python
import jax
import jax.numpy as jnp
from jax import lax
from jax.sharding import PartitionSpec as P


def layer_norm(values):
    centre = values - jnp.mean(values, axis=-1, keepdims=True)
    inverse = lax.rsqrt(jnp.mean(centre * centre, axis=-1, keepdims=True) + 1e-06)
    return (centre * inverse, inverse)


def norm_back(gradient, normed, inverse):
    return inverse * (
        gradient
        - jnp.mean(gradient, axis=-1, keepdims=True)
        - normed * jnp.mean(gradient * normed, axis=-1, keepdims=True)
    )


def unit_rows(values):
    inverse = lax.rsqrt(jnp.sum(values * values, axis=-1, keepdims=True) + 1e-06)
    return (values * inverse, inverse)


def unit_back(gradient, unit_vec, inverse):
    return inverse * (gradient - unit_vec * jnp.sum(gradient * unit_vec, axis=-1, keepdims=True))


def smooth_gate(hidden_val):
    return jax.nn.gelu(hidden_val, approximate=True)


def gelu_back(pre_act, gradient):
    return jax.vjp(smooth_gate, pre_act)[1](gradient)[0]


def visible_mask(item_query, section_query, item_key, section_key):
    return (item_query[:, None] == item_key[None, :]) & (
        section_key[None, :] <= section_query[:, None]
    )


def shards(
    tokens,
    cotangent,
    class_table,
    ada_weight,
    ada_bias,
    qkv_weight,
    q_bias,
    v_bias,
    log_scale,
    proj_weight,
    proj_bias,
    fc1_weight,
    fc1_bias,
    fc2_weight,
    fc2_bias,
    item_lens,
    class_ids,
    section_ids,
    destination,
):
    data_size = lax.axis_size("dp")
    head_size = lax.axis_size("head")
    row_count = tokens.shape[0]
    model_width = tokens.shape[1]
    heads_all = log_scale.shape[0]
    head_dim = model_width // heads_all
    heads_here = heads_all // head_size
    slice_width = model_width // head_size
    pack_len = row_count * head_size
    send_rows = row_count // data_size
    query_rows = min(512, pack_len)
    block_count = pack_len // query_rows
    items_pack = item_lens.shape[1]
    item_count = item_lens.shape[0] * items_pack
    hidden_here = fc1_bias.shape[0]
    hidden_total = hidden_here * head_size
    item_ends = jnp.cumsum(item_lens, axis=1)
    pack_base = pack_len * jnp.arange(item_lens.shape[0], dtype=jnp.int32)
    item_starts = (item_ends - item_lens + pack_base[:, None]).reshape(-1)
    row_item = jnp.sum((destination[:, None] >= item_starts[None, :]).astype(jnp.int32), axis=1) - 1
    class_rows = jnp.take(class_table, class_ids.reshape(-1), axis=0).astype(jnp.float32)
    silu_cond = jax.nn.silu(class_rows).astype(jnp.bfloat16)
    modulation = jnp.dot(
        silu_cond, ada_weight, preferred_element_type=jnp.float32
    ) + ada_bias.astype(jnp.float32)
    mod_rows = jnp.take(modulation, row_item, axis=0)
    gamma_one, gamma_two, scale_one, scale_two, shift_one, shift_two = jnp.split(
        mod_rows, 6, axis=1
    )
    inputs = tokens.astype(jnp.float32)
    normed_one, inverse_one = layer_norm(inputs)
    attn_in = (normed_one * (1.0 + scale_one) + shift_one).astype(jnp.bfloat16)
    projected = jnp.einsum("re,ted->rtd", attn_in, qkv_weight, preferred_element_type=jnp.float32)
    query_pre = (projected[:, 0] + q_bias.astype(jnp.float32)).reshape(
        row_count, heads_all, head_dim
    )
    key_pre = projected[:, 1].reshape(row_count, heads_all, head_dim)
    value_rows = (projected[:, 2] + v_bias.astype(jnp.float32)).astype(jnp.bfloat16)
    query_unit, query_inv = unit_rows(query_pre)
    key_unit, key_inv = unit_rows(key_pre)
    temper = jnp.exp(log_scale)[None, :, None]
    query_sent = (query_unit * temper).reshape(row_count, model_width).astype(jnp.bfloat16)
    key_sent = key_unit.reshape(row_count, model_width).astype(jnp.bfloat16)
    stacked = jnp.stack([query_sent, key_sent, value_rows], axis=1)
    row_order = jnp.argsort(destination)
    sorted_pos = destination[row_order]
    outgoing = stacked[row_order].reshape(data_size, send_rows, 3, head_size, slice_width)
    positions_out = jnp.broadcast_to(
        sorted_pos.reshape(data_size, send_rows, 1, 1), (data_size, send_rows, 1, head_size)
    )
    arrived, arrived_pos = (
        lax.all_to_all(
            lax.all_to_all(outgoing, "dp", split_axis=0, concat_axis=0, tiled=True),
            "head",
            split_axis=3,
            concat_axis=1,
            tiled=True,
        ),
        lax.all_to_all(
            lax.all_to_all(positions_out, "dp", split_axis=0, concat_axis=0, tiled=True),
            "head",
            split_axis=3,
            concat_axis=1,
            tiled=True,
        ),
    )
    slot_of = arrived_pos.reshape(pack_len) % pack_len
    pack_qkv = (
        jnp.zeros((pack_len, 3, slice_width), jnp.bfloat16)
        .at[slot_of]
        .set(arrived.reshape(pack_len, 3, slice_width))
    )
    pack_query = pack_qkv[:, 0].reshape(pack_len, heads_here, head_dim)
    pack_key = pack_qkv[:, 1].reshape(pack_len, heads_here, head_dim)
    pack_value = pack_qkv[:, 2].reshape(pack_len, heads_here, head_dim)
    pack_index = lax.axis_index("dp")
    ends_here = lax.dynamic_index_in_dim(item_ends, pack_index, 0, keepdims=False)
    pack_item = jnp.sum(
        (jnp.arange(pack_len, dtype=jnp.int32)[:, None] >= ends_here[None, :]).astype(jnp.int32),
        axis=1,
    )
    pack_section = section_ids[0]

    def block_scores(first_row):
        query_part = lax.dynamic_slice_in_dim(pack_query, first_row, query_rows, 0)
        item_part = lax.dynamic_slice_in_dim(pack_item, first_row, query_rows, 0)
        section_part = lax.dynamic_slice_in_dim(pack_section, first_row, query_rows, 0)
        allowed = visible_mask(item_part, section_part, pack_item, pack_section)
        scores = jnp.einsum(
            "qhd,khd->hqk", query_part, pack_key, preferred_element_type=jnp.float32
        )
        return (query_part, jnp.where(allowed[None], scores, -1e30))

    def attend(block_index):
        query_part, scores = block_scores(block_index * query_rows)
        highest = jnp.max(scores, axis=-1, keepdims=True)
        raised = jnp.exp(scores - highest)
        totals = jnp.sum(raised, axis=-1, keepdims=True)
        weights_b = (raised / totals).astype(jnp.bfloat16)
        mixed_heads = jnp.einsum(
            "hqk,khd->qhd", weights_b, pack_value, preferred_element_type=jnp.float32
        )
        return (mixed_heads.astype(jnp.bfloat16), (highest + jnp.log(totals))[..., 0])

    block_out, block_lse = lax.map(attend, jnp.arange(block_count))
    pack_out = block_out.reshape(pack_len, slice_width)
    leaving = pack_out[slot_of].reshape(data_size, head_size, send_rows, 1, slice_width)
    returned = lax.all_to_all(
        lax.all_to_all(leaving, "dp", split_axis=0, concat_axis=0, tiled=True),
        "head",
        split_axis=1,
        concat_axis=3,
        tiled=True,
    )
    attn_rows = (
        jnp.zeros((row_count, model_width), jnp.bfloat16)
        .at[row_order]
        .set(returned.reshape(row_count, model_width))
    )
    branch = jnp.dot(attn_rows, proj_weight, preferred_element_type=jnp.float32) + proj_bias.astype(
        jnp.float32
    )
    middle = inputs + gamma_one * branch
    normed_two, inverse_two = layer_norm(middle)
    mlp_in = (normed_two * (1.0 + scale_two) + shift_two).astype(jnp.bfloat16)
    mlp_all = lax.all_gather(mlp_in, "head", axis=0, tiled=True)
    hidden_pre = jnp.dot(mlp_all, fc1_weight, preferred_element_type=jnp.float32) + fc1_bias.astype(
        jnp.float32
    )
    hidden_act = smooth_gate(hidden_pre).astype(jnp.bfloat16)
    part_rows = hidden_act
    mlp_out = lax.psum_scatter(
        jnp.dot(part_rows, fc2_weight, preferred_element_type=jnp.float32).astype(jnp.bfloat16),
        "head",
        scatter_dimension=0,
        tiled=True,
    ).astype(jnp.float32) + fc2_bias.astype(jnp.float32)
    output = (middle + gamma_two * mlp_out).astype(jnp.bfloat16)
    upstream = cotangent.astype(jnp.float32)
    grad_gamma_two = upstream * mlp_out
    grad_mlp = (upstream * gamma_two).astype(jnp.bfloat16)
    grad_mlp_all = lax.all_gather(grad_mlp, "head", axis=0, tiled=True)
    grad_act = jnp.einsum("rd,fd->rf", grad_mlp_all, fc2_weight, preferred_element_type=jnp.float32)
    grad_hidden = gelu_back(hidden_pre, grad_act).astype(jnp.bfloat16)
    up_grad = jnp.einsum("rd,rf->df", mlp_all, grad_hidden, preferred_element_type=jnp.float32)
    down_grad = jnp.einsum(
        "rf,rd->df", hidden_act, grad_mlp_all, preferred_element_type=jnp.float32
    )
    upbias_part = jnp.sum(grad_hidden.astype(jnp.float32), axis=0)
    upbias_grad = lax.dynamic_update_slice(
        jnp.zeros((hidden_total,), jnp.float32),
        upbias_part,
        (lax.axis_index("head") * hidden_here,),
    )
    part_rows = grad_hidden
    grad_mlp_in = lax.psum_scatter(
        jnp.einsum("rf,df->rd", part_rows, fc1_weight, preferred_element_type=jnp.float32).astype(
            jnp.bfloat16
        ),
        "head",
        scatter_dimension=0,
        tiled=True,
    ).astype(jnp.float32)
    grad_middle = upstream + norm_back(grad_mlp_in * (1.0 + scale_two), normed_two, inverse_two)
    grad_scale_two = grad_mlp_in * normed_two
    grad_gamma_one = grad_middle * branch
    grad_branch = (grad_middle * gamma_one).astype(jnp.bfloat16)
    proj_grad = jnp.einsum("re,rd->ed", attn_rows, grad_branch, preferred_element_type=jnp.float32)
    grad_attn = jnp.einsum(
        "rd,ed->re", grad_branch, proj_weight, preferred_element_type=jnp.float32
    ).astype(jnp.bfloat16)
    outbound = grad_attn[row_order].reshape(data_size, send_rows, head_size, slice_width)
    inbound = lax.all_to_all(
        lax.all_to_all(outbound, "dp", split_axis=0, concat_axis=0, tiled=True),
        "head",
        split_axis=2,
        concat_axis=1,
        tiled=True,
    )
    pack_grad = (
        jnp.zeros((pack_len, slice_width), jnp.bfloat16)
        .at[slot_of]
        .set(inbound.reshape(pack_len, slice_width))
    )
    pack_grad = pack_grad.reshape(pack_len, heads_here, head_dim)

    def attend_back(running, block_index):
        key_acc, value_acc = running
        first_row = block_index * query_rows
        query_part, scores = block_scores(first_row)
        weights_f = jnp.exp(scores - block_lse[block_index][:, :, None])
        grad_out = lax.dynamic_slice_in_dim(pack_grad, first_row, query_rows, 0)
        grad_weights = jnp.einsum(
            "qhd,khd->hqk", grad_out, pack_value, preferred_element_type=jnp.float32
        )
        row_dot = jnp.sum(weights_f * grad_weights, axis=-1, keepdims=True)
        grad_scores = (weights_f * (grad_weights - row_dot)).astype(jnp.bfloat16)
        grad_query = jnp.einsum(
            "hqk,khd->qhd", grad_scores, pack_key, preferred_element_type=jnp.float32
        ).astype(jnp.bfloat16)
        key_acc = key_acc + jnp.einsum(
            "hqk,qhd->khd", grad_scores, query_part, preferred_element_type=jnp.float32
        )
        value_acc = value_acc + jnp.einsum(
            "hqk,qhd->khd",
            weights_f.astype(jnp.bfloat16),
            grad_out,
            preferred_element_type=jnp.float32,
        )
        return ((key_acc, value_acc), grad_query)

    zero_state = jnp.zeros((pack_len, heads_here, head_dim), jnp.float32)
    (key_acc, value_acc), query_grads = lax.scan(
        attend_back, (zero_state, zero_state), jnp.arange(block_count)
    )
    pack_grads = jnp.stack(
        [
            query_grads.reshape(pack_len, slice_width),
            key_acc.reshape(pack_len, slice_width).astype(jnp.bfloat16),
            value_acc.reshape(pack_len, slice_width).astype(jnp.bfloat16),
        ],
        axis=1,
    )
    departing = pack_grads[slot_of].reshape(data_size, head_size, send_rows, 3, 1, slice_width)
    homecoming = lax.all_to_all(
        lax.all_to_all(departing, "dp", split_axis=0, concat_axis=0, tiled=True),
        "head",
        split_axis=1,
        concat_axis=4,
        tiled=True,
    )
    row_grads = (
        jnp.zeros((row_count, 3, model_width), jnp.bfloat16)
        .at[row_order]
        .set(homecoming.reshape(row_count, 3, model_width))
    )
    grad_sent_query = row_grads[:, 0].astype(jnp.float32).reshape(row_count, heads_all, head_dim)
    grad_log = jnp.sum(grad_sent_query * query_unit * temper, axis=(0, 2))
    grad_query_pre = (
        unit_back(grad_sent_query * temper, query_unit, query_inv)
        .reshape(row_count, model_width)
        .astype(jnp.bfloat16)
    )
    grad_sent_key = row_grads[:, 1].astype(jnp.float32).reshape(row_count, heads_all, head_dim)
    grad_key_pre = (
        unit_back(grad_sent_key, key_unit, key_inv)
        .reshape(row_count, model_width)
        .astype(jnp.bfloat16)
    )
    grad_value = row_grads[:, 2]
    grad_qkv = jnp.stack([grad_query_pre, grad_key_pre, grad_value], axis=1)
    qkv_grad = jnp.einsum("re,rtd->ted", attn_in, grad_qkv, preferred_element_type=jnp.float32)
    grad_attn_in = jnp.einsum(
        "rtd,ted->re", grad_qkv, qkv_weight, preferred_element_type=jnp.float32
    )
    tokens_grad = grad_middle + norm_back(grad_attn_in * (1.0 + scale_one), normed_one, inverse_one)
    grad_mod = jnp.concatenate(
        [
            grad_gamma_one,
            grad_gamma_two,
            grad_attn_in * normed_one,
            grad_scale_two,
            grad_attn_in,
            grad_mlp_in,
        ],
        axis=1,
    )
    item_grad = jax.ops.segment_sum(grad_mod, row_item, num_segments=item_count)
    item_sums = lax.psum_scatter(item_grad[None], ("dp", "head"), scatter_dimension=2, tiled=True)
    item_low = item_sums[0].astype(jnp.bfloat16)
    ada_grad = jnp.einsum("ie,ic->ec", silu_cond, item_low, preferred_element_type=jnp.float32)
    ada_bias_grad = jnp.sum(item_low.astype(jnp.float32), axis=0)
    qkv_head, proj_head = (
        lax.psum_scatter(
            qkv_grad.astype(jnp.bfloat16), "head", scatter_dimension=1, tiled=True
        ).astype(jnp.float32),
        lax.psum_scatter(
            proj_grad[None].astype(jnp.bfloat16), "head", scatter_dimension=1, tiled=True
        ).astype(jnp.float32),
    )
    bias_totals = lax.psum(
        (
            jnp.sum(grad_query_pre.astype(jnp.float32), axis=0),
            jnp.sum(grad_value.astype(jnp.float32), axis=0),
            grad_log,
            jnp.sum(grad_branch.astype(jnp.float32), axis=0),
            upbias_grad,
            jnp.sum(grad_mlp.astype(jnp.float32), axis=0),
        ),
        ("dp", "head"),
    )
    up_part, down_part, qkv_part, proj_part = (
        lax.psum_scatter(
            up_grad.astype(jnp.bfloat16), "dp", scatter_dimension=0, tiled=True
        ).astype(jnp.float32),
        lax.psum_scatter(
            down_grad.astype(jnp.bfloat16), "dp", scatter_dimension=0, tiled=True
        ).astype(jnp.float32),
        lax.psum_scatter(
            qkv_head.astype(jnp.bfloat16), "dp", scatter_dimension=2, tiled=True
        ).astype(jnp.float32),
        lax.psum_scatter(
            proj_head.astype(jnp.bfloat16), "dp", scatter_dimension=2, tiled=True
        ).astype(jnp.float32),
    )
    fc1_bias_grad = lax.dynamic_slice_in_dim(
        bias_totals[4], lax.axis_index("head") * hidden_here, hidden_here, 0
    )
    return (
        output,
        tokens_grad,
        ada_grad,
        ada_bias_grad,
        qkv_part,
        bias_totals[0],
        bias_totals[1],
        bias_totals[2],
        proj_part[0],
        bias_totals[3],
        up_part,
        fc1_bias_grad,
        down_part.T,
        bias_totals[5],
    )


def solution(mesh):
    in_specs = (
        P(("dp", "head"), None),
        P(("dp", "head"), None),
        P(),
        P(),
        P(),
        P(),
        P(),
        P(),
        P(),
        P(),
        P(),
        P(None, "head"),
        P("head"),
        P("head", None),
        P(),
        P(),
        P(),
        P("dp", None),
        P(("dp", "head")),
    )
    out_specs = (
        P(("dp", "head"), None),
        P(("dp", "head"), None),
        P(None, ("dp", "head")),
        P(("dp", "head")),
        P(None, "head", "dp"),
        P(),
        P(),
        P(),
        P("head", "dp"),
        P(),
        P("dp", "head"),
        P("head"),
        P("head", "dp"),
        P(),
    )
    return jax.shard_map(shards, mesh=mesh, in_specs=in_specs, out_specs=out_specs, check_vma=False)
```

profile of v0, /device:TPU:0, one launch (start us, length us, event | category | flops | bytes accessed | tf_op | source)
XLA Modules:
  0.0 1649.0 jit_solution(6318943352430728249)
XLA Ops:
  112.7 27.5 %all-to-all-done.2 = bf16[8,48,3,4,256]{4,3,1,2,0:T(4,128)(2,1)} async-done(((bf16[8,48,3,4,256]{4,3,1,2,0:T(4,128)(2,1)}), bf16[8,48,3,4,256]{4,3,1,2,0:T(4,128)(2,1)}, u32[]{:S(2)}, u32[]{:S(2)}) %all-to-all-start.2) | async-done | bytes 2359328 | tf_op jit(solution)/shard_map/all_to_all | solution.py:117
  156.6 48.5 %all-to-all-done.3 = bf16[8,48,3,4,256]{4,1,0,2,3:T(8,128)(2,1)} async-done(((bf16[8,48,3,4,256]{4,1,0,2,3:T(8,128)(2,1)}), bf16[8,48,3,4,256]{4,1,0,2,3:T(8,128)(2,1)}, u32[]{:S(2)}, u32[]{:S(2)}) %all-to-all-start.3) | async-done | bytes 2359328 | tf_op jit(solution)/shard_map/all_to_all | solution.py:116
  207.0 13.1 copy.225
  222.7 167.3 %scatter_fusion = bf16[1536,3,256]{2,1,0:T(4,128)(2,1)} fusion(bf16[1536,3,256]{2,1,0:T(4,128)(2,1)} %broadcast_in_dim.91, s32[1536]{0:T(1024)S(1)} %fusion.89, bf16[1536,3,256]{2,1,0:T(4,128)(2,1)} %copy.225), kind=kCustom, calls=%fused_computation.7 | custom fusion | bytes 7084032 | tf_op jit(solution)/shard_map/scatter | solution.py:135
  390.0 9.6 fusion.103
  413.3 73.8 %while.27 = (s32[]{:T(128)}, bf16[3,512,4,64]{1,3,2,0:T(8,128)(2,1)}, f32[3,4,512]{2,1,0:T(4,128)S(1)}, s32[3]{0:T(128)S(1)}, s32[1536]{0:T(1024)S(1)}, /*index=...) while((s32[]{:T(128)}, ...), condition=%wide.region_12.13_spmd, body=%wide.region_9.12_spmd.sunk | while | flops 836106240 | bytes 43094236 | solution.py:169
  501.5 17.2 %all_to_all.94 = bf16[8,4,48,1,256]{4,1,2,3,0:T(4,128)(2,1)S(1)} all-to-all(bf16[8,4,48,1,256]{4,1,2,3,0:T(4,128)(2,1)S(1)} %copy.231), channel_id=1, replica_groups=mesh['dp'=8,'head'=4] {'dp'}, dimensions={0} | all-to-all | bytes 1572864 | tf_op jit(solution)/shard_map/all_to_all | solution.py:173
  524.0 19.7 %all-to-all-done.5 = bf16[8,4,48,1,256]{4,2,0,3,1:T(8,128)(2,1)} async-done(((bf16[8,4,48,1,256]{4,2,0,3,1:T(8,128)(2,1)}), bf16[8,4,48,1,256]{4,2,0,3,1:T(8,128)(2,1)}, u32[]{:S(2)}, u32[]{:S(2)}) %all-to-all-start.5) | async-done | bytes 786464 | tf_op jit(solution)/shard_map/all_to_all | solution.py:172
  561.1 60.8 %all-gather.3.cloned.1.call-done = bf16[1536,1024]{1,0:T(8,128)(2,1)} async-done(((bf16[384,1024]{1,0:T(8,128)(2,1)}), bf16[1536,1024]{1,0:T(8,128)(2,1)}) %all-gather.3.cloned.1.call-update) | async-done | bytes 3145744 | tf_op jit(solution)/shard_map/all_gather | solution.py:190
  621.9 8.6 fusion.105
  630.5 55.7 %all-gather.5.cloned.1.call-done = bf16[1536,1024]{1,0:T(8,128)(2,1)} async-done(((bf16[384,1024]{1,0:T(8,128)(2,1)}), bf16[1536,1024]{1,0:T(8,128)(2,1)}) %all-gather.5.cloned.1.call-update) | async-done | bytes 3145744 | tf_op jit(solution)/shard_map/all_gather | solution.py:206
  686.2 11.8 convert_reduce_fusion
  704.9 8.7 convolution_convert_fusion.2
  714.2 49.7 %reduce-scatter.16.cloned.1.call-done = bf16[384,1024]{1,0:T(8,128)(2,1)} async-done(((bf16[1536,1024]{1,0:T(8,128)(2,1)}), bf16[384,1024]{1,0:T(8,128)(2,1)}) %reduce-scatter.16.cloned.1.call-update) | async-done | bytes 786448 | tf_op jit(solution)/shard_map/reduce_scatter | solution.py:220
  766.1 60.3 %reduce-scatter.14.cloned.1.call-done = bf16[384,1024]{1,0:T(8,128)(2,1)} async-done(((bf16[1536,1024]{1,0:T(8,128)(2,1)}), bf16[384,1024]{1,0:T(8,128)(2,1)}) %reduce-scatter.14.cloned.1.call-update) | async-done | bytes 786448 | tf_op jit(solution)/shard_map/reduce_scatter | solution.py:196
  836.5 16.0 all_to_all.95
  857.2 19.5 %all-to-all-done.7 = bf16[8,48,4,256]{3,1,0,2:T(8,128)(2,1)S(1)} async-done(((bf16[8,48,4,256]{3,1,0,2:T(8,128)(2,1)}), bf16[8,48,4,256]{3,1,0,2:T(8,128)(2,1)S(1)}, u32[]{:S(2)}, u32[]{:S(2)}) %all-to-all-start.7) | async-done | bytes 786464 | tf_op jit(solution)/shard_map/all_to_all | solution.py:237
  886.3 97.6 %while.28 = (s32[]{:T(128)}, f32[1536,4,64]{0,2,1:T(8,128)}, f32[1536,4,64]{0,2,1:T(8,128)}, bf16[3,512,4,64]{1,3,2,0:T(8,128)(2,1)}, s32[3]{0:T(128)S(1)}, /*in...) while((s32[]{:T(128)}, f32[1536,4,64]{0,2,1:T(8,128)}, ...), condition=%wide.region_23.24_spmd.clone, body=%wide.region_21.23_spmd.clone.sunk | while | flops 2055075840 | bytes 132739512 | solution.py:277
  1008.0 9.6 gather_fusion.6
  1020.0 31.9 %all_to_all.96 = bf16[8,4,48,3,1,256]{5,2,1,3,4,0:T(8,128)(2,1)S(1)} all-to-all(bf16[8,4,48,3,1,256]{5,2,1,3,4,0:T(8,128)(2,1)S(1)} %copy.243), channel_id=1, replica_groups=mesh['dp'=8,'head'=4] {'dp'}, dimensions={0} | all-to-all | bytes 4718592 | tf_op jit(solution)/shard_map/all_to_all | solution.py:290
  1060.9 84.4 %all-to-all-done.9 = bf16[8,4,48,3,1,256]{5,2,0,3,4,1:T(8,128)(2,1)} async-done(((bf16[8,4,48,3,1,256]{5,2,0,3,4,1:T(8,128)(2,1)}), bf16[8,4,48,3,1,256]{5,2,0,3,4,1:T(8,128)(2,1)}, u32[]{:S(2)}, u32[]{:S(2)}) %all-to-all-start.9) | async-done | bytes 2359328 | tf_op jit(solution)/shard_map/all_to_all | solution.py:289
  1160.3 49.9 %scatter_fusion.1 = bf16[384,3,1024]{2,1,0:T(4,128)(2,1)} fusion(bf16[384,3,1024]{2,1,0:T(4,128)(2,1)} %broadcast_in_dim.140, s32[384]{0:T(512)S(1)} %copy-done.67, bf16[384,3,1024]{2,1,0:T(4,128)(2,1)} %reshape.654), kind=kCustom, calls=%fused_computation.10 | custom fusion | bytes 7079424 | tf_op jit(solution)/shard_map/scatter | solution.py:299
  1210.2 9.2 fusion.102
  1257.1 9.1 convolution_convert_fusion.3
  1298.0 15.0 scatter_custom_fusion.4
  1318.1 47.3 %reduce-scatter.18.cloned.1.call-done = bf16[3,256,1024]{1,2,0:T(8,128)(2,1)} async-done(((bf16[3,1024,1024]{1,2,0:T(8,128)(2,1)}), bf16[3,256,1024]{1,2,0:T(8,128)(2,1)}) %reduce-scatter.18.cloned.1.call-update) | async-done | bytes 1572880 | tf_op jit(solution)/shard_map/reduce_scatter | solution.py:338
  1365.8 45.0 %reduce-scatter.26.cloned.1.call-done = bf16[128,1024]{1,0:T(8,128)(2,1)} async-done(((bf16[1024,1024]{1,0:T(8,128)(2,1)}), bf16[128,1024]{1,0:T(8,128)(2,1)}) %reduce-scatter.26.cloned.1.call-update) | async-done | bytes 262160 | tf_op jit(solution)/shard_map/reduce_scatter | solution.py:360
  1412.8 42.5 %reduce-scatter.24.cloned.1.call-done = bf16[128,1024]{1,0:T(8,128)(2,1)} async-done(((bf16[1024,1024]{1,0:T(8,128)(2,1)}), bf16[128,1024]{1,0:T(8,128)(2,1)}) %reduce-scatter.24.cloned.1.call-update) | async-done | bytes 262160 | tf_op jit(solution)/shard_map/reduce_scatter | solution.py:357
  1457.1 35.8 %reduce-scatter.30.cloned.1.call-done = bf16[128,256]{1,0:T(8,128)(2,1)} async-done(((bf16[1024,256]{1,0:T(8,128)(2,1)}), bf16[128,256]{1,0:T(8,128)(2,1)}) %reduce-scatter.30.cloned.1.call-update) | async-done | bytes 65552
  1494.8 40.4 %all-reduce = (f32[1024]{0:T(1024)}, f32[1024]{0:T(1024)}, f32[16]{0:T(128)}, f32[1024]{0:T(1024)}, f32[4096]{0:T(1024)S(1)}, /*index=5*/f32[1024]{0:T(1024)}) all-reduce(f32[1024]{0:T(1024)S(1)} %get-tuple-element.357, f32[1024]{0:T(1024)S(1)} %get-tuple-element.355, ...), channel_id=1, replica_groups=mesh['dp'=8,'head'=4] {'dp','head'}, use_global_device_ids=true, to_apply=%region_35.36 | all-reduce | flops 8208 | bytes 65664 | tf_op jit(solution)/shard_map/psum | solution.py:345
  1535.8 63.8 %reduce-scatter.28.cloned.1.call-done = f32[192,32]{1,0:T(8,128)} async-done(((f32[6144,32]{1,0:T(8,128)}), f32[192,32]{1,0:T(8,128)}) %reduce-scatter.28.cloned.1.call-update) | async-done | bytes 24592
  1602.5 38.0 %reduce-scatter.20.cloned.1.call-done = bf16[3,256,128]{1,2,0:T(8,128)(2,1)} async-done(((bf16[3,256,1024]{1,2,0:T(8,128)(2,1)}), bf16[3,256,128]{1,2,0:T(8,128)(2,1)}) %reduce-scatter.20.cloned.1.call-update) | async-done | bytes 196624 | tf_op jit(solution)/shard_map/reduce_scatter | solution.py:363
  (446 shorter events, 507.4 us)
Async XLA Ops:
  7.2 679.1 %copy-start = (bf16[1024,1024]{1,0:T(8,128)(2,1)S(1)}, bf16[1024,1024]{1,0:T(8,128)(2,1)}, u32[]{:S(2)}) copy-start(bf16[1024,1024]{1,0:T(8,128)(2,1)} %param.36) | copy-start | bytes 6291460
  14.2 73.1 %copy-start.62 = (s32[1024]{0:T(1024)}, s32[1024]{0:T(1024)S(1)}, u32[]{:S(2)}) copy-start(s32[1024]{0:T(1024)S(1)} %get-tuple-element.387) | copy-start | bytes 12292
  18.7 87.6 %all-to-all-start = ((s32[8,1,192]{2,1,0:T(1,128)}), s32[8,1,192]{2,1,0:T(1,128)S(1)}, u32[]{:S(2)}, u32[]{:S(2)}) async-start(s32[8,1,192]{2,1,0:T(1,128)} %reshape.672), calls=%async_computation | async-start | bytes 16384 | tf_op jit(solution)/shard_map/all_to_all | solution.py:124
  25.5 53.5 %copy-start.58 = (f32[1024]{0:T(1024)}, f32[1024]{0:T(1024)S(1)}, u32[]{:S(2)}) copy-start(f32[1024]{0:T(1024)S(1)} %convert_element_type.238) | copy-start | bytes 12292
  106.3 33.9 %all-to-all-start.2 = ((bf16[8,48,3,4,256]{4,3,1,2,0:T(4,128)(2,1)}), bf16[8,48,3,4,256]{4,3,1,2,0:T(4,128)(2,1)}, u32[]{:S(2)}, u32[]{:S(2)}) async-start(bf16[8,48,3,4,256]{4,3,1,2,0:T(4,128)(2,1)} %copy.222), calls=%async_computation.2 | async-start | bytes 4718592 | tf_op jit(solution)/shard_map/all_to_all | solution.py:117
  140.2 10.5 all-to-all-start.1
  150.6 54.4 %all-to-all-start.3 = ((bf16[8,48,3,4,256]{4,1,0,2,3:T(8,128)(2,1)}), bf16[8,48,3,4,256]{4,1,0,2,3:T(8,128)(2,1)}, u32[]{:S(2)}, u32[]{:S(2)}) async-start(bf16[8,48,3,4,256]{4,1,0,2,3:T(8,128)(2,1)} %copy.223), calls=%async_computation.3 | async-start | bytes 4718592 | tf_op jit(solution)/shard_map/all_to_all | solution.py:116
  156.6 66.1 %copy-start.51 = (s32[1536]{0:T(1024)}, s32[1536]{0:T(1024)S(1)}, u32[]{:S(2)}) copy-start(s32[1536]{0:T(1024)S(1)} %fusion.89) | copy-start | bytes 18436
  156.6 337.6 %copy-start.49 = (s32[2048]{0:T(1024)}, s32[2048]{0:T(1024)S(1)}, u32[]{:S(2)}) copy-start(s32[2048]{0:T(1024)S(1)} %pad_clamp_fusion) | copy-start | bytes 24580
  519.7 24.0 %all-to-all-start.5 = ((bf16[8,4,48,1,256]{4,2,0,3,1:T(8,128)(2,1)}), bf16[8,4,48,1,256]{4,2,0,3,1:T(8,128)(2,1)}, u32[]{:S(2)}, u32[]{:S(2)}) async-start(bf16[8,4,48,1,256]{4,2,0,3,1:T(8,128)(2,1)} %copy.232), calls=%async_computation.5 | async-start | bytes 1572864 | tf_op jit(solution)/shard_map/all_to_all | solution.py:172
  523.9 98.0 %all-gather.3.cloned.1.call-start = ((), (), s32[]{:S(2)}) async-start(), calls=%async_computation.19 | async-start | bytes 3932160 | tf_op jit(solution)/shard_map/all_gather | solution.py:190
  555.2 271.2 %copy-start.45 = (f32[384]{0:T(512)}, f32[384]{0:T(512)S(1)}, u32[]{:S(2)}) copy-start(f32[384]{0:T(512)S(1)} %broadcast_multiply_fusion.4) | copy-start | bytes 4612
  555.5 270.8 %copy-start.52 = (f32[384]{0:T(512)}, f32[384]{0:T(512)S(1)}, u32[]{:S(2)}) copy-start(f32[384]{0:T(512)S(1)} %add_rsqrt_fusion.2) | copy-start | bytes 4612
  560.3 125.9 %all-gather.5.cloned.1.call-start = ((), (), s32[]{:S(2)}) async-start(), calls=%async_computation.21 | async-start | bytes 3932160 | tf_op jit(solution)/shard_map/all_gather | solution.py:206
  561.0 202.8 %reduce-scatter.16.cloned.1.call-start = ((), (), s32[]{:S(2)}) async-start(), calls=%async_computation.22 | async-start | bytes 3932160 | tf_op jit(solution)/shard_map/reduce_scatter | solution.py:220
  561.1 143.8 %copy-start.74 = (f32[1024]{0:T(1024)}, f32[1024]{0:T(1024)S(1)}, u32[]{:S(2)}) copy-start(f32[1024]{0:T(1024)S(1)} %convert_element_type.245) | copy-start | bytes 12292
  704.8 121.5 %reduce-scatter.14.cloned.1.call-start = ((), (), s32[]{:S(2)}) async-start(), calls=%async_computation.20 | async-start | bytes 3932160 | tf_op jit(solution)/shard_map/reduce_scatter | solution.py:196
  714.2 117.6 %copy-start.54 = (f32[1024]{0:T(1024)}, f32[1024]{0:T(1024)S(1)}, u32[]{:S(2)}) copy-start(f32[1024]{0:T(1024)S(1)} %convert_element_type.249) | copy-start | bytes 12292
  853.4 23.2 %all-to-all-start.7 = ((bf16[8,48,4,256]{3,1,0,2:T(8,128)(2,1)}), bf16[8,48,4,256]{3,1,0,2:T(8,128)(2,1)S(1)}, u32[]{:S(2)}, u32[]{:S(2)}) async-start(bf16[8,48,4,256]{3,1,0,2:T(8,128)(2,1)} %copy.235), calls=%async_computation.9 | async-start | bytes 1572864 | tf_op jit(solution)/shard_map/all_to_all | solution.py:237
  1053.5 91.8 %all-to-all-start.9 = ((bf16[8,4,48,3,1,256]{5,2,0,3,4,1:T(8,128)(2,1)}), bf16[8,4,48,3,1,256]{5,2,0,3,4,1:T(8,128)(2,1)}, u32[]{:S(2)}, u32[]{:S(2)}) async-start(bf16[8,4,48,3,1,256]{5,2,0,3,4,1:T(8,128)(2,1)} %copy.244), calls=%async_computation.11 | async-start | bytes 4718592 | tf_op jit(solution)/shard_map/all_to_all | solution.py:289
  1058.1 221.7 %reduce-scatter.22.cloned.1.call-start = ((), (), s32[]{:S(2)}) async-start(), calls=%async_computation.25 | async-start | bytes 2621440 | tf_op jit(solution)/shard_map/reduce_scatter | solution.py:341
  1060.8 304.6 %reduce-scatter.18.cloned.1.call-start = ((), (), s32[]{:S(2)}) async-start(), calls=%async_computation.23 | async-start | bytes 7864320 | tf_op jit(solution)/shard_map/reduce_scatter | solution.py:338
  1256.5 154.3 %reduce-scatter.26.cloned.1.call-start = ((), (), s32[]{:S(2)}) async-start(), calls=%async_computation.27 | async-start | bytes 2359296 | tf_op jit(solution)/shard_map/reduce_scatter | solution.py:360
  1266.2 189.1 %reduce-scatter.24.cloned.1.call-start = ((), (), s32[]{:S(2)}) async-start(), calls=%async_computation.26 | async-start | bytes 2359296 | tf_op jit(solution)/shard_map/reduce_scatter | solution.py:357
  1273.9 218.9 %reduce-scatter.30.cloned.1.call-start = ((), (), s32[]{:S(2)}) async-start(), calls=%async_computation.29 | async-start | bytes 589824
  1283.2 316.5 %reduce-scatter.28.cloned.1.call-start = ((), (), s32[]{:S(2)}) async-start(), calls=%async_computation.28 | async-start | bytes 3244032
  1318.0 322.5 %reduce-scatter.20.cloned.1.call-start = ((), (), s32[]{:S(2)}) async-start(), calls=%async_computation.24 | async-start | bytes 1769472 | tf_op jit(solution)/shard_map/reduce_scatter | solution.py:363
  1365.4 129.4 %copy-start.68 = (f32[1024]{0:T(1024)S(1)}, f32[1024]{0:T(1024)}, u32[]{:S(2)}) copy-start(f32[1024]{0:T(1024)} %get-tuple-element.348) | copy-start | bytes 12292
  1365.4 129.4 %copy-start.69 = (f32[1024]{0:T(1024)S(1)}, f32[1024]{0:T(1024)}, u32[]{:S(2)}) copy-start(f32[1024]{0:T(1024)} %get-tuple-element.352) | copy-start | bytes 12292
  1365.4 235.8 %copy-start.32 = (bf16[32,1024]{1,0:T(8,128)(2,1)S(1)}, bf16[32,1024]{1,0:T(8,128)(2,1)}, u32[]{:S(2)}) copy-start(bf16[32,1024]{1,0:T(8,128)(2,1)} %copy-done.31) | copy-start | bytes 196612
  1365.4 235.8 %copy-start.73 = (pred[32]{0:T(512)(128)(4,1)S(1)}, pred[32]{0:T(512)(128)(4,1)}, u32[]{:S(2)}) copy-start(pred[32]{0:T(512)(128)(4,1)} %copy-done.72) | copy-start | bytes 100
  1365.5 276.8 %copy-start.1 = (bf16[1024,1024]{1,0:T(8,128)(2,1)S(1)}, bf16[1024,1024]{1,0:T(8,128)(2,1)}, u32[]{:S(2)}) copy-start(bf16[1024,1024]{1,0:T(8,128)(2,1)} %param.36) | copy-start | bytes 6291460
  (79 other events, 606.3 us)
Sparse Core Ops, SparseCore 0:
  560.4 61.4 all-gather.2
  624.1 62.1 all-gather.4
  704.9 58.8 reduce-scatter.15
  766.0 60.2 reduce-scatter.13
  1061.0 77.9 reduce-scatter.21
  1256.6 108.7 reduce-scatter.17
  1369.0 41.7 reduce-scatter.25
  1414.1 41.1 reduce-scatter.23
  1458.7 34.1 reduce-scatter.29
  1498.2 101.4 reduce-scatter.27
  1603.0 37.4 reduce-scatter.19
where the time goes:
time: 1670 us; the launch traced here: 1650 us
  waiting for transfers between devices  702 us (42%)
  local copies, waits for them, and re-layouts  452 us (27%)
  matrix products  194 us (12%)
  other arithmetic  138 us (8%)
  blocking collectives  106 us (6%)
  starting transfers between devices  32.5 us (2%)
    scatter x1, local copies, waits for them, and re-layouts, shards(): pack_qkv = jnp.zeros((pack_len, 3, slice_width), jnp.bfloat16).at[slot_of...  167 us
    unnamed x13, waiting for transfers between devices  100 us
    all_to_all x1, waiting for transfers between devices, shards(): lax.all_to_all(lax.all_to_all(departing, 'dp', split_axis=0, concat_axis=...  84.4 us
    all_gather x1, waiting for transfers between devices, shards(): mlp_all = lax.all_gather(mlp_in, 'head', axis=0, tiled=True)  60.8 us
    reduce_scatter x1, waiting for transfers between devices, shards(): lax.psum_scatter(jnp.dot(part_rows, fc2_weight, preferred_element_type=jn...  60.3 us
    all_gather x1, waiting for transfers between devices, shards(): grad_mlp_all = lax.all_gather(grad_mlp, 'head', axis=0, tiled=True)  55.7 us
    scatter x1, local copies, waits for them, and re-layouts, shards(): row_grads = jnp.zeros((row_count, 3, model_width), jnp.bfloat16).at[row_o...  49.9 us
    reduce_scatter x1, waiting for transfers between devices, shards(): lax.psum_scatter(jnp.einsum('rf,df->rd', part_rows, fc1_weight, preferred...  49.7 us
  transfers between devices with their start and end apart: 18, of which 16 were waited for; matrix products, arithmetic and copies ran while one was open for 17% of the time, Pallas kernels for 0%

commit v1 on v0

v1 whole, which is shorter than its diff:
```python
import functools

import jax
import jax.numpy as jnp
from jax import lax
from jax.experimental import pallas as pl
from jax.experimental.pallas import tpu as pltpu
from jax.sharding import Mesh, PartitionSpec as P

BF = jnp.bfloat16
F32 = jnp.float32


def layer_norm(values):
    centre = values - jnp.mean(values, axis=-1, keepdims=True)
    inverse = lax.rsqrt(jnp.mean(centre * centre, axis=-1, keepdims=True) + 1e-06)
    return (centre * inverse, inverse)


def norm_back(gradient, normed, inverse):
    return inverse * (
        gradient
        - jnp.mean(gradient, axis=-1, keepdims=True)
        - normed * jnp.mean(gradient * normed, axis=-1, keepdims=True)
    )


def unit_rows(values):
    inverse = lax.rsqrt(jnp.sum(values * values, axis=-1, keepdims=True) + 1e-06)
    return (values * inverse, inverse)


def unit_back(gradient, unit_vec, inverse):
    return inverse * (gradient - unit_vec * jnp.sum(gradient * unit_vec, axis=-1, keepdims=True))


def smooth_gate(hidden_val):
    return jax.nn.gelu(hidden_val, approximate=True)


def gelu_back(pre_act, gradient):
    return jax.vjp(smooth_gate, pre_act)[1](gradient)[0]


def dot(left, right, dims):
    return lax.dot_general(left, right, (dims, ((), ())), preferred_element_type=F32)


def head_lanes(width, head_dim):
    return lax.broadcasted_iota(jnp.int32, (1, width), 1) // head_dim


def attend_kernel(
    heads, head_dim, block, first_ref, last_ref, lo_ref, hi_ref, q_ref, k_ref, v_ref,
    out_ref, out_t_ref, lse_ref, v_t, acc, total,
):
    pack_len, width = q_ref.shape
    lanes = head_lanes(width, head_dim)
    v_t[...] = v_ref[...].T

    @pl.loop(0, pack_len // block)
    def _(q_block):
        q_rows = pl.ds(pl.multiple_of(q_block * block, block), block)
        q_t = q_ref[q_rows, :].T
        low, high = lo_ref[:, q_rows], hi_ref[:, q_rows]
        acc[...] = jnp.zeros_like(acc)
        total[...] = jnp.zeros_like(total)

        @pl.loop(first_ref[q_block], last_ref[q_block])
        def _(k_block):
            k_rows = pl.ds(pl.multiple_of(k_block * block, block), block)
            keys = k_ref[k_rows, :]
            index = k_block * block + lax.broadcasted_iota(jnp.int32, (block, block), 0)
            seen = (index >= low) & (index < high)
            for h in range(heads):
                own = pl.ds(h * head_dim, head_dim)
                scores = dot(jnp.where(lanes == h, keys, jnp.zeros_like(keys)), q_t, ((1,), (0,)))
                raised = jnp.where(seen, jnp.exp(scores), 0.0)
                total[h : h + 1, :] += jnp.sum(raised, axis=0, keepdims=True)
                acc[own, :] += dot(v_t[own, k_rows], raised.astype(BF), ((1,), (0,)))

        for h in range(heads):
            own = pl.ds(h * head_dim, head_dim)
            acc[own, :] = acc[own, :] / total[h : h + 1, :]
            lse_ref[h : h + 1, q_rows] = jnp.log(total[h : h + 1, :])
        out_t_ref[:, q_rows] = acc[...]
        out_ref[q_rows, :] = acc[...].T.astype(BF)


def attend(first, last, low, high, queries, keys, values, heads, head_dim, block):
    pack_len, width = queries.shape
    smem = pl.BlockSpec(memory_space=pltpu.SMEM)
    vmem = pl.BlockSpec(memory_space=pltpu.VMEM)
    pairs = heads * pack_len * pack_len // 2
    return pl.pallas_call(
        functools.partial(attend_kernel, heads, head_dim, block),
        out_shape=(
            jax.ShapeDtypeStruct((pack_len, width), BF),
            jax.ShapeDtypeStruct((width, pack_len), F32),
            jax.ShapeDtypeStruct((8, pack_len), F32),
        ),
        in_specs=[smem, smem] + [vmem] * 5,
        out_specs=(vmem, vmem, vmem),
        scratch_shapes=[
            pltpu.VMEM((width, pack_len), BF),
            pltpu.VMEM((width, block), F32),
            pltpu.VMEM((8, block), F32),
        ],
        compiler_params=pltpu.CompilerParams(vmem_limit_bytes=40 * 1024 * 1024),
        cost_estimate=pl.CostEstimate(
            flops=4 * pairs * head_dim, bytes_accessed=8 * pack_len * width, transcendentals=pairs
        ),
    )(first, last, low, high, queries, keys, values)


def attend_back_kernel(
    heads, head_dim, block, first_ref, last_ref, lo_ref, hi_ref, q_ref, k_ref, v_ref, g_ref,
    out_t_ref, lse_ref, dq_ref, dk_ref, dv_ref, k_t, dk_acc, dv_acc, acc, sums,
):
    pack_len, width = q_ref.shape
    lanes = head_lanes(width, head_dim)
    k_t[...] = k_ref[...].T
    dk_acc[...] = jnp.zeros_like(dk_acc)
    dv_acc[...] = jnp.zeros_like(dv_acc)

    @pl.loop(0, pack_len // block)
    def _(q_block):
        q_rows = pl.ds(pl.multiple_of(q_block * block, block), block)
        queries, grads = q_ref[q_rows, :], g_ref[q_rows, :]
        q_t, g_t = queries.T, grads.T
        low, high = lo_ref[:, q_rows], hi_ref[:, q_rows]
        weighted = g_t.astype(F32) * out_t_ref[:, q_rows]
        for h in range(heads):
            sums[h : h + 1, :] = jnp.sum(
                weighted[h * head_dim : (h + 1) * head_dim, :], axis=0, keepdims=True
            )
        acc[...] = jnp.zeros_like(acc)

        @pl.loop(first_ref[q_block], last_ref[q_block])
        def _(k_block):
            k_rows = pl.ds(pl.multiple_of(k_block * block, block), block)
            keys, values = k_ref[k_rows, :], v_ref[k_rows, :]
            index = k_block * block + lax.broadcasted_iota(jnp.int32, (block, block), 0)
            seen = (index >= low) & (index < high)
            for h in range(heads):
                own = pl.ds(h * head_dim, head_dim)
                mine = lanes == h
                scores = dot(jnp.where(mine, keys, jnp.zeros_like(keys)), q_t, ((1,), (0,)))
                probs = jnp.where(seen, jnp.exp(scores - lse_ref[h : h + 1, q_rows]), 0.0)
                grad_probs = dot(jnp.where(mine, values, jnp.zeros_like(values)), g_t, ((1,), (0,)))
                grad_scores = (probs * (grad_probs - sums[h : h + 1, :])).astype(BF)
                acc[own, :] += dot(k_t[own, k_rows], grad_scores, ((1,), (0,)))
                dk_acc[k_rows, :] += dot(
                    grad_scores, jnp.where(mine, queries, jnp.zeros_like(queries)), ((1,), (0,))
                )
                dv_acc[k_rows, :] += dot(
                    probs.astype(BF), jnp.where(mine, grads, jnp.zeros_like(grads)), ((1,), (0,))
                )

        dq_ref[q_rows, :] = acc[...].T.astype(BF)

    dk_ref[...] = dk_acc[...].astype(BF)
    dv_ref[...] = dv_acc[...].astype(BF)


def attend_back(
    first, last, low, high, queries, keys, values, grads, out_t, lse, heads, head_dim, block
):
    pack_len, width = queries.shape
    smem = pl.BlockSpec(memory_space=pltpu.SMEM)
    vmem = pl.BlockSpec(memory_space=pltpu.VMEM)
    pairs = heads * pack_len * pack_len // 2
    return pl.pallas_call(
        functools.partial(attend_back_kernel, heads, head_dim, block),
        out_shape=(jax.ShapeDtypeStruct((pack_len, width), BF),) * 3,
        in_specs=[smem, smem] + [vmem] * 8,
        out_specs=(vmem,) * 3,
        scratch_shapes=[
            pltpu.VMEM((width, pack_len), BF),
            pltpu.VMEM((pack_len, width), F32),
            pltpu.VMEM((pack_len, width), F32),
            pltpu.VMEM((width, block), F32),
            pltpu.VMEM((8, block), F32),
        ],
        compiler_params=pltpu.CompilerParams(vmem_limit_bytes=40 * 1024 * 1024),
        cost_estimate=pl.CostEstimate(
            flops=10 * pairs * head_dim, bytes_accessed=16 * pack_len * width, transcendentals=pairs
        ),
    )(first, last, low, high, queries, keys, values, grads, out_t, lse)


def to_packs(rows):
    return lax.all_to_all(rows, ("yy", "head"), split_axis=0, concat_axis=0, tiled=True)


def bits(count):
    steps = []
    while count > 1:
        count //= 2
        steps.append(count)
    return steps


def xor_swap(values, axis, step):
    size = lax.axis_size(axis)
    return lax.ppermute(values, axis, [(i, i ^ step) for i in range(size)])


def xor_gather(block, axis):
    blocks = {0: block}
    for step in bits(lax.axis_size(axis)):
        for k in list(blocks):
            blocks[k ^ step] = xor_swap(blocks[k], axis, step)
    return [blocks[k] for k in range(len(blocks))]


def xor_scatter(blocks, axis):
    blocks = list(blocks)
    for step in reversed(bits(lax.axis_size(axis))):
        blocks = {k: b for k, b in enumerate(blocks)} if isinstance(blocks, list) else blocks
        kept = {}
        for k in blocks:
            if not k & step:
                arrived = xor_swap(blocks[k ^ step], axis, step)
                kept[k] = (blocks[k].astype(F32) + arrived.astype(F32)).astype(blocks[k].dtype)
        blocks = kept
    return blocks[0]


def butterfly(values, axes):
    for axis in axes:
        for step in reversed(bits(lax.axis_size(axis))):
            values = values + xor_swap(values, axis, step)
    return values


def pick(values, index, axis):
    return lax.dynamic_index_in_dim(values, index, axis, keepdims=False)


def xor_blocks(values, axis, dim):
    me = lax.axis_index(axis)
    return [pick(values, me ^ k, dim) for k in range(lax.axis_size(axis))]


def sum_packs(parts):
    half = xor_scatter(xor_blocks(parts, "yy", 0), "yy")
    arrived = lax.all_to_all(half, "head", split_axis=0, concat_axis=0, tiled=True)
    return jnp.sum(arrived.astype(F32), axis=0)


def shards(
    tokens,
    cotangent,
    class_table,
    ada_weight,
    ada_bias,
    qkv_weight,
    q_bias,
    v_bias,
    log_scale,
    proj_weight,
    proj_bias,
    fc1_weight,
    fc1_bias,
    fc2_weight,
    fc2_bias,
    item_lens,
    class_ids,
    section_ids,
    destination,
):
    yy_size = lax.axis_size("yy")
    g_size = lax.axis_size("g")
    head_size = lax.axis_size("head")
    yy, g, z = lax.axis_index("yy"), lax.axis_index("g"), lax.axis_index("head")
    pack = yy * head_size + z
    row_count, model_width = tokens.shape
    heads_all = log_scale.shape[0]
    head_dim = model_width // heads_all
    heads_here = heads_all // g_size
    width = model_width // g_size
    dp_size = yy_size * g_size
    pack_len = row_count * head_size
    seg = row_count // yy_size
    items_pack = item_lens.shape[1]
    block = min(256, pack_len)
    col = model_width // dp_size
    parts = yy_size if col % head_dim == 0 else 1
    sub = width // parts

    def own_cols(values):
        shape = values.shape[:-1]
        return pick(values.reshape(*shape, parts, g_size, sub), g, len(shape) + 1).reshape(
            *shape, width
        )

    row_pack = destination // pack_len
    index = jnp.arange(row_count, dtype=jnp.int32)
    before = (row_pack[None, :] < row_pack[:, None]) | (
        (row_pack[None, :] == row_pack[:, None]) & (index[None, :] < index[:, None])
    )
    slot = jnp.sum(before.astype(jnp.int32), axis=1)
    to_slot = (slot[None, :] == index[:, None]).astype(BF)
    sorted_tokens = dot(to_slot, tokens, ((1,), (0,))).astype(BF)
    sorted_cotangent = dot(to_slot, cotangent, ((1,), (0,))).astype(BF)
    inputs = to_packs(sorted_tokens).astype(F32)
    upstream = to_packs(sorted_cotangent).astype(F32)

    hidden = fc1_weight.shape[1] // g_size
    half = model_width // yy_size
    fc1_own = lax.dynamic_slice(fc1_weight, (yy * half, g * hidden), (half, hidden))
    fc1_bias_own = lax.dynamic_slice(fc1_bias, (g * hidden,), (hidden,))
    fc1_sent = jnp.concatenate(
        [fc1_own, jnp.broadcast_to(fc1_bias_own[None, :], (16, hidden))], axis=0
    )
    fc1_all = lax.all_gather(fc1_sent, ("yy", "head"), axis=0)
    fc1_all = fc1_all.reshape(yy_size, head_size, half + 16, hidden)
    fc1_here = (
        fc1_all[:, :, :half].transpose(0, 2, 1, 3).reshape(model_width, head_size * hidden)
    )
    fc1_bias_here = fc1_all[0, :, half].reshape(head_size * hidden)
    fc2_own = lax.dynamic_slice(fc2_weight, (g * hidden, yy * half), (hidden, half))
    fc2_all = lax.all_gather(fc2_own, ("yy", "head"), axis=0)
    fc2_here = (
        fc2_all.reshape(yy_size, head_size, hidden, half)
        .transpose(1, 2, 0, 3)
        .reshape(head_size * hidden, model_width)
    )

    lens_here = pick(item_lens, pack, 0)
    class_here = pick(class_ids, pack, 0)
    item_index = jnp.arange(items_pack, dtype=jnp.int32)
    order_key = class_here * items_pack + item_index
    item_rank = jnp.sum(
        jnp.where(order_key[None, :] < order_key[:, None], lens_here[None, :], 0), axis=1
    )
    item_pos = jnp.cumsum(lens_here) - lens_here
    item_end = item_rank + lens_here

    def items_of(rank):
        return (rank[:, None] >= item_rank[None, :]) & (rank[:, None] < item_end[None, :])

    rank_all = jnp.arange(pack_len, dtype=jnp.int32)
    member = items_of(rank_all)

    def of_item(values):
        return jnp.sum(jnp.where(member, values[None, :], 0), axis=1)

    section_here = lax.ppermute(
        section_ids[0],
        ("g", "head"),
        [(a * head_size + b, b * head_size + a) for a in range(g_size) for b in range(head_size)],
    )
    position = rank_all - of_item(item_rank - item_pos)
    section_rank = jnp.sum(
        jnp.where(rank_all[None, :] == position[:, None], section_here[None, :], 0), axis=1
    )
    up_to = jnp.sum((section_here[None, :] <= section_rank[:, None]).astype(jnp.int32), axis=1)
    low = of_item(item_rank)
    high = jnp.minimum(up_to + of_item(item_rank - item_pos), of_item(item_end))
    first = low[::block] // block
    last = (high[block - 1 :: block] + block - 1) // block
    low, high = low[None, :], high[None, :]

    row_rank = (
        (jnp.arange(yy_size, dtype=jnp.int32)[:, None] * g_size + g) * seg
        + jnp.arange(seg, dtype=jnp.int32)[None, :]
    ).reshape(row_count)
    row_member = items_of(row_rank)

    class_rows = jnp.take(class_table, class_ids.reshape(-1), axis=0).astype(F32)
    silu_cond = jax.nn.silu(class_rows).astype(BF)
    silu_here = lax.dynamic_slice_in_dim(silu_cond, pack * items_pack, items_pack, 0)
    modulation = jnp.dot(silu_here, ada_weight, preferred_element_type=F32) + ada_bias.astype(F32)

    def mod_part(part):
        values = modulation[:, part * model_width : (part + 1) * model_width]
        rows = jnp.zeros((row_count, model_width), F32)
        for item in range(items_pack):
            rows = jnp.where(row_member[:, item : item + 1], values[item : item + 1], rows)
        return rows

    gamma_one, gamma_two, scale_one, scale_two, shift_one, shift_two = (
        mod_part(part) for part in range(6)
    )

    def rank_order(blocks):
        stacked = jnp.stack(blocks).reshape(g_size, yy_size, seg, -1)
        ordered = jnp.stack([pick(stacked, g ^ k, 0) for k in range(g_size)], axis=1)
        return ordered.reshape(pack_len, -1)

    def xor_order(values):
        by_g = values.reshape(yy_size, g_size, seg, -1)
        ordered = jnp.stack([pick(by_g, g ^ k, 1) for k in range(g_size)])
        return ordered.reshape(pack_len, -1)

    def split_blocks(values):
        return [values[k * row_count : (k + 1) * row_count] for k in range(g_size)]

    normed_one, inverse_one = layer_norm(inputs)
    attn_in = (normed_one * (1.0 + scale_one) + shift_one).astype(BF)
    attn_in_all = jnp.concatenate(xor_gather(attn_in, "g"), axis=0)
    qkv_own = own_cols(qkv_weight)
    query_pre = dot(attn_in_all, qkv_own[0], ((1,), (0,))) + own_cols(q_bias).astype(F32)
    key_pre = dot(attn_in_all, qkv_own[1], ((1,), (0,)))
    value_all = (dot(attn_in_all, qkv_own[2], ((1,), (0,))) + own_cols(v_bias).astype(F32)).astype(BF)

    def by_head(values):
        return values.reshape(pack_len, heads_here, head_dim)

    query_unit, query_inv = unit_rows(by_head(query_pre))
    key_unit, key_inv = unit_rows(by_head(key_pre))
    heads_part = sub // head_dim
    scale_here = pick(log_scale.reshape(parts, g_size, heads_part), g, 1).reshape(heads_here)
    temper = jnp.exp(scale_here)[None, :, None]
    query_all = (query_unit * temper).reshape(pack_len, width).astype(BF)
    key_all = key_unit.reshape(pack_len, width).astype(BF)

    def ranked(values):
        return rank_order(split_blocks(values))

    pack_query, pack_key, pack_value = ranked(query_all), ranked(key_all), ranked(value_all)
    out_rank, out_t, lse = attend(
        first, last, low, high, pack_query, pack_key, pack_value, heads_here, head_dim, block
    )
    leaving = out_rank.reshape(yy_size, g_size, seg, width).transpose(1, 0, 2, 3)
    returned = lax.all_to_all(
        leaving.reshape(g_size, row_count, width), "g", split_axis=0, concat_axis=0, tiled=True
    )
    attn_rows = (
        returned.reshape(g_size, row_count, parts, sub)
        .transpose(1, 2, 0, 3)
        .reshape(row_count, model_width)
    )
    branch = jnp.dot(attn_rows, proj_weight, preferred_element_type=F32) + proj_bias.astype(F32)
    middle = inputs + gamma_one * branch
    normed_two, inverse_two = layer_norm(middle)
    mlp_in = (normed_two * (1.0 + scale_two) + shift_two).astype(BF)

    grad_mlp = (upstream * gamma_two).astype(BF)
    grad_mlp_all = jnp.concatenate(xor_gather(grad_mlp, "g"), axis=0)
    mlp_all = jnp.concatenate(xor_gather(mlp_in, "g"), axis=0)
    hidden_pre = dot(mlp_all, fc1_here, ((1,), (0,))) + fc1_bias_here.astype(F32)
    hidden_act = smooth_gate(hidden_pre).astype(BF)
    grad_act = dot(grad_mlp_all, fc2_here, ((1,), (1,)))
    grad_hidden = gelu_back(hidden_pre, grad_act).astype(BF)
    grad_in_part = dot(grad_hidden, fc1_here, ((1,), (1,))).astype(BF)
    out_part = dot(hidden_act, fc2_here, ((1,), (0,))).astype(BF)
    grad_mlp_in = xor_scatter(split_blocks(grad_in_part), "g").astype(F32)
    mlp_out = xor_scatter(split_blocks(out_part), "g").astype(F32) + fc2_bias.astype(F32)
    output_rows = (middle + gamma_two * mlp_out).astype(BF)
    grad_gamma_two = upstream * mlp_out
    up_grad = dot(mlp_all, grad_hidden, ((0,), (0,))).astype(BF)
    down_grad = dot(hidden_act, grad_mlp_all, ((0,), (0,))).astype(BF)
    up_sum = sum_packs(up_grad.reshape(yy_size, half, head_size, hidden).transpose(0, 2, 1, 3))
    down_sum = sum_packs(down_grad.reshape(head_size, hidden, yy_size, half).transpose(2, 0, 1, 3))
    up_part = lax.all_to_all(
        up_sum.astype(BF).reshape(g_size, half // g_size, hidden), "g", 0, 0, tiled=True
    )
    up_part = up_part.transpose(1, 0, 2).reshape(half // g_size, g_size * hidden).astype(F32)
    down_part = lax.all_to_all(
        down_sum.astype(BF).reshape(hidden, g_size, half // g_size).transpose(1, 0, 2),
        "g",
        0,
        0,
        tiled=True,
    )
    down_part = down_part.reshape(g_size * hidden, half // g_size).astype(F32)

    grad_middle = upstream + norm_back(grad_mlp_in * (1.0 + scale_two), normed_two, inverse_two)
    grad_branch = (grad_middle * gamma_one).astype(BF)
    grad_attn = dot(grad_branch, proj_weight, ((1,), (1,))).astype(BF)
    outbound = (
        grad_attn.reshape(row_count, parts, g_size, sub)
        .transpose(2, 0, 1, 3)
        .reshape(g_size, row_count, width)
    )
    inbound = lax.all_to_all(outbound, "g", split_axis=0, concat_axis=0, tiled=True)
    pack_grad = (
        inbound.reshape(g_size, yy_size, seg, width).transpose(1, 0, 2, 3).reshape(pack_len, width)
    )
    proj_grad = dot(attn_rows, grad_branch, ((0,), (0,))).astype(BF)
    grad_query, grad_key, grad_value = attend_back(
        first, last, low, high, pack_query, pack_key, pack_value, pack_grad, out_t, lse,
        heads_here, head_dim, block,
    )
    grad_query = by_head(xor_order(grad_query)).astype(F32)
    grad_key = by_head(xor_order(grad_key)).astype(F32)
    grad_value = xor_order(grad_value)
    grad_log = jnp.sum(grad_query * query_unit * temper, axis=(0, 2))
    grad_query_pre = (
        unit_back(grad_query * temper, query_unit, query_inv).reshape(pack_len, width).astype(BF)
    )
    grad_key_pre = unit_back(grad_key, key_unit, key_inv).reshape(pack_len, width).astype(BF)
    grad_qkv = jnp.concatenate([grad_query_pre, grad_key_pre, grad_value], axis=1)
    weights_here = jnp.concatenate([qkv_own[0], qkv_own[1], qkv_own[2]], axis=1)
    grad_in_part = dot(grad_qkv, weights_here, ((1,), (1,))).astype(BF)
    grad_attn_in = xor_scatter(split_blocks(grad_in_part), "g").astype(F32)
    qkv_grad = dot(attn_in_all, grad_qkv, ((0,), (0,))).astype(BF)
    tokens_grad_rows = grad_middle + norm_back(
        grad_attn_in * (1.0 + scale_one), normed_one, inverse_one
    )

    def to_data(rows):
        return dot(to_slot, to_packs(rows), ((0,), (0,)))

    output = to_data(output_rows).astype(BF)
    tokens_grad = to_data(tokens_grad_rows.astype(BF))

    grad_mod = jnp.concatenate(
        [
            grad_middle * branch,
            grad_gamma_two,
            grad_attn_in * normed_one,
            grad_mlp_in * normed_two,
            grad_attn_in,
            grad_mlp_in,
        ],
        axis=1,
    )
    item_part = lax.dot_general(
        row_member.astype(F32), grad_mod, (((0,), (0,)), ((), ())), precision=lax.Precision.HIGHEST
    )
    ada_cols = 6 * model_width // (dp_size * head_size)
    item_part = item_part.reshape(items_pack, yy_size, g_size, head_size, ada_cols)
    item_own = xor_scatter(xor_blocks(item_part, "g", 2), "g")
    item_all = lax.all_to_all(
        item_own.reshape(items_pack, yy_size * head_size, ada_cols).transpose(1, 0, 2),
        ("yy", "head"),
        0,
        0,
        tiled=True,
    )
    item_low = item_all.reshape(-1, ada_cols).astype(BF)
    ada_grad = dot(silu_cond, item_low, ((0,), (0,)))
    ada_bias_grad = jnp.sum(item_low.astype(F32), axis=0)

    proj_own = xor_scatter(
        [
            block_cols.reshape(model_width, width)
            for block_cols in xor_blocks(
                proj_grad.reshape(model_width, parts, g_size, sub), "g", 2
            )
        ],
        "g",
    )
    rows_z = model_width // head_size
    if parts == yy_size:
        both = jnp.concatenate(
            [
                proj_own.reshape(1, head_size, rows_z, yy_size, col),
                qkv_grad.reshape(head_size, rows_z, 3, yy_size, col).transpose(2, 0, 1, 3, 4),
            ],
            axis=0,
        )
        summed = sum_packs(both.transpose(3, 1, 0, 2, 4))
        proj_part, qkv_part = summed[0], summed[1:]
    else:
        both = jnp.concatenate(
            [
                proj_own.reshape(1, model_width, width),
                qkv_grad.reshape(model_width, 3, width).transpose(1, 0, 2),
            ],
            axis=0,
        )
        full = lax.dynamic_update_slice(
            jnp.zeros((4, model_width, model_width), BF), both, (0, 0, g * width)
        )
        summed = lax.psum_scatter(full, ("yy", "g"), scatter_dimension=2, tiled=True)
        summed = lax.psum_scatter(summed, "head", scatter_dimension=1, tiled=True).astype(F32)
        proj_part, qkv_part = summed[0], summed[1:]

    def spread(values):
        zero = jnp.zeros((parts, g_size, values.shape[0] // parts), F32)
        return lax.dynamic_update_slice(
            zero, values.reshape(parts, 1, values.shape[0] // parts), (0, g, 0)
        ).reshape(-1)

    def spread_hidden(values):
        zero = jnp.zeros((head_size, g_size, hidden), F32)
        return lax.dynamic_update_slice(
            zero, values.reshape(head_size, 1, hidden), (0, g, 0)
        ).reshape(-1)

    vectors = [
        spread(jnp.sum(grad_query_pre.astype(F32), axis=0)),
        spread(jnp.sum(grad_value.astype(F32), axis=0)),
        spread(grad_log),
        jnp.sum(grad_branch.astype(F32), axis=0),
        spread_hidden(jnp.sum(grad_hidden.astype(F32), axis=0)),
        jnp.sum(grad_mlp.astype(F32), axis=0),
    ]
    joined = jnp.concatenate(vectors)
    filler = -joined.shape[0] % 1024
    joined = jnp.pad(joined, (0, filler)).reshape(-1, 128)
    joined = butterfly(joined, ("yy", "g", "head")).reshape(-1)
    totals, start = [], 0
    for vector in vectors:
        totals.append(joined[start : start + vector.shape[0]])
        start += vector.shape[0]
    fc1_bias_grad = pick(totals[4].reshape(head_size, -1), z, 0)
    return (
        output,
        tokens_grad,
        ada_grad,
        ada_bias_grad,
        qkv_part,
        totals[0],
        totals[1],
        totals[2],
        proj_part,
        totals[3],
        up_part,
        fc1_bias_grad,
        down_part,
        totals[5],
    )


def solution(mesh):
    head_size = mesh.shape["head"]
    dp_size = mesh.shape["dp"]
    inner = Mesh(
        mesh.devices.reshape(dp_size // head_size, head_size, head_size), ("yy", "g", "head")
    )
    dp = ("yy", "g")
    everything = ("yy", "g", "head")
    in_specs = (
        P(everything, None),
        P(everything, None),
        P(),
        P(),
        P(),
        P(),
        P(),
        P(),
        P(),
        P(),
        P(),
        P(None, "head"),
        P("head"),
        P("head", None),
        P(),
        P(),
        P(),
        P(dp, None),
        P(everything),
    )
    out_specs = (
        P(everything, None),
        P(everything, None),
        P(None, everything),
        P(everything),
        P(None, "head", dp),
        P(),
        P(),
        P(),
        P("head", dp),
        P(),
        P(dp, "head"),
        P("head"),
        P("head", dp),
        P(),
    )
    return jax.shard_map(
        shards, mesh=inner, in_specs=in_specs, out_specs=out_specs, check_vma=False
    )
```

time: 1670 us -> 654 us (0.39)
  waiting for transfers between devices: 702 us -> 146 us
  local copies, waits for them, and re-layouts: 452 us -> 169 us
  blocking collectives: 106 us -> 0 us
  matrix products: 194 us -> 93 us
  starting transfers between devices: 32.5 us -> 78.1 us
  Pallas kernels: 0 us -> 44.3 us
  other arithmetic: 138 us -> 97.3 us
    reduce_scatter x7 -> x0, waiting for transfers between devices: 283 us -> none  [the longest x1 60.3 us: shards(): lax.psum_scatter(jnp.dot(part_rows, fc2_weight, preferred_element_type=jn...]
    scatter x5 -> x0, local copies, waits for them, and re-layouts: 230 us -> none  [the longest x1 167 us: shards(): pack_qkv = jnp.zeros((pack_len, 3, slice_width), jnp.bfloat16).at[slot_of...]
    all_to_all x7 -> x12, waiting for transfers between devices: 202 us -> 67.3 us  [the longest x3 25.4 us: sum_packs(): lax.all_to_all(half, 'head', split_axis=0, concat_axis=0, tiled=True)]
    all_gather x2, waiting for transfers between devices: 117 us -> 0.01 us  [the longest x1 0.01 us: shards(): fc2_all = lax.all_gather(fc2_own, ('yy', 'head'), axis=0)]
    dot_general x35 -> x21, matrix products: 194 us -> 93 us  [the longest x18 76 us: dot(): lax.dot_general(left, right, (dims, ((), ())), preferred_element_type=F32)]
    unnamed x13 -> x2, waiting for transfers between devices: 100 us -> 0.03 us
    ppermute x0 -> x33, waiting for transfers between devices: none -> 78.2 us  [the longest x32 78.2 us: xor_swap(): return lax.ppermute(values, axis, [(i, i ^ step) for i in range(size)])]
    all_to_all x3 -> x0, blocking collectives: 65.1 us -> none  [the longest x1 31.9 us: shards(): lax.all_to_all(departing, 'dp', split_axis=0, concat_axis=0, tiled=True)]
  transfers between devices with their start and end apart: 18 -> 47, of which waited for: 16 -> 18; matrix products, arithmetic and copies ran while one was open for 17% -> 48% of each run, Pallas kernels for 0% -> 7%
where the time goes in v1:
time: 654 us; the launch traced here: 643 us
  local copies, waits for them, and re-layouts  169 us (26%)
  waiting for transfers between devices  146 us (22%)
  other arithmetic  97.3 us (15%)
  matrix products  93 us (14%)
  starting transfers between devices  78.1 us (12%)
  Pallas kernels  44.3 us (7%)
  between operations  15.9 us (2%)
    ppermute x32, waiting for transfers between devices, xor_swap(): return lax.ppermute(values, axis, [(i, i ^ step) for i in range(size)])  78.2 us
    dot_general x18, matrix products, dot(): lax.dot_general(left, right, (dims, ((), ())), preferred_element_type=F32)  76 us
    unnamed x215, local copies, waits for them, and re-layouts  27.3 us
    pallas_call x1, Pallas kernels, attend_back(): pl.pallas_call(functools.partial(attend_back_kernel, heads, head_dim, blo...  26.5 us
    all_to_all x3, waiting for transfers between devices, sum_packs(): lax.all_to_all(half, 'head', split_axis=0, concat_axis=0, tiled=True)  25.4 us
    all_to_all x4, starting transfers between devices, to_packs(): lax.all_to_all(rows, ('yy', 'head'), split_axis=0, concat_axis=0, tiled=T...  23.2 us
    all_to_all x4, waiting for transfers between devices, to_packs(): lax.all_to_all(rows, ('yy', 'head'), split_axis=0, concat_axis=0, tiled=T...  22.4 us
    ppermute x32, starting transfers between devices, xor_swap(): return lax.ppermute(values, axis, [(i, i ^ step) for i in range(size)])  18.7 us
  transfers between devices with their start and end apart: 47, of which 18 were waited for; matrix products, arithmetic and copies ran while one was open for 48% of the time, Pallas kernels for 7%

profile of v1, /device:TPU:0, one launch (start us, length us, event | category | flops | bytes accessed | tf_op | source)
XLA Modules:
  0.0 643.4 jit_solution(15504391765458553607)
XLA Ops:
  14.1 9.2 %all-to-all-start = ((bf16[8,48,1024]{2,1,0:T(8,128)(2,1)}), bf16[8,48,1024]{2,1,0:T(8,128)(2,1)S(1)}, u32[]{:S(2)}, u32[]{:S(2)}) async-start(bf16[8,48,1024]{2,1,0:T(8,128)(2,1)} %bitcast.333), calls=%async_computation | async-start | bytes 1572864 | tf_op jit(solution)/shard_map/all_to_all | solution.py:193
  26.7 11.0 %reshape.569 = bf16[3,1024,2,4,128]{4,3,2,1,0:T(4,128)(2,1)} reshape(bf16[3,1024,1024]{2,1,0:T(8,128)(2,1)} %param.24) | data formatting | bytes 12582912 | tf_op jit(solution)/shard_map/reshape | solution.py:294
  40.4 6.3 convolution_add_fusion
  57.2 6.2 constant_dynamic-slice_fusion.22
  115.7 17.8 %shard_map.290 = (bf16[1536,256]{1,0:T(8,128)(2,1)S(1)}, f32[256,1536]{1,0:T(8,128)S(1)}, f32[8,1536]{1,0:T(8,128)S(1)}) custom-call(s32[6]{0:T(128)S(1)} %get-tuple-element.194.first_ref, s32[6]{0:T(128)S(1)} %get-tuple-element.193.last_ref, s32[1,1536]{1,0:T(1,128)S(1)} %broadcast_in_dim.431.lo_ref, s32[1,1536]{1,0:T(1,128)S(1)} %min.14.hi_ref, ...), custom_call_target="tpu_custom_call" | custom-call | flops 1207959552 | bytes 3145728 | tf_op jit(solution)/shard_map/pallas_call | solution.py:95
  139.1 11.8 %all-to-all-done.1 = bf16[4,384,256]{2,1,0:T(8,128)(2,1)} async-done(((bf16[4,384,256]{2,1,0:T(8,128)(2,1)}), bf16[4,384,256]{2,1,0:T(8,128)(2,1)}, u32[]{:S(2)}, u32[]{:S(2)}) %all-to-all-start.1) | async-done | bytes 786464 | tf_op jit(solution)/shard_map/all_to_all | solution.py:428
  164.4 19.2 %collective-permute-done.5 = bf16[384,1024]{1,0:T(8,128)(2,1)} collective-permute-done((bf16[384,1024]{1,0:T(8,128)(2,1)}, bf16[384,1024]{1,0:T(8,128)(2,1)}, u32[]{:S(2)}, u32[]{:S(2)}) %collective-permute-start.5) | collective-permute-done | bytes 786464 | tf_op jit(solution)/shard_map/ppermute | solution.py:206
  193.9 5.5 fusion.53
  208.1 4.6 all-to-all-start.3
  215.9 18.3 %all-to-all-done.3 = bf16[8,48,1024]{2,1,0:T(8,128)(2,1)} async-done(((bf16[8,48,1024]{2,1,0:T(8,128)(2,1)}), bf16[8,48,1024]{2,1,0:T(8,128)(2,1)}, u32[]{:S(2)}, u32[]{:S(2)}) %all-to-all-start.3) | async-done | bytes 786464 | tf_op jit(solution)/shard_map/all_to_all | solution.py:193
  235.6 4.7 bitcast_multiply_fusion.2
  240.8 19.0 %collective-permute-done.11 = bf16[384,1024]{1,0:T(8,128)(2,1)} collective-permute-done((bf16[384,1024]{1,0:T(8,128)(2,1)}, bf16[384,1024]{1,0:T(8,128)(2,1)}, u32[]{:S(2)}, u32[]{:S(2)}) %collective-permute-start.11) | collective-permute-done | bytes 786464 | tf_op jit(solution)/shard_map/ppermute | solution.py:206
  262.4 12.0 %convert_reduce_fusion.1 = (f32[1024]{0:T(1024)}, bf16[1536,1024]{1,0:T(8,128)(2,1)S(1)}) fusion(f32[1536,1024]{1,0:T(8,128)} %copy-done.100, f32[1024]{0:T(1024)S(1)} %bitcast.439, bf16[1024,1024]{1,0:T(8,128)(2,1)} %bitcast.342, bf16[384,1024]{1,0:T(8,128)(2,1)} %collective-permute-done.12, bf16[384,1024]{1,0:T(8,128)(2,1)} %collective-permute-done.11, ...), kind=kOutput, calls=%fused_computation.16 | convolution fusion | flops 3269983232 | bytes 14688256 | tf_op jit(solution)/shard_map/dot_general | solution.py:46
  280.0 9.4 %convolution_convert_fusion.4 = bf16[1024,1024]{1,0:T(8,128)(2,1)} fusion(bf16[384,1024]{1,0:T(8,128)(2,1)} %collective-permute-done.12, bf16[384,1024]{1,0:T(8,128)(2,1)} %collective-permute-done.11, bf16[384,1024]{1,0:T(8,128)(2,1)} %collective-permute-done.10, bf16[384,1024]{1,0:T(8,128)(2,1)} %get-tuple-element.119, f32[1536,1024]{1,0:T(8,128)} %copy-done.100, ...), kind=kOutput, calls=%fused_computation.52 | convolution fusion | flops 3250585600 | bytes 11538432 | tf_op jit(solution)/shard_map/dot_general | solution.py:46
  291.1 6.6 %convolution_convert_fusion.5 = bf16[1024,1024]{1,0:T(8,128)(2,1)} fusion(bf16[1536,1024]{1,0:T(8,128)(2,1)S(1)} %get-tuple-element.192, bf16[384,1024]{1,0:T(8,128)(2,1)} %collective-permute-done.6, bf16[384,1024]{1,0:T(8,128)(2,1)} %collective-permute-done.5, bf16[384,1024]{1,0:T(8,128)(2,1)} %collective-permute-done.4, ...), kind=kOutput, calls=%fused_computation.53 | convolution fusion | flops 3234856960 | bytes 8388608 | tf_op jit(solution)/shard_map/dot_general | solution.py:46
  297.7 4.5 reshape.610
  302.2 4.5 reshape.613
  315.8 4.9 convert_reduce_fusion.5
  332.7 7.9 %constant_dynamic-slice_fusion.3 = (bf16[4,256,1,512]{3,2,1,0:T(2,128)(2,1)}, bf16[4,256,1,512]{3,2,1,0:T(2,128)(2,1)S(1)}) fusion(bf16[4,256,2,512]{3,2,1,0:T(2,128)(2,1)} %reshape.613, s32[]{:T(128)S(6)} %select_n.269, s32[]{:T(128)S(6)} %select_n.270), kind=kLoop, calls=%fused_computation.211 | loop fusion | bytes 4194312 | tf_op jit(solution)/shard_map/dynamic-slice.4
  344.9 5.8 all-to-all-start.2
  356.0 26.5 %shard_map.291 = (bf16[1536,256]{1,0:T(8,128)(2,1)S(1)}, bf16[1536,256]{1,0:T(8,128)(2,1)S(1)}, bf16[1536,256]{1,0:T(8,128)(2,1)S(1)}) custom-call(s32[6]{0:T(128)S(1)} %get-tuple-element.194.first_ref, s32[6]{0:T(128)S(1)} %get-tuple-element.193.last_ref, s32[1,1536]{1,0:T(1,128)S(1)} %broadcast_in_dim.431.lo_ref, s32[1,1536]{1,0:T(1,128)S(1)} %min.14.hi_ref, ...), custom_call_target="tpu_custom_call" | custom-call | flops 3019898880 | bytes 6291456 | tf_op jit(solution)/shard_map/pallas_call | solution.py:173
  449.8 6.5 %all-to-all-start.8 = ((bf16[4,512,256]{2,1,0:T(8,128)(2,1)}), bf16[4,512,256]{2,1,0:T(8,128)(2,1)}, u32[]{:S(2)}, u32[]{:S(2)}) async-start(bf16[4,512,256]{2,1,0:T(8,128)(2,1)} %fusion.17), calls=%async_computation.8 | async-start | bytes 2097152 | tf_op jit(solution)/shard_map/all_to_all | solution.py:248
  467.8 14.7 %all-to-all-done.8 = bf16[4,512,256]{2,1,0:T(8,128)(2,1)} async-done(((bf16[4,512,256]{2,1,0:T(8,128)(2,1)}), bf16[4,512,256]{2,1,0:T(8,128)(2,1)}, u32[]{:S(2)}, u32[]{:S(2)}) %all-to-all-start.8) | async-done | bytes 1048608 | tf_op jit(solution)/shard_map/all_to_all | solution.py:248
  482.5 4.5 all-to-all-start.10
  487.0 4.9 convert_dynamic-update-slice_fusion
  493.2 6.8 %fusion.92 = f32[4,6144]{1,0:T(4,128)S(1)} fusion(pred[384,4]{0,1:T(4,128)(4,1)S(1)} %copy-done.64, f32[384,6144]{1,0:T(8,128)} %convert_dynamic-update-slice_fusion.1), kind=kOutput, calls=%fused_computation.301 | convolution fusion | flops 113246208 | bytes 9537024 | tf_op jit(solution)/shard_map/dot_general | solution.py:522
  507.8 4.6 all-to-all-done.10
  515.7 6.4 convolution_convert_fusion.6
  538.8 4.7 all-to-all-done.11
  543.5 5.0 all-to-all-start.6
  566.3 25.9 %collective-permute-done.26 = f32[72,128]{1,0:T(8,128)S(1)} collective-permute-done((f32[72,128]{1,0:T(8,128)S(1)}, f32[72,128]{1,0:T(8,128)S(1)}, u32[]{:S(2)}, u32[]{:S(2)}) %collective-permute-start.26) | collective-permute-done | bytes 36896 | tf_op jit(solution)/shard_map/ppermute | solution.py:206
  628.6 6.1 all-to-all-done.7
  (510 shorter events, 321.7 us)
Async XLA Ops:
  7.2 176.4 %all-gather.7.cloned.1.call-start = ((), (), s32[]{:S(2)}) async-start(), calls=%async_computation.13 | async-start | bytes 2359296 | tf_op jit(solution)/shard_map/all_gather | solution.py:324
  9.8 65.4 %collective-permute-start = (s32[1536]{0:T(1024)S(1)}, s32[1536]{0:T(1024)S(1)}, u32[]{:S(2)}, u32[]{:S(2)}) collective-permute-start(s32[1536]{0:T(1024)S(1)} %reduce.16), channel_id=1, source_target_pairs={{0,0},{1,4},{2,8},{3,12},{4,1},{5,5},{6,9},{7,13},{8,2},{9,6},{10,... | collective-permute-start | bytes 18440 | tf_op jit(solution)/shard_map/ppermute | solution.py:350
  14.1 36.8 %all-to-all-start = ((bf16[8,48,1024]{2,1,0:T(8,128)(2,1)}), bf16[8,48,1024]{2,1,0:T(8,128)(2,1)S(1)}, u32[]{:S(2)}, u32[]{:S(2)}) async-start(bf16[8,48,1024]{2,1,0:T(8,128)(2,1)} %bitcast.333), calls=%async_computation | async-start | bytes 1572864 | tf_op jit(solution)/shard_map/all_to_all | solution.py:193
  23.3 165.9 %all-gather.5.cloned.1.call-start = ((), (), s32[]{:S(2)}) async-start(), calls=%async_computation.12 | async-start | bytes 2433024 | tf_op jit(solution)/shard_map/all_gather | solution.py:317
  55.2 19.9 %collective-permute-start.2 = (bf16[384,1024]{1,0:T(8,128)(2,1)}, bf16[384,1024]{1,0:T(8,128)(2,1)}, u32[]{:S(2)}, u32[]{:S(2)}) collective-permute-start(bf16[384,1024]{1,0:T(8,128)(2,1)} %get-tuple-element.121), channel_id=1, source_target_pairs={{0,8},{4,12},{8,0},{12,4},{1,9},{5,13},{9,1},{13,5},{2,10},{6,14},... | collective-permute-start | bytes 2359304 | tf_op jit(solution)/shard_map/ppermute | solution.py:206
  164.1 19.5 %collective-permute-start.5 = (bf16[384,1024]{1,0:T(8,128)(2,1)}, bf16[384,1024]{1,0:T(8,128)(2,1)}, u32[]{:S(2)}, u32[]{:S(2)}) collective-permute-start(bf16[384,1024]{1,0:T(8,128)(2,1)} %add_convert_fusion.11), channel_id=1, source_target_pairs={{0,8},{4,12},{8,0},{12,4},{1,9},{5,13},{9,1},{13,5},{2,10},{6,14},... | collective-permute-start | bytes 2359304 | tf_op jit(solution)/shard_map/ppermute | solution.py:206
  164.4 29.5 %collective-permute-start.4 = (bf16[384,1024]{1,0:T(8,128)(2,1)}, bf16[384,1024]{1,0:T(8,128)(2,1)}, u32[]{:S(2)}, u32[]{:S(2)}) collective-permute-start(bf16[384,1024]{1,0:T(8,128)(2,1)} %add_convert_fusion.11), channel_id=1, source_target_pairs={{0,4},{4,0},{8,12},{12,8},{1,5},{5,1},{9,13},{13,9},{2,6},{6,2},{1... | collective-permute-start | bytes 2359304 | tf_op jit(solution)/shard_map/ppermute | solution.py:206
  208.1 26.1 %all-to-all-start.3 = ((bf16[8,48,1024]{2,1,0:T(8,128)(2,1)}), bf16[8,48,1024]{2,1,0:T(8,128)(2,1)}, u32[]{:S(2)}, u32[]{:S(2)}) async-start(bf16[8,48,1024]{2,1,0:T(8,128)(2,1)} %bitcast.335), calls=%async_computation.3 | async-start | bytes 1572864 | tf_op jit(solution)/shard_map/all_to_all | solution.py:193
  212.7 21.4 %collective-permute-start.7 = (bf16[384,1024]{1,0:T(8,128)(2,1)}, bf16[384,1024]{1,0:T(8,128)(2,1)}, u32[]{:S(2)}, u32[]{:S(2)}) collective-permute-start(bf16[384,1024]{1,0:T(8,128)(2,1)} %get-tuple-element.105), channel_id=1, source_target_pairs={{0,4},{4,0},{8,12},{12,8},{1,5},{5,1},{9,13},{13,9},{2,6},{6,2},{1... | collective-permute-start | bytes 2359304 | tf_op jit(solution)/shard_map/ppermute | solution.py:206
  215.4 20.2 %collective-permute-start.9 = (bf16[384,1024]{1,0:T(8,128)(2,1)}, bf16[384,1024]{1,0:T(8,128)(2,1)}, u32[]{:S(2)}, u32[]{:S(2)}) collective-permute-start(bf16[384,1024]{1,0:T(8,128)(2,1)} %add_convert_fusion.9), channel_id=1, source_target_pairs={{0,8},{4,12},{8,0},{12,4},{1,9},{5,13},{9,1},{13,5},{2,10},{6,14},... | collective-permute-start | bytes 2359304 | tf_op jit(solution)/shard_map/ppermute | solution.py:206
  240.3 19.5 %collective-permute-start.11 = (bf16[384,1024]{1,0:T(8,128)(2,1)}, bf16[384,1024]{1,0:T(8,128)(2,1)}, u32[]{:S(2)}, u32[]{:S(2)}) collective-permute-start(bf16[384,1024]{1,0:T(8,128)(2,1)} %get-tuple-element.119), channel_id=1, source_target_pairs={{0,8},{4,12},{8,0},{12,4},{1,9},{5,13},{9,1},{13,5},{2,10},{6,14},... | collective-permute-start | bytes 2359304 | tf_op jit(solution)/shard_map/ppermute | solution.py:206
  240.8 19.0 %collective-permute-start.10 = (bf16[384,1024]{1,0:T(8,128)(2,1)}, bf16[384,1024]{1,0:T(8,128)(2,1)}, u32[]{:S(2)}, u32[]{:S(2)}) collective-permute-start(bf16[384,1024]{1,0:T(8,128)(2,1)} %get-tuple-element.119), channel_id=1, source_target_pairs={{0,4},{4,0},{8,12},{12,8},{1,5},{5,1},{9,13},{13,9},{2,6},{6,2},{1... | collective-permute-start | bytes 2359304 | tf_op jit(solution)/shard_map/ppermute | solution.py:206
  279.5 33.5 %collective-permute-start.13 = (bf16[384,1024]{1,0:T(8,128)(2,1)}, bf16[384,1024]{1,0:T(8,128)(2,1)}, u32[]{:S(2)}, u32[]{:S(2)}) collective-permute-start(bf16[384,1024]{1,0:T(8,128)(2,1)} %get-tuple-element.103), channel_id=1, source_target_pairs={{0,4},{4,0},{8,12},{12,8},{1,5},{5,1},{9,13},{13,9},{2,6},{6,2},{1... | collective-permute-start | bytes 2359304 | tf_op jit(solution)/shard_map/ppermute | solution.py:206
  290.6 22.4 %collective-permute-start.15 = (bf16[384,1024]{1,0:T(8,128)(2,1)}, bf16[384,1024]{1,0:T(8,128)(2,1)}, u32[]{:S(2)}, u32[]{:S(2)}) collective-permute-start(bf16[384,1024]{1,0:T(8,128)(2,1)} %add_convert_fusion.5), channel_id=1, source_target_pairs={{0,8},{4,12},{8,0},{12,4},{1,9},{5,13},{9,1},{13,5},{2,10},{6,14},... | collective-permute-start | bytes 2359304 | tf_op jit(solution)/shard_map/ppermute | solution.py:206
  311.0 31.4 %collective-permute-start.31 = (bf16[4,512,256]{2,1,0:T(8,128)(2,1)}, bf16[4,512,256]{2,1,0:T(8,128)(2,1)}, u32[]{:S(2)}, u32[]{:S(2)}) collective-permute-start(bf16[4,512,256]{2,1,0:T(8,128)(2,1)} %bitcast.314), channel_id=1, source_target_pairs={{0,16},{16,0},{1,17},{17,1},{2,18},{18,2},{3,19},{19,3},{4,20},{20... | collective-permute-start | bytes 3145736 | tf_op jit(solution)/shard_map/ppermute | solution.py:206
  328.5 16.4 %all-to-all-start.4 = ((bf16[4,384,256]{1,2,0:T(8,128)(2,1)}), bf16[4,384,256]{1,2,0:T(8,128)(2,1)}, u32[]{:S(2)}, u32[]{:S(2)}) async-start(bf16[4,384,256]{1,2,0:T(8,128)(2,1)} %bitcast.334), calls=%async_computation.4 | async-start | bytes 1572864 | tf_op jit(solution)/shard_map/all_to_all | solution.py:479
  341.8 87.4 %collective-permute-start.32 = (bf16[4,256,512]{2,1,0:T(8,128)(2,1)}, bf16[4,256,512]{2,1,0:T(8,128)(2,1)}, u32[]{:S(2)}, u32[]{:S(2)}) collective-permute-start(bf16[4,256,512]{2,1,0:T(8,128)(2,1)} %bitcast.313), channel_id=1, source_target_pairs={{0,16},{16,0},{1,17},{17,1},{2,18},{18,2},{3,19},{19,3},{4,20},{20... | collective-permute-start | bytes 3145736 | tf_op jit(solution)/shard_map/ppermute | solution.py:206
  344.9 104.9 %all-to-all-start.2 = ((bf16[8,48,1024]{2,1,0:T(8,128)(2,1)}), bf16[8,48,1024]{2,1,0:T(8,128)(2,1)}, u32[]{:S(2)}, u32[]{:S(2)}) async-start(bf16[8,48,1024]{2,1,0:T(8,128)(2,1)} %bitcast.340), calls=%async_computation.2 | async-start | bytes 1572864 | tf_op jit(solution)/shard_map/all_to_all | solution.py:193
  437.3 63.5 %collective-permute-start.23 = (bf16[1024,256]{1,0:T(8,128)(2,1)}, bf16[1024,256]{1,0:T(8,128)(2,1)}, u32[]{:S(2)}, u32[]{:S(2)}) collective-permute-start(bf16[1024,256]{1,0:T(8,128)(2,1)} %copy.240), channel_id=1, source_target_pairs={{0,4},{4,0},{8,12},{12,8},{1,5},{5,1},{9,13},{13,9},{2,6},{6,2},{1... | collective-permute-start | bytes 1572872 | tf_op jit(solution)/shard_map/ppermute | solution.py:206
  437.3 111.3 %collective-permute-start.22 = (bf16[1024,256]{1,0:T(8,128)(2,1)}, bf16[1024,256]{1,0:T(8,128)(2,1)}, u32[]{:S(2)}, u32[]{:S(2)}) collective-permute-start(bf16[1024,256]{1,0:T(8,128)(2,1)} %copy.238), channel_id=1, source_target_pairs={{0,4},{4,0},{8,12},{12,8},{1,5},{5,1},{9,13},{13,9},{2,6},{6,2},{1... | collective-permute-start | bytes 1572872 | tf_op jit(solution)/shard_map/ppermute | solution.py:206
  437.8 21.4 %collective-permute-start.16 = (bf16[384,1024]{1,0:T(8,128)(2,1)}, bf16[384,1024]{1,0:T(8,128)(2,1)}, u32[]{:S(2)}, u32[]{:S(2)}) collective-permute-start(bf16[384,1024]{1,0:T(8,128)(2,1)} %get-tuple-element.101), channel_id=1, source_target_pairs={{0,4},{4,0},{8,12},{12,8},{1,5},{5,1},{9,13},{13,9},{2,6},{6,2},{1... | collective-permute-start | bytes 2359304 | tf_op jit(solution)/shard_map/ppermute | solution.py:206
  440.4 20.5 %collective-permute-start.18 = (bf16[384,1024]{1,0:T(8,128)(2,1)}, bf16[384,1024]{1,0:T(8,128)(2,1)}, u32[]{:S(2)}, u32[]{:S(2)}) collective-permute-start(bf16[384,1024]{1,0:T(8,128)(2,1)} %add_convert_fusion.2), channel_id=1, source_target_pairs={{0,8},{4,12},{8,0},{12,4},{1,9},{5,13},{9,1},{13,5},{2,10},{6,14},... | collective-permute-start | bytes 2359304 | tf_op jit(solution)/shard_map/ppermute | solution.py:206
  449.8 32.7 %all-to-all-start.8 = ((bf16[4,512,256]{2,1,0:T(8,128)(2,1)}), bf16[4,512,256]{2,1,0:T(8,128)(2,1)}, u32[]{:S(2)}, u32[]{:S(2)}) async-start(bf16[4,512,256]{2,1,0:T(8,128)(2,1)} %fusion.17), calls=%async_computation.8 | async-start | bytes 2097152 | tf_op jit(solution)/shard_map/all_to_all | solution.py:248
  482.5 29.8 %all-to-all-start.10 = ((bf16[4,256,512]{2,1,0:T(8,128)(2,1)}), bf16[4,256,512]{2,1,0:T(8,128)(2,1)}, u32[]{:S(2)}, u32[]{:S(2)}) async-start(bf16[4,256,512]{2,1,0:T(8,128)(2,1)} %fusion.16), calls=%async_computation.10 | async-start | bytes 2097152 | tf_op jit(solution)/shard_map/all_to_all | solution.py:248
  502.7 45.8 %collective-permute-start.24 = (bf16[1024,256]{1,0:T(8,128)(2,1)}, bf16[1024,256]{1,0:T(8,128)(2,1)}, u32[]{:S(2)}, u32[]{:S(2)}) collective-permute-start(bf16[1024,256]{1,0:T(8,128)(2,1)} %add_convert_fusion.14), channel_id=1, source_target_pairs={{0,8},{4,12},{8,0},{12,4},{1,9},{5,13},{9,1},{13,5},{2,10},{6,14},... | collective-permute-start | bytes 1572872 | tf_op jit(solution)/shard_map/ppermute | solution.py:206
  505.2 32.2 %collective-permute-start.19 = (f32[4,2,4,192]{3,2,1,0:T(4,128)}, f32[4,2,4,192]{3,2,1,0:T(4,128)}, u32[]{:S(2)}, u32[]{:S(2)}) collective-permute-start(f32[4,2,4,192]{3,2,1,0:T(4,128)} %get-tuple-element.156), channel_id=1, source_target_pairs={{0,4},{4,0},{8,12},{12,8},{1,5},{5,1},{9,13},{13,9},{2,6},{6,2},{1... | collective-permute-start | bytes 73736 | tf_op jit(solution)/shard_map/ppermute | solution.py:206
  506.0 31.4 %collective-permute-start.21 = (f32[4,2,4,192]{3,2,1,0:T(4,128)}, f32[4,2,4,192]{3,2,1,0:T(4,128)}, u32[]{:S(2)}, u32[]{:S(2)}) collective-permute-start(f32[4,2,4,192]{3,2,1,0:T(4,128)} %bitcast_add_fusion.4), channel_id=1, source_target_pairs={{0,8},{4,12},{8,0},{12,4},{1,9},{5,13},{9,1},{13,5},{2,10},{6,14},... | collective-permute-start | bytes 73736 | tf_op jit(solution)/shard_map/ppermute | solution.py:206
  512.3 21.0 %all-to-all-start.9 = ((bf16[4,128,256]{2,1,0:T(8,128)(2,1)}), bf16[4,128,256]{2,1,0:T(8,128)(2,1)S(1)}, u32[]{:S(2)}, u32[]{:S(2)}) async-start(bf16[4,128,256]{2,1,0:T(8,128)(2,1)} %bitcast.138), calls=%async_computation.9 | async-start | bytes 524288 | tf_op jit(solution)/shard_map/all_to_all | solution.py:458
  555.1 51.4 %all-to-all-start.5 = ((bf16[8,48,1024]{2,1,0:T(8,128)(2,1)}), bf16[8,48,1024]{2,1,0:T(8,128)(2,1)S(1)}, u32[]{:S(2)}, u32[]{:S(2)}) async-start(bf16[8,48,1024]{2,1,0:T(8,128)(2,1)} %bitcast.104), calls=%async_computation.5 | async-start | bytes 1572864 | tf_op jit(solution)/shard_map/all_to_all | solution.py:193
  561.0 42.8 %collective-permute-start.25 = (bf16[4,4,256,128]{3,2,1,0:T(8,128)(2,1)}, bf16[4,4,256,128]{3,2,1,0:T(8,128)(2,1)}, u32[]{:S(2)}, u32[]{:S(2)}) collective-permute-start(bf16[4,4,256,128]{3,2,1,0:T(8,128)(2,1)} %fusion.44), channel_id=1, source_target_pairs={{0,16},{16,0},{1,17},{17,1},{2,18},{18,2},{3,19},{19,3},{4,20},{20... | collective-permute-start | bytes 3145736 | tf_op jit(solution)/shard_map/ppermute | solution.py:206
  566.1 26.1 %collective-permute-start.26 = (f32[72,128]{1,0:T(8,128)S(1)}, f32[72,128]{1,0:T(8,128)S(1)}, u32[]{:S(2)}, u32[]{:S(2)}) collective-permute-start(f32[72,128]{1,0:T(8,128)S(1)} %pad_bitcast_fusion), channel_id=1, source_target_pairs={{0,16},{16,0},{1,17},{17,1},{2,18},{18,2},{3,19},{19,3},{4,20},{20... | collective-permute-start | bytes 110600 | tf_op jit(solution)/shard_map/ppermute | solution.py:206
  607.4 27.2 %all-to-all-start.7 = ((bf16[4,4,256,128]{3,2,1,0:T(8,128)(2,1)}), bf16[4,4,256,128]{3,2,1,0:T(8,128)(2,1)S(1)}, u32[]{:S(2)}, u32[]{:S(2)}) async-start(bf16[4,4,256,128]{3,2,1,0:T(8,128)(2,1)} %fusion.18), calls=%async_computation.7 | async-start | bytes 2097152 | tf_op jit(solution)/shard_map/all_to_all | solution.py:248
  (117 other events, 2611.7 us)
Sparse Core Ops, SparseCore 0:
  10.1 61.6 all-gather.6
  74.5 48.5 all-gather.4

commit v2 on v1

v2 whole, which is shorter than its diff:
```python
import functools

import jax
import jax.numpy as jnp
from jax import lax
from jax.experimental import pallas as pl
from jax.experimental.pallas import tpu as pltpu
from jax.sharding import Mesh, PartitionSpec as P

BF = jnp.bfloat16
F32 = jnp.float32
SMEM = pl.BlockSpec(memory_space=pltpu.SMEM)
VMEM = pl.BlockSpec(memory_space=pltpu.VMEM)
ANY = pl.BlockSpec(memory_space=pl.ANY)
PLAIN = ((1,), (0,))
BY_ROW = ((1,), (1,))


def shape_of(shape, dtype):
    return jax.ShapeDtypeStruct(shape, dtype)


def dot(left, right, dims=PLAIN):
    return lax.dot_general(left, right, (dims, ((), ())), preferred_element_type=F32)


def call(name, kernel, operands, specs, outs, scratch=(), flops=0, exps=0):
    size = sum(a.size * a.dtype.itemsize for a, s in zip(operands, specs) if s is VMEM)
    size += sum(o.size * o.dtype.itemsize for o in outs)
    return pl.pallas_call(
        kernel,
        name=name,
        out_shape=tuple(outs),
        in_specs=list(specs),
        out_specs=(VMEM,) * len(outs),
        scratch_shapes=list(scratch),
        compiler_params=pltpu.CompilerParams(vmem_limit_bytes=48 * 1024 * 1024),
        cost_estimate=pl.CostEstimate(flops=flops, bytes_accessed=size, transcendentals=exps),
    )(*operands)


def row_norm(values):
    centre = values - jnp.mean(values, axis=-1, keepdims=True)
    inverse = lax.rsqrt(jnp.mean(centre * centre, axis=-1, keepdims=True) + 1e-06)
    return (centre * inverse, inverse)


def norm_back(gradient, normed, inverse):
    return inverse * (
        gradient
        - jnp.mean(gradient, axis=-1, keepdims=True)
        - normed * jnp.mean(gradient * normed, axis=-1, keepdims=True)
    )


def mod_rows(mod_ref, part, item, width):
    cols = slice(part * width, (part + 1) * width)
    rows = jnp.broadcast_to(mod_ref[0:1, cols], (item.shape[0], width))
    for index in range(1, mod_ref.shape[0]):
        rows = jnp.where(item == index, mod_ref[index : index + 1, cols], rows)
    return rows


def add_item_sums(sums_ref, part, item, values, count):
    width = values.shape[1]
    cols = slice(part * width, (part + 1) * width)
    for index in range(count):
        kept = jnp.where(item == index, values, 0.0)
        sums_ref[index : index + 1, cols] += jnp.sum(kept, axis=0, keepdims=True)


def same_head(width, head_dim):
    row = lax.broadcasted_iota(jnp.int32, (width, width), 0) // head_dim
    col = lax.broadcasted_iota(jnp.int32, (width, width), 1) // head_dim
    return (row == col).astype(BF)


def head_sums(values, same):
    high = values.astype(BF)
    low = (values - high.astype(F32)).astype(BF)
    return dot(high, same) + dot(low, same)


def chunks(rows, size):
    return pl.loop(0, rows // size)


def at(index, size):
    return pl.ds(pl.multiple_of(index * size, size), size)


def first_norm_kernel(x_ref, mod_ref, item_ref, out_ref):
    rows, width = x_ref.shape

    @chunks(rows, 64)
    def _(i):
        r = at(i, 64)
        item = item_ref[r, :]
        normed, _ = row_norm(x_ref[r, :].astype(F32))
        scale, shift = mod_rows(mod_ref, 2, item, width), mod_rows(mod_ref, 4, item, width)
        out_ref[r, :] = (normed * (1.0 + scale) + shift).astype(BF)


def grad_mlp_kernel(up_ref, mod_ref, item_ref, out_ref, sum_ref):
    rows, width = up_ref.shape
    sum_ref[...] = jnp.zeros_like(sum_ref)

    @chunks(rows, 64)
    def _(i):
        r = at(i, 64)
        gamma = mod_rows(mod_ref, 1, item_ref[r, :], width)
        grad = (up_ref[r, :].astype(F32) * gamma).astype(BF)
        out_ref[r, :] = grad
        sum_ref[0:1, :] += jnp.sum(grad.astype(F32), axis=0, keepdims=True)


def load_columns(weight_ref, held, sems, offset_of, parts, sub):
    copies = []
    for t in range(3):
        for p in range(parts):
            copies.append(
                pltpu.make_async_copy(
                    weight_ref.at[t, :, pl.ds(pl.multiple_of(offset_of(p), sub), sub)],
                    held.at[:, pl.ds((t * parts + p) * sub, sub)],
                    sems.at[t * parts + p],
                )
            )
    for copy in copies:
        copy.start()
    return copies


def attend_kernel(dims, *refs):
    group, segs, heads, head_dim, parts, block = dims
    me_ref, first_ref, last_ref, lo_ref, hi_ref, temper_ref, qb_ref, vb_ref, w_ref = refs[:9]
    blocks = refs[9 : 9 + group]
    outs = refs[9 + group :]
    out_ref, out_t_ref, lse_ref, q_ref, k_ref, v_ref, qp_ref, kp_ref = outs[:8]
    held, v_t, out_s, acc, total, sems = outs[8:]
    pack_len, width = q_ref.shape
    rows = blocks[0].shape[0]
    seg, sub = rows // segs, width // parts
    me = me_ref[0]
    copies = load_columns(w_ref, held, sems, lambda p: (p * group + me) * sub, parts, sub)
    same = same_head(width, head_dim)
    for copy in copies:
        copy.wait()
    for k in range(group):
        for y in range(segs):
            ranks = pl.ds(pl.multiple_of((y * group + (me ^ k)) * seg, 16), seg)
            made = dot(blocks[k][y * seg : (y + 1) * seg, :], held[...])
            query = made[:, :width] + qb_ref[...]
            key = made[:, width : 2 * width]
            qp_ref[ranks, :] = query
            kp_ref[ranks, :] = key
            inverse = lax.rsqrt(head_sums(query * query, same) + 1e-06)
            q_ref[ranks, :] = (query * inverse * temper_ref[...]).astype(BF)
            inverse = lax.rsqrt(head_sums(key * key, same) + 1e-06)
            k_ref[ranks, :] = (key * inverse).astype(BF)
            v_ref[ranks, :] = (made[:, 2 * width :] + vb_ref[...]).astype(BF)
    v_t[...] = v_ref[...].T
    lanes = lax.broadcasted_iota(jnp.int32, (1, width), 1) // head_dim

    @pl.loop(0, pack_len // block)
    def _(q_block):
        q_rows = at(q_block, block)
        q_t = q_ref[q_rows, :].T
        low, high = lo_ref[:, q_rows], hi_ref[:, q_rows]
        acc[...] = jnp.zeros_like(acc)
        total[...] = jnp.zeros_like(total)

        @pl.loop(first_ref[q_block], last_ref[q_block])
        def _(k_block):
            k_rows = at(k_block, block)
            keys = k_ref[k_rows, :]
            index = k_block * block + lax.broadcasted_iota(jnp.int32, (block, block), 0)
            seen = (index >= low) & (index < high)
            for h in range(heads):
                own = pl.ds(h * head_dim, head_dim)
                scores = dot(jnp.where(lanes == h, keys, jnp.zeros_like(keys)), q_t)
                raised = jnp.where(seen, jnp.exp(scores), 0.0)
                total[h : h + 1, :] += jnp.sum(raised, axis=0, keepdims=True)
                acc[own, :] += dot(v_t[own, k_rows], raised.astype(BF))

        for h in range(heads):
            own = pl.ds(h * head_dim, head_dim)
            acc[own, :] = acc[own, :] / total[h : h + 1, :]
            lse_ref[h : h + 1, q_rows] = jnp.log(total[h : h + 1, :])
        out_t_ref[:, q_rows] = acc[...]
        out_s[q_rows, :] = acc[...].T.astype(BF)

    for y in range(segs):
        for g in range(group):
            start = (y * group + g) * seg
            out_ref[g, y * seg : (y + 1) * seg, :] = out_s[start : start + seg, :]


def attend_back_kernel(dims, *refs):
    group, segs, heads, head_dim, parts, block = dims
    me_ref, first_ref, last_ref, lo_ref, hi_ref, temper_ref, w_ref, in_ref = refs[:8]
    q_ref, k_ref, v_ref, qp_ref, kp_ref, out_t_ref, lse_ref = refs[8:15]
    sent = refs[15 : 15 + group]
    dqkv_ref, sums_ref = refs[15 + group : 17 + group]
    held, g_s, k_t, dq_s, dk_acc, dv_acc, acc, sums, sems = refs[17 + group :]
    pack_len, width = q_ref.shape
    rows = in_ref.shape[1]
    seg, sub = rows // segs, width // parts
    me = me_ref[0]
    copies = load_columns(w_ref, held, sems, lambda p: (p * group + me) * sub, parts, sub)
    for y in range(segs):
        for g in range(group):
            start = (y * group + g) * seg
            g_s[start : start + seg, :] = in_ref[g, y * seg : (y + 1) * seg, :]
    lanes = lax.broadcasted_iota(jnp.int32, (1, width), 1) // head_dim
    k_t[...] = k_ref[...].T
    dk_acc[...] = jnp.zeros_like(dk_acc)
    dv_acc[...] = jnp.zeros_like(dv_acc)

    @pl.loop(0, pack_len // block)
    def _(q_block):
        q_rows = at(q_block, block)
        queries, grads = q_ref[q_rows, :], g_s[q_rows, :]
        q_t, g_t = queries.T, grads.T
        low, high = lo_ref[:, q_rows], hi_ref[:, q_rows]
        weighted = g_t.astype(F32) * out_t_ref[:, q_rows]
        for h in range(heads):
            sums[h : h + 1, :] = jnp.sum(
                weighted[h * head_dim : (h + 1) * head_dim, :], axis=0, keepdims=True
            )
        acc[...] = jnp.zeros_like(acc)

        @pl.loop(first_ref[q_block], last_ref[q_block])
        def _(k_block):
            k_rows = at(k_block, block)
            keys, values = k_ref[k_rows, :], v_ref[k_rows, :]
            index = k_block * block + lax.broadcasted_iota(jnp.int32, (block, block), 0)
            seen = (index >= low) & (index < high)
            for h in range(heads):
                own = pl.ds(h * head_dim, head_dim)
                mine = lanes == h
                scores = dot(jnp.where(mine, keys, jnp.zeros_like(keys)), q_t)
                probs = jnp.where(seen, jnp.exp(scores - lse_ref[h : h + 1, q_rows]), 0.0)
                grad_probs = dot(jnp.where(mine, values, jnp.zeros_like(values)), g_t)
                grad_scores = (probs * (grad_probs - sums[h : h + 1, :])).astype(BF)
                acc[own, :] += dot(k_t[own, k_rows], grad_scores)
                dk_acc[k_rows, :] += dot(
                    grad_scores, jnp.where(mine, queries, jnp.zeros_like(queries))
                )
                dv_acc[k_rows, :] += dot(
                    probs.astype(BF), jnp.where(mine, grads, jnp.zeros_like(grads))
                )

        dq_s[q_rows, :] = acc[...].T

    for copy in copies:
        copy.wait()
    same = same_head(width, head_dim)
    sums_ref[...] = jnp.zeros_like(sums_ref)

    def back(gradient, pre):
        inverse = lax.rsqrt(head_sums(pre * pre, same) + 1e-06)
        unit = pre * inverse
        return inverse * (gradient - unit * head_sums(gradient * unit, same)), unit

    for k in range(group):
        for y in range(segs):
            ranks = pl.ds(pl.multiple_of((y * group + (me ^ k)) * seg, 16), seg)
            own = slice(k * rows + y * seg, k * rows + (y + 1) * seg)
            grad = dq_s[ranks, :].astype(BF).astype(F32) * temper_ref[...]
            grad_query, unit = back(grad, qp_ref[ranks, :])
            grad_query = grad_query.astype(BF)
            grad_key, _ = back(dk_acc[ranks, :].astype(BF).astype(F32), kp_ref[ranks, :])
            grad_value = dv_acc[ranks, :].astype(BF)
            dqkv_ref[own, :width] = grad_query
            dqkv_ref[own, width : 2 * width] = grad_key.astype(BF)
            dqkv_ref[own, 2 * width :] = grad_value
            for index, values in enumerate((grad_query, grad_value, grad * unit)):
                sums_ref[index : index + 1, :] += jnp.sum(
                    values.astype(F32), axis=0, keepdims=True
                )
        sent[k][...] = dot(
            dqkv_ref[k * rows : (k + 1) * rows, :], held[...], BY_ROW
        ).astype(BF)


def project_kernel(
    parts, ret_ref, wp_ref, pb_ref, x_ref, mod_ref, item_ref, attn_ref, branch_ref, middle_ref, out_ref
):
    group, rows, width = ret_ref.shape
    model = x_ref.shape[1]
    sub = width // parts
    for g in range(group):
        for p in range(parts):
            start = (p * group + g) * sub
            attn_ref[:, start : start + sub] = ret_ref[g, :, p * sub : (p + 1) * sub]
    branch_ref[...] = dot(attn_ref[...], wp_ref[...]) + pb_ref[...].astype(F32)

    @chunks(rows, 64)
    def _(i):
        r = at(i, 64)
        item = item_ref[r, :]
        middle = x_ref[r, :].astype(F32) + mod_rows(mod_ref, 0, item, model) * branch_ref[r, :]
        middle_ref[r, :] = middle
        normed, _ = row_norm(middle)
        scale, shift = mod_rows(mod_ref, 3, item, model), mod_rows(mod_ref, 5, item, model)
        out_ref[r, :] = (normed * (1.0 + scale) + shift).astype(BF)


def load_tiles(tiles_ref, held, sems, first, depth):
    count_a, count_b = tiles_ref.shape[:2]
    tall = held.shape[0] // (count_a if depth == 0 else count_b)
    wide = held.shape[1] // (count_b if depth == 0 else count_a)
    copies = []
    for a in range(count_a):
        for b in range(count_b):
            r, c = (a, b) if depth == 0 else (b, a)
            copies.append(
                pltpu.make_async_copy(
                    tiles_ref.at[a, b, pl.ds(0, tall), :],
                    held.at[pl.ds(r * tall, tall), pl.ds(c * wide, wide)],
                    sems.at[first + a * count_b + b],
                )
            )
    for copy in copies:
        copy.start()
    return copies


def feed_kernel(count, *refs):
    fc1_ref, fc2_ref, b1_ref = refs[:3]
    ins = refs[3 : 3 + count]
    grads = refs[3 + count : 3 + 2 * count]
    rest = refs[3 + 2 * count :]
    back, outs = rest[:count], rest[count : 2 * count]
    act_ref, gh_ref, sum_ref, w1, w2, pre, grad, sems = rest[2 * count :]
    tiles = fc1_ref.shape[0] * fc1_ref.shape[1]
    first = load_tiles(fc1_ref, w1, sems, 0, 0)
    second = load_tiles(fc2_ref, w2, sems, tiles, 1)
    rows = ins[0].shape[0]
    sum_ref[...] = jnp.zeros_like(sum_ref)
    for copy in first:
        copy.wait()
    for k in range(count):
        pre[...] = dot(ins[k][...], w1[...]) + b1_ref[...]
        if k == 0:
            for copy in second:
                copy.wait()
        grad[...] = dot(grads[k][...], w2[...], BY_ROW)

        @chunks(rows, 32)
        def _(i):
            r = at(i, 32)
            to = pl.ds(pl.multiple_of(k * rows + i * 32, 32), 32)
            value = pre[r, :]
            square = value * value
            gate = jnp.tanh(value * (0.7978845608028654 + 0.035677408136300125 * square))
            half = 0.5 + 0.5 * gate
            act = value * half
            slope = half + act * (1.0 - gate) * (0.7978845608028654 + 0.10703222440890037 * square)
            back_grad = (slope * grad[r, :]).astype(BF)
            act_ref[to, :] = act.astype(BF)
            gh_ref[to, :] = back_grad
            sum_ref[0:1, :] += jnp.sum(back_grad.astype(F32), axis=0, keepdims=True)

        own = slice(k * rows, (k + 1) * rows)
        back[k][...] = dot(gh_ref[own, :], w1[...], BY_ROW).astype(BF)
        outs[k][...] = dot(act_ref[own, :], w2[...]).astype(BF)


def feed_weights_kernel(dims, *refs):
    count, group, split = dims
    me_ref, act_ref, gh_ref = refs[:3]
    ins = refs[3 : 3 + count]
    grads = refs[3 + count : 3 + 2 * count]
    up_ref, down_ref, left_t, right, act_t = refs[3 + 2 * count :]
    rows, model = ins[0].shape
    for k in range(count):
        own = slice(k * rows, (k + 1) * rows)
        left_t[:, own] = ins[k][...].T
        right[own, :] = grads[k][...]
    act_t[...] = act_ref[...].T
    part = model // split
    fine = part // group
    head_size = up_ref.shape[2]
    hidden = up_ref.shape[4]
    for y in range(split):
        start = pl.multiple_of((me_ref[1] ^ y) * part, part) if split > 1 else 0
        for z in range(head_size):
            cols = slice(z * hidden, (z + 1) * hidden)
            made = dot(left_t[pl.ds(start, part), :], gh_ref[:, cols]).astype(BF)
            for g in range(group):
                up_ref[y, g, z] = made[g * fine : (g + 1) * fine, :]
            made = dot(act_t[cols, :], right[:, pl.ds(start, part)]).astype(BF)
            for g in range(group):
                down_ref[y, g, z] = made[:, g * fine : (g + 1) * fine]


def middle_back_kernel(
    dims, kept_ref, came_ref, middle_ref, branch_ref, up_ref, mod_ref, item_ref, wp_ref,
    out_ref, gb_ref, gm_ref, sums_ref, col_ref, attn,
):
    parts, items = dims
    rows, model = middle_ref.shape
    group, _, width = out_ref.shape
    sub = width // parts
    sums_ref[...] = jnp.zeros_like(sums_ref)
    col_ref[...] = jnp.zeros_like(col_ref)

    @chunks(rows, 64)
    def _(i):
        r = at(i, 64)
        item = item_ref[r, :]
        grad_in = kept_ref[r, :].astype(F32) + came_ref[r, :].astype(F32)
        normed, inverse = row_norm(middle_ref[r, :])
        scale = mod_rows(mod_ref, 3, item, model)
        grad_middle = up_ref[r, :].astype(F32) + norm_back(grad_in * (1.0 + scale), normed, inverse)
        gm_ref[r, :] = grad_middle
        grad_branch = (grad_middle * mod_rows(mod_ref, 0, item, model)).astype(BF)
        gb_ref[r, :] = grad_branch
        col_ref[0:1, :] += jnp.sum(grad_branch.astype(F32), axis=0, keepdims=True)
        add_item_sums(sums_ref, 0, item, grad_middle * branch_ref[r, :], items)
        add_item_sums(sums_ref, 1, item, grad_in * normed, items)
        add_item_sums(sums_ref, 2, item, grad_in, items)

    attn[...] = dot(gb_ref[...], wp_ref[...], BY_ROW).astype(BF)
    for g in range(group):
        for p in range(parts):
            start = (p * group + g) * sub
            out_ref[g, :, p * sub : (p + 1) * sub] = attn[:, start : start + sub]


def output_kernel(
    items, kept_ref, came_ref, middle_ref, up_ref, mod_ref, item_ref, bias_ref, out_ref, sums_ref
):
    rows, model = middle_ref.shape
    sums_ref[...] = jnp.zeros_like(sums_ref)

    @chunks(rows, 64)
    def _(i):
        r = at(i, 64)
        item = item_ref[r, :]
        made = kept_ref[r, :].astype(F32) + came_ref[r, :].astype(F32) + bias_ref[...].astype(F32)
        gamma = mod_rows(mod_ref, 1, item, model)
        out_ref[r, :] = (middle_ref[r, :] + gamma * made).astype(BF)
        add_item_sums(sums_ref, 0, item, up_ref[r, :].astype(F32) * made, items)


def tokens_back_kernel(
    items, kept_ref, came_ref, x_ref, gm_ref, mod_ref, item_ref, out_ref, sums_ref
):
    rows, model = x_ref.shape
    sums_ref[...] = jnp.zeros_like(sums_ref)

    @chunks(rows, 64)
    def _(i):
        r = at(i, 64)
        item = item_ref[r, :]
        grad_in = kept_ref[r, :].astype(F32) + came_ref[r, :].astype(F32)
        normed, inverse = row_norm(x_ref[r, :].astype(F32))
        scale = mod_rows(mod_ref, 2, item, model)
        out_ref[r, :] = (
            gm_ref[r, :] + norm_back(grad_in * (1.0 + scale), normed, inverse)
        ).astype(BF)
        add_item_sums(sums_ref, 0, item, grad_in * normed, items)
        add_item_sums(sums_ref, 1, item, grad_in, items)


def proj_weights_kernel(dims, me_ref, attn_ref, gb_ref, *refs):
    group, parts, split = dims
    outs, left_t, right = refs[:group], refs[group], refs[group + 1]
    left_t[...] = attn_ref[...].T
    chunk, head_size, tall, wide = outs[0].shape
    for k in range(group):
        for y in range(chunk):
            part = (me_ref[1] ^ y) if split else y
            start = pl.multiple_of((part * group + (me_ref[0] ^ k)) * wide, wide)
            right[:, y * wide : (y + 1) * wide] = gb_ref[:, pl.ds(start, wide)]
        made = dot(left_t[...], right[...]).astype(BF)
        for y in range(chunk):
            for z in range(head_size):
                outs[k][y, z] = made[z * tall : (z + 1) * tall, y * wide : (y + 1) * wide]


def qkv_weights_kernel(dims, me_ref, dqkv_ref, *refs):
    count, parts, split = dims
    ins, (out_ref, left_t, right) = refs[:count], refs[count:]
    rows = ins[0].shape[0]
    for k in range(count):
        left_t[:, k * rows : (k + 1) * rows] = ins[k][...].T
    chunk, head_size, _, tall, wide = out_ref.shape
    for y in range(chunk):
        part = (me_ref[1] ^ y) if split else y
        for t in range(3):
            start = pl.multiple_of((t * parts + part) * wide, wide)
            right[:, t * wide : (t + 1) * wide] = dqkv_ref[:, pl.ds(start, wide)]
        made = dot(left_t[...], right[...]).astype(BF)
        for z in range(head_size):
            for t in range(3):
                out_ref[y, z, t] = made[z * tall : (z + 1) * tall, t * wide : (t + 1) * wide]


def to_packs(rows):
    return lax.all_to_all(rows, ("yy", "head"), split_axis=0, concat_axis=0, tiled=True)


def over_group(blocks):
    return lax.all_to_all(blocks, "g", split_axis=0, concat_axis=0, tiled=True)


def bits(count):
    steps = []
    while count > 1:
        count //= 2
        steps.append(count)
    return steps


def xor_swap(values, axis, step):
    size = lax.axis_size(axis)
    return lax.ppermute(values, axis, [(i, i ^ step) for i in range(size)])


def xor_gather(block, axis):
    blocks = {0: block}
    for step in bits(lax.axis_size(axis)):
        for k in list(blocks):
            blocks[k ^ step] = xor_swap(blocks[k], axis, step)
    return [blocks[k] for k in range(len(blocks))]


def xor_scatter(blocks, axis):
    blocks = dict(enumerate(blocks))
    for step in reversed(bits(lax.axis_size(axis))):
        kept = {}
        for k in blocks:
            if not k & step:
                kept[k] = (blocks[k], xor_swap(blocks[k ^ step], axis, step))
        if len(kept) == 1:
            return kept[0]
        blocks = {k: add_low(*pair) for k, pair in kept.items()}


def add_low(left, right):
    return (left.astype(F32) + right.astype(F32)).astype(left.dtype)


def butterfly(values, axes):
    for axis in axes:
        for step in reversed(bits(lax.axis_size(axis))):
            values = values + xor_swap(values, axis, step)
    return values


def pick(values, index, axis):
    return lax.dynamic_index_in_dim(values, index, axis, keepdims=False)


def xor_blocks(values, axis, dim):
    me = lax.axis_index(axis)
    return [pick(values, me ^ k, dim) for k in range(lax.axis_size(axis))]


def tie(*values):
    return lax.optimization_barrier(values)


def shards(
    tokens,
    cotangent,
    class_table,
    ada_weight,
    ada_bias,
    qkv_weight,
    q_bias,
    v_bias,
    log_scale,
    proj_weight,
    proj_bias,
    fc1_weight,
    fc1_bias,
    fc2_weight,
    fc2_bias,
    item_lens,
    class_ids,
    section_ids,
    destination,
):
    segs = lax.axis_size("yy")
    group = lax.axis_size("g")
    head_size = lax.axis_size("head")
    yy, g, z = lax.axis_index("yy"), lax.axis_index("g"), lax.axis_index("head")
    me = jnp.stack([g, yy]).astype(jnp.int32)
    pack = yy * head_size + z
    rows, model = tokens.shape
    heads_all = log_scale.shape[0]
    head_dim = model // heads_all
    heads = heads_all // group
    width = model // group
    dp_size = segs * group
    pack_len = rows * head_size
    seg = rows // segs
    items = item_lens.shape[1]
    block = min(256, pack_len)
    col = model // dp_size
    parts = segs if col % 128 == 0 else 1
    sub = width // parts

    def own_cols(values):
        return pick(values.reshape(parts, group, sub), g, 1).reshape(1, width)

    row_pack = destination // pack_len
    index = jnp.arange(rows, dtype=jnp.int32)
    before = (row_pack[None, :] < row_pack[:, None]) | (
        (row_pack[None, :] == row_pack[:, None]) & (index[None, :] < index[:, None])
    )
    slot = jnp.sum(before.astype(jnp.int32), axis=1)
    to_slot = (slot[None, :] == index[:, None]).astype(BF)
    sorted_tokens = dot(to_slot, tokens).astype(BF)
    sorted_cotangent = dot(to_slot, cotangent).astype(BF)
    inputs = to_packs(sorted_tokens)

    hidden = fc1_weight.shape[1] // group
    units = head_size * hidden
    half = model // segs
    fc1_own = lax.dynamic_slice(fc1_weight, (yy * half, g * hidden), (half, hidden))
    fc1_bias_own = lax.dynamic_slice(fc1_bias, (g * hidden,), (hidden,))
    fc1_sent = jnp.concatenate(
        [fc1_own, jnp.broadcast_to(fc1_bias_own[None, :], (16, hidden))], axis=0
    )
    fc1_all = lax.all_gather(fc1_sent, ("yy", "head"), axis=0)
    fc1_all = fc1_all.reshape(segs, head_size, half + 16, hidden)
    fc2_own = lax.dynamic_slice(fc2_weight, (g * hidden, yy * half), (hidden, half))
    fc2_all = lax.all_gather(fc2_own, ("yy", "head"), axis=0)
    fc2_all = fc2_all.reshape(segs, head_size, hidden, half)
    fc1_bias_here = fc1_all[0, :, half].reshape(1, units).astype(F32)
    tiled = hidden % 128 == 0
    if not tiled:
        fc1_all = fc1_all[:, :, :half].transpose(0, 2, 1, 3).reshape(1, 1, model, units)
        fc2_all = fc2_all.transpose(1, 2, 0, 3).reshape(1, 1, units, model)

    lens_here = pick(item_lens, pack, 0)
    class_here = pick(class_ids, pack, 0)
    order_key = class_here * items + jnp.arange(items, dtype=jnp.int32)
    item_rank = jnp.sum(
        jnp.where(order_key[None, :] < order_key[:, None], lens_here[None, :], 0), axis=1
    )
    item_pos = jnp.cumsum(lens_here) - lens_here
    item_end = item_rank + lens_here

    def items_of(rank):
        return (rank[:, None] >= item_rank[None, :]) & (rank[:, None] < item_end[None, :])

    rank_all = jnp.arange(pack_len, dtype=jnp.int32)
    member = items_of(rank_all)

    def of_item(values):
        return jnp.sum(jnp.where(member, values[None, :], 0), axis=1)

    section_here = lax.ppermute(
        section_ids[0],
        ("g", "head"),
        [(a * head_size + b, b * head_size + a) for a in range(group) for b in range(head_size)],
    )
    position = rank_all - of_item(item_rank - item_pos)
    section_rank = jnp.sum(
        jnp.where(rank_all[None, :] == position[:, None], section_here[None, :], 0), axis=1
    )
    up_to = jnp.sum((section_here[None, :] <= section_rank[:, None]).astype(jnp.int32), axis=1)
    low = of_item(item_rank)
    high = jnp.minimum(up_to + of_item(item_rank - item_pos), of_item(item_end))
    first = low[::block] // block
    last = (high[block - 1 :: block] + block - 1) // block
    low, high = low[None, :], high[None, :]

    row_rank = (
        (jnp.arange(segs, dtype=jnp.int32)[:, None] * group + g) * seg
        + jnp.arange(seg, dtype=jnp.int32)[None, :]
    ).reshape(rows)
    row_item = jnp.sum(
        jnp.where(items_of(row_rank), jnp.arange(items, dtype=jnp.int32)[None, :], 0), axis=1
    )[:, None]

    class_rows = jnp.take(class_table, class_ids.reshape(-1), axis=0).astype(F32)
    silu_cond = jax.nn.silu(class_rows).astype(BF)
    silu_here = lax.dynamic_slice_in_dim(silu_cond, pack * items, items, 0)
    mod = jnp.dot(silu_here, ada_weight, preferred_element_type=F32) + ada_bias.astype(F32)

    (attn_in,) = call("first_norm",
        first_norm_kernel, (inputs, mod, row_item), (VMEM,) * 3, (shape_of((rows, model), BF),)
    )
    attn_blocks = xor_gather(attn_in, "g")
    sorted_cotangent, _ = tie(sorted_cotangent, inputs)
    upstream = to_packs(sorted_cotangent)
    grad_mlp, grad_mlp_sum = call("grad_mlp",
        grad_mlp_kernel,
        (upstream, mod, row_item),
        (VMEM,) * 3,
        (shape_of((rows, model), BF), shape_of((8, model), F32)),
    )
    grad_blocks = xor_gather(grad_mlp, "g")
    per_part = sub // head_dim
    scale_here = pick(log_scale.reshape(parts, group, per_part), g, 1).reshape(heads)
    temper = jnp.repeat(jnp.exp(scale_here), head_dim)[None, :]
    dims = (group, segs, heads, head_dim, parts, block)
    pairs = heads * pack_len * pack_len // 2
    wide = shape_of((pack_len, width), BF)
    wide_f32 = shape_of((pack_len, width), F32)
    out_blocks, out_t, lse, queries, keys, values, query_pre, key_pre = call("attend",
        functools.partial(attend_kernel, dims),
        (me, first, last, low, high, temper, own_cols(q_bias).astype(F32),
         own_cols(v_bias).astype(F32), qkv_weight, *attn_blocks),
        (SMEM, SMEM, SMEM) + (VMEM,) * 5 + (ANY,) + (VMEM,) * group,
        (shape_of((group, rows, width), BF), shape_of((width, pack_len), F32),
         shape_of((8, pack_len), F32), wide, wide, wide, wide_f32, wide_f32),
        [
            pltpu.VMEM((model, 3 * width), BF),
            pltpu.VMEM((width, pack_len), BF),
            pltpu.VMEM((pack_len, width), BF),
            pltpu.VMEM((width, block), F32),
            pltpu.VMEM((8, block), F32),
            pltpu.SemaphoreType.DMA((3 * parts,)),
        ],
        flops=4 * pairs * head_dim + 6 * pack_len * model * width,
        exps=pairs,
    )
    returned = over_group(out_blocks)
    rows_bf, rows_f32 = shape_of((rows, model), BF), shape_of((rows, model), F32)
    attn_rows, branch, middle, mlp_in = call("project",
        functools.partial(project_kernel, parts),
        (returned, proj_weight, proj_bias[None, :], inputs, mod, row_item),
        (VMEM,) * 6,
        (rows_bf, rows_f32, rows_f32, rows_bf),
        flops=2 * rows * model * model,
    )

    mlp_blocks = xor_gather(mlp_in, "g")
    tiles = fc1_all.shape[0] * fc1_all.shape[1]
    made = call("feed",
        functools.partial(feed_kernel, group),
        (fc1_all, fc2_all, fc1_bias_here, *mlp_blocks, *grad_blocks),
        (ANY, ANY) + (VMEM,) * (1 + 2 * group),
        (rows_bf,) * (2 * group)
        + (shape_of((pack_len, units), BF),) * 2
        + (shape_of((8, units), F32),),
        [
            pltpu.VMEM((model, units), BF),
            pltpu.VMEM((units, model), BF),
            pltpu.VMEM((rows, units), F32),
            pltpu.VMEM((rows, units), F32),
            pltpu.SemaphoreType.DMA((2 * tiles,)),
        ],
        flops=8 * pack_len * model * units,
        exps=pack_len * units,
    )
    back_parts, out_parts = made[:group], made[group : 2 * group]
    act, grad_hidden, grad_hidden_sum = made[2 * group :]
    grad_in_pair = xor_scatter(back_parts, "g")
    out_pair = xor_scatter(out_parts, "g")
    if tiled:
        up_shape = (segs, group, head_size, half // group, hidden)
        down_shape = (segs, group, head_size, hidden, half // group)
        feed_dims = (group, group, segs)
    else:
        up_shape, down_shape = (1, 1, 1, model, units), (1, 1, 1, units, model)
        feed_dims = (group, 1, 1)
    up_grad, down_grad = call("feed_weights",
        functools.partial(feed_weights_kernel, feed_dims),
        (me, act, grad_hidden, *mlp_blocks, *grad_blocks),
        (SMEM,) + (VMEM,) * (2 + 2 * group),
        (shape_of(up_shape, BF), shape_of(down_shape, BF)),
        [
            pltpu.VMEM((model, pack_len), BF),
            pltpu.VMEM((pack_len, model), BF),
            pltpu.VMEM((units, pack_len), BF),
        ],
        flops=4 * pack_len * model * units,
    )
    if not tiled:
        fine = half // group
        up_grad = up_grad.reshape(segs, group, fine, head_size, hidden).transpose(0, 1, 3, 2, 4)
        down_grad = down_grad.reshape(head_size, hidden, segs, group, fine)
        down_grad = down_grad.transpose(2, 3, 0, 1, 4)
        up_grad = jnp.stack(xor_blocks(up_grad, "yy", 0))
        down_grad = jnp.stack(xor_blocks(down_grad, "yy", 0))

    def sum_tiles(tiles):
        half_sum = add_low(*xor_scatter([tiles[y] for y in range(segs)], "yy"))
        shape = half_sum.shape[2:]
        came = lax.all_to_all(
            half_sum.reshape(group * head_size, *shape), ("g", "head"), 0, 0, tiled=True
        )
        return jnp.sum(came.reshape(group, head_size, *shape).astype(F32), axis=1)

    up_sum, down_sum = sum_tiles(up_grad), sum_tiles(down_grad)
    up_part = up_sum.transpose(1, 0, 2).reshape(half // group, group * hidden)
    down_part = down_sum.reshape(group * hidden, half // group)

    outbound, grad_branch, grad_middle, middle_sums, branch_sum = call("middle_back",
        functools.partial(middle_back_kernel, (parts, items)),
        (*grad_in_pair, middle, branch, upstream, mod, row_item, proj_weight),
        (VMEM,) * 8,
        (shape_of((group, rows, width), BF), rows_bf, rows_f32, shape_of((8, 3 * model), F32),
         shape_of((8, model), F32)),
        [pltpu.VMEM((rows, model), BF)],
        flops=2 * rows * model * model,
    )
    inbound = over_group(outbound)
    output_rows, output_sums = call("output",
        functools.partial(output_kernel, items),
        (*out_pair, middle, upstream, mod, row_item, fc2_bias[None, :]),
        (VMEM,) * 7,
        (rows_bf, shape_of((8, model), F32)),
    )
    proj_parts = call("proj_weights",
        functools.partial(proj_weights_kernel, (group, parts, parts == segs)),
        (me, attn_rows, grad_branch),
        (SMEM, VMEM, VMEM),
        (shape_of((parts, head_size, model // head_size, sub), BF),) * group,
        [pltpu.VMEM((model, rows), BF), pltpu.VMEM((rows, width), BF)],
        flops=2 * rows * model * model,
    )
    proj_own = add_low(*xor_scatter(proj_parts, "g"))
    made = call("attend_back",
        functools.partial(attend_back_kernel, dims),
        (me, first, last, low, high, temper, qkv_weight, inbound, queries, keys, values,
         query_pre, key_pre, out_t, lse),
        (SMEM, SMEM, SMEM, VMEM, VMEM, VMEM, ANY) + (VMEM,) * 8,
        (rows_bf,) * group + (shape_of((pack_len, 3 * width), BF), shape_of((8, width), F32)),
        [
            pltpu.VMEM((model, 3 * width), BF),
            pltpu.VMEM((pack_len, width), BF),
            pltpu.VMEM((width, pack_len), BF),
            pltpu.VMEM((pack_len, width), F32),
            pltpu.VMEM((pack_len, width), F32),
            pltpu.VMEM((pack_len, width), F32),
            pltpu.VMEM((width, block), F32),
            pltpu.VMEM((8, block), F32),
            pltpu.SemaphoreType.DMA((3 * parts,)),
        ],
        flops=10 * pairs * head_dim + 6 * pack_len * model * width,
        exps=pairs,
    )
    grad_qkv, qkv_sums = made[group:]
    attn_pair = xor_scatter(made[:group], "g")
    (qkv_grad,) = call("qkv_weights",
        functools.partial(qkv_weights_kernel, (group, parts, parts == segs)),
        (me, grad_qkv, *attn_blocks),
        (SMEM,) + (VMEM,) * (1 + group),
        (shape_of((parts, head_size, 3, model // head_size, sub), BF),),
        [pltpu.VMEM((model, pack_len), BF), pltpu.VMEM((pack_len, 3 * sub), BF)],
        flops=6 * pack_len * model * width,
    )
    tokens_grad_rows, tokens_sums = call("tokens_back",
        functools.partial(tokens_back_kernel, items),
        (*attn_pair, inputs, grad_middle, mod, row_item),
        (VMEM,) * 6,
        (rows_bf, shape_of((8, 2 * model), F32)),
    )

    def to_data(values):
        return dot(to_slot, to_packs(values), ((0,), (0,)))

    output = to_data(output_rows).astype(BF)
    tokens_grad = to_data(tokens_grad_rows)

    item_part = jnp.concatenate(
        [
            middle_sums[:items, :model],
            output_sums[:items],
            tokens_sums[:items, :model],
            middle_sums[:items, model : 2 * model],
            tokens_sums[:items, model:],
            middle_sums[:items, 2 * model :],
        ],
        axis=1,
    )
    ada_cols = 6 * model // (dp_size * head_size)
    item_part = item_part.reshape(items, segs, group, head_size, ada_cols)
    item_own = add_low(*xor_scatter(xor_blocks(item_part, "g", 2), "g"))
    item_all = to_packs(
        item_own.reshape(items, segs * head_size, ada_cols).transpose(1, 0, 2)
    )
    item_low = item_all.reshape(-1, ada_cols).astype(BF)
    ada_grad = dot(silu_cond, item_low, ((0,), (0,)))
    ada_bias_grad = jnp.sum(item_low.astype(F32), axis=0)

    both = jnp.concatenate([proj_own[:, :, None], qkv_grad], axis=2)
    if parts == segs:
        half_sum = add_low(*xor_scatter([both[y] for y in range(segs)], "yy"))
        came = lax.all_to_all(half_sum, "head", 0, 0, tiled=True)
        summed = jnp.sum(came.astype(F32), axis=0)
    else:
        both = both.transpose(2, 1, 3, 0, 4).reshape(4, model, width)
        full = lax.dynamic_update_slice(
            jnp.zeros((4, model, model), BF), both, (0, 0, g * width)
        )
        summed = lax.psum_scatter(full, ("yy", "g"), scatter_dimension=2, tiled=True)
        summed = lax.psum_scatter(summed, "head", scatter_dimension=1, tiled=True).astype(F32)
    proj_part, qkv_part = summed[0], summed[1:]

    def spread(values, count, size):
        zero = jnp.zeros((count, group, size), F32)
        return lax.dynamic_update_slice(zero, values.reshape(count, 1, size), (0, g, 0)).reshape(-1)

    log_sums = jnp.sum(qkv_sums[2].reshape(heads, head_dim), axis=1)
    vectors = [
        spread(qkv_sums[0], parts, sub),
        spread(qkv_sums[1], parts, sub),
        spread(log_sums, parts, per_part),
        branch_sum[0],
        spread(grad_hidden_sum[0], head_size, hidden),
        grad_mlp_sum[0],
    ]
    joined = jnp.concatenate(vectors)
    filler = -joined.shape[0] % 1024
    joined = jnp.pad(joined, (0, filler)).reshape(-1, 128)
    joined = butterfly(joined, ("yy", "g", "head")).reshape(-1)
    totals, start = [], 0
    for vector in vectors:
        totals.append(joined[start : start + vector.shape[0]])
        start += vector.shape[0]
    fc1_bias_grad = pick(totals[4].reshape(head_size, -1), z, 0)
    return (
        output,
        tokens_grad,
        ada_grad,
        ada_bias_grad,
        qkv_part,
        totals[0],
        totals[1],
        totals[2],
        proj_part,
        totals[3],
        up_part,
        fc1_bias_grad,
        down_part,
        totals[5],
    )


def solution(mesh):
    head_size = mesh.shape["head"]
    dp_size = mesh.shape["dp"]
    inner = Mesh(
        mesh.devices.reshape(dp_size // head_size, head_size, head_size), ("yy", "g", "head")
    )
    dp = ("yy", "g")
    everything = ("yy", "g", "head")
    in_specs = (
        P(everything, None),
        P(everything, None),
        P(),
        P(),
        P(),
        P(),
        P(),
        P(),
        P(),
        P(),
        P(),
        P(None, "head"),
        P("head"),
        P("head", None),
        P(),
        P(),
        P(),
        P(dp, None),
        P(everything),
    )
    out_specs = (
        P(everything, None),
        P(everything, None),
        P(None, everything),
        P(everything),
        P(None, "head", dp),
        P(),
        P(),
        P(),
        P("head", dp),
        P(),
        P(dp, "head"),
        P("head"),
        P("head", dp),
        P(),
    )
    return jax.shard_map(
        shards, mesh=inner, in_specs=in_specs, out_specs=out_specs, check_vma=False
    )
```

time: 654 us -> 499 us (0.76)
  local copies, waits for them, and re-layouts: 169 us -> 35 us
  Pallas kernels: 44.3 us -> 139 us
  matrix products: 93 us -> 17.3 us
  other arithmetic: 97.3 us -> 29.2 us
  waiting for transfers between devices: 146 us -> 183 us
  starting transfers between devices: 78.1 us -> 71.3 us
    pallas_call x2 -> x12, Pallas kernels: 44.3 us -> 139 us  [call(): pl.pallas_call(kernel, name=name, out_shape=tuple(outs), in_specs=list(sp...]
    ppermute x32, waiting for transfers between devices: 78.2 us -> 145 us  [xor_swap(): return lax.ppermute(values, axis, [(i, i ^ step) for i in range(size)])]
    dot_general x18 -> x5, matrix products: 76 us -> 10.9 us  [dot(): lax.dot_general(left, right, (dims, ((), ())), preferred_element_type=F32)]
    reshape x20 -> x5, local copies, waits for them, and re-layouts: 46.8 us -> 1.9 us  [the longest x1 1.03 us: shards(): item_part = item_part.reshape(items, segs, group, head_size, ada_cols)]
    all_to_all x8 -> x5, waiting for transfers between devices: 44.9 us -> 16 us  [the longest x2 8.24 us: over_group(): return lax.all_to_all(blocks, 'g', split_axis=0, concat_axis=0, tiled=True)]
    convert_element_type x9 -> x0, local copies, waits for them, and re-layouts: 25.3 us -> none  [the longest x2 8.19 us: shards(): grad_key = by_head(xor_order(grad_key)).astype(F32)]
    slice x14 -> x5, local copies, waits for them, and re-layouts: 23.9 us -> 0.78 us  [the longest x1 0.75 us: shards(): fc1_bias_here = fc1_all[0, :, half].reshape(1, units).astype(F32)]
    reduce_sum x14 -> x5, other arithmetic: 22 us -> 4.01 us  [the longest x2 3.64 us: sum_tiles(): return jnp.sum(came.reshape(group, head_size, *shape).astype(F32), axis=1)]
  transfers between devices with their start and end apart: 47 -> 45, of which waited for: 18 -> 19; matrix products, arithmetic and copies ran while one was open for 48% -> 13% of each run, Pallas kernels for 7% -> 23%
where the time goes in v2:
time: 499 us; the launch traced here: 490 us
  waiting for transfers between devices  183 us (37%)
  Pallas kernels  139 us (28%)
  starting transfers between devices  71.3 us (14%)
  local copies, waits for them, and re-layouts  35 us (7%)
  other arithmetic  29.2 us (6%)
  matrix products  17.3 us (3%)
  between operations  15.3 us (3%)
    ppermute x32, waiting for transfers between devices, xor_swap(): return lax.ppermute(values, axis, [(i, i ^ step) for i in range(size)])  145 us
    pallas_call x12, Pallas kernels, call(): pl.pallas_call(kernel, name=name, out_shape=tuple(outs), in_specs=list(sp...  139 us
    all_to_all x5, starting transfers between devices, to_packs(): lax.all_to_all(rows, ('yy', 'head'), split_axis=0, concat_axis=0, tiled=T...  25.3 us
    all_to_all x5, waiting for transfers between devices, to_packs(): lax.all_to_all(rows, ('yy', 'head'), split_axis=0, concat_axis=0, tiled=T...  22.5 us
    ppermute x32, starting transfers between devices, xor_swap(): return lax.ppermute(values, axis, [(i, i ^ step) for i in range(size)])  21.9 us
    unnamed x97, local copies, waits for them, and re-layouts  18.4 us
    convert_element_type x10, other arithmetic, add_low(): return (left.astype(F32) + right.astype(F32)).astype(left.dtype)  16.2 us
    dot_general x5, matrix products, dot(): lax.dot_general(left, right, (dims, ((), ())), preferred_element_type=F32)  10.9 us
  transfers between devices with their start and end apart: 45, of which 19 were waited for; matrix products, arithmetic and copies ran while one was open for 13% of the time, Pallas kernels for 23%

profile of v2, /device:TPU:0, one launch (start us, length us, event | category | flops | bytes accessed | tf_op | source)
XLA Modules:
  0.0 490.2 jit_solution(7880036077996175448)
XLA Ops:
  14.8 9.1 %all-to-all-start = ((bf16[8,48,1024]{2,1,0:T(8,128)(2,1)}), bf16[8,48,1024]{2,1,0:T(8,128)(2,1)S(1)}, u32[]{:S(2)}, u32[]{:S(2)}) async-start(bf16[8,48,1024]{2,1,0:T(8,128)(2,1)} %bitcast.137), calls=%async_computation | async-start | bytes 1572864 | tf_op jit(solution)/shard_map/all_to_all | solution.py:503
  27.9 6.4 %convolution_add_fusion.mod_ref = f32[4,6144]{1,0:T(4,128)S(1)} fusion(bf16[1024,6144]{1,0:T(8,128)(2,1)} %param.22, f32[6144]{0:T(1024)S(1)} %convert_element_type.196, bf16[32,1024]{1,0:T(8,128)(2,1)S(1)} %fusion.17, s32[]{:T(128)S(6)} %select_n.114), kind=kOutput, calls=%fused_computation.4 | convolution fusion | flops 50356224 | bytes 12713988 | tf_op jit(solution)/shard_map/dot_general | solution.py:686
  34.4 17.4 %all-to-all-done = bf16[8,48,1024]{2,1,0:T(8,128)(2,1)S(1)} async-done(((bf16[8,48,1024]{2,1,0:T(8,128)(2,1)}), bf16[8,48,1024]{2,1,0:T(8,128)(2,1)S(1)}, u32[]{:S(2)}, u32[]{:S(2)}) %all-to-all-start) | async-done | bytes 786464 | tf_op jit(solution)/shard_map/all_to_all | solution.py:503
  56.7 3.6 all-to-all-start.2
  60.8 12.2 %collective-permute-done.2.refs_11_.refs_2_ = bf16[384,1024]{1,0:T(8,128)(2,1)} collective-permute-done((bf16[384,1024]{1,0:T(8,128)(2,1)S(1)}, bf16[384,1024]{1,0:T(8,128)(2,1)}, u32[]{:S(2)}, u32[]{:S(2)}) %collective-permute-start.2) | collective-permute-done | bytes 786464 | tf_op jit(solution)/shard_map/ppermute | solution.py:520
  75.7 27.5 %attend.1 = (bf16[4,384,256]{2,1,0:T(8,128)(2,1)S(1)}, f32[256,1536]{1,0:T(8,128)}, f32[8,1536]{1,0:T(8,128)S(1)}, bf16[1536,256]{1,0:T(8,128)(2,1)S(1)}, bf16[1...) custom-call(s32[2]{0:T(128)S(1)} %pad_add_fusion.refs_0_.me_ref, ...), custom_call_target="tpu_custom_call" | custom-call | flops 3623878656 | bytes 11074560 | tf_op jit(solution)/shard_map/attend/pallas_call | solution.py:30
  106.8 3.9 all-to-all-start.1
  114.6 8.2 %all-to-all-done.1.ret_ref = bf16[4,384,256]{2,1,0:T(8,128)(2,1)S(1)} async-done(((bf16[4,384,256]{2,1,0:T(8,128)(2,1)}), bf16[4,384,256]{2,1,0:T(8,128)(2,1)S(1)}, u32[]{:S(2)}, u32[]{:S(2)}) %all-to-all-start.1) | async-done | bytes 786464 | tf_op jit(solution)/shard_map/all_to_all | solution.py:507
  122.8 6.1 %project.1 = (bf16[384,1024]{1,0:T(8,128)(2,1)S(1)}, f32[384,1024]{1,0:T(8,128)S(1)}, f32[384,1024]{1,0:T(8,128)}, bf16[384,1024]{1,0:T(8,128)(2,1)}) custom-call(bf16[4,384,256]{2,1,0:T(8,128)(2,1)S(1)} %all-to-all-done.1.ret_ref, bf16[1024,1024]{1,0:T(8,128)(2,1)} %wp_ref.3, bf16[1,1024]{1,0:T(2,128)(2,1)S(1)} %broadcast_in_dim.145.pb_ref, ...), custom_call_target="tpu_custom_call" | custom-call | flops 805306368 | bytes 8490496 | tf_op jit(solution)/shard_map/project/pallas_call | solution.py:30
  131.6 8.2 %collective-permute-done.8.refs_9_ = bf16[384,1024]{1,0:T(8,128)(2,1)} collective-permute-done((bf16[384,1024]{1,0:T(8,128)(2,1)}, bf16[384,1024]{1,0:T(8,128)(2,1)}, u32[]{:S(2)}, u32[]{:S(2)}) %collective-permute-start.8) | collective-permute-done | bytes 786464 | tf_op jit(solution)/shard_map/ppermute | solution.py:520
  139.8 16.4 %collective-permute-done.5.refs_5_ = bf16[384,1024]{1,0:T(8,128)(2,1)S(1)} collective-permute-done((bf16[384,1024]{1,0:T(8,128)(2,1)}, bf16[384,1024]{1,0:T(8,128)(2,1)S(1)}, u32[]{:S(2)}, u32[]{:S(2)}) %collective-permute-start.5) | collective-permute-done | bytes 786464 | tf_op jit(solution)/shard_map/ppermute | solution.py:520
  158.6 25.3 %feed.1 = (bf16[384,1024]{1,0:T(8,128)(2,1)S(1)}, bf16[384,1024]{1,0:T(8,128)(2,1)S(1)}, bf16[384,1024]{1,0:T(8,128)(2,1)S(1)}, bf16[384,1024]{1,0:T(8,128)(2,1)...) custom-call(bf16[2,4,528,256]{3,2,1,0:T(8,128)(2,1)} %bitcast.160, ...), custom_call_target="tpu_custom_call" | custom-call | flops 12884901888 | bytes 18911232 | tf_op jit(solution)/shard_map/feed/pallas_call | solution.py:30
  190.5 16.5 %collective-permute-done.15.came_ref = bf16[384,1024]{1,0:T(8,128)(2,1)S(1)} collective-permute-done((bf16[384,1024]{1,0:T(8,128)(2,1)S(1)}, bf16[384,1024]{1,0:T(8,128)(2,1)S(1)}, u32[]{:S(2)}, u32[]{:S(2)}) %collective-permute-start.15) | collective-permute-done | bytes 786464 | tf_op jit(solution)/shard_map/ppermute | solution.py:520
  207.1 8.3 %middle_back.1 = (bf16[4,384,256]{2,1,0:T(8,128)(2,1)S(1)}, bf16[384,1024]{1,0:T(8,128)(2,1)S(1)}, f32[384,1024]{1,0:T(8,128)S(1)}, f32[8,3072]{1,0:T(8,128)S(1)}, f32[8,1024]{1,0:T(8,128)S(1)}) custom-call(bf16[384,1024]{1,0:T(8,128)(2,1)S(1)} %add_convert_fusion.3.kept_ref, bf16[384,1024]{1,0:T(8,128)(2,1)S(1)} %collective-permute-done.15.came_ref, ...), custom_call_target="tpu_custom_call" | custom-call | flops 805306368 | bytes 10978816 | tf_op jit(solution)/shard_map/middle_back/pallas_call | solution.py:30
  218.3 4.2 all-to-all-start.4
  223.6 14.3 %feed_weights.1 = (bf16[2,4,4,128,256]{4,3,2,1,0:T(8,128)(2,1)}, bf16[2,4,4,256,128]{4,3,2,1,0:T(8,128)(2,1)}) custom-call(s32[2]{0:T(128)S(1)} %pad_add_fusion.refs_0_.me_ref, bf16[1536,1024]{1,0:T(8,128)(2,1)} %get-tuple-element.104.refs_1_, bf16[1536,1024]{1,0:T(8,128)(2,1)} %get-tuple-element.105.refs_2_, bf16[384,1024]{1,0:T(8,128)(2,1)} %get-tuple-element.62.refs_3_, ...), custom_call_target="tpu_custom_call" | custom-call | flops 6442450944 | bytes 16777216 | tf_op jit(solution)/shard_map/feed_weights/pallas_call | solution.py:30
  243.1 4.4 all-to-all-start.3
  253.4 28.6 %collective-permute-done.32 = bf16[4,4,256,128]{3,2,1,0:T(8,128)(2,1)S(1)} collective-permute-done((bf16[4,4,256,128]{3,2,1,0:T(8,128)(2,1)S(1)}, bf16[4,4,256,128]{3,2,1,0:T(8,128)(2,1)S(1)}, u32[]{:S(2)}, u32[]{:S(2)}) %collective-permute-start.32) | collective-permute-done | bytes 1048608 | tf_op jit(solution)/shard_map/ppermute | solution.py:520
  283.3 5.4 %all-to-all-start.9 = ((bf16[16,256,128]{2,1,0:T(8,128)(2,1)}), bf16[16,256,128]{2,1,0:T(8,128)(2,1)}, u32[]{:S(2)}, u32[]{:S(2)}) async-start(bf16[16,256,128]{2,1,0:T(8,128)(2,1)} %bitcast.136), calls=%async_computation.9 | async-start | bytes 2097152 | tf_op jit(solution)/shard_map/all_to_all | solution.py:789
  288.7 38.5 %attend_back.1 = (bf16[384,1024]{1,0:T(8,128)(2,1)S(1)}, bf16[384,1024]{1,0:T(8,128)(2,1)}, bf16[384,1024]{1,0:T(8,128)(2,1)S(1)}, bf16[384,1024]{1,0:T(8,128)(2...) custom-call(s32[2]{0:T(128)S(1)} %pad_add_fusion.refs_0_.me_ref, s32[6]{0:T(128)S(1)} %get-tuple-element.153.refs_1_, ...), custom_call_target="tpu_custom_call" | custom-call | flops 5435817984 | bytes 13440000 | tf_op jit(solution)/shard_map/attend_back/pallas_call | solution.py:30
  342.0 5.0 %all-to-all-start.8 = ((bf16[16,128,256]{2,1,0:T(8,128)(2,1)}), bf16[16,128,256]{2,1,0:T(8,128)(2,1)}, u32[]{:S(2)}, u32[]{:S(2)}) async-start(bf16[16,128,256]{2,1,0:T(8,128)(2,1)} %bitcast.135), calls=%async_computation.8 | async-start | bytes 2097152 | tf_op jit(solution)/shard_map/all_to_all | solution.py:789
  348.8 13.6 %collective-permute-done.18.came_ref = bf16[384,1024]{1,0:T(8,128)(2,1)S(1)} collective-permute-done((bf16[384,1024]{1,0:T(8,128)(2,1)}, bf16[384,1024]{1,0:T(8,128)(2,1)S(1)}, u32[]{:S(2)}, u32[]{:S(2)}) %collective-permute-start.18) | collective-permute-done | bytes 786464 | tf_op jit(solution)/shard_map/ppermute | solution.py:520
  362.4 4.0 tokens_back.1
  375.1 6.1 %qkv_weights.1 = bf16[2,4,3,256,128]{4,3,2,1,0:T(8,128)(2,1)S(1)} custom-call(s32[2]{0:T(128)S(1)} %pad_add_fusion.refs_0_.me_ref, bf16[1536,768]{1,0:T(8,128)(2,1)} %get-tuple-element.99.dqkv_ref, bf16[384,1024]{1,0:T(8,128)(2,1)S(1)} %copy-done.7, bf16[384,1024]{1,0:T(8,128)(2,1)} %collective-permute-done.1.refs_10_.refs_1_, ...), custom_call_target="tpu_custom_call" | custom-call | flops 2415919104 | bytes 7077888 | tf_op jit(solution)/shard_map/qkv_weights/pallas_call | solution.py:30
  381.2 6.8 %collective-permute-done.21 = f32[4,2,4,192]{3,2,1,0:T(4,128)S(1)} collective-permute-done((f32[4,2,4,192]{3,2,1,0:T(4,128)S(1)}, f32[4,2,4,192]{3,2,1,0:T(4,128)S(1)}, u32[]{:S(2)}, u32[]{:S(2)}) %collective-permute-start.21) | collective-permute-done | bytes 24608 | tf_op jit(solution)/shard_map/ppermute | solution.py:520
  388.6 4.6 all-to-all-start.6
  394.7 5.2 %all-to-all-done.6 = bf16[8,4,192]{2,1,0:T(4,128)(2,1)S(1)} async-done(((bf16[8,4,192]{2,1,0:T(4,128)(2,1)}), bf16[8,4,192]{2,1,0:T(4,128)(2,1)S(1)}, u32[]{:S(2)}, u32[]{:S(2)}) %all-to-all-start.6) | async-done | bytes 12320 | tf_op jit(solution)/shard_map/all_to_all | solution.py:503
  399.8 3.5 all-to-all-start.5
  407.3 29.1 %collective-permute-done.26 = f32[72,128]{1,0:T(8,128)S(1)} collective-permute-done((f32[72,128]{1,0:T(8,128)S(1)}, f32[72,128]{1,0:T(8,128)S(1)}, u32[]{:S(2)}, u32[]{:S(2)}) %collective-permute-start.26) | collective-permute-done | bytes 36896 | tf_op jit(solution)/shard_map/ppermute | solution.py:520
  453.9 4.8 all-to-all-start.7
  470.5 3.0 fusion.6
  473.5 7.8 %all-to-all-done.7 = bf16[4,4,256,128]{3,2,1,0:T(8,128)(2,1)S(1)} async-done(((bf16[4,4,256,128]{3,2,1,0:T(8,128)(2,1)}), bf16[4,4,256,128]{3,2,1,0:T(8,128)(2,1)S(1)}, u32[]{:S(2)}, u32[]{:S(2)}) %all-to-all-start.7) | async-done | bytes 1048608 | tf_op jit(solution)/shard_map/all_to_all | solution.py:890
  (280 shorter events, 116.8 us)
Async XLA Ops:
  7.2 149.0 %all-gather.5.cloned.1.call-start = ((), (), s32[]{:S(2)}) async-start(), calls=%async_computation.10 | async-start | bytes 2433024 | tf_op jit(solution)/shard_map/all_gather | solution.py:630
  10.6 62.4 %collective-permute-start = (s32[1536]{0:T(1024)S(1)}, s32[1536]{0:T(1024)S(1)}, u32[]{:S(2)}, u32[]{:S(2)}) collective-permute-start(s32[1536]{0:T(1024)S(1)} %reduce.3), channel_id=1, source_target_pairs={{0,0},{1,4},{2,8},{3,12},{4,1},{5,5},{6,9},{7,13},{8,2},{9,6},{10,... | collective-permute-start | bytes 18440 | tf_op jit(solution)/shard_map/ppermute | solution.py:659
  14.8 36.9 %all-to-all-start = ((bf16[8,48,1024]{2,1,0:T(8,128)(2,1)}), bf16[8,48,1024]{2,1,0:T(8,128)(2,1)S(1)}, u32[]{:S(2)}, u32[]{:S(2)}) async-start(bf16[8,48,1024]{2,1,0:T(8,128)(2,1)} %bitcast.137), calls=%async_computation | async-start | bytes 1572864 | tf_op jit(solution)/shard_map/all_to_all | solution.py:503
  23.9 133.0 %all-gather.7.cloned.1.call-start = ((), (), s32[]{:S(2)}) async-start(), calls=%async_computation.11 | async-start | bytes 2359296 | tf_op jit(solution)/shard_map/all_gather | solution.py:633
  53.3 19.7 %collective-permute-start.2 = (bf16[384,1024]{1,0:T(8,128)(2,1)S(1)}, bf16[384,1024]{1,0:T(8,128)(2,1)}, u32[]{:S(2)}, u32[]{:S(2)}) collective-permute-start(bf16[384,1024]{1,0:T(8,128)(2,1)S(1)} %first_norm.1.refs_9_.refs_0_), channel_id=1, source_target_pairs={{0,8},{4,12},{8,0},{12,4},{1,9},{5,13},{9,1},{13,5},{2,10},{6,14},... | collective-permute-start | bytes 2359304 | tf_op jit(solution)/shard_map/ppermute | solution.py:520
  56.7 50.1 %all-to-all-start.2 = ((bf16[8,48,1024]{2,1,0:T(8,128)(2,1)}), bf16[8,48,1024]{2,1,0:T(8,128)(2,1)S(1)}, u32[]{:S(2)}, u32[]{:S(2)}) async-start(bf16[8,48,1024]{2,1,0:T(8,128)(2,1)} %bitcast.138), calls=%async_computation.2 | async-start | bytes 1572864 | tf_op jit(solution)/shard_map/all_to_all | solution.py:503
  60.8 14.9 %collective-permute-start.1 = (bf16[384,1024]{1,0:T(8,128)(2,1)S(1)}, bf16[384,1024]{1,0:T(8,128)(2,1)}, u32[]{:S(2)}, u32[]{:S(2)}) collective-permute-start(bf16[384,1024]{1,0:T(8,128)(2,1)S(1)} %first_norm.1.refs_9_.refs_0_), channel_id=1, source_target_pairs={{0,4},{4,0},{8,12},{12,8},{1,5},{5,1},{9,13},{13,9},{2,6},{6,2},{1... | collective-permute-start | bytes 2359304 | tf_op jit(solution)/shard_map/ppermute | solution.py:520
  106.8 16.0 %all-to-all-start.1 = ((bf16[4,384,256]{2,1,0:T(8,128)(2,1)}), bf16[4,384,256]{2,1,0:T(8,128)(2,1)S(1)}, u32[]{:S(2)}, u32[]{:S(2)}) async-start(bf16[4,384,256]{2,1,0:T(8,128)(2,1)} %copy-done.10), calls=%async_computation.1 | async-start | bytes 1572864 | tf_op jit(solution)/shard_map/all_to_all | solution.py:507
  112.6 27.2 %collective-permute-start.8 = (bf16[384,1024]{1,0:T(8,128)(2,1)}, bf16[384,1024]{1,0:T(8,128)(2,1)}, u32[]{:S(2)}, u32[]{:S(2)}) collective-permute-start(bf16[384,1024]{1,0:T(8,128)(2,1)} %get-tuple-element.64.refs_7_), channel_id=1, source_target_pairs={{0,8},{4,12},{8,0},{12,4},{1,9},{5,13},{9,1},{13,5},{2,10},{6,14},... | collective-permute-start | bytes 2359304 | tf_op jit(solution)/shard_map/ppermute | solution.py:520
  130.9 25.2 %collective-permute-start.5 = (bf16[384,1024]{1,0:T(8,128)(2,1)}, bf16[384,1024]{1,0:T(8,128)(2,1)S(1)}, u32[]{:S(2)}, u32[]{:S(2)}) collective-permute-start(bf16[384,1024]{1,0:T(8,128)(2,1)} %get-tuple-element.62.refs_3_), channel_id=1, source_target_pairs={{0,8},{4,12},{8,0},{12,4},{1,9},{5,13},{9,1},{13,5},{2,10},{6,14},... | collective-permute-start | bytes 2359304 | tf_op jit(solution)/shard_map/ppermute | solution.py:520
  131.0 25.9 %collective-permute-start.7 = (bf16[384,1024]{1,0:T(8,128)(2,1)}, bf16[384,1024]{1,0:T(8,128)(2,1)}, u32[]{:S(2)}, u32[]{:S(2)}) collective-permute-start(bf16[384,1024]{1,0:T(8,128)(2,1)} %get-tuple-element.64.refs_7_), channel_id=1, source_target_pairs={{0,4},{4,0},{8,12},{12,8},{1,5},{5,1},{9,13},{13,9},{2,6},{6,2},{1... | collective-permute-start | bytes 2359304 | tf_op jit(solution)/shard_map/ppermute | solution.py:520
  131.1 25.9 %collective-permute-start.4 = (bf16[384,1024]{1,0:T(8,128)(2,1)}, bf16[384,1024]{1,0:T(8,128)(2,1)}, u32[]{:S(2)}, u32[]{:S(2)}) collective-permute-start(bf16[384,1024]{1,0:T(8,128)(2,1)} %get-tuple-element.62.refs_3_), channel_id=1, source_target_pairs={{0,4},{4,0},{8,12},{12,8},{1,5},{5,1},{9,13},{13,9},{2,6},{6,2},{1... | collective-permute-start | bytes 2359304 | tf_op jit(solution)/shard_map/ppermute | solution.py:520
  139.8 17.2 %collective-permute-start.9 = (bf16[384,1024]{1,0:T(8,128)(2,1)}, bf16[384,1024]{1,0:T(8,128)(2,1)}, u32[]{:S(2)}, u32[]{:S(2)}) collective-permute-start(bf16[384,1024]{1,0:T(8,128)(2,1)} %collective-permute-done.8.refs_9_), channel_id=1, source_target_pairs={{0,4},{4,0},{8,12},{12,8},{1,5},{5,1},{9,13},{13,9},{2,6},{6,2},{1... | collective-permute-start | bytes 2359304 | tf_op jit(solution)/shard_map/ppermute | solution.py:520
  186.6 20.4 %collective-permute-start.15 = (bf16[384,1024]{1,0:T(8,128)(2,1)S(1)}, bf16[384,1024]{1,0:T(8,128)(2,1)S(1)}, u32[]{:S(2)}, u32[]{:S(2)}) collective-permute-start(bf16[384,1024]{1,0:T(8,128)(2,1)S(1)} %add_convert_fusion.2), channel_id=1, source_target_pairs={{0,8},{4,12},{8,0},{12,4},{1,9},{5,13},{9,1},{13,5},{2,10},{6,14},... | collective-permute-start | bytes 2359304 | tf_op jit(solution)/shard_map/ppermute | solution.py:520
  187.0 51.0 %collective-permute-start.10 = (bf16[384,1024]{1,0:T(8,128)(2,1)}, bf16[384,1024]{1,0:T(8,128)(2,1)}, u32[]{:S(2)}, u32[]{:S(2)}) collective-permute-start(bf16[384,1024]{1,0:T(8,128)(2,1)} %get-tuple-element.66), channel_id=1, source_target_pairs={{0,4},{4,0},{8,12},{12,8},{1,5},{5,1},{9,13},{13,9},{2,6},{6,2},{1... | collective-permute-start | bytes 2359304 | tf_op jit(solution)/shard_map/ppermute | solution.py:520
  189.9 49.6 %collective-permute-start.12 = (bf16[384,1024]{1,0:T(8,128)(2,1)}, bf16[384,1024]{1,0:T(8,128)(2,1)}, u32[]{:S(2)}, u32[]{:S(2)}) collective-permute-start(bf16[384,1024]{1,0:T(8,128)(2,1)} %add_convert_fusion.4), channel_id=1, source_target_pairs={{0,8},{4,12},{8,0},{12,4},{1,9},{5,13},{9,1},{13,5},{2,10},{6,14},... | collective-permute-start | bytes 2359304 | tf_op jit(solution)/shard_map/ppermute | solution.py:520
  218.3 24.8 %all-to-all-start.4 = ((bf16[4,384,256]{2,1,0:T(8,128)(2,1)}), bf16[4,384,256]{2,1,0:T(8,128)(2,1)}, u32[]{:S(2)}, u32[]{:S(2)}) async-start(bf16[4,384,256]{2,1,0:T(8,128)(2,1)} %copy-done.8), calls=%async_computation.4 | async-start | bytes 1572864 | tf_op jit(solution)/shard_map/all_to_all | solution.py:507
  243.1 40.2 %all-to-all-start.3 = ((bf16[8,48,1024]{2,1,0:T(8,128)(2,1)}), bf16[8,48,1024]{2,1,0:T(8,128)(2,1)}, u32[]{:S(2)}, u32[]{:S(2)}) async-start(bf16[8,48,1024]{2,1,0:T(8,128)(2,1)} %bitcast.134), calls=%async_computation.3 | async-start | bytes 1572864 | tf_op jit(solution)/shard_map/all_to_all | solution.py:503
  249.0 33.0 %collective-permute-start.32 = (bf16[4,4,256,128]{3,2,1,0:T(8,128)(2,1)S(1)}, bf16[4,4,256,128]{3,2,1,0:T(8,128)(2,1)S(1)}, u32[]{:S(2)}, u32[]{:S(2)}) collective-permute-start(bf16[4,4,256,128]{3,2,1,0:T(8,128)(2,1)S(1)} %slice_bitcast_fusion), channel_id=1, source_target_pairs={{0,16},{16,0},{1,17},{17,1},{2,18},{18,2},{3,19},{19,3},{4,20},{20... | collective-permute-start | bytes 3145736 | tf_op jit(solution)/shard_map/ppermute | solution.py:520
  253.3 76.1 %collective-permute-start.31 = (bf16[4,4,128,256]{3,2,1,0:T(8,128)(2,1)}, bf16[4,4,128,256]{3,2,1,0:T(8,128)(2,1)}, u32[]{:S(2)}, u32[]{:S(2)}) collective-permute-start(bf16[4,4,128,256]{3,2,1,0:T(8,128)(2,1)} %slice_bitcast_fusion.1), channel_id=1, source_target_pairs={{0,16},{16,0},{1,17},{17,1},{2,18},{18,2},{3,19},{19,3},{4,20},{20... | collective-permute-start | bytes 3145736 | tf_op jit(solution)/shard_map/ppermute | solution.py:520
  283.3 58.7 %all-to-all-start.9 = ((bf16[16,256,128]{2,1,0:T(8,128)(2,1)}), bf16[16,256,128]{2,1,0:T(8,128)(2,1)}, u32[]{:S(2)}, u32[]{:S(2)}) async-start(bf16[16,256,128]{2,1,0:T(8,128)(2,1)} %bitcast.136), calls=%async_computation.9 | async-start | bytes 2097152 | tf_op jit(solution)/shard_map/all_to_all | solution.py:789
  332.3 14.7 %collective-permute-start.16 = (bf16[384,1024]{1,0:T(8,128)(2,1)}, bf16[384,1024]{1,0:T(8,128)(2,1)}, u32[]{:S(2)}, u32[]{:S(2)}) collective-permute-start(bf16[384,1024]{1,0:T(8,128)(2,1)} %get-tuple-element.85), channel_id=1, source_target_pairs={{0,4},{4,0},{8,12},{12,8},{1,5},{5,1},{9,13},{13,9},{2,6},{6,2},{1... | collective-permute-start | bytes 2359304 | tf_op jit(solution)/shard_map/ppermute | solution.py:520
  334.8 27.6 %collective-permute-start.18 = (bf16[384,1024]{1,0:T(8,128)(2,1)}, bf16[384,1024]{1,0:T(8,128)(2,1)S(1)}, u32[]{:S(2)}, u32[]{:S(2)}) collective-permute-start(bf16[384,1024]{1,0:T(8,128)(2,1)} %add_convert_fusion), channel_id=1, source_target_pairs={{0,8},{4,12},{8,0},{12,4},{1,9},{5,13},{9,1},{13,5},{2,10},{6,14},... | collective-permute-start | bytes 2359304 | tf_op jit(solution)/shard_map/ppermute | solution.py:520
  340.3 29.7 %collective-permute-start.23 = (bf16[2,4,256,128]{3,2,1,0:T(8,128)(2,1)}, bf16[2,4,256,128]{3,2,1,0:T(8,128)(2,1)}, u32[]{:S(2)}, u32[]{:S(2)}) collective-permute-start(bf16[2,4,256,128]{3,2,1,0:T(8,128)(2,1)} %get-tuple-element.98), channel_id=1, source_target_pairs={{0,4},{4,0},{8,12},{12,8},{1,5},{5,1},{9,13},{13,9},{2,6},{6,2},{1... | collective-permute-start | bytes 1572872 | tf_op jit(solution)/shard_map/ppermute | solution.py:520
  340.3 53.0 %collective-permute-start.22 = (bf16[2,4,256,128]{3,2,1,0:T(8,128)(2,1)}, bf16[2,4,256,128]{3,2,1,0:T(8,128)(2,1)}, u32[]{:S(2)}, u32[]{:S(2)}) collective-permute-start(bf16[2,4,256,128]{3,2,1,0:T(8,128)(2,1)} %get-tuple-element.96), channel_id=1, source_target_pairs={{0,4},{4,0},{8,12},{12,8},{1,5},{5,1},{9,13},{13,9},{2,6},{6,2},{1... | collective-permute-start | bytes 1572872 | tf_op jit(solution)/shard_map/ppermute | solution.py:520
  342.0 46.6 %all-to-all-start.8 = ((bf16[16,128,256]{2,1,0:T(8,128)(2,1)}), bf16[16,128,256]{2,1,0:T(8,128)(2,1)}, u32[]{:S(2)}, u32[]{:S(2)}) async-start(bf16[16,128,256]{2,1,0:T(8,128)(2,1)} %bitcast.135), calls=%async_computation.8 | async-start | bytes 2097152 | tf_op jit(solution)/shard_map/all_to_all | solution.py:789
  372.0 21.3 %collective-permute-start.24 = (bf16[2,4,256,128]{3,2,1,0:T(8,128)(2,1)}, bf16[2,4,256,128]{3,2,1,0:T(8,128)(2,1)}, u32[]{:S(2)}, u32[]{:S(2)}) collective-permute-start(bf16[2,4,256,128]{3,2,1,0:T(8,128)(2,1)} %add_convert_fusion.7), channel_id=1, source_target_pairs={{0,8},{4,12},{8,0},{12,4},{1,9},{5,13},{9,1},{13,5},{2,10},{6,14},... | collective-permute-start | bytes 1572872 | tf_op jit(solution)/shard_map/ppermute | solution.py:520
  374.7 13.3 %collective-permute-start.21 = (f32[4,2,4,192]{3,2,1,0:T(4,128)S(1)}, f32[4,2,4,192]{3,2,1,0:T(4,128)S(1)}, u32[]{:S(2)}, u32[]{:S(2)}) collective-permute-start(f32[4,2,4,192]{3,2,1,0:T(4,128)S(1)} %bitcast_add_fusion), channel_id=1, source_target_pairs={{0,8},{4,12},{8,0},{12,4},{1,9},{5,13},{9,1},{13,5},{2,10},{6,14},... | collective-permute-start | bytes 73736 | tf_op jit(solution)/shard_map/ppermute | solution.py:520
  399.8 53.2 %all-to-all-start.5 = ((bf16[8,48,1024]{2,1,0:T(8,128)(2,1)}), bf16[8,48,1024]{2,1,0:T(8,128)(2,1)S(1)}, u32[]{:S(2)}, u32[]{:S(2)}) async-start(bf16[8,48,1024]{2,1,0:T(8,128)(2,1)} %bitcast.20), calls=%async_computation.5 | async-start | bytes 1572864 | tf_op jit(solution)/shard_map/all_to_all | solution.py:503
  404.5 46.0 %collective-permute-start.25 = (bf16[4,4,256,128]{3,2,1,0:T(8,128)(2,1)}, bf16[4,4,256,128]{3,2,1,0:T(8,128)(2,1)}, u32[]{:S(2)}, u32[]{:S(2)}) collective-permute-start(bf16[4,4,256,128]{3,2,1,0:T(8,128)(2,1)} %fusion.5), channel_id=1, source_target_pairs={{0,16},{16,0},{1,17},{17,1},{2,18},{18,2},{3,19},{19,3},{4,20},{20... | collective-permute-start | bytes 3145736 | tf_op jit(solution)/shard_map/ppermute | solution.py:520
  407.1 29.3 %collective-permute-start.26 = (f32[72,128]{1,0:T(8,128)S(1)}, f32[72,128]{1,0:T(8,128)S(1)}, u32[]{:S(2)}, u32[]{:S(2)}) collective-permute-start(f32[72,128]{1,0:T(8,128)S(1)} %pad_bitcast_fusion), channel_id=1, source_target_pairs={{0,16},{16,0},{1,17},{17,1},{2,18},{18,2},{3,19},{19,3},{4,20},{20... | collective-permute-start | bytes 110600 | tf_op jit(solution)/shard_map/ppermute | solution.py:520
  453.9 27.4 %all-to-all-start.7 = ((bf16[4,4,256,128]{3,2,1,0:T(8,128)(2,1)}), bf16[4,4,256,128]{3,2,1,0:T(8,128)(2,1)S(1)}, u32[]{:S(2)}, u32[]{:S(2)}) async-start(bf16[4,4,256,128]{3,2,1,0:T(8,128)(2,1)} %fusion.2), calls=%async_computation.7 | async-start | bytes 2097152 | tf_op jit(solution)/shard_map/all_to_all | solution.py:890
  (57 other events, 581.9 us)
Sparse Core Ops, SparseCore 0:
  10.7 75.1 all-gather.4
  88.6 48.0 all-gather.6

commit v3 on v2

v3 whole, which is shorter than its diff:
```python
import functools

import jax
import jax.numpy as jnp
from jax import lax
from jax.experimental import pallas as pl
from jax.experimental.pallas import tpu as pltpu
from jax.sharding import Mesh, PartitionSpec as P

BF = jnp.bfloat16
F32 = jnp.float32
SMEM = pl.BlockSpec(memory_space=pltpu.SMEM)
VMEM = pl.BlockSpec(memory_space=pltpu.VMEM)
ANY = pl.BlockSpec(memory_space=pl.ANY)
HBM = "hbm"
LIMIT = 40
PLAIN = ((1,), (0,))
BY_ROW = ((1,), (1,))


def shape_of(shape, dtype):
    return jax.ShapeDtypeStruct(shape, dtype)


def dot(left, right, dims=PLAIN):
    return lax.dot_general(left, right, (dims, ((), ())), preferred_element_type=F32)


def call(name, kernel, operands, specs, outs, scratch=(), limit=LIMIT, out_specs=None):
    out_specs = out_specs or tuple(HBM if o.size >= 65536 else VMEM for o in outs)
    n_in, n_out, n_scratch = len(specs), len(outs), len(scratch)
    staged_in = [i for i, spec in enumerate(specs) if spec is HBM]
    staged_out = [i for i, spec in enumerate(out_specs) if spec is HBM]
    staged = [pltpu.VMEM(operands[i].shape, operands[i].dtype) for i in staged_in]
    staged += [pltpu.VMEM(outs[i].shape, outs[i].dtype) for i in staged_out]
    sems = [pltpu.SemaphoreType.DMA((len(staged),))] if staged else []

    def body(*refs):
        given, made = list(refs[:n_in]), list(refs[n_in : n_in + n_out])
        own = refs[n_in + n_out : n_in + n_out + n_scratch]
        held = refs[n_in + n_out + n_scratch :]
        copies = []
        for place, i in enumerate(staged_in):
            copies.append(pltpu.make_async_copy(given[i], held[place], held[-1].at[place]))
            copies[-1].start()
            given[i] = held[place]
        backs = []
        for place, i in enumerate(staged_out, len(staged_in)):
            backs.append(pltpu.make_async_copy(held[place], made[i], held[-1].at[place]))
            made[i] = held[place]
        for copy in copies:
            copy.wait()
        kernel(*given, *made, *own)
        for copy in backs:
            copy.start()
        for copy in backs:
            copy.wait()

    return pl.pallas_call(
        body,
        name=name,
        out_shape=tuple(outs),
        in_specs=[ANY if spec is HBM else spec for spec in specs],
        out_specs=tuple(ANY if spec is HBM else spec for spec in out_specs),
        scratch_shapes=list(scratch) + staged + sems,
        compiler_params=pltpu.CompilerParams(vmem_limit_bytes=limit * 1024 * 1024),
        cost_estimate=pl.CostEstimate(flops=1, bytes_accessed=1, transcendentals=0),
    )(*operands)


def row_norm(values):
    centre = values - jnp.mean(values, axis=-1, keepdims=True)
    inverse = lax.rsqrt(jnp.mean(centre * centre, axis=-1, keepdims=True) + 1e-06)
    return (centre * inverse, inverse)


def norm_back(gradient, normed, inverse):
    return inverse * (
        gradient
        - jnp.mean(gradient, axis=-1, keepdims=True)
        - normed * jnp.mean(gradient * normed, axis=-1, keepdims=True)
    )


def mod_rows(mod_ref, part, item, width):
    cols = slice(part * width, (part + 1) * width)
    rows = jnp.broadcast_to(mod_ref[0:1, cols], (item.shape[0], width))
    for index in range(1, mod_ref.shape[0]):
        rows = jnp.where(item == index, mod_ref[index : index + 1, cols], rows)
    return rows


def add_item_sums(sums_ref, part, item, values, count):
    width = values.shape[1]
    cols = slice(part * width, (part + 1) * width)
    for index in range(count):
        kept = jnp.where(item == index, values, 0.0)
        sums_ref[index : index + 1, cols] += jnp.sum(kept, axis=0, keepdims=True)


def same_head(width, head_dim):
    row = lax.broadcasted_iota(jnp.int32, (width, width), 0) // head_dim
    col = lax.broadcasted_iota(jnp.int32, (width, width), 1) // head_dim
    return (row == col).astype(BF)


def head_sums(values, same):
    high = values.astype(BF)
    low = (values - high.astype(F32)).astype(BF)
    return dot(high, same) + dot(low, same)


def chunks(rows, size):
    return pl.loop(0, rows // size)


def at(index, size):
    return pl.ds(pl.multiple_of(index * size, size), size)


def first_norm_kernel(x_ref, mod_ref, item_ref, out_ref):
    rows, width = x_ref.shape

    @chunks(rows, 64)
    def _(i):
        r = at(i, 64)
        item = item_ref[r, :]
        normed, _ = row_norm(x_ref[r, :].astype(F32))
        scale, shift = mod_rows(mod_ref, 2, item, width), mod_rows(mod_ref, 4, item, width)
        out_ref[r, :] = (normed * (1.0 + scale) + shift).astype(BF)


def grad_mlp_kernel(up_ref, mod_ref, item_ref, out_ref, sum_ref):
    rows, width = up_ref.shape
    sum_ref[...] = jnp.zeros_like(sum_ref)

    @chunks(rows, 64)
    def _(i):
        r = at(i, 64)
        gamma = mod_rows(mod_ref, 1, item_ref[r, :], width)
        grad = (up_ref[r, :].astype(F32) * gamma).astype(BF)
        out_ref[r, :] = grad
        sum_ref[0:1, :] += jnp.sum(grad.astype(F32), axis=0, keepdims=True)


def load_columns(weight_ref, held, sems, offset_of, parts, sub):
    copies = []
    for t in range(3):
        for p in range(parts):
            copies.append(
                pltpu.make_async_copy(
                    weight_ref.at[t, :, pl.ds(pl.multiple_of(offset_of(p), sub), sub)],
                    held.at[:, pl.ds((t * parts + p) * sub, sub)],
                    sems.at[t * parts + p],
                )
            )
    for copy in copies:
        copy.start()
    return copies


def qkv_kernel(dims, *refs):
    group, segs, head_dim, parts = dims
    me_ref, temper_ref, qb_ref, vb_ref, w_ref = refs[:5]
    blocks = refs[5 : 5 + group]
    q_ref, k_ref, v_ref, qp_ref, kp_ref, held, sems = refs[5 + group :]
    width = q_ref.shape[1]
    rows = blocks[0].shape[0]
    seg, sub = rows // segs, width // parts
    me = me_ref[0]
    copies = load_columns(w_ref, held, sems, lambda p: (p * group + me) * sub, parts, sub)
    same = same_head(width, head_dim)
    for copy in copies:
        copy.wait()
    for k in range(group):
        for y in range(segs):
            ranks = pl.ds(pl.multiple_of((y * group + (me ^ k)) * seg, 16), seg)
            made = dot(blocks[k][y * seg : (y + 1) * seg, :], held[...])
            query = made[:, :width] + qb_ref[...]
            key = made[:, width : 2 * width]
            qp_ref[ranks, :] = query
            kp_ref[ranks, :] = key
            inverse = lax.rsqrt(head_sums(query * query, same) + 1e-06)
            q_ref[ranks, :] = (query * inverse * temper_ref[...]).astype(BF)
            inverse = lax.rsqrt(head_sums(key * key, same) + 1e-06)
            k_ref[ranks, :] = (key * inverse).astype(BF)
            v_ref[ranks, :] = (made[:, 2 * width :] + vb_ref[...]).astype(BF)


def attend_kernel(
    dims, first_ref, last_ref, lo_ref, hi_ref, q_ref, k_ref, v_ref,
    out_ref, out_t_ref, lse_ref, v_t, out_s, acc, total,
):
    group, segs, head_dim, block = dims
    pack_len, width = q_ref.shape
    rows = out_ref.shape[1]
    seg = rows // segs
    pair = 128 // head_dim
    heads = width // head_dim
    lanes = lax.broadcasted_iota(jnp.int32, (1, 128), 1) // head_dim
    v_t[...] = v_ref[...].T

    @pl.loop(0, pack_len // block)
    def _(q_block):
        q_rows = at(q_block, block)
        q_t = q_ref[q_rows, :].T
        low, high = lo_ref[:, q_rows], hi_ref[:, q_rows]
        acc[...] = jnp.zeros_like(acc)
        total[...] = jnp.zeros_like(total)

        @pl.loop(first_ref[q_block], last_ref[q_block])
        def _(k_block):
            k_rows = at(k_block, block)
            index = k_block * block + lax.broadcasted_iota(jnp.int32, (block, block), 0)
            seen = (index >= low) & (index < high)
            for h in range(heads):
                own = pl.ds(h * head_dim, head_dim)
                near = slice(h // pair * 128, (h // pair + 1) * 128)
                keys = k_ref[k_rows, near]
                scores = dot(jnp.where(lanes == h % pair, keys, jnp.zeros_like(keys)), q_t[near, :])
                raised = jnp.where(seen, jnp.exp(scores), 0.0)
                total[h : h + 1, :] += jnp.sum(raised, axis=0, keepdims=True)
                acc[own, :] += dot(v_t[own, k_rows], raised.astype(BF))

        for h in range(heads):
            own = pl.ds(h * head_dim, head_dim)
            acc[own, :] = acc[own, :] / total[h : h + 1, :]
            lse_ref[h : h + 1, q_rows] = jnp.log(total[h : h + 1, :])
        out_t_ref[:, q_rows] = acc[...]
        out_s[q_rows, :] = acc[...].T.astype(BF)

    for y in range(segs):
        for g in range(group):
            start = (y * group + g) * seg
            out_ref[g, y * seg : (y + 1) * seg, :] = out_s[start : start + seg, :]


def attend_back_heads(dims, refs, scratch, outs):
    group, segs, head_dim, block, near = dims
    first_ref, last_ref, lo_ref, hi_ref, in_ref, q_ref, k_ref, v_ref, out_t_ref, lse_ref = refs
    g_s, k_t, dk_acc, dv_acc, acc, sums = scratch
    dq_ref, dk_ref, dv_ref = outs
    pack_len = q_ref.shape[0]
    seg = in_ref.shape[1] // segs
    pair = 128 // head_dim
    cols = slice(near * 128, (near + 1) * 128)
    lanes = lax.broadcasted_iota(jnp.int32, (1, 128), 1) // head_dim
    for y in range(segs):
        for g in range(group):
            start = (y * group + g) * seg
            g_s[start : start + seg, :] = in_ref[g, y * seg : (y + 1) * seg, cols]
    k_t[...] = k_ref[:, cols].T
    dk_acc[...] = jnp.zeros_like(dk_acc)
    dv_acc[...] = jnp.zeros_like(dv_acc)

    @pl.loop(0, pack_len // block)
    def _(q_block):
        q_rows = at(q_block, block)
        queries, grads = q_ref[q_rows, cols], g_s[q_rows, :]
        q_t, g_t = queries.T, grads.T
        low, high = lo_ref[:, q_rows], hi_ref[:, q_rows]
        weighted = g_t.astype(F32) * out_t_ref[cols, q_rows]
        for h in range(pair):
            sums[h : h + 1, :] = jnp.sum(
                weighted[h * head_dim : (h + 1) * head_dim, :], axis=0, keepdims=True
            )
        acc[...] = jnp.zeros_like(acc)

        @pl.loop(first_ref[q_block], last_ref[q_block])
        def _(k_block):
            k_rows = at(k_block, block)
            keys, values = k_ref[k_rows, cols], v_ref[k_rows, cols]
            index = k_block * block + lax.broadcasted_iota(jnp.int32, (block, block), 0)
            seen = (index >= low) & (index < high)
            for h in range(pair):
                own = pl.ds(h * head_dim, head_dim)
                row = near * pair + h
                mine = lanes == h
                scores = dot(jnp.where(mine, keys, jnp.zeros_like(keys)), q_t)
                probs = jnp.where(seen, jnp.exp(scores - lse_ref[row : row + 1, q_rows]), 0.0)
                grad_probs = dot(jnp.where(mine, values, jnp.zeros_like(values)), g_t)
                grad_scores = (probs * (grad_probs - sums[h : h + 1, :])).astype(BF)
                acc[own, :] += dot(k_t[own, k_rows], grad_scores)
                dk_acc[k_rows, :] += dot(
                    grad_scores, jnp.where(mine, queries, jnp.zeros_like(queries))
                )
                dv_acc[k_rows, :] += dot(
                    probs.astype(BF), jnp.where(mine, grads, jnp.zeros_like(grads))
                )

        dq_ref[q_rows, :] = acc[...].T.astype(BF)

    dk_ref[...] = dk_acc[...].astype(BF)
    dv_ref[...] = dv_acc[...].astype(BF)


def attend_back_kernel(dims, *refs):
    attend_back_heads(dims, refs[:10], refs[13:], refs[10:13])


def qkv_back_kernel(dims, *refs):
    group, segs, head_dim, parts, pairs, tile_count = dims
    add_blocks(refs[:tile_count], refs[-4:-2])
    refs = refs[tile_count:-4] + refs[-2:]
    me_ref, temper_ref, w_ref, qp_ref, kp_ref = refs[:5]
    grads = [refs[5 + 3 * p : 8 + 3 * p] for p in range(pairs)]
    rest = refs[5 + 3 * pairs :]
    sent = rest[:group]
    dqkv_ref, sums_ref, held, sems = rest[group:]
    width = qp_ref.shape[1]
    rows = sent[0].shape[0]
    seg, sub = rows // segs, width // parts
    me = me_ref[0]
    copies = load_columns(w_ref, held, sems, lambda p: (p * group + me) * sub, parts, sub)
    same = same_head(width, head_dim)
    sums_ref[...] = jnp.zeros_like(sums_ref)

    def back(gradient, pre):
        inverse = lax.rsqrt(head_sums(pre * pre, same) + 1e-06)
        unit = pre * inverse
        return inverse * (gradient - unit * head_sums(gradient * unit, same)), unit

    def joined(which, ranks):
        return jnp.concatenate([grads[p][which][ranks, :] for p in range(pairs)], axis=1)

    for copy in copies:
        copy.wait()
    for k in reversed(range(group)):
        for y in range(segs):
            ranks = pl.ds(pl.multiple_of((y * group + (me ^ k)) * seg, 16), seg)
            own = slice(k * rows + y * seg, k * rows + (y + 1) * seg)
            grad = joined(0, ranks).astype(F32) * temper_ref[...]
            grad_query, unit = back(grad, qp_ref[ranks, :])
            grad_query = grad_query.astype(BF)
            grad_key, _ = back(joined(1, ranks).astype(F32), kp_ref[ranks, :])
            grad_value = joined(2, ranks)
            dqkv_ref[own, :width] = grad_query
            dqkv_ref[own, width : 2 * width] = grad_key.astype(BF)
            dqkv_ref[own, 2 * width :] = grad_value
            for index, values in enumerate((grad_query, grad_value, grad * unit)):
                sums_ref[index : index + 1, :] += jnp.sum(
                    values.astype(F32), axis=0, keepdims=True
                )
        sent[k][...] = dot(
            dqkv_ref[k * rows : (k + 1) * rows, :], held[...], BY_ROW
        ).astype(BF)


def project_kernel(
    parts, ret_ref, wp_ref, pb_ref, x_ref, mod_ref, item_ref, attn_ref, branch_ref, middle_ref, out_ref
):
    group, rows, width = ret_ref.shape
    model = x_ref.shape[1]
    sub = width // parts
    for g in range(group):
        for p in range(parts):
            start = (p * group + g) * sub
            attn_ref[:, start : start + sub] = ret_ref[g, :, p * sub : (p + 1) * sub]
    branch_ref[...] = dot(attn_ref[...], wp_ref[...]) + pb_ref[...].astype(F32)

    @chunks(rows, 64)
    def _(i):
        r = at(i, 64)
        item = item_ref[r, :]
        middle = x_ref[r, :].astype(F32) + mod_rows(mod_ref, 0, item, model) * branch_ref[r, :]
        middle_ref[r, :] = middle
        normed, _ = row_norm(middle)
        scale, shift = mod_rows(mod_ref, 3, item, model), mod_rows(mod_ref, 5, item, model)
        out_ref[r, :] = (normed * (1.0 + scale) + shift).astype(BF)


def add_blocks(terms, outs):
    count = outs[0].shape[0]
    for j in range(terms[0].shape[0]):
        made = sum(term[j].astype(F32) for term in terms).astype(BF)
        outs[j // count][j % count] = made


def weights_kernel(fc1_ref, fc2_ref, w1_ref, w2_ref, sems):
    segs, head_size, _, hidden = fc1_ref.shape
    half = fc2_ref.shape[3]
    copies = []
    for y in range(segs):
        for z in range(head_size):
            own = pl.ds(z * hidden, hidden)
            rows = pl.ds(y * half, half)
            for source, target in (
                (fc1_ref.at[y, z, pl.ds(0, half), :], w1_ref.at[rows, own]),
                (fc2_ref.at[y, z], w2_ref.at[own, rows]),
            ):
                copies.append(pltpu.make_async_copy(source, target, sems.at[len(copies)]))
                copies[-1].start()
    for copy in copies:
        copy.wait()


def feed_kernel(count, *refs):
    w1, w2, b1_ref = refs[:3]
    ins, grads = refs[3 : 3 + count], refs[3 + count : 3 + 2 * count]
    rest = refs[3 + 2 * count :]
    back, outs = rest[:count], rest[count : 2 * count]
    act_ref, gh_ref, sum_ref = rest[2 * count : 2 * count + 3]
    in_s, grad_s, back_s, out_s, act_s, gh_s, pre, grad, in_sems, out_sems = rest[2 * count + 3 :]
    rows = ins[0].shape[0]
    loads, stores = [], []
    for k in range(count):
        pair = (
            pltpu.make_async_copy(ins[k], in_s.at[k], in_sems.at[2 * k]),
            pltpu.make_async_copy(grads[k], grad_s.at[k], in_sems.at[2 * k + 1]),
        )
        pair[0].start()
        pair[1].start()
        loads.append(pair)
    sum_ref[...] = jnp.zeros_like(sum_ref)

    def store(source, target, index):
        stores.append(pltpu.make_async_copy(source, target, out_sems.at[index]))
        stores[-1].start()

    def front(k):
        loads[k][0].wait()
        pre[k % 2] = dot(in_s[k], w1[...]) + b1_ref[...]
        loads[k][1].wait()
        grad[k % 2] = dot(grad_s[k], w2[...], BY_ROW)

    def middle(k):
        total = 0.0
        for start in range(0, rows, 32):
            r = slice(start, start + 32)
            value = pre[k % 2, r, :]
            square = value * value
            gate = jnp.tanh(value * (0.7978845608028654 + 0.035677408136300125 * square))
            half = 0.5 + 0.5 * gate
            act = value * half
            slope = half + act * (1.0 - gate) * (0.7978845608028654 + 0.10703222440890037 * square)
            back_grad = (slope * grad[k % 2, r, :]).astype(BF)
            act_s[k, r, :] = act.astype(BF)
            gh_s[k, r, :] = back_grad
            total = total + jnp.sum(back_grad.astype(F32), axis=0, keepdims=True)
        sum_ref[0:1, :] += total
        own = pl.ds(k * rows, rows)
        store(act_s.at[k], act_ref.at[own, :], 4 * k)
        store(gh_s.at[k], gh_ref.at[own, :], 4 * k + 1)

    def end(k):
        back_s[k] = dot(gh_s[k], w1[...], BY_ROW).astype(BF)
        store(back_s.at[k], back[k], 4 * k + 2)
        out_s[k] = dot(act_s[k], w2[...]).astype(BF)
        store(out_s.at[k], outs[k], 4 * k + 3)

    order = list(reversed(range(count)))
    front(order[0])
    for place, k in enumerate(order):
        if place + 1 < count:
            front(order[place + 1])
        middle(k)
        end(k)
    for started in stores:
        started.wait()


def turned(index, count):
    made = 0
    while count > 1:
        made, index, count = made * 2 + index % 2, index // 2, count // 2
    return made


def feed_weights_kernel(dims, *refs):
    count, group, split, halves = dims
    me_ref, acts, ghs = refs[0], refs[1 : 1 + halves], refs[1 + halves : 1 + 2 * halves]
    refs = refs[1 + 2 * halves :]
    ins, grads, rest = refs[:count], refs[count : 2 * count], refs[2 * count :]
    outs, (in_t, grad_t, act_s, gh_s) = rest[:split], rest[split:]
    rows, model = ins[0].shape
    for k in range(count):
        own = slice(k * rows, (k + 1) * rows)
        in_t[:, own] = ins[k][...].T
        grad_t[:, own] = grads[k][...].T
    for k in range(halves):
        own = slice(k * acts[k].shape[0], (k + 1) * acts[k].shape[0])
        act_s[own, :] = acts[k][...]
        gh_s[own, :] = ghs[k][...]
    part = model // split
    fine = part // group
    head_size, _, _, _, hidden = outs[0].shape
    for y in reversed(range(split)):
        for which, left, right in ((0, in_t, gh_s), (1, grad_t, act_s)):
            start = pl.multiple_of((me_ref[1] ^ y) * part, part) if split > 1 else 0
            for j in range(head_size):
                z = me_ref[2] ^ turned(j, head_size)
                cols = slice(None)
                if split > 1:
                    cols = pl.ds(pl.multiple_of(z * hidden, hidden), hidden)
                made = dot(left[pl.ds(start, part), :], right[:, cols]).astype(BF)
                for g in range(group):
                    to = (me_ref[0] ^ g) if group > 1 else 0
                    outs[y][j, to, which] = made[g * fine : (g + 1) * fine, :]


def middle_back_kernel(
    dims, middle_ref, branch_ref, up_ref, mod_ref, item_ref, wp_ref, *refs
):
    parts, items, count = dims
    terms, (out_ref, gb_ref, gm_ref, sums_ref, col_ref, attn) = refs[:count], refs[count:]
    rows, model = middle_ref.shape
    group, _, width = out_ref.shape
    sub = width // parts
    sums_ref[...] = jnp.zeros_like(sums_ref)
    col_ref[...] = jnp.zeros_like(col_ref)

    @chunks(rows, 64)
    def _(i):
        r = at(i, 64)
        item = item_ref[r, :]
        grad_in = sum(term[r, :].astype(F32) for term in terms)
        normed, inverse = row_norm(middle_ref[r, :])
        scale = mod_rows(mod_ref, 3, item, model)
        grad_middle = up_ref[r, :].astype(F32) + norm_back(grad_in * (1.0 + scale), normed, inverse)
        gm_ref[r, :] = grad_middle
        grad_branch = (grad_middle * mod_rows(mod_ref, 0, item, model)).astype(BF)
        gb_ref[r, :] = grad_branch
        col_ref[0:1, :] += jnp.sum(grad_branch.astype(F32), axis=0, keepdims=True)
        add_item_sums(sums_ref, 0, item, grad_middle * branch_ref[r, :], items)
        add_item_sums(sums_ref, 1, item, grad_in * normed, items)
        add_item_sums(sums_ref, 2, item, grad_in, items)

    attn[...] = dot(gb_ref[...], wp_ref[...], BY_ROW).astype(BF)
    for g in range(group):
        for p in range(parts):
            start = (p * group + g) * sub
            out_ref[g, :, p * sub : (p + 1) * sub] = attn[:, start : start + sub]


def output_kernel(dims, middle_ref, up_ref, mod_ref, item_ref, bias_ref, *refs):
    items, count, proj_count = dims
    terms, refs = refs[:count], refs[count:]
    projs, (out_ref, sums_ref, proj_ref) = refs[:proj_count], refs[proj_count:]
    proj_ref[...] = sum(proj[...].astype(F32) for proj in projs).astype(BF)
    rows, model = middle_ref.shape
    sums_ref[...] = jnp.zeros_like(sums_ref)

    @chunks(rows, 64)
    def _(i):
        r = at(i, 64)
        item = item_ref[r, :]
        made = sum(term[r, :].astype(F32) for term in terms) + bias_ref[...].astype(F32)
        gamma = mod_rows(mod_ref, 1, item, model)
        out_ref[r, :] = (middle_ref[r, :] + gamma * made).astype(BF)
        add_item_sums(sums_ref, 0, item, up_ref[r, :].astype(F32) * made, items)


def tokens_back_kernel(dims, x_ref, gm_ref, mod_ref, item_ref, *refs):
    items, count, tile_count = dims
    terms, refs = refs[:count], refs[count:]
    tiles, (out_ref, sums_ref, kept_ref, sent_ref) = refs[:tile_count], refs[tile_count:]
    add_blocks(tiles, (kept_ref, sent_ref))
    rows, model = x_ref.shape
    sums_ref[...] = jnp.zeros_like(sums_ref)

    @chunks(rows, 64)
    def _(i):
        r = at(i, 64)
        item = item_ref[r, :]
        grad_in = sum(term[r, :].astype(F32) for term in terms)
        normed, inverse = row_norm(x_ref[r, :].astype(F32))
        scale = mod_rows(mod_ref, 2, item, model)
        out_ref[r, :] = (
            gm_ref[r, :] + norm_back(grad_in * (1.0 + scale), normed, inverse)
        ).astype(BF)
        add_item_sums(sums_ref, 0, item, grad_in * normed, items)
        add_item_sums(sums_ref, 1, item, grad_in, items)


def proj_weights_kernel(dims, me_ref, attn_ref, gb_ref, *refs):
    group, split, count = dims
    terms, refs = refs[:count], refs[count:]
    outs, (sum_ref, left_t, right) = refs[:group], refs[group:]
    sum_ref[...] = sum(term[...].astype(F32) for term in terms).astype(BF)
    left_t[...] = attn_ref[...].T
    chunk, head_size, tall, wide = outs[0].shape
    for k in range(group):
        for y in range(chunk):
            part = (me_ref[1] ^ y) if split else y
            start = pl.multiple_of((part * group + (me_ref[0] ^ k)) * wide, wide)
            right[:, y * wide : (y + 1) * wide] = gb_ref[:, pl.ds(start, wide)]
        for j in range(head_size):
            z = (me_ref[2] ^ turned(j, head_size)) if split else j
            made = dot(left_t[pl.ds(pl.multiple_of(z * tall, tall), tall), :], right[...])
            for y in range(chunk):
                outs[k][y, j] = made[:, y * wide : (y + 1) * wide].astype(BF)


def qkv_weights_kernel(dims, me_ref, dqkv_ref, *refs):
    count, chunk, split, proj_count = dims
    ins, refs = refs[:count], refs[count:]
    projs, refs = refs[:proj_count], refs[proj_count:]
    outs, (left_t, right) = refs[:chunk], refs[chunk:]
    rows = ins[0].shape[0]
    for k in range(count):
        left_t[:, k * rows : (k + 1) * rows] = ins[k][...].T
    head_size, _, tall, wide = outs[0].shape
    for y in reversed(range(chunk)):
        part = (me_ref[1] ^ y) if split else y
        for t in range(3):
            start = pl.multiple_of((t * chunk + part) * wide, wide)
            right[:, t * wide : (t + 1) * wide] = dqkv_ref[:, pl.ds(start, wide)]
        for j in range(head_size):
            z = (me_ref[2] ^ turned(j, head_size)) if split else j
            made = dot(left_t[pl.ds(pl.multiple_of(z * tall, tall), tall), :], right[...])
            outs[y][j, 0] = sum(proj[y, j].astype(F32) for proj in projs).astype(BF)
            for t in range(3):
                outs[y][j, 1 + t] = made[:, t * wide : (t + 1) * wide].astype(BF)


def sort_kernel(pack_len, dest_ref, tokens_ref, cot_ref, to_slot_ref, tokens_out, cot_out):
    rows = tokens_ref.shape[0]
    pack = dest_ref[...] // pack_len
    other = jnp.broadcast_to(pack, (8, rows)).astype(F32).T[:, 0:1].astype(jnp.int32)
    this = lax.broadcasted_iota(jnp.int32, (rows, rows), 1)
    that = lax.broadcasted_iota(jnp.int32, (rows, rows), 0)
    before = (other < pack) | ((other == pack) & (that < this))
    slot = jnp.sum(before.astype(jnp.int32), axis=0, keepdims=True)
    to_slot_ref[...] = (slot == that).astype(F32).astype(BF)
    tokens_out[...] = dot(to_slot_ref[...], tokens_ref[...]).astype(BF)
    cot_out[...] = dot(to_slot_ref[...], cot_ref[...]).astype(BF)


def item_blocks_kernel(dims, me_ref, middle_ref, output_ref, tokens_ref, out_ref, joined):
    group, segs, head_size, size = dims
    model = output_ref.shape[1]
    parts = (
        (middle_ref, 0), (output_ref, 0), (tokens_ref, 0),
        (middle_ref, 1), (tokens_ref, 1), (middle_ref, 2),
    )
    for part, (ref, start) in enumerate(parts):
        joined[:, part * model : (part + 1) * model] = ref[:, start * model : (start + 1) * model]
    place = me_ref[1] * head_size + me_ref[2]
    for g in range(group):
        for y in range(segs):
            for z in range(head_size):
                start = ((y * group + g) * head_size + z) * size
                block = place ^ (y * head_size + z)
                rows = pl.ds(pl.multiple_of(block * 8, 8), 8)
                out_ref[me_ref[0] ^ g, rows, 0:size] = joined[:, start : start + size]


def group_sums_kernel(count, bit, kept_ref, came_ref, vector_ref, own_ref, sent_ref, sum_ref):
    rows = kept_ref.shape[1]
    vectors = vector_ref[...] + came_ref[pl.ds(came_ref.shape[0] - 64, 64), :]
    sum_ref[...] = vectors
    last = count == 2
    place = 0
    for k in range(0, count, 2):
        made = kept_ref[k] + came_ref[pl.ds(k // 2 * rows, rows), :]
        if last:
            half = rows // 2
            own_ref[...] = made[:half]
            sent_ref[0:half, :] = made[half:]
        elif k // 2 % 2 == 0:
            own_ref[k // 2] = made
        else:
            own_ref[k // 2] = made
            sent_ref[place * rows : (place + 1) * rows, :] = made
            place += 1
    sent_ref[pl.ds(sent_ref.shape[0] - 64, 64), :] = vectors


def pack_sums_kernel(kept_ref, came_ref, vector_ref, own_ref, *refs):
    blocks, senders = own_ref.shape[0] * (2 if len(refs) == 2 else 1), kept_ref.shape[1]
    vectors = vector_ref[...] + came_ref[pl.ds(came_ref.shape[0] - 64, 64), :]
    refs[-1][...] = vectors
    for c in range(blocks):
        for t in range(2 * senders):
            if t < senders:
                value = kept_ref[c, t]
            else:
                value = came_ref[pl.ds((c * senders + t - senders) * 8, 8), :]
            if len(refs) == 1 or c < blocks // 2:
                own_ref[c, t] = value
            else:
                refs[0][pl.ds(((c - blocks // 2) * 2 * senders + t) * 8, 8), :] = value
    if len(refs) == 2:
        refs[0][pl.ds(refs[0].shape[0] - 64, 64), :] = vectors


def ada_kernel(me_ref, silu_ref, blocks_ref, grad_ref, bias_ref, held):
    head_size = me_ref[3]
    place = me_ref[1] * head_size + me_ref[2]
    for c in range(blocks_ref.shape[0]):
        sender = place ^ turned(c, blocks_ref.shape[0])
        held[pl.ds(pl.multiple_of(sender * 8, 8), 8), :] = blocks_ref[c]
    low = held[:, 0 : grad_ref.shape[1]].astype(BF)
    bias_ref[...] = jnp.broadcast_to(
        jnp.sum(low.astype(F32), axis=0, keepdims=True), bias_ref.shape
    )
    grad_ref[...] = lax.dot_general(
        silu_ref[...], low, (((0,), (0,)), ((), ())), preferred_element_type=F32
    )


def own_tiles_kernel(count, *refs):
    terms, outs = refs[:count], refs[count:]
    for i, out in enumerate(outs):
        out[...] = sum(term[0, i].astype(F32) for term in terms).astype(BF)


def place_kernel(group, me_ref, *refs):
    blocks, (up_ref, down_ref) = refs[:group], refs[group:]
    hidden = blocks[0].shape[2]
    for i in range(group):
        own = pl.ds(pl.multiple_of((me_ref[0] ^ i) * hidden, hidden), hidden)
        up_ref[:, own] = blocks[i][0].astype(F32)
        down_ref[own, :] = blocks[i][1].astype(F32).T


def vector_parts_kernel(dims, me_ref, qkv_ref, branch_ref, mlp_ref, *refs):
    group, parts, head_size = dims
    hidden_refs, (flat_ref, out_ref) = refs[:-2], refs[-2:]
    sub = qkv_ref.shape[1] // parts
    hidden = hidden_refs[0].shape[1] // head_size
    out_ref[...] = jnp.zeros_like(out_ref)
    for p in range(parts):
        own = pl.ds(pl.multiple_of((p * group + me_ref[0]) * sub, sub), sub)
        for row in range(3):
            out_ref[row : row + 1, own] = qkv_ref[row : row + 1, p * sub : (p + 1) * sub]
    out_ref[3:4, :] = branch_ref[0:1, :]
    out_ref[4:5, :] = mlp_ref[0:1, :]
    if hidden % 128 == 0:
        own = pl.ds(pl.multiple_of(me_ref[0] * hidden, hidden), hidden)
        for z in range(head_size):
            cols = slice(z * hidden, (z + 1) * hidden)
            out_ref[8 + z : 9 + z, own] = sum(ref[0:1, cols] for ref in hidden_refs)
    for c in range(out_ref.shape[1] // 256):
        flat_ref[c * 16 : (c + 1) * 16, :] = out_ref[:, c * 256 : (c + 1) * 256]


def to_packs(rows):
    return lax.all_to_all(rows, ("yy", "head"), split_axis=0, concat_axis=0, tiled=True)


def over_group(blocks):
    return lax.all_to_all(blocks, "g", split_axis=0, concat_axis=0, tiled=True)


def bits(count):
    steps = []
    while count > 1:
        count //= 2
        steps.append(count)
    return steps


def xor_swap(values, axis, step):
    size = lax.axis_size(axis)
    return lax.ppermute(values, axis, [(i, i ^ step) for i in range(size)])


def xor_gather(block, axis):
    blocks = {0: block}
    for step in bits(lax.axis_size(axis)):
        for k in list(blocks):
            blocks[k ^ step] = xor_swap(blocks[k], axis, step)
    return [blocks[k] for k in range(len(blocks))]


def xor_scatter(blocks, axis):
    terms = {k: [block] for k, block in enumerate(blocks)}
    for step in reversed(bits(lax.axis_size(axis))):
        for k in reversed([k for k in terms if k & step]):
            terms[k ^ step].append(xor_swap(add_low(*terms.pop(k)), axis, step))
    return terms[0]


def halves_over_head(values):
    count = lax.axis_size("head")
    step = count // values.shape[0]
    half = values.shape[0] // 2
    return values[:half], xor_swap(values[half:], "head", step)


def add_low(*terms):
    if len(terms) == 1:
        return terms[0]
    return sum(term.astype(F32) for term in terms).astype(terms[0].dtype)


def butterfly(values, axis):
    for step in bits(lax.axis_size(axis)):
        values = values + xor_swap(values, axis, step)
    return values


def pick(values, index, axis):
    return lax.dynamic_index_in_dim(values, index, axis, keepdims=False)


def xor_blocks(values, axis, dim):
    me = lax.axis_index(axis)
    return [pick(values, me ^ k, dim) for k in range(lax.axis_size(axis))]


def tie(*values):
    return lax.optimization_barrier(values)


def shards(
    tokens,
    cotangent,
    class_table,
    ada_weight,
    ada_bias,
    qkv_weight,
    q_bias,
    v_bias,
    log_scale,
    proj_weight,
    proj_bias,
    fc1_weight,
    fc1_bias,
    fc2_weight,
    fc2_bias,
    item_lens,
    class_ids,
    section_ids,
    destination,
):
    segs = lax.axis_size("yy")
    group = lax.axis_size("g")
    head_size = lax.axis_size("head")
    yy, g, z = lax.axis_index("yy"), lax.axis_index("g"), lax.axis_index("head")
    me = jnp.stack([g, yy, z, jnp.int32(head_size)]).astype(jnp.int32)
    pack = yy * head_size + z
    rows, model = tokens.shape
    heads_all = log_scale.shape[0]
    head_dim = model // heads_all
    heads = heads_all // group
    width = model // group
    dp_size = segs * group
    pack_len = rows * head_size
    seg = rows // segs
    items = item_lens.shape[1]
    block = min(256, pack_len)
    col = model // dp_size
    parts = segs if col % 128 == 0 else 1
    sub = width // parts

    def own_cols(values):
        return pick(values.reshape(parts, group, sub), g, 1).reshape(1, width)

    rows_bf, rows_f32 = shape_of((rows, model), BF), shape_of((rows, model), F32)
    to_slot, sorted_tokens, sorted_cotangent = call(
        "sort",
        functools.partial(sort_kernel, pack_len),
        (destination[None, :], tokens, cotangent),
        (VMEM, HBM, HBM),
        (shape_of((rows, rows), BF), rows_bf, rows_bf),
    )
    inputs = to_packs(sorted_tokens)

    hidden = fc1_weight.shape[1] // group
    units = head_size * hidden
    half = model // segs
    fc1_own = lax.dynamic_slice(fc1_weight, (yy * half, g * hidden), (half, hidden))
    fc1_bias_own = lax.dynamic_slice(fc1_bias, (g * hidden,), (hidden,))
    fc2_own = lax.dynamic_slice(fc2_weight, (g * hidden, yy * half), (hidden, half))
    fc1_sent = jnp.concatenate(
        [fc1_own, jnp.broadcast_to(fc1_bias_own[None, :], (16, hidden))], axis=0
    )
    fc1_all = lax.all_gather(fc1_sent, ("yy", "head"), axis=0)
    fc1_all = fc1_all.reshape(segs, head_size, half + 16, hidden)
    fc2_all = lax.all_gather(fc2_own, ("yy", "head"), axis=0)
    fc2_all = fc2_all.reshape(segs, head_size, hidden, half)
    fc1_bias_here = fc1_all[0, :, half].reshape(1, units).astype(F32)
    tiled = hidden % 128 == 0
    if tiled:
        fc1_here, fc2_here = call(
            "weights",
            weights_kernel,
            (fc1_all, fc2_all),
            (ANY, ANY),
            (shape_of((model, units), BF), shape_of((units, model), BF)),
            [pltpu.SemaphoreType.DMA((2 * segs * head_size,))],
            out_specs=(VMEM, VMEM),
        )
    else:
        fc1_here = fc1_all[:, :, :half].transpose(0, 2, 1, 3).reshape(model, units)
        fc2_here = fc2_all.transpose(1, 2, 0, 3).reshape(units, model)

    lens_here = pick(item_lens, pack, 0)
    class_here = pick(class_ids, pack, 0)
    order_key = class_here * items + jnp.arange(items, dtype=jnp.int32)
    item_rank = jnp.sum(
        jnp.where(order_key[None, :] < order_key[:, None], lens_here[None, :], 0), axis=1
    )
    item_pos = jnp.cumsum(lens_here) - lens_here
    item_end = item_rank + lens_here

    def items_of(rank):
        return (rank[:, None] >= item_rank[None, :]) & (rank[:, None] < item_end[None, :])

    rank_all = jnp.arange(pack_len, dtype=jnp.int32)
    member = items_of(rank_all)

    def of_item(values):
        return jnp.sum(jnp.where(member, values[None, :], 0), axis=1)

    section_here = lax.ppermute(
        section_ids[0],
        ("g", "head"),
        [(a * head_size + b, b * head_size + a) for a in range(group) for b in range(head_size)],
    )
    position = rank_all - of_item(item_rank - item_pos)
    section_rank = jnp.sum(
        jnp.where(rank_all[None, :] == position[:, None], section_here[None, :], 0), axis=1
    )
    up_to = jnp.sum((section_here[None, :] <= section_rank[:, None]).astype(jnp.int32), axis=1)
    low = of_item(item_rank)
    high = jnp.minimum(up_to + of_item(item_rank - item_pos), of_item(item_end))
    first = low[::block] // block
    last = (high[block - 1 :: block] + block - 1) // block
    low, high = low[None, :], high[None, :]

    row_rank = (
        (jnp.arange(segs, dtype=jnp.int32)[:, None] * group + g) * seg
        + jnp.arange(seg, dtype=jnp.int32)[None, :]
    ).reshape(rows)
    row_item = jnp.sum(
        jnp.where(items_of(row_rank), jnp.arange(items, dtype=jnp.int32)[None, :], 0), axis=1
    )[:, None]

    class_rows = jnp.take(class_table, class_ids.reshape(-1), axis=0).astype(F32)
    silu_cond = jax.nn.silu(class_rows).astype(BF)
    silu_here = lax.dynamic_slice_in_dim(silu_cond, pack * items, items, 0)
    mod = jnp.dot(silu_here, ada_weight, preferred_element_type=F32) + ada_bias.astype(F32)

    (attn_in,) = call("first_norm",
        first_norm_kernel, (inputs, mod, row_item), (HBM, VMEM, VMEM), (shape_of((rows, model), BF),)
    )
    attn_blocks = xor_gather(attn_in, "g")
    per_part = sub // head_dim
    scale_here = pick(log_scale.reshape(parts, group, per_part), g, 1).reshape(heads)
    temper = jnp.repeat(jnp.exp(scale_here), head_dim)[None, :]
    wide = shape_of((pack_len, width), BF)
    wide_f32 = shape_of((pack_len, width), F32)
    weights_held = [
        pltpu.VMEM((model, 3 * width), BF),
        pltpu.SemaphoreType.DMA((3 * parts,)),
    ]
    queries, keys, values, query_pre, key_pre = call(
        "qkv",
        functools.partial(qkv_kernel, (group, segs, head_dim, parts)),
        (me, temper, own_cols(q_bias).astype(F32), own_cols(v_bias).astype(F32), qkv_weight,
         *attn_blocks),
        (SMEM, VMEM, VMEM, VMEM, ANY) + (HBM,) * group,
        (wide, wide, wide, wide_f32, wide_f32),
        weights_held,
    )
    sorted_cotangent, _ = tie(sorted_cotangent, inputs)
    upstream = to_packs(sorted_cotangent)
    def near_blocks(own):
        blocks = {0: own}
        for step in bits(group)[1:]:
            for k in list(blocks):
                blocks[k ^ step] = xor_swap(blocks[k], "g", step)
        return [blocks[k] for k in range(len(blocks))]

    near = group // 2
    out_blocks, out_t, lse = call(
        "attend",
        functools.partial(attend_kernel, (group, segs, head_dim, block)),
        (first, last, low, high, queries, keys, values),
        (SMEM, SMEM, VMEM, VMEM, HBM, HBM, HBM),
        (shape_of((group, rows, width), BF), shape_of((width, pack_len), F32),
         shape_of((8, pack_len), F32)),
        [
            pltpu.VMEM((width, pack_len), BF),
            pltpu.VMEM((pack_len, width), BF),
            pltpu.VMEM((width, block), F32),
            pltpu.VMEM((8, block), F32),
        ],
    )
    returned = over_group(out_blocks)
    upstream, _ = tie(upstream, out_blocks)
    grad_mlp, grad_mlp_sum = call(
        "grad_mlp",
        grad_mlp_kernel,
        (upstream, mod, row_item),
        (HBM, VMEM, VMEM),
        (rows_bf, shape_of((8, model), F32)),
    )
    grad_far = xor_swap(grad_mlp, "g", near)
    grad_blocks = near_blocks(grad_mlp)
    returned, grad_mlp_sum = tie(returned, grad_mlp_sum)
    attn_rows, branch, middle, mlp_in = call(
        "project",
        functools.partial(project_kernel, parts),
        (returned, proj_weight, proj_bias[None, :], inputs, mod, row_item),
        (HBM, HBM, VMEM, HBM, VMEM, VMEM),
        (rows_bf, rows_f32, rows_f32, rows_bf),
    )

    mlp_blocks = near_blocks(mlp_in)
    mlp_far = xor_swap(mlp_in, "g", near)
    grad_blocks += near_blocks(tie(grad_far, mlp_in)[0])
    back_parts, out_parts, acts, ghs, hidden_sums = [], [], [], [], []
    for start in (0, near):
        if start:
            mlp_blocks += near_blocks(tie(mlp_far, acts[0])[0])
        made = call(
            "feed",
            functools.partial(feed_kernel, near),
            (fc1_here, fc2_here, fc1_bias_here, *mlp_blocks[start : start + near],
             *grad_blocks[start : start + near]),
            (VMEM,) * 3 + (ANY,) * (2 * near),
            (rows_bf,) * (2 * near)
            + (shape_of((near * rows, units), BF),) * 2
            + (shape_of((8, units), F32),),
            [pltpu.VMEM((near, rows, model), BF)] * 4
            + [pltpu.VMEM((near, rows, units), BF)] * 2
            + [pltpu.VMEM((2, rows, units), F32)] * 2
            + [pltpu.SemaphoreType.DMA((2 * near,)), pltpu.SemaphoreType.DMA((4 * near,))],
            out_specs=(ANY,) * (2 * near + 2) + (VMEM,),
        )
        back_parts += made[:near]
        out_parts += made[near : 2 * near]
        acts.append(made[2 * near])
        ghs.append(made[2 * near + 1])
        hidden_sums.append(made[2 * near + 2])
    far_terms = {k: back_parts[k] for k in range(near, group)}
    for step in reversed(bits(group)[1:]):
        for k in reversed([k for k in far_terms if k & step]):
            came = xor_swap(far_terms.pop(k), "g", step)
            far_terms[k ^ step] = add_low(far_terms[k ^ step], came)
    far_sum = far_terms[near]
    back_parts = list(tie(*back_parts[:near], far_sum)[:near])
    in_terms = {k: [back_parts[k]] for k in range(near)}
    for step in reversed(bits(group)[1:]):
        for k in reversed([k for k in in_terms if k & step]):
            in_terms[k ^ step].append(xor_swap(add_low(*in_terms.pop(k)), "g", step))
    in_terms = in_terms[0] + [xor_swap(far_sum, "g", near)]
    acts[0], _ = tie(acts[0], far_sum)
    split = segs if tiled else 1
    if tiled:
        fine = half // group
        tile_shape = (head_size, group, 2, fine, hidden)
        feed_dims = (group, group, segs, 2)
    else:
        tile_shape = (1, 1, 2, model, units)
        feed_dims = (group, 1, 1, 2)
    tile_parts = call(
        "feed_weights",
        functools.partial(feed_weights_kernel, feed_dims),
        (me, *acts, *ghs, *mlp_blocks, *grad_blocks),
        (SMEM,) + (HBM,) * (4 + 2 * group),
        (shape_of(tile_shape, BF),) * split,
        [
            pltpu.VMEM((model, pack_len), BF),
            pltpu.VMEM((model, pack_len), BF),
            pltpu.VMEM((pack_len, units), BF),
            pltpu.VMEM((pack_len, units), BF),
        ],
    )
    if not tiled:
        fine = half // group
        order = jnp.array([turned(j, head_size) for j in range(head_size)]) ^ z
        near_g = jnp.arange(group) ^ g
        near_y = jnp.arange(segs) ^ yy

        full = tile_parts[0].reshape(2, segs, group, fine, head_size, hidden)
        full = full.transpose(1, 4, 2, 0, 3, 5)
        tile_parts = list(full[near_y][:, order][:, :, near_g])

    middle_in, _ = tie(middle, tile_parts[0])
    outbound, grad_branch, grad_middle, middle_sums, branch_sum = call(
        "middle_back",
        functools.partial(middle_back_kernel, (parts, items, len(in_terms))),
        (middle_in, branch, upstream, mod, row_item, proj_weight, *in_terms),
        (HBM, HBM, HBM, VMEM, VMEM, HBM) + (HBM,) * len(in_terms),
        (shape_of((group, rows, width), BF), rows_bf, rows_f32, shape_of((8, 3 * model), F32),
         shape_of((8, model), F32)),
        [pltpu.VMEM((rows, model), BF)],
    )
    inbound = over_group(outbound)
    tile_terms = xor_scatter(tile_parts, "yy")
    def to_last(blocks):
        terms = {k: [block] for k, block in enumerate(blocks)}
        for step in reversed(bits(group)[1:]):
            for k in reversed([k for k in terms if k & step]):
                terms[k ^ step].append(xor_swap(add_low(*terms.pop(k)), "g", step))
        return terms[0], terms[near]

    out_terms, out_last = to_last(tie(*out_parts, tile_parts[0])[:group])
    made = call(
        "proj_weights",
        functools.partial(proj_weights_kernel, (group, parts == segs, len(out_last))),
        (me, attn_rows, grad_branch, *out_last),
        (SMEM,) + (HBM,) * (2 + len(out_last)),
        (shape_of((parts, head_size, model // head_size, sub), BF),) * group + (rows_bf,),
        [pltpu.VMEM((model, rows), BF), pltpu.VMEM((rows, width), BF)],
    )
    out_sent = made[group]
    proj_terms, proj_last = to_last(made[:group])
    inbound, out_sent = tie(inbound, out_sent)
    out_terms.append(xor_swap(out_sent, "g", near))

    def heads_back(index, given):
        return call(
            "attend_back",
            functools.partial(attend_back_kernel, (group, segs, head_dim, block, index)),
            (first, last, low, high, given, queries, keys, values, out_t, lse),
            (SMEM, SMEM, VMEM, VMEM) + (HBM,) * 5 + (VMEM,),
            (shape_of((pack_len, 128), BF),) * 3,
            [
                pltpu.VMEM((pack_len, 128), BF),
                pltpu.VMEM((128, pack_len), BF),
                pltpu.VMEM((pack_len, 128), F32),
                pltpu.VMEM((pack_len, 128), F32),
                pltpu.VMEM((128, block), F32),
                pltpu.VMEM((8, block), F32),
            ],
        )

    head_grads = list(heads_back(0, inbound))
    tied = tie(*out_terms, *proj_last, head_grads[0])[:-1]
    output_rows, output_sums, proj_sent = call(
        "output",
        functools.partial(output_kernel, (items, len(out_terms), len(proj_last))),
        (middle, upstream, mod, row_item, fc2_bias[None, :], *tied),
        (HBM, HBM, VMEM, VMEM, VMEM) + (HBM,) * len(tied),
        (rows_bf, shape_of((8, model), F32), shape_of(proj_last[0].shape, BF)),
    )
    output_back = to_packs(output_rows)
    inbound, output_rows = tie(inbound, output_rows)
    proj_terms.append(xor_swap(proj_sent, "g", near))
    for index in range(1, width // 128):
        head_grads += heads_back(index, inbound)
    tied = tie(*head_grads, output_back, proj_terms[-1])
    head_grads, output_back, proj_terms[-1] = tied[:-2], tied[-2], tied[-1]
    half_tiles = shape_of((head_size // 2, group, 2, fine, hidden), BF)
    quarter_tiles = shape_of((head_size // 4, group, 2, fine, hidden), BF)
    made = call(
        "qkv_back",
        functools.partial(
            qkv_back_kernel, (group, segs, head_dim, parts, width // 128, len(tile_terms))
        ),
        (*tile_terms, me, temper, qkv_weight, query_pre, key_pre, *head_grads),
        (HBM,) * len(tile_terms) + (SMEM, VMEM, ANY) + (HBM,) * (2 + len(head_grads)),
        (rows_bf,) * group
        + (shape_of((pack_len, 3 * width), BF), shape_of((8, width), F32), half_tiles, half_tiles),
        weights_held,
    )
    grad_qkv, qkv_sums, tiles_kept, tiles_sent = made[group:]
    tile_terms = (tiles_kept, xor_swap(tiles_sent, "head", 1))

    (vectors,) = call(
        "vector_parts",
        functools.partial(vector_parts_kernel, (group, parts, head_size)),
        (me, qkv_sums, branch_sum, grad_mlp_sum, *hidden_sums),
        (SMEM,) + (VMEM,) * (3 + len(hidden_sums)),
        (shape_of((64, 256), F32),),
        [pltpu.VMEM((16, model), F32)],
    )
    if not tiled:
        hidden_row = (hidden_sums[0] + hidden_sums[1])[0].reshape(head_size, hidden)
        hidden_row = lax.dynamic_update_slice(
            jnp.zeros((16, model), F32), hidden_row, (8, g * hidden)
        )
        vectors = vectors + hidden_row.reshape(16, 4, 256).transpose(1, 0, 2).reshape(64, 256)

    in_terms, last_terms = to_last(made[:group])
    sent = add_low(*last_terms)
    in_terms.append(xor_swap(sent, "g", near))
    grad_qkv, _ = tie(grad_qkv, sent)
    qkv_parts = call(
        "qkv_weights",
        functools.partial(
            qkv_weights_kernel, (group, parts, parts == segs, len(proj_terms))
        ),
        (me, grad_qkv, *attn_blocks, *proj_terms),
        (SMEM,) + (HBM,) * (1 + group + len(proj_terms)),
        (shape_of((head_size, 4, model // head_size, sub), BF),) * parts,
        [pltpu.VMEM((model, pack_len), BF), pltpu.VMEM((pack_len, 3 * sub), BF)],
    )
    inputs_back, _ = tie(inputs, qkv_parts[0])
    tokens_grad_rows, tokens_sums, tiles_kept, tiles_sent = call(
        "tokens_back",
        functools.partial(tokens_back_kernel, (items, len(in_terms), 2)),
        (inputs_back, grad_middle, mod, row_item, *in_terms, *tile_terms),
        (HBM, HBM, VMEM, VMEM) + (HBM,) * (len(in_terms) + 2),
        (rows_bf, shape_of((8, 2 * model), F32), quarter_tiles, quarter_tiles),
    )
    tile_terms = (tiles_kept, xor_swap(tiles_sent, "head", 2))

    def to_data(values):
        return dot(to_slot, values, ((0,), (0,)))

    output = to_data(output_back).astype(BF)
    tokens_came = to_packs(tokens_grad_rows)
    tokens_grad = to_data(tokens_came)

    def over_head(terms):
        while terms[0].shape[0] > 1:
            terms = halves_over_head(add_low(*terms))
        return terms

    tile_terms = tie(*tile_terms, tokens_came)[:-1]
    tied = over_head(tile_terms)
    own_tiles = call(
        "own_tiles",
        functools.partial(own_tiles_kernel, len(tied)),
        tied,
        (HBM,) * len(tied),
        (shape_of((2, fine, hidden), BF),) * group,
    )
    both_all = [own_tiles[0]]
    for i in range(1, group):
        both_all.append(lax.ppermute(own_tiles[i], "g", [(k, k ^ i) for k in range(group)]))
    if tiled:
        up_part, down_part = call(
            "place",
            functools.partial(place_kernel, group),
            (me, *both_all),
            (SMEM,) + (HBM,) * group,
            (shape_of((fine, group * hidden), F32), shape_of((group * hidden, fine), F32)),
        )
    else:
        placed = jnp.stack(both_all)[jnp.arange(group) ^ g].astype(F32)
        up_part = placed[:, 0].transpose(1, 0, 2).reshape(fine, group * hidden)
        down_part = placed[:, 1].transpose(0, 2, 1).reshape(group * hidden, fine)


    ada_cols = 6 * model // (dp_size * head_size)
    packs = segs * head_size
    (kept,) = call(
        "item_blocks",
        functools.partial(item_blocks_kernel, (group, segs, head_size, ada_cols)),
        (me, middle_sums, output_sums, tokens_sums),
        (SMEM, VMEM, VMEM, VMEM),
        (shape_of((group, packs * 8, 256), F32),),
        [pltpu.VMEM((8, 6 * model), F32)],
        out_specs=(VMEM,),
    )
    sent = jnp.concatenate([kept[k] for k in range(1, group, 2)] + [vectors], axis=0)
    count = group
    for step in reversed(bits(group)):
        came = xor_swap(sent, "g", step)
        left = count // 2
        own = (left, packs * 8, 256) if left > 1 else (packs * 4, 256)
        rows_sent = (left // 2 * packs * 8 if left > 1 else packs * 4) + 64
        kept, sent, vectors = call(
            "group_sums",
            functools.partial(group_sums_kernel, count, step),
            (kept, came, vectors),
            (VMEM,) * 3,
            (shape_of(own, F32), shape_of((rows_sent, 256), F32), shape_of((64, 256), F32)),
            out_specs=(VMEM,) * 3,
        )
        count = left
    kept = kept.reshape(packs // 2, 1, 8, 256)
    sent, _ = tie(sent, tokens_came)
    steps = [("yy", step) for step in bits(segs)] + [("head", step) for step in bits(head_size)]
    for place, (axis, step) in enumerate(steps):
        came = xor_swap(sent, axis, step)
        blocks, senders = kept.shape[0], kept.shape[1]
        end = place + 1 == len(steps)
        own = (blocks if end else blocks // 2, 2 * senders, 8, 256)
        outs = [shape_of(own, F32)]
        if not end:
            outs.append(shape_of((blocks // 2 * 2 * senders * 8 + 64, 256), F32))
        outs.append(shape_of((64, 256), F32))
        made = call(
            "pack_sums", pack_sums_kernel, (kept, came, vectors), (VMEM,) * 3, outs,
            out_specs=(VMEM,) * len(outs),
        )
        kept, vectors = made[0], made[-1]
        sent = made[1] if not end else None
    item_came = kept[0]
    vectors = vectors.reshape(4, 16, 256).transpose(1, 0, 2).reshape(16, model)
    silu_rows = jnp.pad(silu_cond.reshape(packs, items, model), ((0, 0), (0, 8 - items), (0, 0)))
    ada_grad, ada_bias_grad = call(
        "ada",
        ada_kernel,
        (me, silu_rows.reshape(packs * 8, model), item_came),
        (SMEM, VMEM, VMEM),
        (shape_of((model, ada_cols), F32), shape_of((8, ada_cols), F32)),
        [pltpu.VMEM((packs * 8, 256), F32)],
    )
    ada_bias_grad = ada_bias_grad[0]

    if parts == segs:
        terms = tie(*xor_scatter(qkv_parts, "yy"), tokens_came)[:-1]
        terms = over_head(terms)
        summed = sum(term[0].astype(F32) for term in terms)
        proj_part, qkv_part = summed[0], summed[1:]
    else:
        both = qkv_parts[0].transpose(1, 0, 2, 3).reshape(4, model, width)
        full = lax.dynamic_update_slice(
            jnp.zeros((4, model, model), BF), both, (0, 0, g * width)
        )
        summed = lax.psum_scatter(full, ("yy", "g"), scatter_dimension=2, tiled=True)
        summed = lax.psum_scatter(summed, "head", scatter_dimension=1, tiled=True).astype(F32)
        proj_part, qkv_part = summed[0], summed[1:]

    log_scale_grad = jnp.sum(vectors[2].reshape(heads_all, head_dim), axis=1)
    fc1_bias_grad = pick(vectors, 8 + z, 0)[: group * hidden]
    return (
        output,
        tokens_grad,
        ada_grad,
        ada_bias_grad,
        qkv_part,
        vectors[0],
        vectors[1],
        log_scale_grad,
        proj_part,
        vectors[3],
        up_part,
        fc1_bias_grad,
        down_part,
        vectors[4],
    )


def solution(mesh):
    head_size = mesh.shape["head"]
    dp_size = mesh.shape["dp"]
    inner = Mesh(
        mesh.devices.reshape(dp_size // head_size, head_size, head_size), ("yy", "g", "head")
    )
    dp = ("yy", "g")
    everything = ("yy", "g", "head")
    in_specs = (
        P(everything, None),
        P(everything, None),
        P(),
        P(),
        P(),
        P(),
        P(),
        P(),
        P(),
        P(),
        P(),
        P(None, "head"),
        P("head"),
        P("head", None),
        P(),
        P(),
        P(),
        P(dp, None),
        P(everything),
    )
    out_specs = (
        P(everything, None),
        P(everything, None),
        P(None, everything),
        P(everything),
        P(None, "head", dp),
        P(),
        P(),
        P(),
        P("head", dp),
        P(),
        P(dp, "head"),
        P("head"),
        P("head", dp),
        P(),
    )
    return jax.shard_map(
        shards, mesh=inner, in_specs=in_specs, out_specs=out_specs, check_vma=False
    )
```

time: 499 us -> 435 us (0.87)
  waiting for transfers between devices: 183 us -> 103 us
  local copies, waits for them, and re-layouts: 35 us -> 78.4 us
  other arithmetic: 29.2 us -> 10.5 us
  Pallas kernels: 139 us -> 150 us
  starting transfers between devices: 71.3 us -> 60.8 us
  matrix products: 17.3 us -> 11.8 us
    ppermute x32, waiting for transfers between devices: 145 us -> 52.6 us  [xor_swap(): return lax.ppermute(values, axis, [(i, i ^ step) for i in range(size)])]
    unnamed x97 -> x212, local copies, waits for them, and re-layouts: 18.4 us -> 69 us
    all_to_all x5 -> x4, waiting for transfers between devices: 22.5 us -> 41.8 us  [to_packs(): lax.all_to_all(rows, ('yy', 'head'), split_axis=0, concat_axis=0, tiled=T...]
    all_to_all x3 -> x0, starting transfers between devices: 15.2 us -> none  [the longest x2 10.4 us: sum_tiles(): lax.all_to_all(half_sum.reshape(group * head_size, *shape), ('g', 'head')...]
    convert_element_type x10 -> x5, other arithmetic: 16.2 us -> 4.47 us  [the longest x4 4.39 us: add_low(): return sum((term.astype(F32) for term in terms)).astype(terms[0].dtype)]
    pallas_call x12 -> x28, Pallas kernels: 139 us -> 150 us  [call(): pl.pallas_call(body, name=name, out_shape=tuple(outs), in_specs=[ANY if s...]
    all_to_all x3 -> x0, waiting for transfers between devices: 7.8 us -> none  [the longest x1 7.8 us: shards(): came = lax.all_to_all(half_sum, 'head', 0, 0, tiled=True)]
    dot_general x5 -> x2, matrix products: 10.9 us -> 5.48 us  [dot(): lax.dot_general(left, right, (dims, ((), ())), preferred_element_type=F32)]
  transfers between devices with their start and end apart: 45 -> 44, of which waited for: 19 -> 18; matrix products, arithmetic and copies ran while one was open for 13% -> 7% of each run, Pallas kernels for 23% -> 29%
where the time goes in v3:
time: 435 us; the launch traced here: 429 us
  Pallas kernels  150 us (34%)
  waiting for transfers between devices  103 us (24%)
  local copies, waits for them, and re-layouts  78.4 us (18%)
  starting transfers between devices  60.8 us (14%)
  between operations  15.3 us (4%)
  matrix products  11.8 us (3%)
  other arithmetic  10.5 us (2%)
    pallas_call x28, Pallas kernels, call(): pl.pallas_call(body, name=name, out_shape=tuple(outs), in_specs=[ANY if s...  150 us
    unnamed x212, local copies, waits for them, and re-layouts  69 us
    ppermute x32, waiting for transfers between devices, xor_swap(): return lax.ppermute(values, axis, [(i, i ^ step) for i in range(size)])  52.6 us
    all_to_all x4, waiting for transfers between devices, to_packs(): lax.all_to_all(rows, ('yy', 'head'), split_axis=0, concat_axis=0, tiled=T...  41.8 us
    ppermute x32, starting transfers between devices, xor_swap(): return lax.ppermute(values, axis, [(i, i ^ step) for i in range(size)])  25.6 us
    all_to_all x4, starting transfers between devices, to_packs(): lax.all_to_all(rows, ('yy', 'head'), split_axis=0, concat_axis=0, tiled=T...  23.6 us
    all_to_all x2, starting transfers between devices, over_group(): return lax.all_to_all(blocks, 'g', split_axis=0, concat_axis=0, tiled=True)  8.9 us
  transfers between devices with their start and end apart: 44, of which 18 were waited for; matrix products, arithmetic and copies ran while one was open for 7% of the time, Pallas kernels for 29%

profile of v3, /device:TPU:0, one launch (start us, length us, event | category | flops | bytes accessed | tf_op | source)
XLA Modules:
  0.0 429.4 jit_solution(10905766991189967744)
XLA Ops:
  15.5 7.3 %all-to-all-start = ((bf16[8,48,1024]{2,1,0:T(8,128)(2,1)}), bf16[8,48,1024]{2,1,0:T(8,128)(2,1)S(1)}, u32[]{:S(2)}, u32[]{:S(2)}) async-start(bf16[8,48,1024]{2,1,0:T(8,128)(2,1)} %bitcast.88), calls=%async_computation | async-start | bytes 1572864 | tf_op jit(solution)/shard_map/all_to_all | solution.py:739
  26.6 6.4 %convolution_add_fusion.refs_1_.refs_4_.refs_3_.refs_2_ = f32[4,6144]{1,0:T(4,128)S(1)} fusion(bf16[1024,6144]{1,0:T(8,128)(2,1)} %param.22, f32[6144]{0:T(1024)S(1)} %convert_element_type.89, f32[32,1024]{1,0:T(8,128)S(1)} %select_convert_fusion, s32[]{:T(128)S(6)} %select_n.97), kind=kOutput, calls=%fused_computation.4 | convolution fusion | flops 50376704 | bytes 12722180 | tf_op jit(solution)/shard_map/dot_general | solution.py:935
  32.9 18.5 %all-to-all-done = bf16[8,48,1024]{2,1,0:T(8,128)(2,1)S(1)} async-done(((bf16[8,48,1024]{2,1,0:T(8,128)(2,1)}), bf16[8,48,1024]{2,1,0:T(8,128)(2,1)S(1)}, u32[]{:S(2)}, u32[]{:S(2)}) %all-to-all-start) | async-done | bytes 786464 | tf_op jit(solution)/shard_map/all_to_all | solution.py:739
  55.4 6.0 %all-to-all-start.2 = ((bf16[8,48,1024]{2,1,0:T(8,128)(2,1)}), bf16[8,48,1024]{2,1,0:T(8,128)(2,1)S(1)}, u32[]{:S(2)}, u32[]{:S(2)}) async-start(bf16[8,48,1024]{2,1,0:T(8,128)(2,1)} %bitcast.86), calls=%async_computation.2 | async-start | bytes 1572864 | tf_op jit(solution)/shard_map/all_to_all | solution.py:739
  62.0 10.4 %collective-permute-done.2.refs_7_.refs_4_ = bf16[384,1024]{1,0:T(8,128)(2,1)} collective-permute-done((bf16[384,1024]{1,0:T(8,128)(2,1)S(1)}, bf16[384,1024]{1,0:T(8,128)(2,1)}, u32[]{:S(2)}, u32[]{:S(2)}) %collective-permute-start.2) | collective-permute-done | bytes 786464 | tf_op jit(solution)/shard_map/ppermute | solution.py:756
  75.1 7.6 %qkv.1 = (bf16[1536,256]{1,0:T(8,128)(2,1)S(1)}, bf16[1536,256]{1,0:T(8,128)(2,1)S(1)}, bf16[1536,256]{1,0:T(8,128)(2,1)S(1)}, f32[1536,256]{1,0:T(8,128)S(1)}, f32[1536,256]{1,0:T(8,128)S(1)}) custom-call(s32[4]{0:T(128)S(1)} %pad_add_fusion.refs_0_.refs_2_, f32[1,256]{1,0:T(1,128)S(1)} %broadcast_in_dim_reshape.2.refs_1_.refs_3_, ...), custom_call_target="tpu_custom_call" | custom-call | flops 1 | bytes 1 | tf_op jit(solution)/shard_map/qkv/pallas_call | solution.py:59
  85.1 19.1 %attend.1 = (bf16[4,384,256]{2,1,0:T(8,128)(2,1)S(1)}, f32[256,1536]{1,0:T(8,128)S(1)}, f32[8,1536]{1,0:T(8,128)S(1)}) custom-call(s32[6]{0:T(128)S(1)} %get-tuple-element.355.refs_0_, s32[6]{0:T(128)S(1)} %get-tuple-element.354.refs_1_, s32[1,1536]{1,0:T(1,128)S(1)} %broadcast_in_dim.131.refs_2_, s32[1,1536]{1,0:T(1,128)S(1)} %min.14.refs_3_, ...), custom_call_target="tpu_custom_call" | custom-call | flops 1 | bytes 1 | tf_op jit(solution)/shard_map/attend/pallas_call | solution.py:59
  108.9 4.4 %all-to-all-start.1 = ((bf16[4,384,256]{2,1,0:T(8,128)(2,1)}), bf16[4,384,256]{2,1,0:T(8,128)(2,1)}, u32[]{:S(2)}, u32[]{:S(2)}) async-start(bf16[4,384,256]{2,1,0:T(8,128)(2,1)} %copy-done.46), calls=%async_computation.1 | async-start | bytes 1572864 | tf_op jit(solution)/shard_map/all_to_all | solution.py:743
  117.3 8.2 %all-to-all-done.1.refs_0_ = bf16[4,384,256]{2,1,0:T(8,128)(2,1)} async-done(((bf16[4,384,256]{2,1,0:T(8,128)(2,1)}), bf16[4,384,256]{2,1,0:T(8,128)(2,1)}, u32[]{:S(2)}, u32[]{:S(2)}) %all-to-all-start.1) | async-done | bytes 786464 | tf_op jit(solution)/shard_map/all_to_all | solution.py:743
  127.1 5.6 %project.1 = (bf16[384,1024]{1,0:T(8,128)(2,1)S(1)}, f32[384,1024]{1,0:T(8,128)S(1)}, f32[384,1024]{1,0:T(8,128)S(1)}, bf16[384,1024]{1,0:T(8,128)(2,1)}) custom-call(bf16[4,384,256]{2,1,0:T(8,128)(2,1)} %all-to-all-done.1.refs_0_, bf16[1024,1024]{1,0:T(8,128)(2,1)S(1)} %copy-done.2, bf16[1,1024]{1,0:T(2,128)(2,1)S(1)} %broadcast_in_dim.138.refs_2_, ...), custom_call_target="tpu_custom_call" | custom-call | flops 1 | bytes 1 | tf_op jit(solution)/shard_map/project/pallas_call | solution.py:59
  136.1 6.3 %collective-permute-done.8.refs_5_.refs_11_ = bf16[384,1024]{1,0:T(8,128)(2,1)} collective-permute-done((bf16[384,1024]{1,0:T(8,128)(2,1)}, bf16[384,1024]{1,0:T(8,128)(2,1)}, u32[]{:S(2)}, u32[]{:S(2)}) %collective-permute-start.8) | collective-permute-done | bytes 786464 | tf_op jit(solution)/shard_map/ppermute | solution.py:756
  146.2 12.3 %feed.2 = (bf16[384,1024]{1,0:T(8,128)(2,1)S(1)}, bf16[384,1024]{1,0:T(8,128)(2,1)S(1)}, bf16[384,1024]{1,0:T(8,128)(2,1)S(1)}, bf16[384,1024]{1,0:T(8,128)(2,1)...) custom-call(bf16[1024,1024]{1,0:T(8,128)(2,1)S(1)} %get-tuple-element.153.refs_0_, ...), custom_call_target="tpu_custom_call" | custom-call | flops 1 | bytes 1 | tf_op jit(solution)/shard_map/feed/pallas_call | solution.py:59
  164.1 11.4 %feed.3 = (bf16[384,1024]{1,0:T(8,128)(2,1)S(1)}, bf16[384,1024]{1,0:T(8,128)(2,1)S(1)}, bf16[384,1024]{1,0:T(8,128)(2,1)S(1)}, bf16[384,1024]{1,0:T(8,128)(2,1)...) custom-call(bf16[1024,1024]{1,0:T(8,128)(2,1)S(1)} %get-tuple-element.153.refs_0_, ...), custom_call_target="tpu_custom_call" | custom-call | flops 1 | bytes 1 | tf_op jit(solution)/shard_map/feed/pallas_call | solution.py:59
  183.5 14.2 %feed_weights.1 = (bf16[4,4,2,128,256]{4,3,2,1,0:T(8,128)(2,1)}, bf16[4,4,2,128,256]{4,3,2,1,0:T(8,128)(2,1)}) custom-call(s32[4]{0:T(128)S(1)} %pad_add_fusion.refs_0_.refs_2_, bf16[768,1024]{1,0:T(8,128)(2,1)S(1)} %get-tuple-element.162.refs_1_, bf16[768,1024]{1,0:T(8,128)(2,1)S(1)} %copy-done.32, bf16[768,1024]{1,0:T(8,128)(2,1)S(1)} %copy-done.30, ...), custom_call_target="tpu_custom_call" | custom-call | flops 1 | bytes 1 | tf_op jit(solution)/shard_map/feed_weights/pallas_call | solution.py:59
  197.8 2.6 collective-permute-done.12.refs_8_
  200.4 6.7 %middle_back.1 = (bf16[4,384,256]{2,1,0:T(8,128)(2,1)S(1)}, bf16[384,1024]{1,0:T(8,128)(2,1)S(1)}, f32[384,1024]{1,0:T(8,128)S(1)}, f32[8,3072]{1,0:T(8,128)S(1)}, f32[8,1024]{1,0:T(8,128)S(1)}) custom-call(f32[384,1024]{1,0:T(8,128)S(1)} %copy-done.17, f32[384,1024]{1,0:T(8,128)S(1)} %copy-done.36, bf16[384,1024]{1,0:T(8,128)(2,1)S(1)} %bitcast.81, ...), custom_call_target="tpu_custom_call" | custom-call | flops 1 | bytes 1 | tf_op jit(solution)/shard_map/middle_back/pallas_call | solution.py:59
  210.1 4.5 %all-to-all-start.3 = ((bf16[4,384,256]{2,1,0:T(8,128)(2,1)}), bf16[4,384,256]{2,1,0:T(8,128)(2,1)}, u32[]{:S(2)}, u32[]{:S(2)}) async-start(bf16[4,384,256]{2,1,0:T(8,128)(2,1)} %copy-done.45), calls=%async_computation.3 | async-start | bytes 1572864 | tf_op jit(solution)/shard_map/all_to_all | solution.py:743
  218.5 4.0 proj_weights.1
  233.7 16.5 %attend_back.2 = (bf16[1536,128]{1,0:T(8,128)(2,1)S(1)}, bf16[1536,128]{1,0:T(8,128)(2,1)S(1)}, bf16[1536,128]{1,0:T(8,128)(2,1)S(1)}) custom-call(s32[6]{0:T(128)S(1)} %get-tuple-element.355.refs_0_, s32[6]{0:T(128)S(1)} %get-tuple-element.354.refs_1_, s32[1,1536]{1,0:T(1,128)S(1)} %broadcast_in_dim.131.refs_2_, s32[1,1536]{1,0:T(1,128)S(1)} %min.14.refs_3_, ...), custom_call_target="tpu_custom_call" | custom-call | flops 1 | bytes 1 | tf_op jit(solution)/shard_map/attend_back/pallas_call | solution.py:59
  250.3 3.3 output.1
  255.4 4.4 %all-to-all-start.4 = ((bf16[8,48,1024]{2,1,0:T(8,128)(2,1)}), bf16[8,48,1024]{2,1,0:T(8,128)(2,1)}, u32[]{:S(2)}, u32[]{:S(2)}) async-start(bf16[8,48,1024]{2,1,0:T(8,128)(2,1)} %bitcast.89), calls=%async_computation.4 | async-start | bytes 1572864 | tf_op jit(solution)/shard_map/all_to_all | solution.py:739
  263.8 16.3 %attend_back.3 = (bf16[1536,128]{1,0:T(8,128)(2,1)S(1)}, bf16[1536,128]{1,0:T(8,128)(2,1)S(1)}, bf16[1536,128]{1,0:T(8,128)(2,1)S(1)}) custom-call(s32[6]{0:T(128)S(1)} %get-tuple-element.355.refs_0_, s32[6]{0:T(128)S(1)} %get-tuple-element.354.refs_1_, s32[1,1536]{1,0:T(1,128)S(1)} %broadcast_in_dim.131.refs_2_, s32[1,1536]{1,0:T(1,128)S(1)} %min.14.refs_3_, ...), custom_call_target="tpu_custom_call" | custom-call | flops 1 | bytes 1 | tf_op jit(solution)/shard_map/attend_back/pallas_call | solution.py:59
  295.0 10.4 %qkv_back.1 = (bf16[384,1024]{1,0:T(8,128)(2,1)S(1)}, bf16[384,1024]{1,0:T(8,128)(2,1)S(1)}, bf16[384,1024]{1,0:T(8,128)(2,1)S(1)}, bf16[384,1024]{1,0:T(8,128)(...) custom-call(bf16[4,4,2,128,256]{4,3,2,1,0:T(8,128)(2,1)S(1)} %copy-d, ...), custom_call_target="tpu_custom_call" | custom-call | flops 1 | bytes 1 | tf_op jit(solution)/shard_map/qkv_back/pallas_call | solution.py:59
  311.1 7.2 %qkv_weights.1 = (bf16[4,4,256,128]{3,2,1,0:T(8,128)(2,1)S(1)}, bf16[4,4,256,128]{3,2,1,0:T(8,128)(2,1)S(1)}) custom-call(s32[4]{0:T(128)S(1)} %pad_add_fusion.refs_0_.refs_2_, bf16[1536,768]{1,0:T(8,128)(2,1)S(1)} %copy-done.19, bf16[384,1024]{1,0:T(8,128)(2,1)S(1)} %first_norm.1.refs_5_.refs_2_, bf16[384,1024]{1,0:T(8,128)(2,1)} %collective-permute-done.1.refs_6_.refs_3_, ...), custom_call_target="tpu_custom_call" | custom-call | flops 1 | bytes 1 | tf_op jit(solution)/shard_map/qkv_weights/pallas_call | solution.py:59
  319.3 11.9 %collective-permute-done.23.refs_8_ = bf16[2,4,2,128,256]{4,3,2,1,0:T(8,128)(2,1)S(1)} collective-permute-done((bf16[2,4,2,128,256]{4,3,2,1,0:T(8,128)(2,1)S(1)}, bf16[2,4,2,128,256]{4,3,2,1,0:T(8,128)(2,1)S(1)}, u32[]{:S(2)}, u32[]{:S(2)}) %collective-permute-start.23) | collective-permute-done | bytes 1048608 | tf_op jit(solution)/shard_map/ppermute | solution.py:756
  331.2 4.0 tokens_back.1
  337.8 5.9 %all-to-all-start.5 = ((bf16[8,48,1024]{2,1,0:T(8,128)(2,1)}), bf16[8,48,1024]{2,1,0:T(8,128)(2,1)}, u32[]{:S(2)}, u32[]{:S(2)}) async-start(bf16[8,48,1024]{2,1,0:T(8,128)(2,1)} %bitcast.87), calls=%async_computation.5 | async-start | bytes 1572864 | tf_op jit(solution)/shard_map/all_to_all | solution.py:739
  355.8 21.8 %all-to-all-done.5 = bf16[8,48,1024]{2,1,0:T(8,128)(2,1)} async-done(((bf16[8,48,1024]{2,1,0:T(8,128)(2,1)}), bf16[8,48,1024]{2,1,0:T(8,128)(2,1)}, u32[]{:S(2)}, u32[]{:S(2)}) %all-to-all-start.5) | async-done | bytes 786464 | tf_op jit(solution)/shard_map/all_to_all | solution.py:739
  383.6 2.6 convolution_convert_fusion
  392.1 5.4 %collective-permute-start.28 = (f32[96,256]{1,0:T(8,128)S(1)}, f32[96,256]{1,0:T(8,128)S(1)}, u32[]{:S(2)}, u32[]{:S(2)}) collective-permute-start(f32[96,256]{1,0:T(8,128)S(1)} %get-tuple-element.249), channel_id=1, source_target_pairs={{0,1},{1,0},{2,3},{3,2},{4,5},{5,4},{6,7},{7,6},{8,9},{9,8},{10,11... | collective-permute-start | bytes 294920 | tf_op jit(solution)/shard_map/ppermute | solution.py:756
  397.5 2.9 fusion.21
  411.5 8.4 %collective-permute-done.31 = bf16[1,4,256,128]{3,2,1,0:T(8,128)(2,1)S(1)} collective-permute-done((bf16[1,4,256,128]{3,2,1,0:T(8,128)(2,1)S(1)}, bf16[1,4,256,128]{3,2,1,0:T(8,128)(2,1)S(1)}, u32[]{:S(2)}, u32[]{:S(2)}) %collective-permute-start.31) | collective-permute-done | bytes 262176 | tf_op jit(solution)/shard_map/ppermute | solution.py:756
  (369 shorter events, 137.6 us)
Async XLA Ops:
  7.2 135.2 %all-gather.7.cloned.1.call-start = ((), (), s32[]{:S(2)}) async-start(), calls=%async_computation.7 | async-start | bytes 2359296 | tf_op jit(solution)/shard_map/all_gather | solution.py:872
  15.5 35.9 %all-to-all-start = ((bf16[8,48,1024]{2,1,0:T(8,128)(2,1)}), bf16[8,48,1024]{2,1,0:T(8,128)(2,1)S(1)}, u32[]{:S(2)}, u32[]{:S(2)}) async-start(bf16[8,48,1024]{2,1,0:T(8,128)(2,1)} %bitcast.88), calls=%async_computation | async-start | bytes 1572864 | tf_op jit(solution)/shard_map/all_to_all | solution.py:739
  22.8 119.5 %all-gather.5.cloned.1.call-start = ((), (), s32[]{:S(2)}) async-start(), calls=%async_computation.6 | async-start | bytes 2433024 | tf_op jit(solution)/shard_map/all_gather | solution.py:870
  53.1 19.3 %collective-permute-start.2 = (bf16[384,1024]{1,0:T(8,128)(2,1)S(1)}, bf16[384,1024]{1,0:T(8,128)(2,1)}, u32[]{:S(2)}, u32[]{:S(2)}) collective-permute-start(bf16[384,1024]{1,0:T(8,128)(2,1)S(1)} %first_norm.1.refs_5_.refs_2_), channel_id=1, source_target_pairs={{0,8},{4,12},{8,0},{12,4},{1,9},{5,13},{9,1},{13,5},{2,10},{6,14},... | collective-permute-start | bytes 2359304 | tf_op jit(solution)/shard_map/ppermute | solution.py:756
  54.6 17.8 %collective-permute-start = (s32[1536]{0:T(1024)S(1)}, s32[1536]{0:T(1024)S(1)}, u32[]{:S(2)}, u32[]{:S(2)}) collective-permute-start(s32[1536]{0:T(1024)S(1)} %reduce.2), channel_id=1, source_target_pairs={{0,0},{1,4},{2,8},{3,12},{4,1},{5,5},{6,9},{7,13},{8,2},{9,6},{10,... | collective-permute-start | bytes 18440 | tf_op jit(solution)/shard_map/ppermute | solution.py:908
  55.4 53.5 %all-to-all-start.2 = ((bf16[8,48,1024]{2,1,0:T(8,128)(2,1)}), bf16[8,48,1024]{2,1,0:T(8,128)(2,1)S(1)}, u32[]{:S(2)}, u32[]{:S(2)}) async-start(bf16[8,48,1024]{2,1,0:T(8,128)(2,1)} %bitcast.86), calls=%async_computation.2 | async-start | bytes 1572864 | tf_op jit(solution)/shard_map/all_to_all | solution.py:739
  62.0 13.0 %collective-permute-start.1 = (bf16[384,1024]{1,0:T(8,128)(2,1)S(1)}, bf16[384,1024]{1,0:T(8,128)(2,1)}, u32[]{:S(2)}, u32[]{:S(2)}) collective-permute-start(bf16[384,1024]{1,0:T(8,128)(2,1)S(1)} %first_norm.1.refs_5_.refs_2_), channel_id=1, source_target_pairs={{0,4},{4,0},{8,12},{12,8},{1,5},{5,1},{9,13},{13,9},{2,6},{6,2},{1... | collective-permute-start | bytes 2359304 | tf_op jit(solution)/shard_map/ppermute | solution.py:756
  108.9 16.6 %all-to-all-start.1 = ((bf16[4,384,256]{2,1,0:T(8,128)(2,1)}), bf16[4,384,256]{2,1,0:T(8,128)(2,1)}, u32[]{:S(2)}, u32[]{:S(2)}) async-start(bf16[4,384,256]{2,1,0:T(8,128)(2,1)} %copy-done.46), calls=%async_computation.1 | async-start | bytes 1572864 | tf_op jit(solution)/shard_map/all_to_all | solution.py:743
  115.1 27.2 %collective-permute-start.8 = (bf16[384,1024]{1,0:T(8,128)(2,1)}, bf16[384,1024]{1,0:T(8,128)(2,1)}, u32[]{:S(2)}, u32[]{:S(2)}) collective-permute-start(bf16[384,1024]{1,0:T(8,128)(2,1)} %get-tuple-element.156.refs_5_.refs_9_), channel_id=1, source_target_pairs={{0,8},{4,12},{8,0},{12,4},{1,9},{5,13},{9,1},{13,5},{2,10},{6,14},... | collective-permute-start | bytes 2359304 | tf_op jit(solution)/shard_map/ppermute | solution.py:756
  117.2 29.0 %collective-permute-start.5 = (bf16[384,1024]{1,0:T(8,128)(2,1)}, bf16[384,1024]{1,0:T(8,128)(2,1)}, u32[]{:S(2)}, u32[]{:S(2)}) collective-permute-start(bf16[384,1024]{1,0:T(8,128)(2,1)} %get-tuple-element.156.refs_5_.refs_9_), channel_id=1, source_target_pairs={{0,4},{4,0},{8,12},{12,8},{1,5},{5,1},{9,13},{13,9},{2,6},{6,2},{1... | collective-permute-start | bytes 2359304 | tf_op jit(solution)/shard_map/ppermute | solution.py:756
  136.0 25.5 %collective-permute-start.6 = (bf16[384,1024]{1,0:T(8,128)(2,1)}, bf16[384,1024]{1,0:T(8,128)(2,1)}, u32[]{:S(2)}, u32[]{:S(2)}) collective-permute-start(bf16[384,1024]{1,0:T(8,128)(2,1)} %get-tuple-element.155.refs_3_.refs_5_), channel_id=1, source_target_pairs={{0,8},{4,12},{8,0},{12,4},{1,9},{5,13},{9,1},{13,5},{2,10},{6,14},... | collective-permute-start | bytes 2359304 | tf_op jit(solution)/shard_map/ppermute | solution.py:756
  142.3 19.6 %collective-permute-start.9 = (bf16[384,1024]{1,0:T(8,128)(2,1)}, bf16[384,1024]{1,0:T(8,128)(2,1)}, u32[]{:S(2)}, u32[]{:S(2)}) collective-permute-start(bf16[384,1024]{1,0:T(8,128)(2,1)} %collective-permute-done.8.refs_5_.refs_11_), channel_id=1, source_target_pairs={{0,4},{4,0},{8,12},{12,8},{1,5},{5,1},{9,13},{13,9},{2,6},{6,2},{1... | collective-permute-start | bytes 2359304 | tf_op jit(solution)/shard_map/ppermute | solution.py:756
  180.2 17.6 %collective-permute-start.11 = (bf16[384,1024]{1,0:T(8,128)(2,1)S(1)}, bf16[384,1024]{1,0:T(8,128)(2,1)S(1)}, u32[]{:S(2)}, u32[]{:S(2)}) collective-permute-start(bf16[384,1024]{1,0:T(8,128)(2,1)S(1)} %get-tuple-element.172), channel_id=1, source_target_pairs={{0,4},{4,0},{8,12},{12,8},{1,5},{5,1},{9,13},{13,9},{2,6},{6,2},{1... | collective-permute-start | bytes 2359304 | tf_op jit(solution)/shard_map/ppermute | solution.py:756
  180.6 19.8 %collective-permute-start.12 = (bf16[384,1024]{1,0:T(8,128)(2,1)}, bf16[384,1024]{1,0:T(8,128)(2,1)S(1)}, u32[]{:S(2)}, u32[]{:S(2)}) collective-permute-start(bf16[384,1024]{1,0:T(8,128)(2,1)} %add_convert_fusion.2), channel_id=1, source_target_pairs={{0,8},{4,12},{8,0},{12,4},{1,9},{5,13},{9,1},{13,5},{2,10},{6,14},... | collective-permute-start | bytes 2359304 | tf_op jit(solution)/shard_map/ppermute | solution.py:756
  197.7 17.5 %collective-permute-start.13 = (bf16[384,1024]{1,0:T(8,128)(2,1)}, bf16[384,1024]{1,0:T(8,128)(2,1)}, u32[]{:S(2)}, u32[]{:S(2)}) collective-permute-start(bf16[384,1024]{1,0:T(8,128)(2,1)} %get-tuple-element.181), channel_id=1, source_target_pairs={{0,4},{4,0},{8,12},{12,8},{1,5},{5,1},{9,13},{13,9},{2,6},{6,2},{1... | collective-permute-start | bytes 2359304 | tf_op jit(solution)/shard_map/ppermute | solution.py:756
  210.1 16.6 %all-to-all-start.3 = ((bf16[4,384,256]{2,1,0:T(8,128)(2,1)}), bf16[4,384,256]{2,1,0:T(8,128)(2,1)}, u32[]{:S(2)}, u32[]{:S(2)}) async-start(bf16[4,384,256]{2,1,0:T(8,128)(2,1)} %copy-done.45), calls=%async_computation.3 | async-start | bytes 1572864 | tf_op jit(solution)/shard_map/all_to_all | solution.py:743
  214.6 35.7 %collective-permute-start.14 = (bf16[384,1024]{1,0:T(8,128)(2,1)}, bf16[384,1024]{1,0:T(8,128)(2,1)}, u32[]{:S(2)}, u32[]{:S(2)}) collective-permute-start(bf16[384,1024]{1,0:T(8,128)(2,1)} %copy-done.80), channel_id=1, source_target_pairs={{0,4},{4,0},{8,12},{12,8},{1,5},{5,1},{9,13},{13,9},{2,6},{6,2},{1... | collective-permute-start | bytes 2359304 | tf_op jit(solution)/shard_map/ppermute | solution.py:756
  226.6 23.7 %collective-permute-start.15 = (bf16[384,1024]{1,0:T(8,128)(2,1)}, bf16[384,1024]{1,0:T(8,128)(2,1)S(1)}, u32[]{:S(2)}, u32[]{:S(2)}) collective-permute-start(bf16[384,1024]{1,0:T(8,128)(2,1)} %copy-done.81), channel_id=1, source_target_pairs={{0,8},{4,12},{8,0},{12,4},{1,9},{5,13},{9,1},{13,5},{2,10},{6,14},... | collective-permute-start | bytes 2359304 | tf_op jit(solution)/shard_map/ppermute | solution.py:756
  228.3 56.3 %collective-permute-start.18 = (bf16[4,4,2,128,256]{4,3,2,1,0:T(8,128)(2,1)}, bf16[4,4,2,128,256]{4,3,2,1,0:T(8,128)(2,1)}, u32[]{:S(2)}, u32[]{:S(2)}) collective-permute-start(bf16[4,4,2,128,256]{4,3,2,1,0:T(8,128)(2,1)} %get-tuple-element.206), channel_id=1, source_target_pairs={{0,16},{16,0},{1,17},{17,1},{2,18},{18,2},{3,19},{19,3},{4,20},{20... | collective-permute-start | bytes 6291464 | tf_op jit(solution)/shard_map/ppermute | solution.py:756
  228.9 21.4 %collective-permute-start.16 = (bf16[2,4,256,128]{3,2,1,0:T(8,128)(2,1)}, bf16[2,4,256,128]{3,2,1,0:T(8,128)(2,1)S(1)}, u32[]{:S(2)}, u32[]{:S(2)}) collective-permute-start(bf16[2,4,256,128]{3,2,1,0:T(8,128)(2,1)} %copy-done.85), channel_id=1, source_target_pairs={{0,4},{4,0},{8,12},{12,8},{1,5},{5,1},{9,13},{13,9},{2,6},{6,2},{1... | collective-permute-start | bytes 1572872 | tf_op jit(solution)/shard_map/ppermute | solution.py:756
  255.4 29.3 %all-to-all-start.4 = ((bf16[8,48,1024]{2,1,0:T(8,128)(2,1)}), bf16[8,48,1024]{2,1,0:T(8,128)(2,1)}, u32[]{:S(2)}, u32[]{:S(2)}) async-start(bf16[8,48,1024]{2,1,0:T(8,128)(2,1)} %bitcast.89), calls=%async_computation.4 | async-start | bytes 1572864 | tf_op jit(solution)/shard_map/all_to_all | solution.py:739
  259.7 22.6 %collective-permute-start.17 = (bf16[2,4,256,128]{3,2,1,0:T(8,128)(2,1)}, bf16[2,4,256,128]{3,2,1,0:T(8,128)(2,1)S(1)}, u32[]{:S(2)}, u32[]{:S(2)}) collective-permute-start(bf16[2,4,256,128]{3,2,1,0:T(8,128)(2,1)} %copy-done.86), channel_id=1, source_target_pairs={{0,8},{4,12},{8,0},{12,4},{1,9},{5,13},{9,1},{13,5},{2,10},{6,14},... | collective-permute-start | bytes 1572872 | tf_op jit(solution)/shard_map/ppermute | solution.py:756
  305.6 13.7 %collective-permute-start.21 = (bf16[384,1024]{1,0:T(8,128)(2,1)S(1)}, bf16[384,1024]{1,0:T(8,128)(2,1)S(1)}, u32[]{:S(2)}, u32[]{:S(2)}) collective-permute-start(bf16[384,1024]{1,0:T(8,128)(2,1)S(1)} %get-tuple-element.226), channel_id=1, source_target_pairs={{0,4},{4,0},{8,12},{12,8},{1,5},{5,1},{9,13},{13,9},{2,6},{6,2},{1... | collective-permute-start | bytes 2359304 | tf_op jit(solution)/shard_map/ppermute | solution.py:756
  306.1 25.1 %collective-permute-start.23 = (bf16[2,4,2,128,256]{4,3,2,1,0:T(8,128)(2,1)S(1)}, bf16[2,4,2,128,256]{4,3,2,1,0:T(8,128)(2,1)S(1)}, u32[]{:S(2)}, u32[]{:S(2)}) collective-permute-start(bf16[2,4,2,128,256]{4,3,2,1,0:T(8,128)(2,1)S(1)} %get-tuple-element.228), channel_id=1, source_target_pairs={{0,1},{1,0},{2,3},{3,2},{4,5},{5,4},{6,7},{7,6},{8,9},{9,8},{10,11... | collective-permute-start | bytes 3145736 | tf_op jit(solution)/shard_map/ppermute | solution.py:756
  308.2 23.1 %collective-permute-start.22 = (bf16[384,1024]{1,0:T(8,128)(2,1)S(1)}, bf16[384,1024]{1,0:T(8,128)(2,1)S(1)}, u32[]{:S(2)}, u32[]{:S(2)}) collective-permute-start(bf16[384,1024]{1,0:T(8,128)(2,1)S(1)} %add_convert_fusion.1), channel_id=1, source_target_pairs={{0,8},{4,12},{8,0},{12,4},{1,9},{5,13},{9,1},{13,5},{2,10},{6,14},... | collective-permute-start | bytes 2359304 | tf_op jit(solution)/shard_map/ppermute | solution.py:756
  337.8 39.8 %all-to-all-start.5 = ((bf16[8,48,1024]{2,1,0:T(8,128)(2,1)}), bf16[8,48,1024]{2,1,0:T(8,128)(2,1)}, u32[]{:S(2)}, u32[]{:S(2)}) async-start(bf16[8,48,1024]{2,1,0:T(8,128)(2,1)} %bitcast.87), calls=%async_computation.5 | async-start | bytes 1572864 | tf_op jit(solution)/shard_map/all_to_all | solution.py:739
  343.7 34.4 %collective-permute-start.29 = (bf16[4,4,256,128]{3,2,1,0:T(8,128)(2,1)}, bf16[4,4,256,128]{3,2,1,0:T(8,128)(2,1)}, u32[]{:S(2)}, u32[]{:S(2)}) collective-permute-start(bf16[4,4,256,128]{3,2,1,0:T(8,128)(2,1)} %copy-done.79), channel_id=1, source_target_pairs={{0,16},{16,0},{1,17},{17,1},{2,18},{18,2},{3,19},{19,3},{4,20},{20... | collective-permute-start | bytes 3145736 | tf_op jit(solution)/shard_map/ppermute | solution.py:756
  352.1 34.8 %collective-permute-start.32 = (bf16[1,4,2,128,256]{4,3,2,1,0:T(8,128)(2,1)}, bf16[1,4,2,128,256]{4,3,2,1,0:T(8,128)(2,1)S(1)}, u32[]{:S(2)}, u32[]{:S(2)}) collective-permute-start(bf16[1,4,2,128,256]{4,3,2,1,0:T(8,128)(2,1)} %copy-done.84), channel_id=1, source_target_pairs={{0,2},{1,3},{2,0},{3,1},{4,6},{5,7},{6,4},{7,5},{8,10},{9,11},{10,... | collective-permute-start | bytes 1572872 | tf_op jit(solution)/shard_map/ppermute | solution.py:756
  380.5 25.0 %collective-permute-start.30 = (bf16[2,4,256,128]{3,2,1,0:T(8,128)(2,1)}, bf16[2,4,256,128]{3,2,1,0:T(8,128)(2,1)}, u32[]{:S(2)}, u32[]{:S(2)}) collective-permute-start(bf16[2,4,256,128]{3,2,1,0:T(8,128)(2,1)} %slice.84), channel_id=1, source_target_pairs={{0,1},{1,0},{2,3},{3,2},{4,5},{5,4},{6,7},{7,6},{8,9},{9,8},{10,11... | collective-permute-start | bytes 1572872 | tf_op jit(solution)/shard_map/ppermute | solution.py:756
  387.8 12.5 %collective-permute-start.33 = (bf16[2,128,256]{2,1,0:T(8,128)(2,1)S(1)}, bf16[2,128,256]{2,1,0:T(8,128)(2,1)S(1)}, u32[]{:S(2)}, u32[]{:S(2)}) collective-permute-start(bf16[2,128,256]{2,1,0:T(8,128)(2,1)S(1)} %get-tuple-element.263), channel_id=1, source_target_pairs={{0,4},{4,0},{8,12},{12,8},{1,5},{5,1},{9,13},{13,9},{2,6},{6,2},{1... | collective-permute-start | bytes 393224 | tf_op jit(solution)/shard_map/ppermute | solution.py:1218
  387.9 12.5 %collective-permute-start.34 = (bf16[2,128,256]{2,1,0:T(8,128)(2,1)S(1)}, bf16[2,128,256]{2,1,0:T(8,128)(2,1)S(1)}, u32[]{:S(2)}, u32[]{:S(2)}) collective-permute-start(bf16[2,128,256]{2,1,0:T(8,128)(2,1)S(1)} %get-tuple-element.264), channel_id=1, source_target_pairs={{0,8},{4,12},{8,0},{12,4},{1,9},{5,13},{9,1},{13,5},{2,10},{6,14},... | collective-permute-start | bytes 393224 | tf_op jit(solution)/shard_map/ppermute | solution.py:1218
  407.7 12.2 %collective-permute-start.31 = (bf16[1,4,256,128]{3,2,1,0:T(8,128)(2,1)S(1)}, bf16[1,4,256,128]{3,2,1,0:T(8,128)(2,1)S(1)}, u32[]{:S(2)}, u32[]{:S(2)}) collective-permute-start(bf16[1,4,256,128]{3,2,1,0:T(8,128)(2,1)S(1)} %slice.86), channel_id=1, source_target_pairs={{0,2},{1,3},{2,0},{3,1},{4,6},{5,7},{6,4},{7,5},{8,10},{9,11},{10,... | collective-permute-start | bytes 786440 | tf_op jit(solution)/shard_map/ppermute | solution.py:756
  (114 other events, 734.5 us)
Sparse Core Ops, SparseCore 0:
  10.7 76.3 all-gather.6
  89.8 48.2 all-gather.4

commit v4 on v3

--- a/solution.py
+++ b/solution.py
@@ -14,6 +14,13 @@
 ANY = pl.BlockSpec(memory_space=pl.ANY)
 HBM = "hbm"
 LIMIT = 40
+LIMITS = {"attend": 57, "attend_back": 57, "attend_back_end": 57, "feed": 50, "feed_weights": 57, "weights": 57, "qkv_weights": 57}
+FLOPS, BYTES = 1_000_000_000, 3_000_000
+TIMES = {
+    "sort": 2, "first_norm": 2, "grad_mlp": 2, "attend": 26, "project": 5, "weights": 4, "feed": 12,
+    "feed_weights": 12, "middle_back": 7, "proj_weights": 3, "output": 3, "attend_back": 16, "attend_back_end": 21, "add": 3,
+    "qkv_weights": 8, "tokens_back": 5,
+}
 PLAIN = ((1,), (0,))
 BY_ROW = ((1,), (1,))
 
@@ -56,6 +63,7 @@
         for copy in backs:
             copy.wait()
 
+    limit = LIMITS.get(name, limit)
     return pl.pallas_call(
         body,
         name=name,
@@ -64,7 +72,9 @@
         out_specs=tuple(ANY if spec is HBM else spec for spec in out_specs),
         scratch_shapes=list(scratch) + staged + sems,
         compiler_params=pltpu.CompilerParams(vmem_limit_bytes=limit * 1024 * 1024),
-        cost_estimate=pl.CostEstimate(flops=1, bytes_accessed=1, transcendentals=0),
+        cost_estimate=pl.CostEstimate(
+            flops=TIMES.get(name, 1) * FLOPS, bytes_accessed=TIMES.get(name, 1) * BYTES, transcendentals=0
+        ),
     )(*operands)
 
 
@@ -102,12 +112,6 @@
     row = lax.broadcasted_iota(jnp.int32, (width, width), 0) // head_dim
     col = lax.broadcasted_iota(jnp.int32, (width, width), 1) // head_dim
     return (row == col).astype(BF)
-
-
-def head_sums(values, same):
-    high = values.astype(BF)
-    low = (values - high.astype(F32)).astype(BF)
-    return dot(high, same) + dot(low, same)
 
 
 def chunks(rows, size):
@@ -159,44 +163,73 @@
     return copies
 
 
-def qkv_kernel(dims, *refs):
-    group, segs, head_dim, parts = dims
-    me_ref, temper_ref, qb_ref, vb_ref, w_ref = refs[:5]
-    blocks = refs[5 : 5 + group]
-    q_ref, k_ref, v_ref, qp_ref, kp_ref, held, sems = refs[5 + group :]
-    width = q_ref.shape[1]
-    rows = blocks[0].shape[0]
+def pick_heads(width, head_dim, first):
+    row = lax.broadcasted_iota(jnp.int32, (width, 128), 0)
+    col = lax.broadcasted_iota(jnp.int32, (width, 128), 1)
+    return (row == (col - first) * head_dim).astype(BF)
+
+
+def spread_heads(width, head_dim, first):
+    row = lax.broadcasted_iota(jnp.int32, (128, width), 0)
+    col = lax.broadcasted_iota(jnp.int32, (128, width), 1)
+    return (row - first == col // head_dim).astype(BF)
+
+
+def exact_dot(values, ones):
+    high = values.astype(BF)
+    low = (values - high.astype(F32)).astype(BF)
+    return dot(high, ones) + dot(low, ones)
+
+
+def attend_kernel(dims, *refs):
+    group, segs, head_dim, parts, block = dims
+    me_ref, first_ref, last_ref, lo_ref, hi_ref, temper_ref, qb_ref, vb_ref, w_ref = refs[:9]
+    blocks = refs[9 : 9 + group]
+    out_o, out_t_o, lse_ref, q_o, ql_o, k_o, v_o, inv_o = refs[9 + group : 17 + group]
+    (held, block_s, q_ref, ql_ref, k_ref, v_ref, inv_ref, v_t, out_t_ref, out_s, acc, total, sems,
+     in_sems, out_sems) = refs[17 + group :]
+    pack_len, width = q_ref.shape
+    rows = block_s.shape[1]
     seg, sub = rows // segs, width // parts
+    pair, heads = 128 // head_dim, width // head_dim
     me = me_ref[0]
+    loads = [
+        pltpu.make_async_copy(blocks[k], block_s.at[k], in_sems.at[k]) for k in range(group)
+    ]
+    loads[0].start()
     copies = load_columns(w_ref, held, sems, lambda p: (p * group + me) * sub, parts, sub)
+    for load in loads[1:]:
+        load.start()
     same = same_head(width, head_dim)
+    pick_q, pick_k = pick_heads(width, head_dim, 0), pick_heads(width, head_dim, heads)
     for copy in copies:
         copy.wait()
     for k in range(group):
+        loads[k].wait()
         for y in range(segs):
             ranks = pl.ds(pl.multiple_of((y * group + (me ^ k)) * seg, 16), seg)
-            made = dot(blocks[k][y * seg : (y + 1) * seg, :], held[...])
+            made = dot(block_s[k, y * seg : (y + 1) * seg, :], held[...])
             query = made[:, :width] + qb_ref[...]
             key = made[:, width : 2 * width]
-            qp_ref[ranks, :] = query
-            kp_ref[ranks, :] = key
-            inverse = lax.rsqrt(head_sums(query * query, same) + 1e-06)
-            q_ref[ranks, :] = (query * inverse * temper_ref[...]).astype(BF)
-            inverse = lax.rsqrt(head_sums(key * key, same) + 1e-06)
-            k_ref[ranks, :] = (key * inverse).astype(BF)
+            inverse_q = lax.rsqrt(exact_dot(query * query, same) + 1e-06)
+            query = query * inverse_q * temper_ref[...]
+            rounded = query.astype(BF)
+            q_ref[ranks, :] = rounded
+            ql_ref[ranks, :] = (query - rounded.astype(F32)).astype(BF)
+            inverse_k = lax.rsqrt(exact_dot(key * key, same) + 1e-06)
+            k_ref[ranks, :] = (key * inverse_k).astype(BF)
             v_ref[ranks, :] = (made[:, 2 * width :] + vb_ref[...]).astype(BF)
-
-
-def attend_kernel(
-    dims, first_ref, last_ref, lo_ref, hi_ref, q_ref, k_ref, v_ref,
-    out_ref, out_t_ref, lse_ref, v_t, out_s, acc, total,
-):
-    group, segs, head_dim, block = dims
-    pack_len, width = q_ref.shape
-    rows = out_ref.shape[1]
-    seg = rows // segs
-    pair = 128 // head_dim
-    heads = width // head_dim
+            inv_ref[ranks, :] = exact_dot(inverse_q, pick_q) + exact_dot(inverse_k, pick_k)
+    stores = []
+
+    def store(source, target):
+        stores.append(pltpu.make_async_copy(source, target, out_sems.at[len(stores)]))
+        stores[-1].start()
+
+    for source, target in (
+        (q_ref, q_o), (ql_ref, ql_o), (k_ref, k_o), (v_ref, v_o), (inv_ref, inv_o)
+    ):
+        store(source, target)
     lanes = lax.broadcasted_iota(jnp.int32, (1, 128), 1) // head_dim
     v_t[...] = v_ref[...].T
 
@@ -232,34 +265,31 @@
     for y in range(segs):
         for g in range(group):
             start = (y * group + g) * seg
-            out_ref[g, y * seg : (y + 1) * seg, :] = out_s[start : start + seg, :]
+            store(out_s.at[pl.ds(start, seg), :], out_o.at[g, pl.ds(y * seg, seg), :])
+    store(out_t_ref, out_t_o)
+    for copy in stores:
+        copy.wait()
 
 
 def attend_back_heads(dims, refs, scratch, outs):
-    group, segs, head_dim, block, near = dims
-    first_ref, last_ref, lo_ref, hi_ref, in_ref, q_ref, k_ref, v_ref, out_t_ref, lse_ref = refs
-    g_s, k_t, dk_acc, dv_acc, acc, sums = scratch
+    head_dim, block, near = dims
+    first_ref, last_ref, lo_ref, hi_ref, lse_ref, q_ref, k_ref, v_ref, out_t_ref, g_s = refs
+    k_t, dk_acc, dv_acc, acc, sums = scratch
     dq_ref, dk_ref, dv_ref = outs
     pack_len = q_ref.shape[0]
-    seg = in_ref.shape[1] // segs
     pair = 128 // head_dim
-    cols = slice(near * 128, (near + 1) * 128)
     lanes = lax.broadcasted_iota(jnp.int32, (1, 128), 1) // head_dim
-    for y in range(segs):
-        for g in range(group):
-            start = (y * group + g) * seg
-            g_s[start : start + seg, :] = in_ref[g, y * seg : (y + 1) * seg, cols]
-    k_t[...] = k_ref[:, cols].T
+    k_t[...] = k_ref[...].T
     dk_acc[...] = jnp.zeros_like(dk_acc)
     dv_acc[...] = jnp.zeros_like(dv_acc)
 
     @pl.loop(0, pack_len // block)
     def _(q_block):
         q_rows = at(q_block, block)
-        queries, grads = q_ref[q_rows, cols], g_s[q_rows, :]
+        queries, grads = q_ref[q_rows, :], g_s[q_rows, :]
         q_t, g_t = queries.T, grads.T
         low, high = lo_ref[:, q_rows], hi_ref[:, q_rows]
-        weighted = g_t.astype(F32) * out_t_ref[cols, q_rows]
+        weighted = g_t.astype(F32) * out_t_ref[:, q_rows]
         for h in range(pair):
             sums[h : h + 1, :] = jnp.sum(
                 weighted[h * head_dim : (h + 1) * head_dim, :], axis=0, keepdims=True
@@ -269,7 +299,7 @@
         @pl.loop(first_ref[q_block], last_ref[q_block])
         def _(k_block):
             k_rows = at(k_block, block)
-            keys, values = k_ref[k_rows, cols], v_ref[k_rows, cols]
+            keys, values = k_ref[k_rows, :], v_ref[k_rows, :]
             index = k_block * block + lax.broadcasted_iota(jnp.int32, (block, block), 0)
             seen = (index >= low) & (index < high)
             for h in range(pair):
@@ -294,60 +324,113 @@
     dv_ref[...] = dv_acc[...].astype(BF)
 
 
+def load_pair(dims, ins, held, sems):
+    group, segs, near = dims
+    in_ref, q_ref, k_ref, v_ref, out_t_ref = ins
+    q_s, k_s, v_s, out_s, g_s = held
+    cols = pl.ds(near * 128, 128)
+    seg = in_ref.shape[1] // segs
+    moves = [(q_ref.at[:, cols], q_s), (k_ref.at[:, cols], k_s), (v_ref.at[:, cols], v_s)]
+    moves.append((out_t_ref.at[cols, :], out_s))
+    for y in range(segs):
+        for g in range(group):
+            start = (y * group + g) * seg
+            moves.append((in_ref.at[g, pl.ds(y * seg, seg), cols], g_s.at[pl.ds(start, seg), :]))
+    copies = []
+    for place, (source, target) in enumerate(moves):
+        copies.append(pltpu.make_async_copy(source, target, sems.at[place]))
+        copies[-1].start()
+    return copies
+
+
 def attend_back_kernel(dims, *refs):
-    attend_back_heads(dims, refs[:10], refs[13:], refs[10:13])
-
-
-def qkv_back_kernel(dims, *refs):
-    group, segs, head_dim, parts, pairs, tile_count = dims
-    add_blocks(refs[:tile_count], refs[-4:-2])
-    refs = refs[tile_count:-4] + refs[-2:]
-    me_ref, temper_ref, w_ref, qp_ref, kp_ref = refs[:5]
-    grads = [refs[5 + 3 * p : 8 + 3 * p] for p in range(pairs)]
-    rest = refs[5 + 3 * pairs :]
-    sent = rest[:group]
-    dqkv_ref, sums_ref, held, sems = rest[group:]
-    width = qp_ref.shape[1]
-    rows = sent[0].shape[0]
+    group, segs, head_dim, block, near = dims
+    ranges, lse_ref, ins, outs = refs[:4], refs[4], refs[5:10], refs[10:13]
+    held, scratch, made, sems, out_sems = refs[13:18], refs[18:23], refs[23:26], refs[26], refs[27]
+    for copy in load_pair((group, segs, near), ins, held, sems):
+        copy.wait()
+    attend_back_heads((head_dim, block, near), (*ranges, lse_ref, *held), scratch, made)
+    stores = [pltpu.make_async_copy(made[i], outs[i], out_sems.at[i]) for i in range(3)]
+    for copy in stores:
+        copy.start()
+    for copy in stores:
+        copy.wait()
+
+
+def attend_back_end_kernel(dims, *refs):
+    group, segs, head_dim, parts, block, pairs = dims
+    me_ref, temper_ref, w_ref, inv_ref, ql_ref = refs[:5]
+    ranges, lse_ref, ins = refs[5:9], refs[9], refs[10:15]
+    earlier, refs = refs[15 : 12 + 3 * pairs], refs[12 + 3 * pairs :]
+    sent, (dqkv_o, sums_ref), refs = refs[:group], refs[group : 2 + group], refs[2 + group :]
+    held, scratch, made, refs = refs[:5], refs[5:10], refs[10:13], refs[13:]
+    (w_s, inv_s, q_s, ql_s, k_s, dqkv_s, sent_s), (sems, w_sems, in_sems, out_sems) = refs[:7], refs[7:]
+    pack_len, width = q_s.shape
+    rows = sent_s.shape[1]
     seg, sub = rows // segs, width // parts
+    heads = width // head_dim
     me = me_ref[0]
-    copies = load_columns(w_ref, held, sems, lambda p: (p * group + me) * sub, parts, sub)
+    loads = load_pair((group, segs, pairs - 1), ins, held, sems)
+    last = pl.ds((pairs - 1) * 128, 128)
+    copies = load_columns(w_ref, w_s, w_sems, lambda p: (p * group + me) * sub, parts, sub)
+    moves = [(inv_ref, inv_s), (ins[1], q_s), (ql_ref, ql_s), (ins[2], k_s)]
+    for p in range(pairs - 1):
+        for which in range(3):
+            cols = pl.ds(p * 128, 128)
+            moves.append((earlier[3 * p + which], made[which].at[:, cols]))
+    for place, (source, target) in enumerate(moves):
+        copies.append(pltpu.make_async_copy(source, target, in_sems.at[place]))
+        copies[-1].start()
+    for load in loads:
+        load.wait()
+    attend_back_heads(
+        (head_dim, block, pairs - 1),
+        (*ranges, lse_ref, *held),
+        scratch,
+        tuple(ref.at[:, last] for ref in made),
+    )
     same = same_head(width, head_dim)
+    spread_q, spread_k = spread_heads(width, head_dim, 0), spread_heads(width, head_dim, heads)
     sums_ref[...] = jnp.zeros_like(sums_ref)
-
-    def back(gradient, pre):
-        inverse = lax.rsqrt(head_sums(pre * pre, same) + 1e-06)
-        unit = pre * inverse
-        return inverse * (gradient - unit * head_sums(gradient * unit, same)), unit
-
-    def joined(which, ranks):
-        return jnp.concatenate([grads[p][which][ranks, :] for p in range(pairs)], axis=1)
-
     for copy in copies:
         copy.wait()
+    stores = []
+    dq_s, dk_s, dv_s = made
     for k in reversed(range(group)):
+        whole = slice(k * rows, (k + 1) * rows)
         for y in range(segs):
             ranks = pl.ds(pl.multiple_of((y * group + (me ^ k)) * seg, 16), seg)
             own = slice(k * rows + y * seg, k * rows + (y + 1) * seg)
-            grad = joined(0, ranks).astype(F32) * temper_ref[...]
-            grad_query, unit = back(grad, qp_ref[ranks, :])
-            grad_query = grad_query.astype(BF)
-            grad_key, _ = back(joined(1, ranks).astype(F32), kp_ref[ranks, :])
-            grad_value = joined(2, ranks)
-            dqkv_ref[own, :width] = grad_query
-            dqkv_ref[own, width : 2 * width] = grad_key.astype(BF)
-            dqkv_ref[own, 2 * width :] = grad_value
-            for index, values in enumerate((grad_query, grad_value, grad * unit)):
+            inverse = inv_s[ranks, :]
+            query = q_s[ranks, :].astype(F32) + ql_s[ranks, :].astype(F32)
+            unit = query / temper_ref[...]
+            raw = dq_s[ranks, :].astype(F32)
+            grad = raw * temper_ref[...]
+            grad_query = exact_dot(inverse, spread_q) * (grad - unit * exact_dot(grad * unit, same))
+            unit_k = k_s[ranks, :].astype(F32)
+            grad = dk_s[ranks, :].astype(F32)
+            grad_key = exact_dot(inverse, spread_k) * (
+                grad - unit_k * exact_dot(grad * unit_k, same)
+            )
+            grad_query, grad_value = grad_query.astype(BF), dv_s[ranks, :]
+            dqkv_s[own, :width] = grad_query
+            dqkv_s[own, width : 2 * width] = grad_key.astype(BF)
+            dqkv_s[own, 2 * width :] = grad_value
+            for index, values in enumerate((grad_query, grad_value, raw * query)):
                 sums_ref[index : index + 1, :] += jnp.sum(
                     values.astype(F32), axis=0, keepdims=True
                 )
-        sent[k][...] = dot(
-            dqkv_ref[k * rows : (k + 1) * rows, :], held[...], BY_ROW
-        ).astype(BF)
+        sent_s[k] = dot(dqkv_s[whole, :], w_s[...], BY_ROW).astype(BF)
+        own = pl.ds(k * rows, rows)
+        for source, target in ((sent_s.at[k], sent[k]), (dqkv_s.at[own, :], dqkv_o.at[own, :])):
+            stores.append(pltpu.make_async_copy(source, target, out_sems.at[len(stores)]))
+            stores[-1].start()
+    for copy in stores:
+        copy.wait()
 
 
 def project_kernel(
-    parts, ret_ref, wp_ref, pb_ref, x_ref, mod_ref, item_ref, attn_ref, branch_ref, middle_ref, out_ref
+    parts, ret_ref, wp_ref, pb_ref, x_ref, mod_ref, item_ref, attn_ref, branch_ref, middle_ref, out_ref, made
 ):
     group, rows, width = ret_ref.shape
     model = x_ref.shape[1]
@@ -356,13 +439,14 @@
         for p in range(parts):
             start = (p * group + g) * sub
             attn_ref[:, start : start + sub] = ret_ref[g, :, p * sub : (p + 1) * sub]
-    branch_ref[...] = dot(attn_ref[...], wp_ref[...]) + pb_ref[...].astype(F32)
+    made[...] = dot(attn_ref[...], wp_ref[...]) + pb_ref[...].astype(F32)
+    branch_ref[...] = made[...].astype(BF)
 
     @chunks(rows, 64)
     def _(i):
         r = at(i, 64)
         item = item_ref[r, :]
-        middle = x_ref[r, :].astype(F32) + mod_rows(mod_ref, 0, item, model) * branch_ref[r, :]
+        middle = x_ref[r, :].astype(F32) + mod_rows(mod_ref, 0, item, model) * made[r, :]
         middle_ref[r, :] = middle
         normed, _ = row_norm(middle)
         scale, shift = mod_rows(mod_ref, 3, item, model), mod_rows(mod_ref, 5, item, model)
@@ -467,35 +551,74 @@
 
 
 def feed_weights_kernel(dims, *refs):
-    count, group, split, halves = dims
+    count, group, split, halves, term_count = dims
     me_ref, acts, ghs = refs[0], refs[1 : 1 + halves], refs[1 + halves : 1 + 2 * halves]
     refs = refs[1 + 2 * halves :]
-    ins, grads, rest = refs[:count], refs[count : 2 * count], refs[2 * count :]
-    outs, (in_t, grad_t, act_s, gh_s) = rest[:split], rest[split:]
-    rows, model = ins[0].shape
+    ins, grads, refs = refs[:count], refs[count : 2 * count], refs[2 * count :]
+    terms, refs = refs[:term_count], refs[term_count:]
+    outs, sum_o, rest = refs[: 2 * split], refs[2 * split], refs[2 * split + 1 :]
+    in_t, grad_t, act_s, gh_s, in_s, grad_s, term_s, sum_s, tile_s, in_sems, out_sems = rest
+    rows, model = in_s.shape[1:]
+
+    def load(source, target, index):
+        copy = pltpu.make_async_copy(source, target, in_sems.at[index])
+        copy.start()
+        return copy
+
+    part_rows = act_s.shape[0] // halves
+    own = [pl.ds(k * part_rows, part_rows) for k in range(halves)]
+    in_loads = [load(ins[k], in_s.at[k], k) for k in range(count)]
+    index = count
+    gh_loads = [load(ghs[k], gh_s.at[own[k], :], index + k) for k in range(halves)]
+    index += halves
+    grad_loads = [load(grads[k], grad_s.at[k], index + k) for k in range(count)]
+    index += count
+    act_loads = [load(acts[k], act_s.at[own[k], :], index + k) for k in range(halves)]
+    index += halves
+    term_loads = [load(terms[k], term_s.at[k], index + k) for k in range(term_count)]
     for k in range(count):
-        own = slice(k * rows, (k + 1) * rows)
-        in_t[:, own] = ins[k][...].T
-        grad_t[:, own] = grads[k][...].T
-    for k in range(halves):
-        own = slice(k * acts[k].shape[0], (k + 1) * acts[k].shape[0])
-        act_s[own, :] = acts[k][...]
-        gh_s[own, :] = ghs[k][...]
+        in_loads[k].wait()
+        in_t[:, k * rows : (k + 1) * rows] = in_s[k].T
+    for copy in gh_loads:
+        copy.wait()
+    stores = []
+
+    def store(source, target):
+        stores.append(pltpu.make_async_copy(source, target, out_sems.at[len(stores)]))
+        stores[-1].start()
+
     part = model // split
     fine = part // group
-    head_size, _, _, _, hidden = outs[0].shape
+    _, _, head_size, _, _, hidden = tile_s.shape
+
+    def tiles(y, which, left, right):
+        start = pl.multiple_of((me_ref[1] ^ y) * part, part) if split > 1 else 0
+        for j in range(head_size):
+            z = me_ref[2] ^ turned(j, head_size)
+            cols = slice(None)
+            if split > 1:
+                cols = pl.ds(pl.multiple_of(z * hidden, hidden), hidden)
+            made = dot(left[pl.ds(start, part), :], right[:, cols]).astype(BF)
+            for g in range(group):
+                to = (me_ref[0] ^ g) if group > 1 else 0
+                tile_s[which, y, j, to] = made[g * fine : (g + 1) * fine, :]
+        store(tile_s.at[which, y], outs[which * split + y])
+
     for y in reversed(range(split)):
-        for which, left, right in ((0, in_t, gh_s), (1, grad_t, act_s)):
-            start = pl.multiple_of((me_ref[1] ^ y) * part, part) if split > 1 else 0
-            for j in range(head_size):
-                z = me_ref[2] ^ turned(j, head_size)
-                cols = slice(None)
-                if split > 1:
-                    cols = pl.ds(pl.multiple_of(z * hidden, hidden), hidden)
-                made = dot(left[pl.ds(start, part), :], right[:, cols]).astype(BF)
-                for g in range(group):
-                    to = (me_ref[0] ^ g) if group > 1 else 0
-                    outs[y][j, to, which] = made[g * fine : (g + 1) * fine, :]
+        tiles(y, 0, in_t, gh_s)
+    for k in range(count):
+        grad_loads[k].wait()
+        grad_t[:, k * rows : (k + 1) * rows] = grad_s[k].T
+    for copy in act_loads:
+        copy.wait()
+    for y in reversed(range(split)):
+        tiles(y, 1, grad_t, act_s)
+    for copy in term_loads:
+        copy.wait()
+    sum_s[...] = sum(term_s[k].astype(F32) for k in range(term_count)).astype(BF)
+    store(sum_s, sum_o)
+    for copy in stores:
+        copy.wait()
 
 
 def middle_back_kernel(
@@ -521,7 +644,7 @@
         grad_branch = (grad_middle * mod_rows(mod_ref, 0, item, model)).astype(BF)
         gb_ref[r, :] = grad_branch
         col_ref[0:1, :] += jnp.sum(grad_branch.astype(F32), axis=0, keepdims=True)
-        add_item_sums(sums_ref, 0, item, grad_middle * branch_ref[r, :], items)
+        add_item_sums(sums_ref, 0, item, grad_middle * branch_ref[r, :].astype(F32), items)
         add_item_sums(sums_ref, 1, item, grad_in * normed, items)
         add_item_sums(sums_ref, 2, item, grad_in, items)
 
@@ -533,9 +656,11 @@
 
 
 def output_kernel(dims, middle_ref, up_ref, mod_ref, item_ref, bias_ref, *refs):
-    items, count, proj_count = dims
+    items, count, proj_count, tile_count = dims
     terms, refs = refs[:count], refs[count:]
-    projs, (out_ref, sums_ref, proj_ref) = refs[:proj_count], refs[proj_count:]
+    projs, refs = refs[:proj_count], refs[proj_count:]
+    tiles, (out_ref, sums_ref, proj_ref, kept_ref, sent_ref) = refs[:tile_count], refs[tile_count:]
+    add_blocks(tiles, (kept_ref, sent_ref))
     proj_ref[...] = sum(proj[...].astype(F32) for proj in projs).astype(BF)
     rows, model = middle_ref.shape
     sums_ref[...] = jnp.zeros_like(sums_ref)
@@ -551,10 +676,8 @@
 
 
 def tokens_back_kernel(dims, x_ref, gm_ref, mod_ref, item_ref, *refs):
-    items, count, tile_count = dims
-    terms, refs = refs[:count], refs[count:]
-    tiles, (out_ref, sums_ref, kept_ref, sent_ref) = refs[:tile_count], refs[tile_count:]
-    add_blocks(tiles, (kept_ref, sent_ref))
+    items, count = dims
+    terms, (out_ref, sums_ref) = refs[:count], refs[count:]
     rows, model = x_ref.shape
     sums_ref[...] = jnp.zeros_like(sums_ref)
 
@@ -573,10 +696,8 @@
 
 
 def proj_weights_kernel(dims, me_ref, attn_ref, gb_ref, *refs):
-    group, split, count = dims
-    terms, refs = refs[:count], refs[count:]
-    outs, (sum_ref, left_t, right) = refs[:group], refs[group:]
-    sum_ref[...] = sum(term[...].astype(F32) for term in terms).astype(BF)
+    group, split = dims
+    outs, (left_t, right) = refs[:group], refs[group:]
     left_t[...] = attn_ref[...].T
     chunk, head_size, tall, wide = outs[0].shape
     for k in range(group):
@@ -699,10 +820,18 @@
     )
 
 
-def own_tiles_kernel(count, *refs):
-    terms, outs = refs[:count], refs[count:]
+def add_kernel(counts, *refs):
+    terms, outs = refs[: sum(counts)], refs[sum(counts) :]
+    for place, count in enumerate(counts):
+        add_blocks(terms[:count], outs[2 * place : 2 * place + 2])
+        terms = terms[count:]
+
+
+def own_tiles_kernel(*refs):
+    ups, downs, outs = refs[:2], refs[2:4], refs[4:]
     for i, out in enumerate(outs):
-        out[...] = sum(term[0, i].astype(F32) for term in terms).astype(BF)
+        for which, terms in enumerate((ups, downs)):
+            out[which] = sum(term[0, i].astype(F32) for term in terms).astype(BF)
 
 
 def place_kernel(group, me_ref, *refs):
@@ -802,6 +931,11 @@
 
 def tie(*values):
     return lax.optimization_barrier(values)
+
+
+def tie_groups(*groups):
+    tied = list(tie(*[value for group in groups for value in group]))
+    return [[tied.pop(0) for _ in group] for group in groups]
 
 
 def shards(
@@ -942,20 +1076,7 @@
     scale_here = pick(log_scale.reshape(parts, group, per_part), g, 1).reshape(heads)
     temper = jnp.repeat(jnp.exp(scale_here), head_dim)[None, :]
     wide = shape_of((pack_len, width), BF)
-    wide_f32 = shape_of((pack_len, width), F32)
-    weights_held = [
-        pltpu.VMEM((model, 3 * width), BF),
-        pltpu.SemaphoreType.DMA((3 * parts,)),
-    ]
-    queries, keys, values, query_pre, key_pre = call(
-        "qkv",
-        functools.partial(qkv_kernel, (group, segs, head_dim, parts)),
-        (me, temper, own_cols(q_bias).astype(F32), own_cols(v_bias).astype(F32), qkv_weight,
-         *attn_blocks),
-        (SMEM, VMEM, VMEM, VMEM, ANY) + (HBM,) * group,
-        (wide, wide, wide, wide_f32, wide_f32),
-        weights_held,
-    )
+    tall = shape_of((width, pack_len), F32)
     sorted_cotangent, _ = tie(sorted_cotangent, inputs)
     upstream = to_packs(sorted_cotangent)
     def near_blocks(own):
@@ -966,19 +1087,33 @@
         return [blocks[k] for k in range(len(blocks))]
 
     near = group // 2
-    out_blocks, out_t, lse = call(
+    held_bf = pltpu.VMEM((pack_len, width), BF)
+    out_blocks, out_t, lse, queries, queries_low, keys, values, inverses = call(
         "attend",
-        functools.partial(attend_kernel, (group, segs, head_dim, block)),
-        (first, last, low, high, queries, keys, values),
-        (SMEM, SMEM, VMEM, VMEM, HBM, HBM, HBM),
-        (shape_of((group, rows, width), BF), shape_of((width, pack_len), F32),
-         shape_of((8, pack_len), F32)),
+        functools.partial(attend_kernel, (group, segs, head_dim, parts, block)),
+        (me, first, last, low, high, temper, own_cols(q_bias).astype(F32),
+         own_cols(v_bias).astype(F32), qkv_weight, *attn_blocks),
+        (SMEM,) * 3 + (VMEM,) * 5 + (ANY,) * (1 + group),
+        (shape_of((group, rows, width), BF), tall, shape_of((8, pack_len), F32), wide, wide, wide,
+         wide, shape_of((pack_len, 128), F32)),
         [
+            pltpu.VMEM((model, 3 * width), BF),
+            pltpu.VMEM((group, rows, model), BF),
+            held_bf,
+            held_bf,
+            held_bf,
+            held_bf,
+            pltpu.VMEM((pack_len, 128), F32),
             pltpu.VMEM((width, pack_len), BF),
-            pltpu.VMEM((pack_len, width), BF),
+            pltpu.VMEM((width, pack_len), F32),
+            held_bf,
             pltpu.VMEM((width, block), F32),
             pltpu.VMEM((8, block), F32),
+            pltpu.SemaphoreType.DMA((3 * parts,)),
+            pltpu.SemaphoreType.DMA((group,)),
+            pltpu.SemaphoreType.DMA((6 + segs * group,)),
         ],
+        out_specs=(ANY, ANY, VMEM, ANY, ANY, ANY, ANY, ANY),
     )
     returned = over_group(out_blocks)
     upstream, _ = tie(upstream, out_blocks)
@@ -997,7 +1132,8 @@
         functools.partial(project_kernel, parts),
         (returned, proj_weight, proj_bias[None, :], inputs, mod, row_item),
         (HBM, HBM, VMEM, HBM, VMEM, VMEM),
-        (rows_bf, rows_f32, rows_f32, rows_bf),
+        (rows_bf, rows_bf, rows_f32, rows_bf),
+        [pltpu.VMEM((rows, model), F32)],
     )
 
     mlp_blocks = near_blocks(mlp_in)
@@ -1041,37 +1177,58 @@
     in_terms = in_terms[0] + [xor_swap(far_sum, "g", near)]
     acts[0], _ = tie(acts[0], far_sum)
     split = segs if tiled else 1
+
+    def to_last(blocks):
+        terms = {k: [block] for k, block in enumerate(blocks)}
+        for step in reversed(bits(group)[1:]):
+            for k in reversed([k for k in terms if k & step]):
+                terms[k ^ step].append(xor_swap(add_low(*terms.pop(k)), "g", step))
+        return terms[0], terms[near]
+
+    out_terms, out_last = to_last(tie(*out_parts, far_sum)[:group])
     if tiled:
         fine = half // group
-        tile_shape = (head_size, group, 2, fine, hidden)
-        feed_dims = (group, group, segs, 2)
+        tile_shape = (head_size, group, fine, hidden)
+        feed_dims = (group, group, segs, 2, len(out_last))
     else:
-        tile_shape = (1, 1, 2, model, units)
-        feed_dims = (group, 1, 1, 2)
-    tile_parts = call(
+        tile_shape = (1, 1, model, units)
+        feed_dims = (group, 1, 1, 2, len(out_last))
+    made = call(
         "feed_weights",
         functools.partial(feed_weights_kernel, feed_dims),
-        (me, *acts, *ghs, *mlp_blocks, *grad_blocks),
-        (SMEM,) + (HBM,) * (4 + 2 * group),
-        (shape_of(tile_shape, BF),) * split,
+        (me, *acts, *ghs, *mlp_blocks, *grad_blocks, *out_last),
+        (SMEM,) + (ANY,) * (4 + 2 * group + len(out_last)),
+        (shape_of(tile_shape, BF),) * (2 * split) + (rows_bf,),
         [
             pltpu.VMEM((model, pack_len), BF),
             pltpu.VMEM((model, pack_len), BF),
             pltpu.VMEM((pack_len, units), BF),
             pltpu.VMEM((pack_len, units), BF),
+            pltpu.VMEM((group, rows, model), BF),
+            pltpu.VMEM((group, rows, model), BF),
+            pltpu.VMEM((len(out_last), rows, model), BF),
+            pltpu.VMEM((rows, model), BF),
+            pltpu.VMEM((2, split, *tile_shape), BF),
+            pltpu.SemaphoreType.DMA((4 + 2 * group + len(out_last),)),
+            pltpu.SemaphoreType.DMA((2 * split + 1,)),
         ],
-    )
+        out_specs=(ANY,) * (2 * split + 1),
+    )
+    up_parts, down_parts, out_sent = made[:split], made[split : 2 * split], made[2 * split]
+    out_terms.append(xor_swap(out_sent, "g", near))
     if not tiled:
         fine = half // group
         order = jnp.array([turned(j, head_size) for j in range(head_size)]) ^ z
         near_g = jnp.arange(group) ^ g
         near_y = jnp.arange(segs) ^ yy
 
-        full = tile_parts[0].reshape(2, segs, group, fine, head_size, hidden)
-        full = full.transpose(1, 4, 2, 0, 3, 5)
-        tile_parts = list(full[near_y][:, order][:, :, near_g])
-
-    middle_in, _ = tie(middle, tile_parts[0])
+        def in_blocks(full):
+            full = full.reshape(segs, group, fine, head_size, hidden).transpose(0, 3, 1, 2, 4)
+            return list(full[near_y][:, order][:, :, near_g])
+
+        up_parts, down_parts = in_blocks(up_parts[0]), in_blocks(down_parts[0])
+
+    middle_in, _ = tie(middle, up_parts[0])
     outbound, grad_branch, grad_middle, middle_sums, branch_sum = call(
         "middle_back",
         functools.partial(middle_back_kernel, (parts, items, len(in_terms))),
@@ -1082,76 +1239,93 @@
         [pltpu.VMEM((rows, model), BF)],
     )
     inbound = over_group(outbound)
-    tile_terms = xor_scatter(tile_parts, "yy")
-    def to_last(blocks):
-        terms = {k: [block] for k, block in enumerate(blocks)}
-        for step in reversed(bits(group)[1:]):
-            for k in reversed([k for k in terms if k & step]):
-                terms[k ^ step].append(xor_swap(add_low(*terms.pop(k)), "g", step))
-        return terms[0], terms[near]
-
-    out_terms, out_last = to_last(tie(*out_parts, tile_parts[0])[:group])
+    up_terms, down_terms = xor_scatter(up_parts, "yy"), xor_scatter(down_parts, "yy")
     made = call(
         "proj_weights",
-        functools.partial(proj_weights_kernel, (group, parts == segs, len(out_last))),
-        (me, attn_rows, grad_branch, *out_last),
-        (SMEM,) + (HBM,) * (2 + len(out_last)),
-        (shape_of((parts, head_size, model // head_size, sub), BF),) * group + (rows_bf,),
+        functools.partial(proj_weights_kernel, (group, parts == segs)),
+        (me, attn_rows, grad_branch),
+        (SMEM, HBM, HBM),
+        (shape_of((parts, head_size, model // head_size, sub), BF),) * group,
         [pltpu.VMEM((model, rows), BF), pltpu.VMEM((rows, width), BF)],
     )
-    out_sent = made[group]
-    proj_terms, proj_last = to_last(made[:group])
-    inbound, out_sent = tie(inbound, out_sent)
-    out_terms.append(xor_swap(out_sent, "g", near))
-
-    def heads_back(index, given):
-        return call(
-            "attend_back",
-            functools.partial(attend_back_kernel, (group, segs, head_dim, block, index)),
-            (first, last, low, high, given, queries, keys, values, out_t, lse),
-            (SMEM, SMEM, VMEM, VMEM) + (HBM,) * 5 + (VMEM,),
-            (shape_of((pack_len, 128), BF),) * 3,
-            [
-                pltpu.VMEM((pack_len, 128), BF),
-                pltpu.VMEM((128, pack_len), BF),
-                pltpu.VMEM((pack_len, 128), F32),
-                pltpu.VMEM((pack_len, 128), F32),
-                pltpu.VMEM((128, block), F32),
-                pltpu.VMEM((8, block), F32),
-            ],
-        )
-
-    head_grads = list(heads_back(0, inbound))
-    tied = tie(*out_terms, *proj_last, head_grads[0])[:-1]
-    output_rows, output_sums, proj_sent = call(
+    proj_terms, proj_last = to_last(made)
+    tied = tuple(out_terms) + tuple(proj_last) + tuple(up_terms)
+    half_tiles = shape_of((head_size // 2, group, fine, hidden), BF)
+    quarter_tiles = shape_of((head_size // 4, group, fine, hidden), BF)
+    output_rows, output_sums, proj_sent, up_kept, up_sent = call(
         "output",
-        functools.partial(output_kernel, (items, len(out_terms), len(proj_last))),
+        functools.partial(
+            output_kernel, (items, len(out_terms), len(proj_last), len(up_terms))
+        ),
         (middle, upstream, mod, row_item, fc2_bias[None, :], *tied),
         (HBM, HBM, VMEM, VMEM, VMEM) + (HBM,) * len(tied),
-        (rows_bf, shape_of((8, model), F32), shape_of(proj_last[0].shape, BF)),
-    )
+        (rows_bf, shape_of((8, model), F32), shape_of(proj_last[0].shape, BF), half_tiles, half_tiles),
+    )
+    up_terms = (up_kept, xor_swap(up_sent, "head", 1))
+    inbound, output_rows = tie(inbound, output_rows)
     output_back = to_packs(output_rows)
-    inbound, output_rows = tie(inbound, output_rows)
     proj_terms.append(xor_swap(proj_sent, "g", near))
-    for index in range(1, width // 128):
-        head_grads += heads_back(index, inbound)
-    tied = tie(*head_grads, output_back, proj_terms[-1])
-    head_grads, output_back, proj_terms[-1] = tied[:-2], tied[-2], tied[-1]
-    half_tiles = shape_of((head_size // 2, group, 2, fine, hidden), BF)
-    quarter_tiles = shape_of((head_size // 4, group, 2, fine, hidden), BF)
+    pairs = width // 128
+    cols_bf, cols_f32 = pltpu.VMEM((pack_len, 128), BF), pltpu.VMEM((pack_len, 128), F32)
+    pair_held = [cols_bf] * 3 + [pltpu.VMEM((128, pack_len), F32), cols_bf]
+    pair_scratch = [pltpu.VMEM((128, pack_len), BF), cols_f32, cols_f32]
+    pair_scratch += [pltpu.VMEM((128, block), F32), pltpu.VMEM((8, block), F32)]
+    pair_sems = pltpu.SemaphoreType.DMA((4 + segs * group,))
+    given = inbound
+    earlier = []
+    for near_pair in range(pairs - 1):
+        earlier += call(
+            "attend_back",
+            functools.partial(attend_back_kernel, (group, segs, head_dim, block, near_pair)),
+            (first, last, low, high, lse, given, queries, keys, values, out_t),
+            (SMEM,) * 2 + (VMEM,) * 3 + (ANY,) * 5,
+            (shape_of((pack_len, 128), BF),) * 3,
+            pair_held + pair_scratch + [cols_bf] * 3 + [pair_sems, pltpu.SemaphoreType.DMA((3,))],
+            out_specs=(ANY,) * 3,
+        )
+        if near_pair == 0:
+            tied = tie(*down_terms, *up_terms, earlier[0])[:-1]
+            down_kept, down_sent, up_kept, up_sent = call(
+                "add",
+                functools.partial(add_kernel, (len(down_terms), 2)),
+                tied,
+                (HBM,) * len(tied),
+                (half_tiles, half_tiles, quarter_tiles, quarter_tiles),
+            )
+            down_terms = (down_kept, xor_swap(down_sent, "head", 1))
+            up_terms = (up_kept, xor_swap(up_sent, "head", 2))
+            given, _ = tie(given, up_sent)
     made = call(
-        "qkv_back",
+        "attend_back_end",
         functools.partial(
-            qkv_back_kernel, (group, segs, head_dim, parts, width // 128, len(tile_terms))
+            attend_back_end_kernel, (group, segs, head_dim, parts, block, pairs)
         ),
-        (*tile_terms, me, temper, qkv_weight, query_pre, key_pre, *head_grads),
-        (HBM,) * len(tile_terms) + (SMEM, VMEM, ANY) + (HBM,) * (2 + len(head_grads)),
-        (rows_bf,) * group
-        + (shape_of((pack_len, 3 * width), BF), shape_of((8, width), F32), half_tiles, half_tiles),
-        weights_held,
-    )
-    grad_qkv, qkv_sums, tiles_kept, tiles_sent = made[group:]
-    tile_terms = (tiles_kept, xor_swap(tiles_sent, "head", 1))
+        (me, temper, qkv_weight, inverses, queries_low, first, last, low, high, lse, given, queries,
+         keys, values, out_t, *earlier),
+        (SMEM, VMEM, ANY, ANY, ANY, SMEM, SMEM, VMEM, VMEM, VMEM) + (ANY,) * (5 + len(earlier)),
+        (rows_bf,) * group + (shape_of((pack_len, 3 * width), BF), shape_of((8, width), F32)),
+        pair_held
+        + pair_scratch
+        + [held_bf] * 3
+        + [
+            pltpu.VMEM((model, 3 * width), BF),
+            cols_f32,
+            held_bf,
+            held_bf,
+            held_bf,
+            pltpu.VMEM((pack_len, 3 * width), BF),
+            pltpu.VMEM((group, rows, model), BF),
+            pair_sems,
+            pltpu.SemaphoreType.DMA((3 * parts,)),
+            pltpu.SemaphoreType.DMA((4 + 3 * (pairs - 1),)),
+            pltpu.SemaphoreType.DMA((2 * group,)),
+        ],
+        out_specs=(ANY,) * (group + 1) + (VMEM,),
+    )
+    made, down_terms, up_terms, proj_terms, (output_back,) = tie_groups(
+        made, down_terms, up_terms, proj_terms, (output_back,)
+    )
+    grad_qkv, qkv_sums = made[group:]
 
     (vectors,) = call(
         "vector_parts",
@@ -1169,6 +1343,13 @@
         vectors = vectors + hidden_row.reshape(16, 4, 256).transpose(1, 0, 2).reshape(64, 256)
 
     in_terms, last_terms = to_last(made[:group])
+    if pairs == 1:
+        down_terms = halves_over_head(add_low(*down_terms))
+    down_kept, down_sent = call(
+        "add", functools.partial(add_kernel, (2,)), down_terms, (HBM,) * 2, (quarter_tiles,) * 2
+    )
+    down_terms = (down_kept, xor_swap(down_sent, "head", 2))
+    last_terms = tie(*last_terms, down_sent)[:-1]
     sent = add_low(*last_terms)
     in_terms.append(xor_swap(sent, "g", near))
     grad_qkv, _ = tie(grad_qkv, sent)
@@ -1182,53 +1363,21 @@
         (shape_of((head_size, 4, model // head_size, sub), BF),) * parts,
         [pltpu.VMEM((model, pack_len), BF), pltpu.VMEM((pack_len, 3 * sub), BF)],
     )
-    inputs_back, _ = tie(inputs, qkv_parts[0])
-    tokens_grad_rows, tokens_sums, tiles_kept, tiles_sent = call(
+    tied = tie(inputs, *down_terms, qkv_parts[0])
+    inputs_back, down_terms = tied[0], tied[1:3]
+    tokens_grad_rows, tokens_sums = call(
         "tokens_back",
-        functools.partial(tokens_back_kernel, (items, len(in_terms), 2)),
-        (inputs_back, grad_middle, mod, row_item, *in_terms, *tile_terms),
-        (HBM, HBM, VMEM, VMEM) + (HBM,) * (len(in_terms) + 2),
-        (rows_bf, shape_of((8, 2 * model), F32), quarter_tiles, quarter_tiles),
-    )
-    tile_terms = (tiles_kept, xor_swap(tiles_sent, "head", 2))
+        functools.partial(tokens_back_kernel, (items, len(in_terms))),
+        (inputs_back, grad_middle, mod, row_item, *in_terms),
+        (HBM, HBM, VMEM, VMEM) + (HBM,) * len(in_terms),
+        (rows_bf, shape_of((8, 2 * model), F32)),
+    )
 
     def to_data(values):
         return dot(to_slot, values, ((0,), (0,)))
 
     output = to_data(output_back).astype(BF)
     tokens_came = to_packs(tokens_grad_rows)
-    tokens_grad = to_data(tokens_came)
-
-    def over_head(terms):
-        while terms[0].shape[0] > 1:
-            terms = halves_over_head(add_low(*terms))
-        return terms
-
-    tile_terms = tie(*tile_terms, tokens_came)[:-1]
-    tied = over_head(tile_terms)
-    own_tiles = call(
-        "own_tiles",
-        functools.partial(own_tiles_kernel, len(tied)),
-        tied,
-        (HBM,) * len(tied),
-        (shape_of((2, fine, hidden), BF),) * group,
-    )
-    both_all = [own_tiles[0]]
-    for i in range(1, group):
-        both_all.append(lax.ppermute(own_tiles[i], "g", [(k, k ^ i) for k in range(group)]))
-    if tiled:
-        up_part, down_part = call(
-            "place",
-            functools.partial(place_kernel, group),
-            (me, *both_all),
-            (SMEM,) + (HBM,) * group,
-            (shape_of((fine, group * hidden), F32), shape_of((group * hidden, fine), F32)),
-        )
-    else:
-        placed = jnp.stack(both_all)[jnp.arange(group) ^ g].astype(F32)
-        up_part = placed[:, 0].transpose(1, 0, 2).reshape(fine, group * hidden)
-        down_part = placed[:, 1].transpose(0, 2, 1).reshape(group * hidden, fine)
-
 
     ada_cols = 6 * model // (dp_size * head_size)
     packs = segs * head_size
@@ -1258,7 +1407,57 @@
         )
         count = left
     kept = kept.reshape(packs // 2, 1, 8, 256)
+    tokens_sent = sent
+    def over_head(terms):
+        while terms[0].shape[0] > 1:
+            terms = halves_over_head(add_low(*terms))
+        return terms
+
+    down_terms = tie(*down_terms, *up_terms, tokens_grad_rows)[:-1]
+    down_terms, up_terms = down_terms[:2], down_terms[2:]
+    tied = tuple(over_head(up_terms)) + tuple(over_head(down_terms))
+    own_tiles = call(
+        "own_tiles",
+        own_tiles_kernel,
+        tied,
+        (HBM,) * 4,
+        (shape_of((2, fine, hidden), BF),) * group,
+    )
+    both_all = [own_tiles[0]]
+    for i in range(1, group):
+        both_all.append(lax.ppermute(own_tiles[i], "g", [(k, k ^ i) for k in range(group)]))
+    if parts == segs:
+        terms = tie(*xor_scatter(qkv_parts, "yy"), tokens_sent)[:-1]
+        terms = halves_over_head(add_low(*terms))
+        terms, both_all, (tokens_came,) = tie_groups(terms, both_all, (tokens_came,))
+        terms = over_head(terms)
+        summed = sum(term[0].astype(F32) for term in terms)
+        proj_part, qkv_part = summed[0], summed[1:]
+    else:
+        both = qkv_parts[0].transpose(1, 0, 2, 3).reshape(4, model, width)
+        full = lax.dynamic_update_slice(
+            jnp.zeros((4, model, model), BF), both, (0, 0, g * width)
+        )
+        summed = lax.psum_scatter(full, ("yy", "g"), scatter_dimension=2, tiled=True)
+        summed = lax.psum_scatter(summed, "head", scatter_dimension=1, tiled=True).astype(F32)
+        proj_part, qkv_part = summed[0], summed[1:]
+
+    if tiled:
+        up_part, down_part = call(
+            "place",
+            functools.partial(place_kernel, group),
+            (me, *both_all),
+            (SMEM,) + (HBM,) * group,
+            (shape_of((fine, group * hidden), F32), shape_of((group * hidden, fine), F32)),
+        )
+    else:
+        placed = jnp.stack(both_all)[jnp.arange(group) ^ g].astype(F32)
+        up_part = placed[:, 0].transpose(1, 0, 2).reshape(fine, group * hidden)
+        down_part = placed[:, 1].transpose(0, 2, 1).reshape(group * hidden, fine)
+
+
     sent, _ = tie(sent, tokens_came)
+    tokens_grad = to_data(tokens_came)
     steps = [("yy", step) for step in bits(segs)] + [("head", step) for step in bits(head_size)]
     for place, (axis, step) in enumerate(steps):
         came = xor_swap(sent, axis, step)
@@ -1288,20 +1487,6 @@
     )
     ada_bias_grad = ada_bias_grad[0]
 
-    if parts == segs:
-        terms = tie(*xor_scatter(qkv_parts, "yy"), tokens_came)[:-1]
-        terms = over_head(terms)
-        summed = sum(term[0].astype(F32) for term in terms)
-        proj_part, qkv_part = summed[0], summed[1:]
-    else:
-        both = qkv_parts[0].transpose(1, 0, 2, 3).reshape(4, model, width)
-        full = lax.dynamic_update_slice(
-            jnp.zeros((4, model, model), BF), both, (0, 0, g * width)
-        )
-        summed = lax.psum_scatter(full, ("yy", "g"), scatter_dimension=2, tiled=True)
-        summed = lax.psum_scatter(summed, "head", scatter_dimension=1, tiled=True).astype(F32)
-        proj_part, qkv_part = summed[0], summed[1:]
-
     log_scale_grad = jnp.sum(vectors[2].reshape(heads_all, head_dim), axis=1)
     fc1_bias_grad = pick(vectors, 8 + z, 0)[: group * hidden]
     return (

time: 435 us -> 416 us (0.956)
  local copies, waits for them, and re-layouts: 78.4 us -> 53.8 us
  Pallas kernels: 150 us -> 165 us
  waiting for transfers between devices: 103 us -> 88.2 us
    unnamed x212 -> x158, local copies, waits for them, and re-layouts: 69 us -> 41.6 us
    all_to_all x4, waiting for transfers between devices: 41.8 us -> 19.4 us  [to_packs(): lax.all_to_all(rows, ('yy', 'head'), split_axis=0, concat_axis=0, tiled=T...]
    pallas_call x28, Pallas kernels: 150 us -> 165 us  [call(): pl.pallas_call(body, name=name, out_shape=tuple(outs), in_specs=[ANY if s...]
    ppermute x32 -> x35, waiting for transfers between devices: 52.6 us -> 56.8 us  [xor_swap(): return lax.ppermute(values, axis, [(i, i ^ step) for i in range(size)])]
    ppermute x32 -> x35, starting transfers between devices: 25.6 us -> 27.6 us  [xor_swap(): return lax.ppermute(values, axis, [(i, i ^ step) for i in range(size)])]
  transfers between devices with their start and end apart: 44 -> 47, of which waited for: 18 -> 17; matrix products, arithmetic and copies ran while one was open for 7% -> 8% of each run, Pallas kernels for 29% -> 37%
where the time goes in v4:
time: 416 us; the launch traced here: 408 us
  Pallas kernels  165 us (40%)
  waiting for transfers between devices  88.2 us (21%)
  starting transfers between devices  61.3 us (15%)
  local copies, waits for them, and re-layouts  53.8 us (13%)
  between operations  15.5 us (4%)
  other arithmetic  12.2 us (3%)
  matrix products  11.8 us (3%)
    pallas_call x28, Pallas kernels, call(): pl.pallas_call(body, name=name, out_shape=tuple(outs), in_specs=[ANY if s...  165 us
    ppermute x35, waiting for transfers between devices, xor_swap(): return lax.ppermute(values, axis, [(i, i ^ step) for i in range(size)])  56.8 us
    unnamed x158, local copies, waits for them, and re-layouts  41.6 us
    ppermute x35, starting transfers between devices, xor_swap(): return lax.ppermute(values, axis, [(i, i ^ step) for i in range(size)])  27.6 us
    all_to_all x4, starting transfers between devices, to_packs(): lax.all_to_all(rows, ('yy', 'head'), split_axis=0, concat_axis=0, tiled=T...  22.3 us
    all_to_all x4, waiting for transfers between devices, to_packs(): lax.all_to_all(rows, ('yy', 'head'), split_axis=0, concat_axis=0, tiled=T...  19.4 us
    all_to_all x2, starting transfers between devices, over_group(): return lax.all_to_all(blocks, 'g', split_axis=0, concat_axis=0, tiled=True)  8.64 us
  transfers between devices with their start and end apart: 47, of which 17 were waited for; matrix products, arithmetic and copies ran while one was open for 8% of the time, Pallas kernels for 37%

profile of v4, /device:TPU:0, one launch (start us, length us, event | category | flops | bytes accessed | tf_op | source)
XLA Modules:
  0.0 408.1 jit_solution(3146313619546016813)
XLA Ops:
  16.2 7.3 %all-to-all-start = ((bf16[8,48,1024]{2,1,0:T(8,128)(2,1)}), bf16[8,48,1024]{2,1,0:T(8,128)(2,1)S(1)}, u32[]{:S(2)}, u32[]{:S(2)}) async-start(bf16[8,48,1024]{2,1,0:T(8,128)(2,1)} %bitcast.83), calls=%async_computation | async-start | bytes 1572864 | tf_op jit(solution)/shard_map/all_to_all | solution.py:868
  26.3 6.4 %convolution_add_fusion.refs_1_.refs_4_.refs_3_.refs_2_ = f32[4,6144]{1,0:T(4,128)S(1)} fusion(bf16[1024,6144]{1,0:T(8,128)(2,1)} %param.22, f32[6144]{0:T(1024)S(1)} %convert_element_type.89, f32[32,1024]{1,0:T(8,128)S(1)} %select_convert_fusion, s32[]{:T(128)S(6)} %select_n.97), kind=kOutput, calls=%fused_computation.4 | convolution fusion | flops 50376704 | bytes 12722180 | tf_op jit(solution)/shard_map/dot_general | solution.py:1069
  32.7 19.0 %all-to-all-done = bf16[8,48,1024]{2,1,0:T(8,128)(2,1)S(1)} async-done(((bf16[8,48,1024]{2,1,0:T(8,128)(2,1)}), bf16[8,48,1024]{2,1,0:T(8,128)(2,1)S(1)}, u32[]{:S(2)}, u32[]{:S(2)}) %all-to-all-start) | async-done | bytes 786464 | tf_op jit(solution)/shard_map/all_to_all | solution.py:868
  60.8 11.8 %collective-permute-done.2.refs_11_.refs_4_ = bf16[384,1024]{1,0:T(8,128)(2,1)} collective-permute-done((bf16[384,1024]{1,0:T(8,128)(2,1)S(1)}, bf16[384,1024]{1,0:T(8,128)(2,1)}, u32[]{:S(2)}, u32[]{:S(2)}) %collective-permute-start.2) | collective-permute-done | bytes 786464 | tf_op jit(solution)/shard_map/ppermute | solution.py:885
  76.3 3.8 all-to-all-start.2
  80.1 29.9 %attend.1 = (bf16[4,384,256]{2,1,0:T(8,128)(2,1)}, f32[256,1536]{1,0:T(8,128)}, f32[8,1536]{1,0:T(8,128)}, bf16[1536,256]{1,0:T(8,128)(2,1)}, bf16[1536,256]{1,0...) custom-call(s32[4]{0:T(128)} %pad_add_fusion.refs_0_, ...), custom_call_target="tpu_custom_call" | custom-call | flops 25999998976 | bytes 78000000 | tf_op jit(solution)/shard_map/attend/pallas_call | solution.py:67
  110.4 4.5 %all-to-all-start.1 = ((bf16[4,384,256]{2,1,0:T(8,128)(2,1)}), bf16[4,384,256]{2,1,0:T(8,128)(2,1)}, u32[]{:S(2)}, u32[]{:S(2)}) async-start(bf16[4,384,256]{2,1,0:T(8,128)(2,1)} %get-tuple-element.167), calls=%async_computation.1 | async-start | bytes 1572864 | tf_op jit(solution)/shard_map/all_to_all | solution.py:872
  119.1 8.0 %all-to-all-done.1.refs_0_ = bf16[4,384,256]{2,1,0:T(8,128)(2,1)} async-done(((bf16[4,384,256]{2,1,0:T(8,128)(2,1)}), bf16[4,384,256]{2,1,0:T(8,128)(2,1)}, u32[]{:S(2)}, u32[]{:S(2)}) %all-to-all-start.1) | async-done | bytes 786464 | tf_op jit(solution)/shard_map/all_to_all | solution.py:872
  128.7 5.6 %project.1 = (bf16[384,1024]{1,0:T(8,128)(2,1)S(1)}, bf16[384,1024]{1,0:T(8,128)(2,1)S(1)}, f32[384,1024]{1,0:T(8,128)S(1)}, bf16[384,1024]{1,0:T(8,128)(2,1)}) custom-call(bf16[4,384,256]{2,1,0:T(8,128)(2,1)} %all-to-all-done.1.refs_0_, bf16[1024,1024]{1,0:T(8,128)(2,1)S(1)} %copy-done.7, bf16[1,1024]{1,0:T(2,128)(2,1)S(1)} %broadcast_in_dim.138.refs_2_, ...), custom_call_target="tpu_custom_call" | custom-call | flops 5000000000 | bytes 15000000 | tf_op jit(solution)/shard_map/project/pallas_call | solution.py:67
  137.3 6.6 %collective-permute-done.8.refs_5_.refs_11_ = bf16[384,1024]{1,0:T(8,128)(2,1)} collective-permute-done((bf16[384,1024]{1,0:T(8,128)(2,1)}, bf16[384,1024]{1,0:T(8,128)(2,1)}, u32[]{:S(2)}, u32[]{:S(2)}) %collective-permute-start.8) | collective-permute-done | bytes 786464 | tf_op jit(solution)/shard_map/ppermute | solution.py:885
  144.7 4.3 %weights.1 = (bf16[1024,1024]{1,0:T(8,128)(2,1)}, bf16[1024,1024]{1,0:T(8,128)(2,1)}) custom-call(bf16[2,4,528,256]{3,2,1,0:T(8,128)(2,1)} %bitcast.101, bf16[2,4,256,512]{3,2,1,0:T(8,128)(2,1)} %bitcast.102), custom_call_target="tpu_custom_call" | custom-call | flops 4000000000 | bytes 12000000 | tf_op jit(solution)/shard_map/weights/pallas_call | solution.py:67
  149.9 13.3 %feed.2 = (bf16[384,1024]{1,0:T(8,128)(2,1)S(1)}, bf16[384,1024]{1,0:T(8,128)(2,1)S(1)}, bf16[384,1024]{1,0:T(8,128)(2,1)S(1)}, bf16[384,1024]{1,0:T(8,128)(2,1)...) custom-call(bf16[1024,1024]{1,0:T(8,128)(2,1)} %get-tuple-element.174.refs_0_, ...), custom_call_target="tpu_custom_call" | custom-call | flops 12000000000 | bytes 36000000 | tf_op jit(solution)/shard_map/feed/pallas_call | solution.py:67
  167.7 13.3 %feed.3 = (bf16[384,1024]{1,0:T(8,128)(2,1)S(1)}, bf16[384,1024]{1,0:T(8,128)(2,1)S(1)}, bf16[384,1024]{1,0:T(8,128)(2,1)S(1)}, bf16[384,1024]{1,0:T(8,128)(2,1)...) custom-call(bf16[1024,1024]{1,0:T(8,128)(2,1)} %get-tuple-element.174.refs_0_, ...), custom_call_target="tpu_custom_call" | custom-call | flops 12000000000 | bytes 36000000 | tf_op jit(solution)/shard_map/feed/pallas_call | solution.py:67
  187.8 13.2 %feed_weights.1 = (bf16[4,4,128,256]{3,2,1,0:T(8,128)(2,1)}, bf16[4,4,128,256]{3,2,1,0:T(8,128)(2,1)}, bf16[4,4,128,256]{3,2,1,0:T(8,128)(2,1)}, bf16[4,4,128,256]{3,2,1,0:T(8,128)(2,1)}, bf16[384,1024]{1,0:T(8,128)(2,1)}) custom-call(s32[4]{0:T(128)} %pad_add_fusion.refs_0_, bf16[768,1024]{1,0:T(8,128)(2,1)} %get-tuple-element.183.refs_1_, ...), custom_call_target="tpu_custom_call" | custom-call | flops 12000000000 | bytes 36000000 | tf_op jit(solution)/shard_map/feed_weights/pallas_call | solution.py:67
  210.1 6.7 %middle_back.1 = (bf16[4,384,256]{2,1,0:T(8,128)(2,1)S(1)}, bf16[384,1024]{1,0:T(8,128)(2,1)S(1)}, f32[384,1024]{1,0:T(8,128)S(1)}, f32[8,3072]{1,0:T(8,128)S(1)}, f32[8,1024]{1,0:T(8,128)S(1)}) custom-call(f32[384,1024]{1,0:T(8,128)S(1)} %copy-done.26, bf16[384,1024]{1,0:T(8,128)(2,1)S(1)} %copy-done.49, bf16[384,1024]{1,0:T(8,128)(2,1)S(1)} %bitcast.81, ...), custom_call_target="tpu_custom_call" | custom-call | flops 7000000000 | bytes 21000000 | tf_op jit(solution)/shard_map/middle_back/pallas_call | solution.py:67
  216.8 3.1 proj_weights.1
  222.4 4.2 %all-to-all-start.3 = ((bf16[4,384,256]{2,1,0:T(8,128)(2,1)}), bf16[4,384,256]{2,1,0:T(8,128)(2,1)}, u32[]{:S(2)}, u32[]{:S(2)}) async-start(bf16[4,384,256]{2,1,0:T(8,128)(2,1)} %copy-done.3), calls=%async_computation.3 | async-start | bytes 1572864 | tf_op jit(solution)/shard_map/all_to_all | solution.py:872
  226.6 2.6 collective-permute-start.18
  236.1 4.8 %output.1 = (bf16[384,1024]{1,0:T(8,128)(2,1)}, f32[8,1024]{1,0:T(8,128)S(1)}, bf16[2,4,256,128]{3,2,1,0:T(8,128)(2,1)S(1)}, bf16[2,4,128,256]{3,2,1,0:T(8,128)(2,1)S(1)}, bf16[2,4,128,256]{3,2,1,0:T(8,128)(2,1)S(1)}) custom-call(f32[384,1024]{1,0:T(8,128)S(1)} %copy-done.27, bf16[384,1024]{1,0:T(8,128)(2,1)S(1)} %bitcast.82, ...), custom_call_target="tpu_custom_call" | custom-call | flops 3000000000 | bytes 9000000 | tf_op jit(solution)/shard_map/output/pallas_call | solution.py:67
  246.6 4.4 %all-to-all-start.4 = ((bf16[8,48,1024]{2,1,0:T(8,128)(2,1)}), bf16[8,48,1024]{2,1,0:T(8,128)(2,1)}, u32[]{:S(2)}, u32[]{:S(2)}) async-start(bf16[8,48,1024]{2,1,0:T(8,128)(2,1)} %bitcast.20), calls=%async_computation.4 | async-start | bytes 1572864 | tf_op jit(solution)/shard_map/all_to_all | solution.py:868
  251.1 18.0 %attend_back.1 = (bf16[1536,128]{1,0:T(8,128)(2,1)}, bf16[1536,128]{1,0:T(8,128)(2,1)}, bf16[1536,128]{1,0:T(8,128)(2,1)}) custom-call(s32[6]{0:T(128)} %get-tuple-element.399.refs_1_.refs_0_.refs_5_, s32[6]{0:T(128)} %get-tuple-element.398.refs_2_.refs_1_.refs_6_, s32[1,1536]{1,0:T(1,128)} %broadcast_in_dim.132.refs_3_.refs_2_.refs_7_, ...), custom_call_target="tpu_custom_call" | custom-call | flops 16000000000 | bytes 48000000 | tf_op jit(solution)/shard_map/attend_back/pallas_call | solution.py:67
  277.9 25.0 %attend_back_end.1 = (bf16[384,1024]{1,0:T(8,128)(2,1)}, bf16[384,1024]{1,0:T(8,128)(2,1)}, bf16[384,1024]{1,0:T(8,128)(2,1)}, bf16[384,1024]{1,0:T(8,128)(2,1)}...) custom-call(s32[4]{0:T(128)} %pad_add_fusion.refs_0_, f32[1,256]{1,0:T(1,128)} %broadcast_in_dim_reshape.2.refs_5_.refs_1_, ...), custom_call_target="tpu_custom_call" | custom-call | flops 20999999488 | bytes 63000000 | tf_op jit(solution)/shard_map/attend_back_end/pallas_call | solution.py:67
  309.3 9.7 %qkv_weights.1 = (bf16[4,4,256,128]{3,2,1,0:T(8,128)(2,1)}, bf16[4,4,256,128]{3,2,1,0:T(8,128)(2,1)}) custom-call(s32[4]{0:T(128)} %pad_add_fusion.refs_0_, bf16[1536,768]{1,0:T(8,128)(2,1)} %get-tuple-element.250.refs_1_, bf16[384,1024]{1,0:T(8,128)(2,1)} %copy-done.11, bf16[384,1024]{1,0:T(8,128)(2,1)} %collective-permute-done.1.refs_10_.refs_3_, ...), custom_call_target="tpu_custom_call" | custom-call | flops 8000000000 | bytes 24000000 | tf_op jit(solution)/shard_map/qkv_weights/pallas_call | solution.py:67
  319.0 3.7 collective-permute-start.25
  323.4 5.1 %collective-permute-done.28.refs_6_ = bf16[384,1024]{1,0:T(8,128)(2,1)S(1)} collective-permute-done((bf16[384,1024]{1,0:T(8,128)(2,1)}, bf16[384,1024]{1,0:T(8,128)(2,1)S(1)}, u32[]{:S(2)}, u32[]{:S(2)}) %collective-permute-start.28) | collective-permute-done | bytes 786464 | tf_op jit(solution)/shard_map/ppermute | solution.py:885
  329.6 4.4 %tokens_back.1 = (bf16[384,1024]{1,0:T(8,128)(2,1)}, f32[8,2048]{1,0:T(8,128)S(1)}) custom-call(bf16[384,1024]{1,0:T(8,128)(2,1)S(1)} %bitcast.79, f32[384,1024]{1,0:T(8,128)S(1)} %copy-done.43, f32[4,6144]{1,0:T(4,128)S(1)} %convolution_add_fusion.refs_1_.refs_4_.refs_3_.refs_2_, s32[384,1]{1,0:T(8,128)S(1)} %broadcast_in_dim.143.refs_2_.refs_5_.refs_4_.refs_3_, ...), custom_call_target="tpu_custom_call" | custom-call | flops 5000000000 | bytes 15000000 | tf_op jit(solution)/shard_map/tokens_back/pallas_call | solution.py:67
  334.8 6.8 %all-to-all-start.5 = ((bf16[8,48,1024]{2,1,0:T(8,128)(2,1)}), bf16[8,48,1024]{2,1,0:T(8,128)(2,1)}, u32[]{:S(2)}, u32[]{:S(2)}) async-start(bf16[8,48,1024]{2,1,0:T(8,128)(2,1)} %bitcast.24), calls=%async_computation.5 | async-start | bytes 1572864 | tf_op jit(solution)/shard_map/all_to_all | solution.py:868
  342.5 4.8 %collective-permute-done.30.refs_1_ = f32[128,256]{1,0:T(8,128)S(1)} collective-permute-done((f32[128,256]{1,0:T(8,128)S(1)}, f32[128,256]{1,0:T(8,128)S(1)}, u32[]{:S(2)}, u32[]{:S(2)}) %collective-permute-start.30) | collective-permute-done | bytes 131104 | tf_op jit(solution)/shard_map/ppermute | solution.py:885
  361.8 9.6 %collective-permute-done.31 = bf16[2,4,256,128]{3,2,1,0:T(8,128)(2,1)} collective-permute-done((bf16[2,4,256,128]{3,2,1,0:T(8,128)(2,1)}, bf16[2,4,256,128]{3,2,1,0:T(8,128)(2,1)}, u32[]{:S(2)}, u32[]{:S(2)}) %collective-permute-start.31) | collective-permute-done | bytes 524320 | tf_op jit(solution)/shard_map/ppermute | solution.py:885
  377.1 2.9 fusion.22
  382.3 7.2 %collective-permute-done.36.refs_1_ = f32[96,256]{1,0:T(8,128)S(1)} collective-permute-done((f32[96,256]{1,0:T(8,128)S(1)}, f32[96,256]{1,0:T(8,128)S(1)}, u32[]{:S(2)}, u32[]{:S(2)}) %collective-permute-start.36) | collective-permute-done | bytes 98336 | tf_op jit(solution)/shard_map/ppermute | solution.py:885
  391.2 3.2 collective-permute-done.37.refs_1_
  (320 shorter events, 119.4 us)
Async XLA Ops:
  7.2 136.8 %all-gather.5.cloned.1.call-start = ((), (), s32[]{:S(2)}) async-start(), calls=%async_computation.6 | async-start | bytes 2433024 | tf_op jit(solution)/shard_map/all_gather | solution.py:1004
  16.2 35.5 %all-to-all-start = ((bf16[8,48,1024]{2,1,0:T(8,128)(2,1)}), bf16[8,48,1024]{2,1,0:T(8,128)(2,1)S(1)}, u32[]{:S(2)}, u32[]{:S(2)}) async-start(bf16[8,48,1024]{2,1,0:T(8,128)(2,1)} %bitcast.83), calls=%async_computation | async-start | bytes 1572864 | tf_op jit(solution)/shard_map/all_to_all | solution.py:868
  23.5 121.2 %all-gather.7.cloned.1.call-start = ((), (), s32[]{:S(2)}) async-start(), calls=%async_computation.7 | async-start | bytes 2359296 | tf_op jit(solution)/shard_map/all_gather | solution.py:1006
  53.4 19.2 %collective-permute-start.2 = (bf16[384,1024]{1,0:T(8,128)(2,1)S(1)}, bf16[384,1024]{1,0:T(8,128)(2,1)}, u32[]{:S(2)}, u32[]{:S(2)}) collective-permute-start(bf16[384,1024]{1,0:T(8,128)(2,1)S(1)} %first_norm.1.refs_9_.refs_2_), channel_id=1, source_target_pairs={{0,8},{4,12},{8,0},{12,4},{1,9},{5,13},{9,1},{13,5},{2,10},{6,14},... | collective-permute-start | bytes 2359304 | tf_op jit(solution)/shard_map/ppermute | solution.py:885
  54.9 17.6 %collective-permute-start = (s32[1536]{0:T(1024)S(1)}, s32[1536]{0:T(1024)S(1)}, u32[]{:S(2)}, u32[]{:S(2)}) collective-permute-start(s32[1536]{0:T(1024)S(1)} %reduce.3), channel_id=1, source_target_pairs={{0,0},{1,4},{2,8},{3,12},{4,1},{5,5},{6,9},{7,13},{8,2},{9,6},{10,... | collective-permute-start | bytes 18440 | tf_op jit(solution)/shard_map/ppermute | solution.py:1042
  60.2 19.9 %collective-permute-start.1 = (bf16[384,1024]{1,0:T(8,128)(2,1)S(1)}, bf16[384,1024]{1,0:T(8,128)(2,1)}, u32[]{:S(2)}, u32[]{:S(2)}) collective-permute-start(bf16[384,1024]{1,0:T(8,128)(2,1)S(1)} %first_norm.1.refs_9_.refs_2_), channel_id=1, source_target_pairs={{0,4},{4,0},{8,12},{12,8},{1,5},{5,1},{9,13},{13,9},{2,6},{6,2},{1... | collective-permute-start | bytes 2359304 | tf_op jit(solution)/shard_map/ppermute | solution.py:885
  76.3 34.1 %all-to-all-start.2 = ((bf16[8,48,1024]{2,1,0:T(8,128)(2,1)}), bf16[8,48,1024]{2,1,0:T(8,128)(2,1)S(1)}, u32[]{:S(2)}, u32[]{:S(2)}) async-start(bf16[8,48,1024]{2,1,0:T(8,128)(2,1)} %bitcast.14), calls=%async_computation.2 | async-start | bytes 1572864 | tf_op jit(solution)/shard_map/all_to_all | solution.py:868
  110.4 16.6 %all-to-all-start.1 = ((bf16[4,384,256]{2,1,0:T(8,128)(2,1)}), bf16[4,384,256]{2,1,0:T(8,128)(2,1)}, u32[]{:S(2)}, u32[]{:S(2)}) async-start(bf16[4,384,256]{2,1,0:T(8,128)(2,1)} %get-tuple-element.167), calls=%async_computation.1 | async-start | bytes 1572864 | tf_op jit(solution)/shard_map/all_to_all | solution.py:872
  116.8 32.2 %collective-permute-start.5 = (bf16[384,1024]{1,0:T(8,128)(2,1)}, bf16[384,1024]{1,0:T(8,128)(2,1)}, u32[]{:S(2)}, u32[]{:S(2)}) collective-permute-start(bf16[384,1024]{1,0:T(8,128)(2,1)} %get-tuple-element.177.refs_5_.refs_9_), channel_id=1, source_target_pairs={{0,4},{4,0},{8,12},{12,8},{1,5},{5,1},{9,13},{13,9},{2,6},{6,2},{1... | collective-permute-start | bytes 2359304 | tf_op jit(solution)/shard_map/ppermute | solution.py:885
  117.4 26.6 %collective-permute-start.8 = (bf16[384,1024]{1,0:T(8,128)(2,1)}, bf16[384,1024]{1,0:T(8,128)(2,1)}, u32[]{:S(2)}, u32[]{:S(2)}) collective-permute-start(bf16[384,1024]{1,0:T(8,128)(2,1)} %get-tuple-element.177.refs_5_.refs_9_), channel_id=1, source_target_pairs={{0,8},{4,12},{8,0},{12,4},{1,9},{5,13},{9,1},{13,5},{2,10},{6,14},... | collective-permute-start | bytes 2359304 | tf_op jit(solution)/shard_map/ppermute | solution.py:885
  137.2 27.0 %collective-permute-start.6 = (bf16[384,1024]{1,0:T(8,128)(2,1)}, bf16[384,1024]{1,0:T(8,128)(2,1)}, u32[]{:S(2)}, u32[]{:S(2)}) collective-permute-start(bf16[384,1024]{1,0:T(8,128)(2,1)} %get-tuple-element.176.refs_3_.refs_5_), channel_id=1, source_target_pairs={{0,8},{4,12},{8,0},{12,4},{1,9},{5,13},{9,1},{13,5},{2,10},{6,14},... | collective-permute-start | bytes 2359304 | tf_op jit(solution)/shard_map/ppermute | solution.py:885
  143.9 20.8 %collective-permute-start.9 = (bf16[384,1024]{1,0:T(8,128)(2,1)}, bf16[384,1024]{1,0:T(8,128)(2,1)}, u32[]{:S(2)}, u32[]{:S(2)}) collective-permute-start(bf16[384,1024]{1,0:T(8,128)(2,1)} %collective-permute-done.8.refs_5_.refs_11_), channel_id=1, source_target_pairs={{0,4},{4,0},{8,12},{12,8},{1,5},{5,1},{9,13},{13,9},{2,6},{6,2},{1... | collective-permute-start | bytes 2359304 | tf_op jit(solution)/shard_map/ppermute | solution.py:885
  185.0 20.2 %collective-permute-start.13 = (bf16[384,1024]{1,0:T(8,128)(2,1)}, bf16[384,1024]{1,0:T(8,128)(2,1)S(1)}, u32[]{:S(2)}, u32[]{:S(2)}) collective-permute-start(bf16[384,1024]{1,0:T(8,128)(2,1)} %add_convert_fusion.2), channel_id=1, source_target_pairs={{0,8},{4,12},{8,0},{12,4},{1,9},{5,13},{9,1},{13,5},{2,10},{6,14},... | collective-permute-start | bytes 2359304 | tf_op jit(solution)/shard_map/ppermute | solution.py:885
  185.1 19.2 %collective-permute-start.12 = (bf16[384,1024]{1,0:T(8,128)(2,1)S(1)}, bf16[384,1024]{1,0:T(8,128)(2,1)S(1)}, u32[]{:S(2)}, u32[]{:S(2)}) collective-permute-start(bf16[384,1024]{1,0:T(8,128)(2,1)S(1)} %get-tuple-element.199), channel_id=1, source_target_pairs={{0,4},{4,0},{8,12},{12,8},{1,5},{5,1},{9,13},{13,9},{2,6},{6,2},{1... | collective-permute-start | bytes 2359304 | tf_op jit(solution)/shard_map/ppermute | solution.py:885
  185.2 44.1 %collective-permute-start.14 = (bf16[384,1024]{1,0:T(8,128)(2,1)}, bf16[384,1024]{1,0:T(8,128)(2,1)}, u32[]{:S(2)}, u32[]{:S(2)}) collective-permute-start(bf16[384,1024]{1,0:T(8,128)(2,1)} %get-tuple-element.202), channel_id=1, source_target_pairs={{0,4},{4,0},{8,12},{12,8},{1,5},{5,1},{9,13},{13,9},{2,6},{6,2},{1... | collective-permute-start | bytes 2359304 | tf_op jit(solution)/shard_map/ppermute | solution.py:885
  201.1 29.2 %collective-permute-start.15 = (bf16[384,1024]{1,0:T(8,128)(2,1)}, bf16[384,1024]{1,0:T(8,128)(2,1)}, u32[]{:S(2)}, u32[]{:S(2)}) collective-permute-start(bf16[384,1024]{1,0:T(8,128)(2,1)} %get-tuple-element.203), channel_id=1, source_target_pairs={{0,8},{4,12},{8,0},{12,4},{1,9},{5,13},{9,1},{13,5},{2,10},{6,14},... | collective-permute-start | bytes 2359304 | tf_op jit(solution)/shard_map/ppermute | solution.py:885
  201.7 28.5 %collective-permute-start.17 = (bf16[4,4,128,256]{3,2,1,0:T(8,128)(2,1)}, bf16[4,4,128,256]{3,2,1,0:T(8,128)(2,1)}, u32[]{:S(2)}, u32[]{:S(2)}) collective-permute-start(bf16[4,4,128,256]{3,2,1,0:T(8,128)(2,1)} %get-tuple-element.208), channel_id=1, source_target_pairs={{0,16},{16,0},{1,17},{17,1},{2,18},{18,2},{3,19},{19,3},{4,20},{20... | collective-permute-start | bytes 3145736 | tf_op jit(solution)/shard_map/ppermute | solution.py:885
  222.4 21.0 %all-to-all-start.3 = ((bf16[4,384,256]{2,1,0:T(8,128)(2,1)}), bf16[4,384,256]{2,1,0:T(8,128)(2,1)}, u32[]{:S(2)}, u32[]{:S(2)}) async-start(bf16[4,384,256]{2,1,0:T(8,128)(2,1)} %copy-done.3), calls=%async_computation.3 | async-start | bytes 1572864 | tf_op jit(solution)/shard_map/all_to_all | solution.py:872
  226.6 42.5 %collective-permute-start.18 = (bf16[4,4,128,256]{3,2,1,0:T(8,128)(2,1)}, bf16[4,4,128,256]{3,2,1,0:T(8,128)(2,1)}, u32[]{:S(2)}, u32[]{:S(2)}) collective-permute-start(bf16[4,4,128,256]{3,2,1,0:T(8,128)(2,1)} %get-tuple-element.212), channel_id=1, source_target_pairs={{0,16},{16,0},{1,17},{17,1},{2,18},{18,2},{3,19},{19,3},{4,20},{20... | collective-permute-start | bytes 3145736 | tf_op jit(solution)/shard_map/ppermute | solution.py:885
  229.2 73.7 %collective-permute-start.22 = (bf16[2,4,256,128]{3,2,1,0:T(8,128)(2,1)}, bf16[2,4,256,128]{3,2,1,0:T(8,128)(2,1)}, u32[]{:S(2)}, u32[]{:S(2)}) collective-permute-start(bf16[2,4,256,128]{3,2,1,0:T(8,128)(2,1)} %copy-done.14), channel_id=1, source_target_pairs={{0,4},{4,0},{8,12},{12,8},{1,5},{5,1},{9,13},{13,9},{2,6},{6,2},{1... | collective-permute-start | bytes 1572872 | tf_op jit(solution)/shard_map/ppermute | solution.py:885
  243.4 25.7 %collective-permute-start.19 = (bf16[2,4,128,256]{3,2,1,0:T(8,128)(2,1)}, bf16[2,4,128,256]{3,2,1,0:T(8,128)(2,1)S(1)}, u32[]{:S(2)}, u32[]{:S(2)}) collective-permute-start(bf16[2,4,128,256]{3,2,1,0:T(8,128)(2,1)} %copy-done.20), channel_id=1, source_target_pairs={{0,1},{1,0},{2,3},{3,2},{4,5},{5,4},{6,7},{7,6},{8,9},{9,8},{10,11... | collective-permute-start | bytes 1572872 | tf_op jit(solution)/shard_map/ppermute | solution.py:885
  244.9 58.1 %collective-permute-start.23 = (bf16[2,4,256,128]{3,2,1,0:T(8,128)(2,1)}, bf16[2,4,256,128]{3,2,1,0:T(8,128)(2,1)S(1)}, u32[]{:S(2)}, u32[]{:S(2)}) collective-permute-start(bf16[2,4,256,128]{3,2,1,0:T(8,128)(2,1)} %copy-done.15), channel_id=1, source_target_pairs={{0,8},{4,12},{8,0},{12,4},{1,9},{5,13},{9,1},{13,5},{2,10},{6,14},... | collective-permute-start | bytes 1572872 | tf_op jit(solution)/shard_map/ppermute | solution.py:885
  246.6 57.2 %all-to-all-start.4 = ((bf16[8,48,1024]{2,1,0:T(8,128)(2,1)}), bf16[8,48,1024]{2,1,0:T(8,128)(2,1)}, u32[]{:S(2)}, u32[]{:S(2)}) async-start(bf16[8,48,1024]{2,1,0:T(8,128)(2,1)} %bitcast.20), calls=%async_computation.4 | async-start | bytes 1572864 | tf_op jit(solution)/shard_map/all_to_all | solution.py:868
  274.3 28.7 %collective-permute-start.21 = (bf16[1,4,128,256]{3,2,1,0:T(8,128)(2,1)S(1)}, bf16[1,4,128,256]{3,2,1,0:T(8,128)(2,1)S(1)}, u32[]{:S(2)}, u32[]{:S(2)}) collective-permute-start(bf16[1,4,128,256]{3,2,1,0:T(8,128)(2,1)S(1)} %get-tuple-element.224), channel_id=1, source_target_pairs={{0,2},{1,3},{2,0},{3,1},{4,6},{5,7},{6,4},{7,5},{8,10},{9,11},{10,... | collective-permute-start | bytes 786440 | tf_op jit(solution)/shard_map/ppermute | solution.py:885
  276.4 26.6 %collective-permute-start.20 = (bf16[2,4,128,256]{3,2,1,0:T(8,128)(2,1)S(1)}, bf16[2,4,128,256]{3,2,1,0:T(8,128)(2,1)S(1)}, u32[]{:S(2)}, u32[]{:S(2)}) collective-permute-start(bf16[2,4,128,256]{3,2,1,0:T(8,128)(2,1)S(1)} %get-tuple-element.235), channel_id=1, source_target_pairs={{0,1},{1,0},{2,3},{3,2},{4,5},{5,4},{6,7},{7,6},{8,9},{9,8},{10,11... | collective-permute-start | bytes 1572872 | tf_op jit(solution)/shard_map/ppermute | solution.py:885
  306.6 16.2 %collective-permute-start.26 = (bf16[1,4,128,256]{3,2,1,0:T(8,128)(2,1)S(1)}, bf16[1,4,128,256]{3,2,1,0:T(8,128)(2,1)S(1)}, u32[]{:S(2)}, u32[]{:S(2)}) collective-permute-start(bf16[1,4,128,256]{3,2,1,0:T(8,128)(2,1)S(1)} %get-tuple-element.247), channel_id=1, source_target_pairs={{0,2},{1,3},{2,0},{3,1},{4,6},{5,7},{6,4},{7,5},{8,10},{9,11},{10,... | collective-permute-start | bytes 786440 | tf_op jit(solution)/shard_map/ppermute | solution.py:885
  306.7 16.8 %collective-permute-start.27 = (bf16[384,1024]{1,0:T(8,128)(2,1)}, bf16[384,1024]{1,0:T(8,128)(2,1)S(1)}, u32[]{:S(2)}, u32[]{:S(2)}) collective-permute-start(bf16[384,1024]{1,0:T(8,128)(2,1)} %get-tuple-element.262), channel_id=1, source_target_pairs={{0,4},{4,0},{8,12},{12,8},{1,5},{5,1},{9,13},{13,9},{2,6},{6,2},{1... | collective-permute-start | bytes 2359304 | tf_op jit(solution)/shard_map/ppermute | solution.py:885
  308.4 20.1 %collective-permute-start.28 = (bf16[384,1024]{1,0:T(8,128)(2,1)}, bf16[384,1024]{1,0:T(8,128)(2,1)S(1)}, u32[]{:S(2)}, u32[]{:S(2)}) collective-permute-start(bf16[384,1024]{1,0:T(8,128)(2,1)} %add_convert_fusion.1), channel_id=1, source_target_pairs={{0,8},{4,12},{8,0},{12,4},{1,9},{5,13},{9,1},{13,5},{2,10},{6,14},... | collective-permute-start | bytes 2359304 | tf_op jit(solution)/shard_map/ppermute | solution.py:885
  319.0 29.6 %collective-permute-start.25 = (bf16[4,4,256,128]{3,2,1,0:T(8,128)(2,1)}, bf16[4,4,256,128]{3,2,1,0:T(8,128)(2,1)}, u32[]{:S(2)}, u32[]{:S(2)}) collective-permute-start(bf16[4,4,256,128]{3,2,1,0:T(8,128)(2,1)} %get-tuple-element.255), channel_id=1, source_target_pairs={{0,16},{16,0},{1,17},{17,1},{2,18},{18,2},{3,19},{19,3},{4,20},{20... | collective-permute-start | bytes 3145736 | tf_op jit(solution)/shard_map/ppermute | solution.py:885
  334.8 36.6 %all-to-all-start.5 = ((bf16[8,48,1024]{2,1,0:T(8,128)(2,1)}), bf16[8,48,1024]{2,1,0:T(8,128)(2,1)}, u32[]{:S(2)}, u32[]{:S(2)}) async-start(bf16[8,48,1024]{2,1,0:T(8,128)(2,1)} %bitcast.24), calls=%async_computation.5 | async-start | bytes 1572864 | tf_op jit(solution)/shard_map/all_to_all | solution.py:868
  351.5 19.9 %collective-permute-start.31 = (bf16[2,4,256,128]{3,2,1,0:T(8,128)(2,1)}, bf16[2,4,256,128]{3,2,1,0:T(8,128)(2,1)}, u32[]{:S(2)}, u32[]{:S(2)}) collective-permute-start(bf16[2,4,256,128]{3,2,1,0:T(8,128)(2,1)} %get-tuple-element.385), channel_id=1, source_target_pairs={{0,1},{1,0},{2,3},{3,2},{4,5},{5,4},{6,7},{7,6},{8,9},{9,8},{10,11... | collective-permute-start | bytes 1572872 | tf_op jit(solution)/shard_map/ppermute | solution.py:885
  374.0 15.6 %collective-permute-start.38 = (bf16[1,4,256,128]{3,2,1,0:T(8,128)(2,1)S(1)}, bf16[1,4,256,128]{3,2,1,0:T(8,128)(2,1)S(1)}, u32[]{:S(2)}, u32[]{:S(2)}) collective-permute-start(bf16[1,4,256,128]{3,2,1,0:T(8,128)(2,1)S(1)} %slice.86), channel_id=1, source_target_pairs={{0,2},{1,3},{2,0},{3,1},{4,6},{5,7},{6,4},{7,5},{8,10},{9,11},{10,... | collective-permute-start | bytes 786440 | tf_op jit(solution)/shard_map/ppermute | solution.py:885
  (89 other events, 447.2 us)
Sparse Core Ops, SparseCore 0:
  10.7 63.8 all-gather.4
  77.3 58.7 all-gather.6

commit v5 on v4

--- a/solution.py
+++ b/solution.py
@@ -14,11 +14,11 @@
 ANY = pl.BlockSpec(memory_space=pl.ANY)
 HBM = "hbm"
 LIMIT = 40
-LIMITS = {"attend": 57, "attend_back": 57, "attend_back_end": 57, "feed": 50, "feed_weights": 57, "weights": 57, "qkv_weights": 57}
+LIMITS = {"attend": 57, "attend_back": 57, "sort": 57, "middle_back": 50, "output": 50, "feed": 50, "feed_weights": 57, "weights": 57, "qkv_weights": 57}
 FLOPS, BYTES = 1_000_000_000, 3_000_000
 TIMES = {
     "sort": 2, "first_norm": 2, "grad_mlp": 2, "attend": 26, "project": 5, "weights": 4, "feed": 12,
-    "feed_weights": 12, "middle_back": 7, "proj_weights": 3, "output": 3, "attend_back": 16, "attend_back_end": 21, "add": 3,
+    "feed_weights": 12, "middle_back": 7, "proj_weights": 3, "output": 3, "attend_back": 34, "add": 3,
     "qkv_weights": 8, "tokens_back": 5,
 }
 PLAIN = ((1,), (0,))
@@ -179,6 +179,10 @@
     high = values.astype(BF)
     low = (values - high.astype(F32)).astype(BF)
     return dot(high, ones) + dot(low, ones)
+
+
+def own_lanes(values, mine):
+    return jnp.where(mine, values, jnp.zeros_like(values))
 
 
 def attend_kernel(dims, *refs):
@@ -246,14 +250,15 @@
             k_rows = at(k_block, block)
             index = k_block * block + lax.broadcasted_iota(jnp.int32, (block, block), 0)
             seen = (index >= low) & (index < high)
+            scores = []
+            for h in range(heads):
+                near = slice(h // pair * 128, (h // pair + 1) * 128)
+                scores.append(dot(own_lanes(k_ref[k_rows, near], lanes == h % pair), q_t[near, :]))
+            raised = [jnp.where(seen, jnp.exp(values), 0.0) for values in scores]
             for h in range(heads):
                 own = pl.ds(h * head_dim, head_dim)
-                near = slice(h // pair * 128, (h // pair + 1) * 128)
-                keys = k_ref[k_rows, near]
-                scores = dot(jnp.where(lanes == h % pair, keys, jnp.zeros_like(keys)), q_t[near, :])
-                raised = jnp.where(seen, jnp.exp(scores), 0.0)
-                total[h : h + 1, :] += jnp.sum(raised, axis=0, keepdims=True)
-                acc[own, :] += dot(v_t[own, k_rows], raised.astype(BF))
+                total[h : h + 1, :] += jnp.sum(raised[h], axis=0, keepdims=True)
+                acc[own, :] += dot(v_t[own, k_rows], raised[h].astype(BF))
 
         for h in range(heads):
             own = pl.ds(h * head_dim, head_dim)
@@ -271,14 +276,15 @@
         copy.wait()
 
 
-def attend_back_heads(dims, refs, scratch, outs):
-    head_dim, block, near = dims
+def attend_back_blocks(dims, refs, scratch, outs):
+    head_dim, block = dims
     first_ref, last_ref, lo_ref, hi_ref, lse_ref, q_ref, k_ref, v_ref, out_t_ref, g_s = refs
     k_t, dk_acc, dv_acc, acc, sums = scratch
     dq_ref, dk_ref, dv_ref = outs
-    pack_len = q_ref.shape[0]
-    pair = 128 // head_dim
+    pack_len, width = q_ref.shape
+    pair, heads = 128 // head_dim, width // head_dim
     lanes = lax.broadcasted_iota(jnp.int32, (1, 128), 1) // head_dim
+    cols = [slice(p * 128, (p + 1) * 128) for p in range(width // 128)]
     k_t[...] = k_ref[...].T
     dk_acc[...] = jnp.zeros_like(dk_acc)
     dv_acc[...] = jnp.zeros_like(dv_acc)
@@ -290,7 +296,7 @@
         q_t, g_t = queries.T, grads.T
         low, high = lo_ref[:, q_rows], hi_ref[:, q_rows]
         weighted = g_t.astype(F32) * out_t_ref[:, q_rows]
-        for h in range(pair):
+        for h in range(heads):
             sums[h : h + 1, :] = jnp.sum(
                 weighted[h * head_dim : (h + 1) * head_dim, :], axis=0, keepdims=True
             )
@@ -299,24 +305,28 @@
         @pl.loop(first_ref[q_block], last_ref[q_block])
         def _(k_block):
             k_rows = at(k_block, block)
-            keys, values = k_ref[k_rows, :], v_ref[k_rows, :]
             index = k_block * block + lax.broadcasted_iota(jnp.int32, (block, block), 0)
             seen = (index >= low) & (index < high)
-            for h in range(pair):
+            scores, grad_probs, probs, grad_scores = [], [], [], []
+            for h in range(heads):
+                near, mine = cols[h // pair], lanes == h % pair
+                scores.append(dot(own_lanes(k_ref[k_rows, near], mine), q_t[near, :]))
+                grad_probs.append(dot(own_lanes(v_ref[k_rows, near], mine), g_t[near, :]))
+            for h in range(heads):
+                made = jnp.where(seen, jnp.exp(scores[h] - lse_ref[h : h + 1, q_rows]), 0.0)
+                probs.append(made.astype(BF))
+                grad_scores.append((made * (grad_probs[h] - sums[h : h + 1, :])).astype(BF))
+            for h in range(heads):
                 own = pl.ds(h * head_dim, head_dim)
-                row = near * pair + h
-                mine = lanes == h
-                scores = dot(jnp.where(mine, keys, jnp.zeros_like(keys)), q_t)
-                probs = jnp.where(seen, jnp.exp(scores - lse_ref[row : row + 1, q_rows]), 0.0)
-                grad_probs = dot(jnp.where(mine, values, jnp.zeros_like(values)), g_t)
-                grad_scores = (probs * (grad_probs - sums[h : h + 1, :])).astype(BF)
-                acc[own, :] += dot(k_t[own, k_rows], grad_scores)
-                dk_acc[k_rows, :] += dot(
-                    grad_scores, jnp.where(mine, queries, jnp.zeros_like(queries))
-                )
-                dv_acc[k_rows, :] += dot(
-                    probs.astype(BF), jnp.where(mine, grads, jnp.zeros_like(grads))
-                )
+                acc[own, :] += dot(k_t[own, k_rows], grad_scores[h])
+            for p, near in enumerate(cols):
+                grad_k = grad_v = 0.0
+                for h in range(p * pair, (p + 1) * pair):
+                    mine = lanes == h % pair
+                    grad_k += dot(grad_scores[h], own_lanes(queries[:, near], mine))
+                    grad_v += dot(probs[h], own_lanes(grads[:, near], mine))
+                dk_acc[k_rows, near] += grad_k
+                dv_acc[k_rows, near] += grad_v
 
         dq_ref[q_rows, :] = acc[...].T.astype(BF)
 
@@ -324,70 +334,34 @@
     dv_ref[...] = dv_acc[...].astype(BF)
 
 
-def load_pair(dims, ins, held, sems):
-    group, segs, near = dims
-    in_ref, q_ref, k_ref, v_ref, out_t_ref = ins
-    q_s, k_s, v_s, out_s, g_s = held
-    cols = pl.ds(near * 128, 128)
-    seg = in_ref.shape[1] // segs
-    moves = [(q_ref.at[:, cols], q_s), (k_ref.at[:, cols], k_s), (v_ref.at[:, cols], v_s)]
-    moves.append((out_t_ref.at[cols, :], out_s))
-    for y in range(segs):
-        for g in range(group):
-            start = (y * group + g) * seg
-            moves.append((in_ref.at[g, pl.ds(y * seg, seg), cols], g_s.at[pl.ds(start, seg), :]))
-    copies = []
-    for place, (source, target) in enumerate(moves):
-        copies.append(pltpu.make_async_copy(source, target, sems.at[place]))
-        copies[-1].start()
-    return copies
-
-
 def attend_back_kernel(dims, *refs):
-    group, segs, head_dim, block, near = dims
-    ranges, lse_ref, ins, outs = refs[:4], refs[4], refs[5:10], refs[10:13]
-    held, scratch, made, sems, out_sems = refs[13:18], refs[18:23], refs[23:26], refs[26], refs[27]
-    for copy in load_pair((group, segs, near), ins, held, sems):
-        copy.wait()
-    attend_back_heads((head_dim, block, near), (*ranges, lse_ref, *held), scratch, made)
-    stores = [pltpu.make_async_copy(made[i], outs[i], out_sems.at[i]) for i in range(3)]
-    for copy in stores:
-        copy.start()
-    for copy in stores:
-        copy.wait()
-
-
-def attend_back_end_kernel(dims, *refs):
-    group, segs, head_dim, parts, block, pairs = dims
+    group, segs, head_dim, parts, block = dims
     me_ref, temper_ref, w_ref, inv_ref, ql_ref = refs[:5]
     ranges, lse_ref, ins = refs[5:9], refs[9], refs[10:15]
-    earlier, refs = refs[15 : 12 + 3 * pairs], refs[12 + 3 * pairs :]
-    sent, (dqkv_o, sums_ref), refs = refs[:group], refs[group : 2 + group], refs[2 + group :]
-    held, scratch, made, refs = refs[:5], refs[5:10], refs[10:13], refs[13:]
-    (w_s, inv_s, q_s, ql_s, k_s, dqkv_s, sent_s), (sems, w_sems, in_sems, out_sems) = refs[:7], refs[7:]
+    sent, (dqkv_o, sums_ref), refs = refs[15 : 15 + group], refs[15 + group : 17 + group], refs[17 + group :]
+    (q_s, k_s, v_s, out_s, g_s), scratch, made, refs = refs[:5], refs[5:10], refs[10:13], refs[13:]
+    (w_s, inv_s, ql_s, dqkv_s, sent_s), (sems, w_sems, out_sems) = refs[:5], refs[5:]
     pack_len, width = q_s.shape
     rows = sent_s.shape[1]
     seg, sub = rows // segs, width // parts
     heads = width // head_dim
     me = me_ref[0]
-    loads = load_pair((group, segs, pairs - 1), ins, held, sems)
-    last = pl.ds((pairs - 1) * 128, 128)
+    moves = [(ins[1], q_s), (ins[2], k_s), (ins[3], v_s), (ins[4], out_s)]
+    for y in range(segs):
+        for g in range(group):
+            to = pl.ds((y * group + g) * seg, seg)
+            moves.append((ins[0].at[g, pl.ds(y * seg, seg), :], g_s.at[to, :]))
+    moves += [(inv_ref, inv_s), (ql_ref, ql_s)]
+    loads = []
+    for place, (source, target) in enumerate(moves):
+        loads.append(pltpu.make_async_copy(source, target, sems.at[place]))
+        loads[-1].start()
     copies = load_columns(w_ref, w_s, w_sems, lambda p: (p * group + me) * sub, parts, sub)
-    moves = [(inv_ref, inv_s), (ins[1], q_s), (ql_ref, ql_s), (ins[2], k_s)]
-    for p in range(pairs - 1):
-        for which in range(3):
-            cols = pl.ds(p * 128, 128)
-            moves.append((earlier[3 * p + which], made[which].at[:, cols]))
-    for place, (source, target) in enumerate(moves):
-        copies.append(pltpu.make_async_copy(source, target, in_sems.at[place]))
-        copies[-1].start()
-    for load in loads:
+    copies += loads[-2:]
+    for load in loads[:-2]:
         load.wait()
-    attend_back_heads(
-        (head_dim, block, pairs - 1),
-        (*ranges, lse_ref, *held),
-        scratch,
-        tuple(ref.at[:, last] for ref in made),
+    attend_back_blocks(
+        (head_dim, block), (*ranges, lse_ref, q_s, k_s, v_s, out_s, g_s), scratch, made
     )
     same = same_head(width, head_dim)
     spread_q, spread_k = spread_heads(width, head_dim, 0), spread_heads(width, head_dim, heads)
@@ -624,8 +598,11 @@
 def middle_back_kernel(
     dims, middle_ref, branch_ref, up_ref, mod_ref, item_ref, wp_ref, *refs
 ):
-    parts, items, count = dims
-    terms, (out_ref, gb_ref, gm_ref, sums_ref, col_ref, attn) = refs[:count], refs[count:]
+    parts, items, count, chunk = dims
+    me_ref, attn_rows_ref = refs[0], refs[1]
+    terms, refs = refs[2 : 2 + count], refs[2 + count :]
+    out_ref, gb_ref, gm_ref, sums_ref, col_ref = refs[:5]
+    proj_refs, (attn, left_t, right) = refs[5:-3], refs[-3:]
     rows, model = middle_ref.shape
     group, _, width = out_ref.shape
     sub = width // parts
@@ -653,6 +630,9 @@
         for p in range(parts):
             start = (p * group + g) * sub
             out_ref[g, :, p * sub : (p + 1) * sub] = attn[:, start : start + sub]
+    proj_weights_kernel(
+        (group, chunk), me_ref, attn_rows_ref, gb_ref, *proj_refs, left_t, right
+    )
 
 
 def output_kernel(dims, middle_ref, up_ref, mod_ref, item_ref, bias_ref, *refs):
@@ -756,12 +736,15 @@
     )
     for part, (ref, start) in enumerate(parts):
         joined[:, part * model : (part + 1) * model] = ref[:, start * model : (start + 1) * model]
-    place = me_ref[1] * head_size + me_ref[2]
     for g in range(group):
         for y in range(segs):
             for z in range(head_size):
                 start = ((y * group + g) * head_size + z) * size
-                block = place ^ (y * head_size + z)
+                near = me_ref[2] ^ z
+                turn, count = jnp.int32(0), head_size
+                while count > 1:
+                    turn, near, count = turn * 2 + near % 2, near // 2, count // 2
+                block = (me_ref[1] ^ y) * head_size + turn
                 rows = pl.ds(pl.multiple_of(block * 8, 8), 8)
                 out_ref[me_ref[0] ^ g, rows, 0:size] = joined[:, start : start + size]
 
@@ -805,11 +788,9 @@
         refs[0][pl.ds(refs[0].shape[0] - 64, 64), :] = vectors
 
 
-def ada_kernel(me_ref, silu_ref, blocks_ref, grad_ref, bias_ref, held):
-    head_size = me_ref[3]
-    place = me_ref[1] * head_size + me_ref[2]
+def ada_kernel(segs, me_ref, silu_ref, blocks_ref, grad_ref, bias_ref, held):
     for c in range(blocks_ref.shape[0]):
-        sender = place ^ turned(c, blocks_ref.shape[0])
+        sender = (me_ref[1] ^ turned(c % segs, segs)) * me_ref[3] + (me_ref[2] ^ c // segs)
         held[pl.ds(pl.multiple_of(sender * 8, 8), 8), :] = blocks_ref[c]
     low = held[:, 0 : grad_ref.shape[1]].astype(BF)
     bias_ref[...] = jnp.broadcast_to(
@@ -1068,7 +1049,9 @@
     silu_here = lax.dynamic_slice_in_dim(silu_cond, pack * items, items, 0)
     mod = jnp.dot(silu_here, ada_weight, preferred_element_type=F32) + ada_bias.astype(F32)
 
-    (attn_in,) = call("first_norm",
+    inputs, first, last, low, high = tie(inputs, first, last, low, high)
+    (attn_in,) = call(
+        "first_norm",
         first_norm_kernel, (inputs, mod, row_item), (HBM, VMEM, VMEM), (shape_of((rows, model), BF),)
     )
     attn_blocks = xor_gather(attn_in, "g")
@@ -1138,7 +1121,7 @@
 
     mlp_blocks = near_blocks(mlp_in)
     mlp_far = xor_swap(mlp_in, "g", near)
-    grad_blocks += near_blocks(tie(grad_far, mlp_in)[0])
+    grad_blocks += near_blocks(tie(grad_far, mlp_in, fc1_here)[0])
     back_parts, out_parts, acts, ghs, hidden_sums = [], [], [], [], []
     for start in (0, near):
         if start:
@@ -1229,26 +1212,25 @@
         up_parts, down_parts = in_blocks(up_parts[0]), in_blocks(down_parts[0])
 
     middle_in, _ = tie(middle, up_parts[0])
-    outbound, grad_branch, grad_middle, middle_sums, branch_sum = call(
+    outbound, _, grad_middle, middle_sums, branch_sum, *proj_parts = call(
         "middle_back",
-        functools.partial(middle_back_kernel, (parts, items, len(in_terms))),
-        (middle_in, branch, upstream, mod, row_item, proj_weight, *in_terms),
-        (HBM, HBM, HBM, VMEM, VMEM, HBM) + (HBM,) * len(in_terms),
+        functools.partial(
+            middle_back_kernel, (parts, items, len(in_terms), parts == segs)
+        ),
+        (middle_in, branch, upstream, mod, row_item, proj_weight, me, attn_rows, *in_terms),
+        (HBM, HBM, HBM, VMEM, VMEM, HBM, SMEM) + (HBM,) * (1 + len(in_terms)),
         (shape_of((group, rows, width), BF), rows_bf, rows_f32, shape_of((8, 3 * model), F32),
-         shape_of((8, model), F32)),
-        [pltpu.VMEM((rows, model), BF)],
+         shape_of((8, model), F32))
+        + (shape_of((parts, head_size, model // head_size, sub), BF),) * group,
+        [
+            pltpu.VMEM((rows, model), BF),
+            pltpu.VMEM((model, rows), BF),
+            pltpu.VMEM((rows, width), BF),
+        ],
     )
     inbound = over_group(outbound)
     up_terms, down_terms = xor_scatter(up_parts, "yy"), xor_scatter(down_parts, "yy")
-    made = call(
-        "proj_weights",
-        functools.partial(proj_weights_kernel, (group, parts == segs)),
-        (me, attn_rows, grad_branch),
-        (SMEM, HBM, HBM),
-        (shape_of((parts, head_size, model // head_size, sub), BF),) * group,
-        [pltpu.VMEM((model, rows), BF), pltpu.VMEM((rows, width), BF)],
-    )
-    proj_terms, proj_last = to_last(made)
+    proj_terms, proj_last = to_last(proj_parts)
     tied = tuple(out_terms) + tuple(proj_last) + tuple(up_terms)
     half_tiles = shape_of((head_size // 2, group, fine, hidden), BF)
     quarter_tiles = shape_of((head_size // 4, group, fine, hidden), BF)
@@ -1265,59 +1247,36 @@
     inbound, output_rows = tie(inbound, output_rows)
     output_back = to_packs(output_rows)
     proj_terms.append(xor_swap(proj_sent, "g", near))
-    pairs = width // 128
-    cols_bf, cols_f32 = pltpu.VMEM((pack_len, 128), BF), pltpu.VMEM((pack_len, 128), F32)
-    pair_held = [cols_bf] * 3 + [pltpu.VMEM((128, pack_len), F32), cols_bf]
-    pair_scratch = [pltpu.VMEM((128, pack_len), BF), cols_f32, cols_f32]
-    pair_scratch += [pltpu.VMEM((128, block), F32), pltpu.VMEM((8, block), F32)]
-    pair_sems = pltpu.SemaphoreType.DMA((4 + segs * group,))
-    given = inbound
-    earlier = []
-    for near_pair in range(pairs - 1):
-        earlier += call(
-            "attend_back",
-            functools.partial(attend_back_kernel, (group, segs, head_dim, block, near_pair)),
-            (first, last, low, high, lse, given, queries, keys, values, out_t),
-            (SMEM,) * 2 + (VMEM,) * 3 + (ANY,) * 5,
-            (shape_of((pack_len, 128), BF),) * 3,
-            pair_held + pair_scratch + [cols_bf] * 3 + [pair_sems, pltpu.SemaphoreType.DMA((3,))],
-            out_specs=(ANY,) * 3,
-        )
-        if near_pair == 0:
-            tied = tie(*down_terms, *up_terms, earlier[0])[:-1]
-            down_kept, down_sent, up_kept, up_sent = call(
-                "add",
-                functools.partial(add_kernel, (len(down_terms), 2)),
-                tied,
-                (HBM,) * len(tied),
-                (half_tiles, half_tiles, quarter_tiles, quarter_tiles),
-            )
-            down_terms = (down_kept, xor_swap(down_sent, "head", 1))
-            up_terms = (up_kept, xor_swap(up_sent, "head", 2))
-            given, _ = tie(given, up_sent)
+    cols_f32 = pltpu.VMEM((pack_len, 128), F32)
+    held_f32 = pltpu.VMEM((pack_len, width), F32)
     made = call(
-        "attend_back_end",
-        functools.partial(
-            attend_back_end_kernel, (group, segs, head_dim, parts, block, pairs)
-        ),
-        (me, temper, qkv_weight, inverses, queries_low, first, last, low, high, lse, given, queries,
-         keys, values, out_t, *earlier),
-        (SMEM, VMEM, ANY, ANY, ANY, SMEM, SMEM, VMEM, VMEM, VMEM) + (ANY,) * (5 + len(earlier)),
+        "attend_back",
+        functools.partial(attend_back_kernel, (group, segs, head_dim, parts, block)),
+        (me, temper, qkv_weight, inverses, queries_low, first, last, low, high, lse, inbound, queries,
+         keys, values, out_t),
+        (SMEM, VMEM, ANY, ANY, ANY, SMEM, SMEM, VMEM, VMEM, VMEM) + (ANY,) * 5,
         (rows_bf,) * group + (shape_of((pack_len, 3 * width), BF), shape_of((8, width), F32)),
-        pair_held
-        + pair_scratch
-        + [held_bf] * 3
-        + [
+        [
+            held_bf,
+            held_bf,
+            held_bf,
+            pltpu.VMEM((width, pack_len), F32),
+            held_bf,
+            pltpu.VMEM((width, pack_len), BF),
+            held_f32,
+            held_f32,
+            pltpu.VMEM((width, block), F32),
+            pltpu.VMEM((8, block), F32),
+            held_bf,
+            held_bf,
+            held_bf,
             pltpu.VMEM((model, 3 * width), BF),
             cols_f32,
             held_bf,
-            held_bf,
-            held_bf,
             pltpu.VMEM((pack_len, 3 * width), BF),
             pltpu.VMEM((group, rows, model), BF),
-            pair_sems,
+            pltpu.SemaphoreType.DMA((6 + segs * group,)),
             pltpu.SemaphoreType.DMA((3 * parts,)),
-            pltpu.SemaphoreType.DMA((4 + 3 * (pairs - 1),)),
             pltpu.SemaphoreType.DMA((2 * group,)),
         ],
         out_specs=(ANY,) * (group + 1) + (VMEM,),
@@ -1343,16 +1302,19 @@
         vectors = vectors + hidden_row.reshape(16, 4, 256).transpose(1, 0, 2).reshape(64, 256)
 
     in_terms, last_terms = to_last(made[:group])
-    if pairs == 1:
-        down_terms = halves_over_head(add_low(*down_terms))
-    down_kept, down_sent = call(
-        "add", functools.partial(add_kernel, (2,)), down_terms, (HBM,) * 2, (quarter_tiles,) * 2
-    )
-    down_terms = (down_kept, xor_swap(down_sent, "head", 2))
-    last_terms = tie(*last_terms, down_sent)[:-1]
     sent = add_low(*last_terms)
     in_terms.append(xor_swap(sent, "g", near))
-    grad_qkv, _ = tie(grad_qkv, sent)
+    tied = tie(*down_terms, *up_terms, sent)[:-1]
+    down_kept, down_sent, up_kept, up_sent = call(
+        "add",
+        functools.partial(add_kernel, (len(down_terms), 2)),
+        tied,
+        (HBM,) * len(tied),
+        (half_tiles, half_tiles, quarter_tiles, quarter_tiles),
+    )
+    down_terms = (down_kept, xor_swap(down_sent, "head", 1))
+    up_terms = (up_kept, xor_swap(up_sent, "head", 2))
+    grad_qkv, _ = tie(grad_qkv, down_sent)
     qkv_parts = call(
         "qkv_weights",
         functools.partial(
@@ -1363,8 +1325,12 @@
         (shape_of((head_size, 4, model // head_size, sub), BF),) * parts,
         [pltpu.VMEM((model, pack_len), BF), pltpu.VMEM((pack_len, 3 * sub), BF)],
     )
-    tied = tie(inputs, *down_terms, qkv_parts[0])
-    inputs_back, down_terms = tied[0], tied[1:3]
+    down_terms, up_terms, _ = tie_groups(down_terms, up_terms, qkv_parts)
+    down_kept, down_sent = call(
+        "add", functools.partial(add_kernel, (2,)), down_terms, (HBM,) * 2, (quarter_tiles,) * 2
+    )
+    down_terms = (down_kept, xor_swap(down_sent, "head", 2))
+    inputs_back, _ = tie(inputs, down_sent)
     tokens_grad_rows, tokens_sums = call(
         "tokens_back",
         functools.partial(tokens_back_kernel, (items, len(in_terms))),
@@ -1372,6 +1338,8 @@
         (HBM, HBM, VMEM, VMEM) + (HBM,) * len(in_terms),
         (rows_bf, shape_of((8, 2 * model), F32)),
     )
+
+    tokens_grad_rows, *down_terms = tie(tokens_grad_rows, *down_terms)
 
     def to_data(values):
         return dot(to_slot, values, ((0,), (0,)))
@@ -1458,7 +1426,7 @@
 
     sent, _ = tie(sent, tokens_came)
     tokens_grad = to_data(tokens_came)
-    steps = [("yy", step) for step in bits(segs)] + [("head", step) for step in bits(head_size)]
+    steps = [("yy", step) for step in bits(segs)] + [("head", step) for step in reversed(bits(head_size))]
     for place, (axis, step) in enumerate(steps):
         came = xor_swap(sent, axis, step)
         blocks, senders = kept.shape[0], kept.shape[1]
@@ -1479,7 +1447,7 @@
     silu_rows = jnp.pad(silu_cond.reshape(packs, items, model), ((0, 0), (0, 8 - items), (0, 0)))
     ada_grad, ada_bias_grad = call(
         "ada",
-        ada_kernel,
+        functools.partial(ada_kernel, segs),
         (me, silu_rows.reshape(packs * 8, model), item_came),
         (SMEM, VMEM, VMEM),
         (shape_of((model, ada_cols), F32), shape_of((8, ada_cols), F32)),

time: 416 us -> 376 us (0.904)
  local copies, waits for them, and re-layouts: 53.8 us -> 30.9 us
  Pallas kernels: 165 us -> 144 us
  starting transfers between devices: 61.3 us -> 66.3 us
    unnamed x158 -> x108, local copies, waits for them, and re-layouts: 41.6 us -> 18.1 us
    pallas_call x28 -> x26, Pallas kernels: 165 us -> 144 us  [call(): pl.pallas_call(body, name=name, out_shape=tuple(outs), in_specs=[ANY if s...]
  transfers between devices with their start and end apart: 47 -> 47, of which waited for: 17 -> 23; matrix products, arithmetic and copies ran while one was open for 8% -> 9% of each run, Pallas kernels for 37% -> 34%
where the time goes in v5:
time: 376 us; the launch traced here: 370 us
  Pallas kernels  144 us (38%)
  waiting for transfers between devices  90.1 us (24%)
  starting transfers between devices  66.3 us (18%)
  local copies, waits for them, and re-layouts  30.9 us (8%)
  between operations  15.2 us (4%)
  matrix products  11.8 us (3%)
  other arithmetic  11.3 us (3%)
    pallas_call x26, Pallas kernels, call(): pl.pallas_call(body, name=name, out_shape=tuple(outs), in_specs=[ANY if s...  144 us
    ppermute x35, waiting for transfers between devices, xor_swap(): return lax.ppermute(values, axis, [(i, i ^ step) for i in range(size)])  54.1 us
    ppermute x35, starting transfers between devices, xor_swap(): return lax.ppermute(values, axis, [(i, i ^ step) for i in range(size)])  30 us
    all_to_all x4, starting transfers between devices, to_packs(): lax.all_to_all(rows, ('yy', 'head'), split_axis=0, concat_axis=0, tiled=T...  25.7 us
    all_to_all x4, waiting for transfers between devices, to_packs(): lax.all_to_all(rows, ('yy', 'head'), split_axis=0, concat_axis=0, tiled=T...  20.4 us
    unnamed x108, local copies, waits for them, and re-layouts  18.1 us
    all_to_all x2, waiting for transfers between devices, over_group(): return lax.all_to_all(blocks, 'g', split_axis=0, concat_axis=0, tiled=True)  9.33 us
    all_to_all x2, starting transfers between devices, over_group(): return lax.all_to_all(blocks, 'g', split_axis=0, concat_axis=0, tiled=True)  7.88 us
  transfers between devices with their start and end apart: 47, of which 23 were waited for; matrix products, arithmetic and copies ran while one was open for 9% of the time, Pallas kernels for 34%

profile of v5, /device:TPU:0, one launch (start us, length us, event | category | flops | bytes accessed | tf_op | source)
XLA Modules:
  0.0 369.8 jit_solution(4652143231679021949)
XLA Ops:
  8.6 4.4 %sort.1 = (bf16[384,384]{1,0:T(8,128)(2,1)}, bf16[384,1024]{1,0:T(8,128)(2,1)}, bf16[384,1024]{1,0:T(8,128)(2,1)}) custom-call(s32[1,384]{1,0:T(1,128)} %broadcast_in_dim.123.refs_0_, bf16[384,1024]{1,0:T(8,128)(2,1)} %refs_1_.2, bf16[384,1024]{1,0:T(8,128)(2,1)} %refs_2_.2), custom_call_target="tpu_custom_call" | custom-call | flops 2000000000 | bytes 6000000 | tf_op jit(solution)/shard_map/sort/pallas_call | solution.py:67
  13.0 7.4 %all-to-all-start = ((bf16[8,48,1024]{2,1,0:T(8,128)(2,1)}), bf16[8,48,1024]{2,1,0:T(8,128)(2,1)S(1)}, u32[]{:S(2)}, u32[]{:S(2)}) async-start(bf16[8,48,1024]{2,1,0:T(8,128)(2,1)} %bitcast.87), calls=%async_computation | async-start | bytes 1572864 | tf_op jit(solution)/shard_map/all_to_all | solution.py:849
  25.6 6.3 %convolution_add_fusion.refs_1_.refs_4_.refs_3_.refs_2_ = f32[4,6144]{1,0:T(4,128)S(1)} fusion(bf16[1024,6144]{1,0:T(8,128)(2,1)} %param.22, f32[6144]{0:T(1024)S(1)} %convert_element_type.89, f32[32,1024]{1,0:T(8,128)S(1)} %select_convert_fusion, s32[]{:T(128)S(6)} %select_n.97), kind=kOutput, calls=%fused_computation.4 | convolution fusion | flops 50376704 | bytes 12722180 | tf_op jit(solution)/shard_map/dot_general | solution.py:1050
  36.8 11.8 %all-to-all-done = bf16[8,48,1024]{2,1,0:T(8,128)(2,1)S(1)} async-done(((bf16[8,48,1024]{2,1,0:T(8,128)(2,1)}), bf16[8,48,1024]{2,1,0:T(8,128)(2,1)S(1)}, u32[]{:S(2)}, u32[]{:S(2)}) %all-to-all-start) | async-done | bytes 786464 | tf_op jit(solution)/shard_map/all_to_all | solution.py:849
  50.2 5.5 %collective-permute-start.2 = (bf16[384,1024]{1,0:T(8,128)(2,1)S(1)}, bf16[384,1024]{1,0:T(8,128)(2,1)}, u32[]{:S(2)}, u32[]{:S(2)}) collective-permute-start(bf16[384,1024]{1,0:T(8,128)(2,1)S(1)} %first_norm.1.refs_9_.refs_2_), channel_id=1, source_target_pairs={{0,8},{4,12},{8,0},{12,4},{1,9},{5,13},{9,1},{13,5},{2,10},{6,14},... | collective-permute-start | bytes 2359304 | tf_op jit(solution)/shard_map/ppermute | solution.py:866
  55.7 10.1 %collective-permute-done.2.refs_11_.refs_4_ = bf16[384,1024]{1,0:T(8,128)(2,1)} collective-permute-done((bf16[384,1024]{1,0:T(8,128)(2,1)S(1)}, bf16[384,1024]{1,0:T(8,128)(2,1)}, u32[]{:S(2)}, u32[]{:S(2)}) %collective-permute-start.2) | collective-permute-done | bytes 786464 | tf_op jit(solution)/shard_map/ppermute | solution.py:866
  69.5 9.1 %all-to-all-start.2 = ((bf16[8,48,1024]{2,1,0:T(8,128)(2,1)}), bf16[8,48,1024]{2,1,0:T(8,128)(2,1)S(1)}, u32[]{:S(2)}, u32[]{:S(2)}) async-start(bf16[8,48,1024]{2,1,0:T(8,128)(2,1)} %bitcast.86), calls=%async_computation.2 | async-start | bytes 1572864 | tf_op jit(solution)/shard_map/all_to_all | solution.py:849
  78.7 21.0 %attend.1 = (bf16[4,384,256]{2,1,0:T(8,128)(2,1)}, f32[256,1536]{1,0:T(8,128)}, f32[8,1536]{1,0:T(8,128)}, bf16[1536,256]{1,0:T(8,128)(2,1)}, bf16[1536,256]{1,0...) custom-call(s32[4]{0:T(128)} %pad_add_fusion.refs_0_.refs_6_, ...), custom_call_target="tpu_custom_call" | custom-call | flops 25999998976 | bytes 78000000 | tf_op jit(solution)/shard_map/attend/pallas_call | solution.py:67
  99.7 8.6 %all-to-all-done.2 = bf16[8,48,1024]{2,1,0:T(8,128)(2,1)S(1)} async-done(((bf16[8,48,1024]{2,1,0:T(8,128)(2,1)}), bf16[8,48,1024]{2,1,0:T(8,128)(2,1)S(1)}, u32[]{:S(2)}, u32[]{:S(2)}) %all-to-all-start.2) | async-done | bytes 786464 | tf_op jit(solution)/shard_map/all_to_all | solution.py:849
  108.3 3.7 all-to-all-start.1
  116.0 8.0 %all-to-all-done.1.refs_0_ = bf16[4,384,256]{2,1,0:T(8,128)(2,1)S(1)} async-done(((bf16[4,384,256]{2,1,0:T(8,128)(2,1)}), bf16[4,384,256]{2,1,0:T(8,128)(2,1)S(1)}, u32[]{:S(2)}, u32[]{:S(2)}) %all-to-all-start.1) | async-done | bytes 786464 | tf_op jit(solution)/shard_map/all_to_all | solution.py:853
  125.7 3.9 %project.1 = (bf16[384,1024]{1,0:T(8,128)(2,1)S(1)}, bf16[384,1024]{1,0:T(8,128)(2,1)S(1)}, f32[384,1024]{1,0:T(8,128)S(1)}, bf16[384,1024]{1,0:T(8,128)(2,1)S(1)}) custom-call(bf16[4,384,256]{2,1,0:T(8,128)(2,1)S(1)} %all-to-all-done.1.refs_0_, bf16[1024,1024]{1,0:T(8,128)(2,1)S(1)} %copy-done.6, bf16[1,1024]{1,0:T(2,128)(2,1)S(1)} %broadcast_in_dim.138.refs_2_, ...), custom_call_target="tpu_custom_call" | custom-call | flops 5000000000 | bytes 15000000 | tf_op jit(solution)/shard_map/project/pallas_call | solution.py:67
  135.8 4.3 %weights.1 = (bf16[1024,1024]{1,0:T(8,128)(2,1)}, bf16[1024,1024]{1,0:T(8,128)(2,1)}) custom-call(bf16[2,4,528,256]{3,2,1,0:T(8,128)(2,1)} %bitcast.102, bf16[2,4,256,512]{3,2,1,0:T(8,128)(2,1)} %bitcast.103), custom_call_target="tpu_custom_call" | custom-call | flops 4000000000 | bytes 12000000 | tf_op jit(solution)/shard_map/weights/pallas_call | solution.py:67
  141.0 12.7 %feed.2 = (bf16[384,1024]{1,0:T(8,128)(2,1)S(1)}, bf16[384,1024]{1,0:T(8,128)(2,1)S(1)}, bf16[384,1024]{1,0:T(8,128)(2,1)S(1)}, bf16[384,1024]{1,0:T(8,128)(2,1)...) custom-call(bf16[1024,1024]{1,0:T(8,128)(2,1)} %get-tuple-element.182.refs_0_, ...), custom_call_target="tpu_custom_call" | custom-call | flops 12000000000 | bytes 36000000 | tf_op jit(solution)/shard_map/feed/pallas_call | solution.py:67
  160.5 13.6 %feed.3 = (bf16[384,1024]{1,0:T(8,128)(2,1)S(1)}, bf16[384,1024]{1,0:T(8,128)(2,1)S(1)}, bf16[384,1024]{1,0:T(8,128)(2,1)S(1)}, bf16[384,1024]{1,0:T(8,128)(2,1)...) custom-call(bf16[1024,1024]{1,0:T(8,128)(2,1)} %get-tuple-element.182.refs_0_, ...), custom_call_target="tpu_custom_call" | custom-call | flops 12000000000 | bytes 36000000 | tf_op jit(solution)/shard_map/feed/pallas_call | solution.py:67
  180.0 13.2 %feed_weights.1 = (bf16[4,4,128,256]{3,2,1,0:T(8,128)(2,1)}, bf16[4,4,128,256]{3,2,1,0:T(8,128)(2,1)}, bf16[4,4,128,256]{3,2,1,0:T(8,128)(2,1)}, bf16[4,4,128,256]{3,2,1,0:T(8,128)(2,1)}, bf16[384,1024]{1,0:T(8,128)(2,1)}) custom-call(s32[4]{0:T(128)} %pad_add_fusion.refs_0_.refs_6_, bf16[768,1024]{1,0:T(8,128)(2,1)} %get-tuple-element.191.refs_1_, ...), custom_call_target="tpu_custom_call" | custom-call | flops 12000000000 | bytes 36000000 | tf_op jit(solution)/shard_map/feed_weights/pallas_call | solution.py:67
  194.3 3.0 collective-permute-done.13.refs_10_
  198.2 12.5 %middle_back.1 = (bf16[4,384,256]{2,1,0:T(8,128)(2,1)}, bf16[384,1024]{1,0:T(8,128)(2,1)}, f32[384,1024]{1,0:T(8,128)}, f32[8,3072]{1,0:T(8,128)S(1)}, f32[8,102...) custom-call(f32[384,1024]{1,0:T(8,128)} %copy-done.10, ...), custom_call_target="tpu_custom_call" | custom-call | flops 7000000000 | bytes 21000000 | tf_op jit(solution)/shard_map/middle_back/pallas_call | solution.py:67
  212.3 4.2 %all-to-all-start.3 = ((bf16[4,384,256]{2,1,0:T(8,128)(2,1)}), bf16[4,384,256]{2,1,0:T(8,128)(2,1)}, u32[]{:S(2)}, u32[]{:S(2)}) async-start(bf16[4,384,256]{2,1,0:T(8,128)(2,1)} %get-tuple-element.209), calls=%async_computation.3 | async-start | bytes 1572864 | tf_op jit(solution)/shard_map/all_to_all | solution.py:853
  219.9 6.2 %output.1 = (bf16[384,1024]{1,0:T(8,128)(2,1)}, f32[8,1024]{1,0:T(8,128)S(1)}, bf16[2,4,256,128]{3,2,1,0:T(8,128)(2,1)}, bf16[2,4,128,256]{3,2,1,0:T(8,128)(2,1)S(1)}, bf16[2,4,128,256]{3,2,1,0:T(8,128)(2,1)}) custom-call(f32[384,1024]{1,0:T(8,128)} %copy-done.10, bf16[384,1024]{1,0:T(8,128)(2,1)} %bitcast.82, ...), custom_call_target="tpu_custom_call" | custom-call | flops 3000000000 | bytes 9000000 | tf_op jit(solution)/shard_map/output/pallas_call | solution.py:67
  228.6 4.4 %all-to-all-start.4 = ((bf16[8,48,1024]{2,1,0:T(8,128)(2,1)}), bf16[8,48,1024]{2,1,0:T(8,128)(2,1)}, u32[]{:S(2)}, u32[]{:S(2)}) async-start(bf16[8,48,1024]{2,1,0:T(8,128)(2,1)} %bitcast.20), calls=%async_computation.4 | async-start | bytes 1572864 | tf_op jit(solution)/shard_map/all_to_all | solution.py:849
  233.0 27.3 %attend_back.1 = (bf16[384,1024]{1,0:T(8,128)(2,1)}, bf16[384,1024]{1,0:T(8,128)(2,1)}, bf16[384,1024]{1,0:T(8,128)(2,1)}, bf16[384,1024]{1,0:T(8,128)(2,1)}, bf...) custom-call(s32[4]{0:T(128)} %pad_add_fusion.refs_0_.refs_6_, f32[1,256]{1,0:T(1,128)} %broadcast_in_dim_reshape.2.refs_5_.refs_1_, ...), custom_call_target="tpu_custom_call" | custom-call | flops 33999998976 | bytes 102000000 | tf_op jit(solution)/shard_map/attend_back/pallas_call | solution.py:67
  271.1 4.2 %collective-permute-start.25 = (bf16[1,4,128,256]{3,2,1,0:T(8,128)(2,1)S(1)}, bf16[1,4,128,256]{3,2,1,0:T(8,128)(2,1)S(1)}, u32[]{:S(2)}, u32[]{:S(2)}) collective-permute-start(bf16[1,4,128,256]{3,2,1,0:T(8,128)(2,1)S(1)} %get-tuple-element.259), channel_id=1, source_target_pairs={{0,2},{1,3},{2,0},{3,1},{4,6},{5,7},{6,4},{7,5},{8,10},{9,11},{10,... | collective-permute-start | bytes 786440 | tf_op jit(solution)/shard_map/ppermute | solution.py:866
  275.3 9.6 %qkv_weights.1 = (bf16[4,4,256,128]{3,2,1,0:T(8,128)(2,1)}, bf16[4,4,256,128]{3,2,1,0:T(8,128)(2,1)}) custom-call(s32[4]{0:T(128)} %pad_add_fusion.refs_0_.refs_6_, bf16[1536,768]{1,0:T(8,128)(2,1)} %get-tuple-element.249.refs_1_, bf16[384,1024]{1,0:T(8,128)(2,1)} %copy-done.7, bf16[384,1024]{1,0:T(8,128)(2,1)} %collective-permute-done.1.refs_10_.refs_3_, ...), custom_call_target="tpu_custom_call" | custom-call | flops 8000000000 | bytes 24000000 | tf_op jit(solution)/shard_map/qkv_weights/pallas_call | solution.py:67
  289.1 3.5 collective-permute-start.31
  292.7 4.4 %tokens_back.1 = (bf16[384,1024]{1,0:T(8,128)(2,1)}, f32[8,2048]{1,0:T(8,128)S(1)}) custom-call(bf16[384,1024]{1,0:T(8,128)(2,1)S(1)} %bitcast.79, f32[384,1024]{1,0:T(8,128)S(1)} %copy-done.19, f32[4,6144]{1,0:T(4,128)S(1)} %convolution_add_fusion.refs_1_.refs_4_.refs_3_.refs_2_, s32[384,1]{1,0:T(8,128)S(1)} %broadcast_in_dim.143.refs_2_.refs_5_.refs_4_.refs_3_, ...), custom_call_target="tpu_custom_call" | custom-call | flops 5000000000 | bytes 15000000 | tf_op jit(solution)/shard_map/tokens_back/pallas_call | solution.py:67
  297.9 5.9 %collective-permute-done.31.refs_3_ = bf16[1,4,128,256]{3,2,1,0:T(8,128)(2,1)S(1)} collective-permute-done((bf16[1,4,128,256]{3,2,1,0:T(8,128)(2,1)S(1)}, bf16[1,4,128,256]{3,2,1,0:T(8,128)(2,1)S(1)}, u32[]{:S(2)}, u32[]{:S(2)}) %collective-permute-start.31) | collective-permute-done | bytes 262176 | tf_op jit(solution)/shard_map/ppermute | solution.py:866
  303.8 4.8 %all-to-all-start.5 = ((bf16[8,48,1024]{2,1,0:T(8,128)(2,1)}), bf16[8,48,1024]{2,1,0:T(8,128)(2,1)}, u32[]{:S(2)}, u32[]{:S(2)}) async-start(bf16[8,48,1024]{2,1,0:T(8,128)(2,1)} %bitcast.24), calls=%async_computation.5 | async-start | bytes 1572864 | tf_op jit(solution)/shard_map/all_to_all | solution.py:849
  309.5 4.4 %collective-permute-done.29.refs_1_ = f32[128,256]{1,0:T(8,128)S(1)} collective-permute-done((f32[128,256]{1,0:T(8,128)S(1)}, f32[128,256]{1,0:T(8,128)S(1)}, u32[]{:S(2)}, u32[]{:S(2)}) %collective-permute-start.29) | collective-permute-done | bytes 131104 | tf_op jit(solution)/shard_map/ppermute | solution.py:866
  328.2 9.0 %collective-permute-done.30 = bf16[2,4,256,128]{3,2,1,0:T(8,128)(2,1)} collective-permute-done((bf16[2,4,256,128]{3,2,1,0:T(8,128)(2,1)}, bf16[2,4,256,128]{3,2,1,0:T(8,128)(2,1)}, u32[]{:S(2)}, u32[]{:S(2)}) %collective-permute-start.30) | collective-permute-done | bytes 524320 | tf_op jit(solution)/shard_map/ppermute | solution.py:866
  342.0 2.9 fusion.22
  349.2 5.5 %collective-permute-done.38 = bf16[1,4,256,128]{3,2,1,0:T(8,128)(2,1)S(1)} collective-permute-done((bf16[1,4,256,128]{3,2,1,0:T(8,128)(2,1)S(1)}, bf16[1,4,256,128]{3,2,1,0:T(8,128)(2,1)S(1)}, u32[]{:S(2)}, u32[]{:S(2)}) %collective-permute-start.38) | collective-permute-done | bytes 262176 | tf_op jit(solution)/shard_map/ppermute | solution.py:866
  (268 shorter events, 99.4 us)
Async XLA Ops:
  13.0 35.6 %all-to-all-start = ((bf16[8,48,1024]{2,1,0:T(8,128)(2,1)}), bf16[8,48,1024]{2,1,0:T(8,128)(2,1)S(1)}, u32[]{:S(2)}, u32[]{:S(2)}) async-start(bf16[8,48,1024]{2,1,0:T(8,128)(2,1)} %bitcast.87), calls=%async_computation | async-start | bytes 1572864 | tf_op jit(solution)/shard_map/all_to_all | solution.py:849
  20.4 112.1 %all-gather.5.cloned.1.call-start = ((), (), s32[]{:S(2)}) async-start(), calls=%async_computation.6 | async-start | bytes 2433024 | tf_op jit(solution)/shard_map/all_gather | solution.py:985
  23.7 112.1 %all-gather.7.cloned.1.call-start = ((), (), s32[]{:S(2)}) async-start(), calls=%async_computation.7 | async-start | bytes 2359296 | tf_op jit(solution)/shard_map/all_gather | solution.py:987
  50.2 15.6 %collective-permute-start.2 = (bf16[384,1024]{1,0:T(8,128)(2,1)S(1)}, bf16[384,1024]{1,0:T(8,128)(2,1)}, u32[]{:S(2)}, u32[]{:S(2)}) collective-permute-start(bf16[384,1024]{1,0:T(8,128)(2,1)S(1)} %first_norm.1.refs_9_.refs_2_), channel_id=1, source_target_pairs={{0,8},{4,12},{8,0},{12,4},{1,9},{5,13},{9,1},{13,5},{2,10},{6,14},... | collective-permute-start | bytes 2359304 | tf_op jit(solution)/shard_map/ppermute | solution.py:866
  55.7 22.9 %collective-permute-start.1 = (bf16[384,1024]{1,0:T(8,128)(2,1)S(1)}, bf16[384,1024]{1,0:T(8,128)(2,1)}, u32[]{:S(2)}, u32[]{:S(2)}) collective-permute-start(bf16[384,1024]{1,0:T(8,128)(2,1)S(1)} %first_norm.1.refs_9_.refs_2_), channel_id=1, source_target_pairs={{0,4},{4,0},{8,12},{12,8},{1,5},{5,1},{9,13},{13,9},{2,6},{6,2},{1... | collective-permute-start | bytes 2359304 | tf_op jit(solution)/shard_map/ppermute | solution.py:866
  65.8 12.9 %collective-permute-start.3 = (bf16[384,1024]{1,0:T(8,128)(2,1)}, bf16[384,1024]{1,0:T(8,128)(2,1)}, u32[]{:S(2)}, u32[]{:S(2)}) collective-permute-start(bf16[384,1024]{1,0:T(8,128)(2,1)} %collective-permute-done.2.refs_11_.refs_4_), channel_id=1, source_target_pairs={{0,4},{4,0},{8,12},{12,8},{1,5},{5,1},{9,13},{13,9},{2,6},{6,2},{1... | collective-permute-start | bytes 2359304 | tf_op jit(solution)/shard_map/ppermute | solution.py:866
  69.5 38.7 %all-to-all-start.2 = ((bf16[8,48,1024]{2,1,0:T(8,128)(2,1)}), bf16[8,48,1024]{2,1,0:T(8,128)(2,1)S(1)}, u32[]{:S(2)}, u32[]{:S(2)}) async-start(bf16[8,48,1024]{2,1,0:T(8,128)(2,1)} %bitcast.86), calls=%async_computation.2 | async-start | bytes 1572864 | tf_op jit(solution)/shard_map/all_to_all | solution.py:849
  108.3 15.8 %all-to-all-start.1 = ((bf16[4,384,256]{2,1,0:T(8,128)(2,1)}), bf16[4,384,256]{2,1,0:T(8,128)(2,1)S(1)}, u32[]{:S(2)}, u32[]{:S(2)}) async-start(bf16[4,384,256]{2,1,0:T(8,128)(2,1)} %get-tuple-element.175), calls=%async_computation.1 | async-start | bytes 1572864 | tf_op jit(solution)/shard_map/all_to_all | solution.py:853
  113.8 27.2 %collective-permute-start.5 = (bf16[384,1024]{1,0:T(8,128)(2,1)}, bf16[384,1024]{1,0:T(8,128)(2,1)}, u32[]{:S(2)}, u32[]{:S(2)}) collective-permute-start(bf16[384,1024]{1,0:T(8,128)(2,1)} %get-tuple-element.185.refs_5_.refs_9_), channel_id=1, source_target_pairs={{0,4},{4,0},{8,12},{12,8},{1,5},{5,1},{9,13},{13,9},{2,6},{6,2},{1... | collective-permute-start | bytes 2359304 | tf_op jit(solution)/shard_map/ppermute | solution.py:866
  114.4 26.7 %collective-permute-start.8 = (bf16[384,1024]{1,0:T(8,128)(2,1)}, bf16[384,1024]{1,0:T(8,128)(2,1)}, u32[]{:S(2)}, u32[]{:S(2)}) collective-permute-start(bf16[384,1024]{1,0:T(8,128)(2,1)} %get-tuple-element.185.refs_5_.refs_9_), channel_id=1, source_target_pairs={{0,8},{4,12},{8,0},{12,4},{1,9},{5,13},{9,1},{13,5},{2,10},{6,14},... | collective-permute-start | bytes 2359304 | tf_op jit(solution)/shard_map/ppermute | solution.py:866
  132.5 24.8 %collective-permute-start.6 = (bf16[384,1024]{1,0:T(8,128)(2,1)S(1)}, bf16[384,1024]{1,0:T(8,128)(2,1)S(1)}, u32[]{:S(2)}, u32[]{:S(2)}) collective-permute-start(bf16[384,1024]{1,0:T(8,128)(2,1)S(1)} %get-tuple-element.184.refs_3_.refs_5_), channel_id=1, source_target_pairs={{0,8},{4,12},{8,0},{12,4},{1,9},{5,13},{9,1},{13,5},{2,10},{6,14},... | collective-permute-start | bytes 2359304 | tf_op jit(solution)/shard_map/ppermute | solution.py:866
  141.0 16.3 %collective-permute-start.9 = (bf16[384,1024]{1,0:T(8,128)(2,1)}, bf16[384,1024]{1,0:T(8,128)(2,1)S(1)}, u32[]{:S(2)}, u32[]{:S(2)}) collective-permute-start(bf16[384,1024]{1,0:T(8,128)(2,1)} %collective-permute-done.8.refs_5_.refs_11_), channel_id=1, source_target_pairs={{0,4},{4,0},{8,12},{12,8},{1,5},{5,1},{9,13},{13,9},{2,6},{6,2},{1... | collective-permute-start | bytes 2359304 | tf_op jit(solution)/shard_map/ppermute | solution.py:866
  177.0 20.3 %collective-permute-start.13 = (bf16[384,1024]{1,0:T(8,128)(2,1)S(1)}, bf16[384,1024]{1,0:T(8,128)(2,1)S(1)}, u32[]{:S(2)}, u32[]{:S(2)}) collective-permute-start(bf16[384,1024]{1,0:T(8,128)(2,1)S(1)} %add_convert_fusion.2), channel_id=1, source_target_pairs={{0,8},{4,12},{8,0},{12,4},{1,9},{5,13},{9,1},{13,5},{2,10},{6,14},... | collective-permute-start | bytes 2359304 | tf_op jit(solution)/shard_map/ppermute | solution.py:866
  177.3 16.9 %collective-permute-start.12 = (bf16[384,1024]{1,0:T(8,128)(2,1)S(1)}, bf16[384,1024]{1,0:T(8,128)(2,1)S(1)}, u32[]{:S(2)}, u32[]{:S(2)}) collective-permute-start(bf16[384,1024]{1,0:T(8,128)(2,1)S(1)} %get-tuple-element.208), channel_id=1, source_target_pairs={{0,4},{4,0},{8,12},{12,8},{1,5},{5,1},{9,13},{13,9},{2,6},{6,2},{1... | collective-permute-start | bytes 2359304 | tf_op jit(solution)/shard_map/ppermute | solution.py:866
  177.4 39.8 %collective-permute-start.14 = (bf16[384,1024]{1,0:T(8,128)(2,1)}, bf16[384,1024]{1,0:T(8,128)(2,1)}, u32[]{:S(2)}, u32[]{:S(2)}) collective-permute-start(bf16[384,1024]{1,0:T(8,128)(2,1)} %get-tuple-element.211), channel_id=1, source_target_pairs={{0,4},{4,0},{8,12},{12,8},{1,5},{5,1},{9,13},{13,9},{2,6},{6,2},{1... | collective-permute-start | bytes 2359304 | tf_op jit(solution)/shard_map/ppermute | solution.py:866
  193.2 24.2 %collective-permute-start.15 = (bf16[384,1024]{1,0:T(8,128)(2,1)}, bf16[384,1024]{1,0:T(8,128)(2,1)}, u32[]{:S(2)}, u32[]{:S(2)}) collective-permute-start(bf16[384,1024]{1,0:T(8,128)(2,1)} %get-tuple-element.212), channel_id=1, source_target_pairs={{0,8},{4,12},{8,0},{12,4},{1,9},{5,13},{9,1},{13,5},{2,10},{6,14},... | collective-permute-start | bytes 2359304 | tf_op jit(solution)/shard_map/ppermute | solution.py:866
  193.7 25.2 %collective-permute-start.17 = (bf16[4,4,128,256]{3,2,1,0:T(8,128)(2,1)}, bf16[4,4,128,256]{3,2,1,0:T(8,128)(2,1)}, u32[]{:S(2)}, u32[]{:S(2)}) collective-permute-start(bf16[4,4,128,256]{3,2,1,0:T(8,128)(2,1)} %get-tuple-element.215), channel_id=1, source_target_pairs={{0,16},{16,0},{1,17},{17,1},{2,18},{18,2},{3,19},{19,3},{4,20},{20... | collective-permute-start | bytes 3145736 | tf_op jit(solution)/shard_map/ppermute | solution.py:866
  212.3 15.9 %all-to-all-start.3 = ((bf16[4,384,256]{2,1,0:T(8,128)(2,1)}), bf16[4,384,256]{2,1,0:T(8,128)(2,1)}, u32[]{:S(2)}, u32[]{:S(2)}) async-start(bf16[4,384,256]{2,1,0:T(8,128)(2,1)} %get-tuple-element.209), calls=%async_computation.3 | async-start | bytes 1572864 | tf_op jit(solution)/shard_map/all_to_all | solution.py:853
  216.6 43.8 %collective-permute-start.18 = (bf16[4,4,128,256]{3,2,1,0:T(8,128)(2,1)}, bf16[4,4,128,256]{3,2,1,0:T(8,128)(2,1)S(1)}, u32[]{:S(2)}, u32[]{:S(2)}) collective-permute-start(bf16[4,4,128,256]{3,2,1,0:T(8,128)(2,1)} %get-tuple-element.229), channel_id=1, source_target_pairs={{0,16},{16,0},{1,17},{17,1},{2,18},{18,2},{3,19},{19,3},{4,20},{20... | collective-permute-start | bytes 3145736 | tf_op jit(solution)/shard_map/ppermute | solution.py:866
  217.2 43.2 %collective-permute-start.20 = (bf16[2,4,256,128]{3,2,1,0:T(8,128)(2,1)S(1)}, bf16[2,4,256,128]{3,2,1,0:T(8,128)(2,1)}, u32[]{:S(2)}, u32[]{:S(2)}) collective-permute-start(bf16[2,4,256,128]{3,2,1,0:T(8,128)(2,1)S(1)} %get-tuple-element.233), channel_id=1, source_target_pairs={{0,4},{4,0},{8,12},{12,8},{1,5},{5,1},{9,13},{13,9},{2,6},{6,2},{1... | collective-permute-start | bytes 1572872 | tf_op jit(solution)/shard_map/ppermute | solution.py:866
  228.2 32.1 %collective-permute-start.19 = (bf16[2,4,128,256]{3,2,1,0:T(8,128)(2,1)}, bf16[2,4,128,256]{3,2,1,0:T(8,128)(2,1)}, u32[]{:S(2)}, u32[]{:S(2)}) collective-permute-start(bf16[2,4,128,256]{3,2,1,0:T(8,128)(2,1)} %get-tuple-element.231), channel_id=1, source_target_pairs={{0,1},{1,0},{2,3},{3,2},{4,5},{5,4},{6,7},{7,6},{8,9},{9,8},{10,11... | collective-permute-start | bytes 1572872 | tf_op jit(solution)/shard_map/ppermute | solution.py:866
  228.3 32.1 %collective-permute-start.21 = (bf16[2,4,256,128]{3,2,1,0:T(8,128)(2,1)}, bf16[2,4,256,128]{3,2,1,0:T(8,128)(2,1)}, u32[]{:S(2)}, u32[]{:S(2)}) collective-permute-start(bf16[2,4,256,128]{3,2,1,0:T(8,128)(2,1)} %get-tuple-element.234), channel_id=1, source_target_pairs={{0,8},{4,12},{8,0},{12,4},{1,9},{5,13},{9,1},{13,5},{2,10},{6,14},... | collective-permute-start | bytes 1572872 | tf_op jit(solution)/shard_map/ppermute | solution.py:866
  228.6 31.8 %all-to-all-start.4 = ((bf16[8,48,1024]{2,1,0:T(8,128)(2,1)}), bf16[8,48,1024]{2,1,0:T(8,128)(2,1)}, u32[]{:S(2)}, u32[]{:S(2)}) async-start(bf16[8,48,1024]{2,1,0:T(8,128)(2,1)} %bitcast.20), calls=%async_computation.4 | async-start | bytes 1572864 | tf_op jit(solution)/shard_map/all_to_all | solution.py:849
  260.5 32.2 %collective-permute-start.26 = (bf16[384,1024]{1,0:T(8,128)(2,1)}, bf16[384,1024]{1,0:T(8,128)(2,1)S(1)}, u32[]{:S(2)}, u32[]{:S(2)}) collective-permute-start(bf16[384,1024]{1,0:T(8,128)(2,1)} %get-tuple-element.266), channel_id=1, source_target_pairs={{0,4},{4,0},{8,12},{12,8},{1,5},{5,1},{9,13},{13,9},{2,6},{6,2},{1... | collective-permute-start | bytes 2359304 | tf_op jit(solution)/shard_map/ppermute | solution.py:866
  264.2 28.5 %collective-permute-start.27 = (bf16[384,1024]{1,0:T(8,128)(2,1)}, bf16[384,1024]{1,0:T(8,128)(2,1)S(1)}, u32[]{:S(2)}, u32[]{:S(2)}) collective-permute-start(bf16[384,1024]{1,0:T(8,128)(2,1)} %add_convert_fusion.1), channel_id=1, source_target_pairs={{0,8},{4,12},{8,0},{12,4},{1,9},{5,13},{9,1},{13,5},{2,10},{6,14},... | collective-permute-start | bytes 2359304 | tf_op jit(solution)/shard_map/ppermute | solution.py:866
  269.1 19.5 %collective-permute-start.24 = (bf16[2,4,128,256]{3,2,1,0:T(8,128)(2,1)S(1)}, bf16[2,4,128,256]{3,2,1,0:T(8,128)(2,1)S(1)}, u32[]{:S(2)}, u32[]{:S(2)}) collective-permute-start(bf16[2,4,128,256]{3,2,1,0:T(8,128)(2,1)S(1)} %get-tuple-element.248), channel_id=1, source_target_pairs={{0,1},{1,0},{2,3},{3,2},{4,5},{5,4},{6,7},{7,6},{8,9},{9,8},{10,11... | collective-permute-start | bytes 1572872 | tf_op jit(solution)/shard_map/ppermute | solution.py:866
  271.1 16.8 %collective-permute-start.25 = (bf16[1,4,128,256]{3,2,1,0:T(8,128)(2,1)S(1)}, bf16[1,4,128,256]{3,2,1,0:T(8,128)(2,1)S(1)}, u32[]{:S(2)}, u32[]{:S(2)}) collective-permute-start(bf16[1,4,128,256]{3,2,1,0:T(8,128)(2,1)S(1)} %get-tuple-element.259), channel_id=1, source_target_pairs={{0,2},{1,3},{2,0},{3,1},{4,6},{5,7},{6,4},{7,5},{8,10},{9,11},{10,... | collective-permute-start | bytes 786440 | tf_op jit(solution)/shard_map/ppermute | solution.py:866
  284.8 29.1 %collective-permute-start.23 = (bf16[4,4,256,128]{3,2,1,0:T(8,128)(2,1)}, bf16[4,4,256,128]{3,2,1,0:T(8,128)(2,1)}, u32[]{:S(2)}, u32[]{:S(2)}) collective-permute-start(bf16[4,4,256,128]{3,2,1,0:T(8,128)(2,1)} %get-tuple-element.254), channel_id=1, source_target_pairs={{0,16},{16,0},{1,17},{17,1},{2,18},{18,2},{3,19},{19,3},{4,20},{20... | collective-permute-start | bytes 3145736 | tf_op jit(solution)/shard_map/ppermute | solution.py:866
  289.1 14.7 %collective-permute-start.31 = (bf16[1,4,128,256]{3,2,1,0:T(8,128)(2,1)S(1)}, bf16[1,4,128,256]{3,2,1,0:T(8,128)(2,1)S(1)}, u32[]{:S(2)}, u32[]{:S(2)}) collective-permute-start(bf16[1,4,128,256]{3,2,1,0:T(8,128)(2,1)S(1)} %get-tuple-element.262), channel_id=1, source_target_pairs={{0,2},{1,3},{2,0},{3,1},{4,6},{5,7},{6,4},{7,5},{8,10},{9,11},{10,... | collective-permute-start | bytes 786440 | tf_op jit(solution)/shard_map/ppermute | solution.py:866
  303.8 33.4 %all-to-all-start.5 = ((bf16[8,48,1024]{2,1,0:T(8,128)(2,1)}), bf16[8,48,1024]{2,1,0:T(8,128)(2,1)}, u32[]{:S(2)}, u32[]{:S(2)}) async-start(bf16[8,48,1024]{2,1,0:T(8,128)(2,1)} %bitcast.24), calls=%async_computation.5 | async-start | bytes 1572864 | tf_op jit(solution)/shard_map/all_to_all | solution.py:849
  316.9 20.4 %collective-permute-start.30 = (bf16[2,4,256,128]{3,2,1,0:T(8,128)(2,1)}, bf16[2,4,256,128]{3,2,1,0:T(8,128)(2,1)}, u32[]{:S(2)}, u32[]{:S(2)}) collective-permute-start(bf16[2,4,256,128]{3,2,1,0:T(8,128)(2,1)} %get-tuple-element.391), channel_id=1, source_target_pairs={{0,1},{1,0},{2,3},{3,2},{4,5},{5,4},{6,7},{7,6},{8,9},{9,8},{10,11... | collective-permute-start | bytes 1572872 | tf_op jit(solution)/shard_map/ppermute | solution.py:866
  340.1 14.6 %collective-permute-start.38 = (bf16[1,4,256,128]{3,2,1,0:T(8,128)(2,1)S(1)}, bf16[1,4,256,128]{3,2,1,0:T(8,128)(2,1)S(1)}, u32[]{:S(2)}, u32[]{:S(2)}) collective-permute-start(bf16[1,4,256,128]{3,2,1,0:T(8,128)(2,1)S(1)} %slice.86), channel_id=1, source_target_pairs={{0,2},{1,3},{2,0},{3,1},{4,6},{5,7},{6,4},{7,5},{8,10},{9,11},{10,... | collective-permute-start | bytes 786440 | tf_op jit(solution)/shard_map/ppermute | solution.py:866
  (64 other events, 496.7 us)
Sparse Core Ops, SparseCore 0:
  23.9 54.2 all-gather.4
  80.9 54.8 all-gather.6

commit v6 on v5

--- a/solution.py
+++ b/solution.py
@@ -17,7 +17,7 @@
 LIMITS = {"attend": 57, "attend_back": 57, "sort": 57, "middle_back": 50, "output": 50, "feed": 50, "feed_weights": 57, "weights": 57, "qkv_weights": 57}
 FLOPS, BYTES = 1_000_000_000, 3_000_000
 TIMES = {
-    "sort": 2, "first_norm": 2, "grad_mlp": 2, "attend": 26, "project": 5, "weights": 4, "feed": 12,
+    "sort": 2, "first_norm": 2, "grad_mlp": 2, "attend": 26, "project": 0, "weights": 4, "feed": 12,
     "feed_weights": 12, "middle_back": 7, "proj_weights": 3, "output": 3, "attend_back": 34, "add": 3,
     "qkv_weights": 8, "tokens_back": 5,
 }
@@ -73,7 +73,7 @@
         scratch_shapes=list(scratch) + staged + sems,
         compiler_params=pltpu.CompilerParams(vmem_limit_bytes=limit * 1024 * 1024),
         cost_estimate=pl.CostEstimate(
-            flops=TIMES.get(name, 1) * FLOPS, bytes_accessed=TIMES.get(name, 1) * BYTES, transcendentals=0
+            flops=TIMES.get(name, 1) * FLOPS + 1, bytes_accessed=TIMES.get(name, 1) * BYTES + 1, transcendentals=0
         ),
     )(*operands)
 
@@ -434,22 +434,27 @@
         outs[j // count][j % count] = made
 
 
-def weights_kernel(fc1_ref, fc2_ref, w1_ref, w2_ref, sems):
-    segs, head_size, _, hidden = fc1_ref.shape
-    half = fc2_ref.shape[3]
+def weights_kernel(dims, me_ref, *refs):
+    segs, head_size = dims
+    count = segs * head_size
+    tiles, pairs, (w1_ref, w2_ref, bias_ref, bias_s, sems) = refs[:count], refs[count : 2 * count], refs[2 * count :]
+    hidden, half = pairs[0].shape
     copies = []
-    for y in range(segs):
-        for z in range(head_size):
-            own = pl.ds(z * hidden, hidden)
-            rows = pl.ds(y * half, half)
-            for source, target in (
-                (fc1_ref.at[y, z, pl.ds(0, half), :], w1_ref.at[rows, own]),
-                (fc2_ref.at[y, z], w2_ref.at[own, rows]),
-            ):
-                copies.append(pltpu.make_async_copy(source, target, sems.at[len(copies)]))
-                copies[-1].start()
-    for copy in copies:
-        copy.wait()
+
+    def copy(source, target):
+        copies.append(pltpu.make_async_copy(source, target, sems.at[len(copies)]))
+        copies[-1].start()
+
+    for k in range(count):
+        own = pl.ds(pl.multiple_of((me_ref[2] ^ (k % head_size)) * hidden, hidden), hidden)
+        part = pl.ds(pl.multiple_of((me_ref[1] ^ (k // head_size)) * half, half), half)
+        copy(tiles[k].at[pl.ds(0, half), :], w1_ref.at[part, own])
+        copy(pairs[k], w2_ref.at[own, part])
+        if k < head_size:
+            copy(tiles[k].at[pl.ds(half, 16), :], bias_s.at[:, own])
+    for started in copies:
+        started.wait()
+    bias_ref[...] = bias_s[0:1, :].astype(F32)
 
 
 def feed_kernel(count, *refs):
@@ -917,6 +922,16 @@
 def tie_groups(*groups):
     tied = list(tie(*[value for group in groups for value in group]))
     return [[tied.pop(0) for _ in group] for group in groups]
+
+
+def spread_steps(depth, segs, head_size):
+    steps = []
+    for k in range(segs * head_size):
+        if bin(k).count("1") == depth:
+            y, z = k // head_size, k % head_size
+            step = y & -y if y else z & -z
+            steps.append((k, k - step * head_size if y else k - step, "yy" if y else "head", step))
+    return sorted(steps, key=lambda made: made[2])
 
 
 def shards(
@@ -979,28 +994,26 @@
     fc1_own = lax.dynamic_slice(fc1_weight, (yy * half, g * hidden), (half, hidden))
     fc1_bias_own = lax.dynamic_slice(fc1_bias, (g * hidden,), (hidden,))
     fc2_own = lax.dynamic_slice(fc2_weight, (g * hidden, yy * half), (hidden, half))
-    fc1_sent = jnp.concatenate(
+    fc1_own = jnp.concatenate(
         [fc1_own, jnp.broadcast_to(fc1_bias_own[None, :], (16, hidden))], axis=0
     )
-    fc1_all = lax.all_gather(fc1_sent, ("yy", "head"), axis=0)
-    fc1_all = fc1_all.reshape(segs, head_size, half + 16, hidden)
-    fc2_all = lax.all_gather(fc2_own, ("yy", "head"), axis=0)
-    fc2_all = fc2_all.reshape(segs, head_size, hidden, half)
-    fc1_bias_here = fc1_all[0, :, half].reshape(1, units).astype(F32)
     tiled = hidden % 128 == 0
-    if tiled:
-        fc1_here, fc2_here = call(
-            "weights",
-            weights_kernel,
-            (fc1_all, fc2_all),
-            (ANY, ANY),
-            (shape_of((model, units), BF), shape_of((units, model), BF)),
-            [pltpu.SemaphoreType.DMA((2 * segs * head_size,))],
-            out_specs=(VMEM, VMEM),
+    tile_count = segs * head_size
+
+    fc1_tiles, fc2_tiles = {0: fc1_own}, {0: fc2_own}
+
+    def next_hop(tiles, depth):
+        for k, source, axis, step in spread_steps(depth, segs, head_size):
+            tiles[k] = xor_swap(tiles[source], axis, step)
+
+    def with_tiles(values):
+        first, second = sorted(fc1_tiles), sorted(fc2_tiles)
+        values, held, held_too = tie_groups(
+            values, [fc1_tiles[k] for k in first], [fc2_tiles[k] for k in second]
         )
-    else:
-        fc1_here = fc1_all[:, :, :half].transpose(0, 2, 1, 3).reshape(model, units)
-        fc2_here = fc2_all.transpose(1, 2, 0, 3).reshape(units, model)
+        fc1_tiles.update(zip(first, held))
+        fc2_tiles.update(zip(second, held_too))
+        return values
 
     lens_here = pick(item_lens, pack, 0)
     class_here = pick(class_ids, pack, 0)
@@ -1054,7 +1067,22 @@
         "first_norm",
         first_norm_kernel, (inputs, mod, row_item), (HBM, VMEM, VMEM), (shape_of((rows, model), BF),)
     )
-    attn_blocks = xor_gather(attn_in, "g")
+    def near_blocks(own):
+        blocks = {0: own}
+        for step in bits(group)[1:]:
+            for k in list(blocks):
+                blocks[k ^ step] = xor_swap(blocks[k], "g", step)
+        return [blocks[k] for k in range(len(blocks))]
+
+    near = group // 2
+
+    (attn_in,) = with_tiles([attn_in])
+    next_hop(fc1_tiles, 1)
+    attn_blocks = near_blocks(attn_in)
+    (attn_far,) = with_tiles([xor_swap(attn_in, "g", near)])
+    next_hop(fc1_tiles, 2)
+    next_hop(fc2_tiles, 1)
+    attn_blocks += near_blocks(attn_far)
     per_part = sub // head_dim
     scale_here = pick(log_scale.reshape(parts, group, per_part), g, 1).reshape(heads)
     temper = jnp.repeat(jnp.exp(scale_here), head_dim)[None, :]
@@ -1062,14 +1090,6 @@
     tall = shape_of((width, pack_len), F32)
     sorted_cotangent, _ = tie(sorted_cotangent, inputs)
     upstream = to_packs(sorted_cotangent)
-    def near_blocks(own):
-        blocks = {0: own}
-        for step in bits(group)[1:]:
-            for k in list(blocks):
-                blocks[k ^ step] = xor_swap(blocks[k], "g", step)
-        return [blocks[k] for k in range(len(blocks))]
-
-    near = group // 2
     held_bf = pltpu.VMEM((pack_len, width), BF)
     out_blocks, out_t, lse, queries, queries_low, keys, values, inverses = call(
         "attend",
@@ -1098,6 +1118,9 @@
         ],
         out_specs=(ANY, ANY, VMEM, ANY, ANY, ANY, ANY, ANY),
     )
+    (out_blocks,) = with_tiles([out_blocks])
+    next_hop(fc1_tiles, 3)
+    next_hop(fc2_tiles, 2)
     returned = over_group(out_blocks)
     upstream, _ = tie(upstream, out_blocks)
     grad_mlp, grad_mlp_sum = call(
@@ -1109,7 +1132,6 @@
     )
     grad_far = xor_swap(grad_mlp, "g", near)
     grad_blocks = near_blocks(grad_mlp)
-    returned, grad_mlp_sum = tie(returned, grad_mlp_sum)
     attn_rows, branch, middle, mlp_in = call(
         "project",
         functools.partial(project_kernel, parts),
@@ -1118,6 +1140,35 @@
         (rows_bf, rows_bf, rows_f32, rows_bf),
         [pltpu.VMEM((rows, model), F32)],
     )
+
+    (middle,) = with_tiles([middle])
+    for depth in range(4, tile_count.bit_length()):
+        next_hop(fc1_tiles, depth)
+    for depth in range(3, tile_count.bit_length()):
+        next_hop(fc2_tiles, depth)
+    if tiled:
+        fc1_here, fc2_here, fc1_bias_here = call(
+            "weights",
+            functools.partial(weights_kernel, (segs, head_size)),
+            (me, *[fc1_tiles[k] for k in range(tile_count)], *[fc2_tiles[k] for k in range(tile_count)]),
+            (SMEM,) + (ANY,) * (2 * tile_count),
+            (shape_of((model, units), BF), shape_of((units, model), BF), shape_of((1, units), F32)),
+            [
+                pltpu.VMEM((16, units), BF),
+                pltpu.SemaphoreType.DMA((2 * tile_count + head_size,)),
+            ],
+            out_specs=(VMEM,) * 3,
+        )
+    else:
+        def placed(tiles):
+            held = jnp.stack([tiles[k] for k in range(tile_count)])
+            held = held.reshape(segs, head_size, *held.shape[1:])
+            return held[jnp.arange(segs) ^ yy][:, jnp.arange(head_size) ^ z]
+
+        fc1_all, fc2_all = placed(fc1_tiles), placed(fc2_tiles)
+        fc1_here = fc1_all[:, :, :half].transpose(0, 2, 1, 3).reshape(model, units)
+        fc1_bias_here = fc1_all[0, :, half].reshape(1, units).astype(F32)
+        fc2_here = fc2_all.transpose(1, 2, 0, 3).reshape(units, model)
 
     mlp_blocks = near_blocks(mlp_in)
     mlp_far = xor_swap(mlp_in, "g", near)

time: 376 us -> 366 us (0.973)
  starting transfers between devices: 66.3 us -> 87.2 us
  waiting for transfers between devices: 90.1 us -> 71.1 us
  between operations: 15.2 us -> 1.88 us
    ppermute x35 -> x49, starting transfers between devices: 30 us -> 52.7 us  [xor_swap(): return lax.ppermute(values, axis, [(i, i ^ step) for i in range(size)])]
    all_to_all x4, waiting for transfers between devices: 20.4 us -> 4.63 us  [to_packs(): lax.all_to_all(rows, ('yy', 'head'), split_axis=0, concat_axis=0, tiled=T...]
    all_to_all x2, waiting for transfers between devices: 9.33 us -> 4.38 us  [over_group(): return lax.all_to_all(blocks, 'g', split_axis=0, concat_axis=0, tiled=True)]
    ppermute x35 -> x49, waiting for transfers between devices: 54.1 us -> 58.3 us  [xor_swap(): return lax.ppermute(values, axis, [(i, i ^ step) for i in range(size)])]
    unnamed x108 -> x138, local copies, waits for them, and re-layouts: 18.1 us -> 20.5 us
  transfers between devices with their start and end apart: 47 -> 59, of which waited for: 23 -> 25; matrix products, arithmetic and copies ran while one was open for 9% -> 8% of each run, Pallas kernels for 34% -> 35%
where the time goes in v6:
time: 366 us; the launch traced here: 360 us
  Pallas kernels  145 us (40%)
  starting transfers between devices  87.2 us (24%)
  waiting for transfers between devices  71.1 us (19%)
  local copies, waits for them, and re-layouts  31.8 us (9%)
  matrix products  11.9 us (3%)
  other arithmetic  10.6 us (3%)
    pallas_call x26, Pallas kernels, call(): pl.pallas_call(body, name=name, out_shape=tuple(outs), in_specs=[ANY if s...  145 us
    ppermute x49, waiting for transfers between devices, xor_swap(): return lax.ppermute(values, axis, [(i, i ^ step) for i in range(size)])  58.3 us
    ppermute x49, starting transfers between devices, xor_swap(): return lax.ppermute(values, axis, [(i, i ^ step) for i in range(size)])  52.7 us
    all_to_all x4, starting transfers between devices, to_packs(): lax.all_to_all(rows, ('yy', 'head'), split_axis=0, concat_axis=0, tiled=T...  24 us
    unnamed x138, local copies, waits for them, and re-layouts  20.5 us
    all_to_all x2, starting transfers between devices, over_group(): return lax.all_to_all(blocks, 'g', split_axis=0, concat_axis=0, tiled=True)  7.85 us
  transfers between devices with their start and end apart: 59, of which 25 were waited for; matrix products, arithmetic and copies ran while one was open for 8% of the time, Pallas kernels for 35%

profile of v6, /device:TPU:0, one launch (start us, length us, event | category | flops | bytes accessed | tf_op | source)
XLA Modules:
  0.0 359.8 jit_solution(1007606514778246019)
XLA Ops:
  2.1 4.4 %sort.1 = (bf16[384,384]{1,0:T(8,128)(2,1)}, bf16[384,1024]{1,0:T(8,128)(2,1)}, bf16[384,1024]{1,0:T(8,128)(2,1)}) custom-call(s32[1,384]{1,0:T(1,128)} %broadcast_in_dim.123.refs_0_, bf16[384,1024]{1,0:T(8,128)(2,1)} %refs_1_.2, bf16[384,1024]{1,0:T(8,128)(2,1)} %refs_2_.2), custom_call_target="tpu_custom_call" | custom-call | flops 2000000000 | bytes 6000001 | tf_op jit(solution)/shard_map/sort/pallas_call | solution.py:67
  6.5 7.3 %all-to-all-start = ((bf16[8,48,1024]{2,1,0:T(8,128)(2,1)}), bf16[8,48,1024]{2,1,0:T(8,128)(2,1)S(1)}, u32[]{:S(2)}, u32[]{:S(2)}) async-start(bf16[8,48,1024]{2,1,0:T(8,128)(2,1)} %bitcast.83), calls=%async_computation | async-start | bytes 1572864 | tf_op jit(solution)/shard_map/all_to_all | solution.py:854
  18.1 6.4 %convolution_add_fusion.refs_1_.refs_4_.refs_3_.refs_2_ = f32[4,6144]{1,0:T(4,128)S(1)} fusion(bf16[1024,6144]{1,0:T(8,128)(2,1)} %param.22, f32[6144]{0:T(1024)S(1)} %convert_element_type.84, f32[32,1024]{1,0:T(8,128)S(1)} %select_convert_fusion, s32[]{:T(128)S(6)} %select_n.97), kind=kOutput, calls=%fused_computation.4 | convolution fusion | flops 50376704 | bytes 12722180 | tf_op jit(solution)/shard_map/dot_general | solution.py:1063
  30.4 4.6 %all-to-all-done = bf16[8,48,1024]{2,1,0:T(8,128)(2,1)S(1)} async-done(((bf16[8,48,1024]{2,1,0:T(8,128)(2,1)}), bf16[8,48,1024]{2,1,0:T(8,128)(2,1)S(1)}, u32[]{:S(2)}, u32[]{:S(2)}) %all-to-all-start) | async-done | bytes 786464 | tf_op jit(solution)/shard_map/all_to_all | solution.py:854
  36.7 4.5 %collective-permute-start.2 = (bf16[384,1024]{1,0:T(8,128)(2,1)S(1)}, bf16[384,1024]{1,0:T(8,128)(2,1)}, u32[]{:S(2)}, u32[]{:S(2)}) collective-permute-start(bf16[384,1024]{1,0:T(8,128)(2,1)S(1)} %first_norm.1.refs_9_.refs_2_), channel_id=1, source_target_pairs={{0,8},{4,12},{8,0},{12,4},{1,9},{5,13},{9,1},{13,5},{2,10},{6,14},... | collective-permute-start | bytes 2359304 | tf_op jit(solution)/shard_map/ppermute | solution.py:871
  43.1 9.1 %collective-permute-done.3.refs_2_ = bf16[528,256]{1,0:T(8,128)(2,1)S(1)} collective-permute-done((bf16[528,256]{1,0:T(8,128)(2,1)S(1)}, bf16[528,256]{1,0:T(8,128)(2,1)S(1)}, u32[]{:S(2)}, u32[]{:S(2)}) %collective-permute-start.3) | collective-permute-done | bytes 270368 | tf_op jit(solution)/shard_map/ppermute | solution.py:871
  59.5 6.4 %all-to-all-start.2 = ((bf16[8,48,1024]{2,1,0:T(8,128)(2,1)}), bf16[8,48,1024]{2,1,0:T(8,128)(2,1)S(1)}, u32[]{:S(2)}, u32[]{:S(2)}) async-start(bf16[8,48,1024]{2,1,0:T(8,128)(2,1)} %bitcast.82), calls=%async_computation.2 | async-start | bytes 1572864 | tf_op jit(solution)/shard_map/all_to_all | solution.py:854
  73.9 21.0 %attend.1 = (bf16[4,384,256]{2,1,0:T(8,128)(2,1)}, f32[256,1536]{1,0:T(8,128)}, f32[8,1536]{1,0:T(8,128)}, bf16[1536,256]{1,0:T(8,128)(2,1)}, bf16[1536,256]{1,0...) custom-call(s32[4]{0:T(128)} %pad_add_fusion.refs_0_.refs_6_, ...), custom_call_target="tpu_custom_call" | custom-call | flops 26000001024 | bytes 78000000 | tf_op jit(solution)/shard_map/attend/pallas_call | solution.py:67
  98.7 3.7 %all-to-all-start.1 = ((bf16[4,384,256]{2,1,0:T(8,128)(2,1)}), bf16[4,384,256]{2,1,0:T(8,128)(2,1)S(1)}, u32[]{:S(2)}, u32[]{:S(2)}) async-start(bf16[4,384,256]{2,1,0:T(8,128)(2,1)} %get-tuple-element.221), calls=%async_computation.1 | async-start | bytes 1572864 | tf_op jit(solution)/shard_map/all_to_all | solution.py:858
  110.1 4.4 %all-to-all-done.1.refs_0_ = bf16[4,384,256]{2,1,0:T(8,128)(2,1)S(1)} async-done(((bf16[4,384,256]{2,1,0:T(8,128)(2,1)}), bf16[4,384,256]{2,1,0:T(8,128)(2,1)S(1)}, u32[]{:S(2)}, u32[]{:S(2)}) %all-to-all-start.1) | async-done | bytes 786464 | tf_op jit(solution)/shard_map/all_to_all | solution.py:858
  116.1 3.9 %project.1 = (bf16[384,1024]{1,0:T(8,128)(2,1)S(1)}, bf16[384,1024]{1,0:T(8,128)(2,1)S(1)}, f32[384,1024]{1,0:T(8,128)S(1)}, bf16[384,1024]{1,0:T(8,128)(2,1)S(1)}) custom-call(bf16[4,384,256]{2,1,0:T(8,128)(2,1)S(1)} %all-to-all-done.1.refs_0_, bf16[1024,1024]{1,0:T(8,128)(2,1)S(1)} %copy-done.2, bf16[1,1024]{1,0:T(2,128)(2,1)S(1)} %broadcast_in_dim.139.refs_2_, ...), custom_call_target="tpu_custom_call" | custom-call | flops 1 | bytes 1 | tf_op jit(solution)/shard_map/project/pallas_call | solution.py:67
  126.0 5.1 %collective-permute-done.17.refs_16_ = bf16[256,512]{1,0:T(8,128)(2,1)S(1)} collective-permute-done((bf16[256,512]{1,0:T(8,128)(2,1)}, bf16[256,512]{1,0:T(8,128)(2,1)S(1)}, u32[]{:S(2)}, u32[]{:S(2)}) %collective-permute-start.17) | collective-permute-done | bytes 262176 | tf_op jit(solution)/shard_map/ppermute | solution.py:871
  131.8 5.0 %weights.1 = (bf16[1024,1024]{1,0:T(8,128)(2,1)}, bf16[1024,1024]{1,0:T(8,128)(2,1)}, f32[1,1024]{1,0:T(1,128)}) custom-call(s32[4]{0:T(128)} %pad_add_fusion.refs_0_.refs_6_, bf16[528,256]{1,0:T(8,128)(2,1)} %copy-done.35, bf16[528,256]{1,0:T(8,128)(2,1)} %copy-done.54, bf16[528,256]{1,0:T(8,128)(2,1)} %copy-done.55, bf16[528,256]{1,0:T(8,128)(2,1)} %copy-done.57, ...), custom_call_target="tpu_custom_call" | custom-call | flops 4000000000 | bytes 12000001 | tf_op jit(solution)/shard_map/weights/pallas_call | solution.py:67
  138.8 13.0 %feed.2 = (bf16[384,1024]{1,0:T(8,128)(2,1)S(1)}, bf16[384,1024]{1,0:T(8,128)(2,1)S(1)}, bf16[384,1024]{1,0:T(8,128)(2,1)S(1)}, bf16[384,1024]{1,0:T(8,128)(2,1)...) custom-call(bf16[1024,1024]{1,0:T(8,128)(2,1)} %get-tuple-element.250.refs_0_, ...), custom_call_target="tpu_custom_call" | custom-call | flops 12000000000 | bytes 36000000 | tf_op jit(solution)/shard_map/feed/pallas_call | solution.py:67
  156.0 13.6 %feed.3 = (bf16[384,1024]{1,0:T(8,128)(2,1)S(1)}, bf16[384,1024]{1,0:T(8,128)(2,1)S(1)}, bf16[384,1024]{1,0:T(8,128)(2,1)S(1)}, bf16[384,1024]{1,0:T(8,128)(2,1)...) custom-call(bf16[1024,1024]{1,0:T(8,128)(2,1)} %get-tuple-element.250.refs_0_, ...), custom_call_target="tpu_custom_call" | custom-call | flops 12000000000 | bytes 36000000 | tf_op jit(solution)/shard_map/feed/pallas_call | solution.py:67
  175.6 13.2 %feed_weights.1 = (bf16[4,4,128,256]{3,2,1,0:T(8,128)(2,1)}, bf16[4,4,128,256]{3,2,1,0:T(8,128)(2,1)}, bf16[4,4,128,256]{3,2,1,0:T(8,128)(2,1)}, bf16[4,4,128,256]{3,2,1,0:T(8,128)(2,1)}, bf16[384,1024]{1,0:T(8,128)(2,1)}) custom-call(s32[4]{0:T(128)} %pad_add_fusion.refs_0_.refs_6_, bf16[768,1024]{1,0:T(8,128)(2,1)} %get-tuple-element.263.refs_1_, ...), custom_call_target="tpu_custom_call" | custom-call | flops 12000000000 | bytes 36000000 | tf_op jit(solution)/shard_map/feed_weights/pallas_call | solution.py:67
  193.5 12.5 %middle_back.1 = (bf16[4,384,256]{2,1,0:T(8,128)(2,1)}, bf16[384,1024]{1,0:T(8,128)(2,1)}, f32[384,1024]{1,0:T(8,128)}, f32[8,3072]{1,0:T(8,128)S(1)}, f32[8,102...) custom-call(f32[384,1024]{1,0:T(8,128)} %copy-done.7, ...), custom_call_target="tpu_custom_call" | custom-call | flops 7000000000 | bytes 21000000 | tf_op jit(solution)/shard_map/middle_back/pallas_call | solution.py:67
  207.6 4.2 %all-to-all-start.3 = ((bf16[4,384,256]{2,1,0:T(8,128)(2,1)}), bf16[4,384,256]{2,1,0:T(8,128)(2,1)}, u32[]{:S(2)}, u32[]{:S(2)}) async-start(bf16[4,384,256]{2,1,0:T(8,128)(2,1)} %get-tuple-element.281), calls=%async_computation.3 | async-start | bytes 1572864 | tf_op jit(solution)/shard_map/all_to_all | solution.py:858
  216.9 6.2 %output.1 = (bf16[384,1024]{1,0:T(8,128)(2,1)}, f32[8,1024]{1,0:T(8,128)S(1)}, bf16[2,4,256,128]{3,2,1,0:T(8,128)(2,1)}, bf16[2,4,128,256]{3,2,1,0:T(8,128)(2,1)S(1)}, bf16[2,4,128,256]{3,2,1,0:T(8,128)(2,1)}) custom-call(f32[384,1024]{1,0:T(8,128)} %copy-done.7, bf16[384,1024]{1,0:T(8,128)(2,1)} %bitcast.78, ...), custom_call_target="tpu_custom_call" | custom-call | flops 3000000000 | bytes 9000001 | tf_op jit(solution)/shard_map/output/pallas_call | solution.py:67
  225.8 4.4 %all-to-all-start.4 = ((bf16[8,48,1024]{2,1,0:T(8,128)(2,1)}), bf16[8,48,1024]{2,1,0:T(8,128)(2,1)}, u32[]{:S(2)}, u32[]{:S(2)}) async-start(bf16[8,48,1024]{2,1,0:T(8,128)(2,1)} %bitcast.16), calls=%async_computation.4 | async-start | bytes 1572864 | tf_op jit(solution)/shard_map/all_to_all | solution.py:854
  230.2 27.3 %attend_back.1 = (bf16[384,1024]{1,0:T(8,128)(2,1)}, bf16[384,1024]{1,0:T(8,128)(2,1)}, bf16[384,1024]{1,0:T(8,128)(2,1)}, bf16[384,1024]{1,0:T(8,128)(2,1)}, bf...) custom-call(s32[4]{0:T(128)} %pad_add_fusion.refs_0_.refs_6_, f32[1,256]{1,0:T(1,128)} %broadcast_in_dim_reshape.2.refs_5_.refs_1_, ...), custom_call_target="tpu_custom_call" | custom-call | flops 34000001024 | bytes 102000000 | tf_op jit(solution)/shard_map/attend_back/pallas_call | solution.py:67
  266.4 3.3 collective-permute-start.39
  269.7 9.5 %qkv_weights.1 = (bf16[4,4,256,128]{3,2,1,0:T(8,128)(2,1)}, bf16[4,4,256,128]{3,2,1,0:T(8,128)(2,1)}) custom-call(s32[4]{0:T(128)} %pad_add_fusion.refs_0_.refs_6_, bf16[1536,768]{1,0:T(8,128)(2,1)} %get-tuple-element.321.refs_1_, bf16[384,1024]{1,0:T(8,128)(2,1)} %copy-done.8, bf16[384,1024]{1,0:T(8,128)(2,1)} %collective-permute-done.1.refs_10_.refs_3_, ...), custom_call_target="tpu_custom_call" | custom-call | flops 8000000000 | bytes 24000000 | tf_op jit(solution)/shard_map/qkv_weights/pallas_call | solution.py:67
  287.2 4.4 %tokens_back.1 = (bf16[384,1024]{1,0:T(8,128)(2,1)}, f32[8,2048]{1,0:T(8,128)S(1)}) custom-call(bf16[384,1024]{1,0:T(8,128)(2,1)S(1)} %bitcast.75, f32[384,1024]{1,0:T(8,128)S(1)} %copy-done.23, f32[4,6144]{1,0:T(4,128)S(1)} %convolution_add_fusion.refs_1_.refs_4_.refs_3_.refs_2_, s32[384,1]{1,0:T(8,128)S(1)} %broadcast_in_dim.143.refs_2_.refs_5_.refs_4_.refs_3_, ...), custom_call_target="tpu_custom_call" | custom-call | flops 5000000000 | bytes 15000001 | tf_op jit(solution)/shard_map/tokens_back/pallas_call | solution.py:67
  292.4 6.6 %collective-permute-done.45.refs_3_ = bf16[1,4,128,256]{3,2,1,0:T(8,128)(2,1)S(1)} collective-permute-done((bf16[1,4,128,256]{3,2,1,0:T(8,128)(2,1)S(1)}, bf16[1,4,128,256]{3,2,1,0:T(8,128)(2,1)S(1)}, u32[]{:S(2)}, u32[]{:S(2)}) %collective-permute-start.45) | collective-permute-done | bytes 262176 | tf_op jit(solution)/shard_map/ppermute | solution.py:871
  299.0 6.0 %all-to-all-start.5 = ((bf16[8,48,1024]{2,1,0:T(8,128)(2,1)}), bf16[8,48,1024]{2,1,0:T(8,128)(2,1)}, u32[]{:S(2)}, u32[]{:S(2)}) async-start(bf16[8,48,1024]{2,1,0:T(8,128)(2,1)} %bitcast.20), calls=%async_computation.5 | async-start | bytes 1572864 | tf_op jit(solution)/shard_map/all_to_all | solution.py:854
  305.9 4.2 %collective-permute-done.43.refs_1_ = f32[128,256]{1,0:T(8,128)S(1)} collective-permute-done((f32[128,256]{1,0:T(8,128)S(1)}, f32[128,256]{1,0:T(8,128)S(1)}, u32[]{:S(2)}, u32[]{:S(2)}) %collective-permute-start.43) | collective-permute-done | bytes 131104 | tf_op jit(solution)/shard_map/ppermute | solution.py:871
  324.6 7.5 %collective-permute-done.44 = bf16[2,4,256,128]{3,2,1,0:T(8,128)(2,1)} collective-permute-done((bf16[2,4,256,128]{3,2,1,0:T(8,128)(2,1)}, bf16[2,4,256,128]{3,2,1,0:T(8,128)(2,1)}, u32[]{:S(2)}, u32[]{:S(2)}) %collective-permute-start.44) | collective-permute-done | bytes 524320 | tf_op jit(solution)/shard_map/ppermute | solution.py:871
  332.1 2.9 collective-permute-start.49
  337.7 2.9 fusion.22
  343.3 2.7 collective-permute-start.51
  346.0 5.0 %collective-permute-done.52 = bf16[1,4,256,128]{3,2,1,0:T(8,128)(2,1)S(1)} collective-permute-done((bf16[1,4,256,128]{3,2,1,0:T(8,128)(2,1)S(1)}, bf16[1,4,256,128]{3,2,1,0:T(8,128)(2,1)S(1)}, u32[]{:S(2)}, u32[]{:S(2)}) %collective-permute-start.52) | collective-permute-done | bytes 262176 | tf_op jit(solution)/shard_map/ppermute | solution.py:871
  (318 shorter events, 122.9 us)
Async XLA Ops:
  6.5 28.6 %all-to-all-start = ((bf16[8,48,1024]{2,1,0:T(8,128)(2,1)}), bf16[8,48,1024]{2,1,0:T(8,128)(2,1)S(1)}, u32[]{:S(2)}, u32[]{:S(2)}) async-start(bf16[8,48,1024]{2,1,0:T(8,128)(2,1)} %bitcast.83), calls=%async_computation | async-start | bytes 1572864 | tf_op jit(solution)/shard_map/all_to_all | solution.py:854
  36.7 19.9 %collective-permute-start.2 = (bf16[384,1024]{1,0:T(8,128)(2,1)S(1)}, bf16[384,1024]{1,0:T(8,128)(2,1)}, u32[]{:S(2)}, u32[]{:S(2)}) collective-permute-start(bf16[384,1024]{1,0:T(8,128)(2,1)S(1)} %first_norm.1.refs_9_.refs_2_), channel_id=1, source_target_pairs={{0,8},{4,12},{8,0},{12,4},{1,9},{5,13},{9,1},{13,5},{2,10},{6,14},... | collective-permute-start | bytes 2359304 | tf_op jit(solution)/shard_map/ppermute | solution.py:871
  42.7 26.8 %collective-permute-start.1 = (bf16[384,1024]{1,0:T(8,128)(2,1)S(1)}, bf16[384,1024]{1,0:T(8,128)(2,1)}, u32[]{:S(2)}, u32[]{:S(2)}) collective-permute-start(bf16[384,1024]{1,0:T(8,128)(2,1)S(1)} %first_norm.1.refs_9_.refs_2_), channel_id=1, source_target_pairs={{0,4},{4,0},{8,12},{12,8},{1,5},{5,1},{9,13},{13,9},{2,6},{6,2},{1... | collective-permute-start | bytes 2359304 | tf_op jit(solution)/shard_map/ppermute | solution.py:871
  59.5 39.2 %all-to-all-start.2 = ((bf16[8,48,1024]{2,1,0:T(8,128)(2,1)}), bf16[8,48,1024]{2,1,0:T(8,128)(2,1)S(1)}, u32[]{:S(2)}, u32[]{:S(2)}) async-start(bf16[8,48,1024]{2,1,0:T(8,128)(2,1)} %bitcast.82), calls=%async_computation.2 | async-start | bytes 1572864 | tf_op jit(solution)/shard_map/all_to_all | solution.py:854
  65.9 31.2 %collective-permute-start.7 = (bf16[528,256]{1,0:T(8,128)(2,1)}, bf16[528,256]{1,0:T(8,128)(2,1)S(1)}, u32[]{:S(2)}, u32[]{:S(2)}) collective-permute-start(bf16[528,256]{1,0:T(8,128)(2,1)} %copy-done.55), channel_id=1, source_target_pairs={{0,1},{1,0},{2,3},{3,2},{4,5},{5,4},{6,7},{7,6},{8,9},{9,8},{10,11... | collective-permute-start | bytes 811016 | tf_op jit(solution)/shard_map/ppermute | solution.py:871
  68.0 29.2 %collective-permute-start.9 = (bf16[528,256]{1,0:T(8,128)(2,1)}, bf16[528,256]{1,0:T(8,128)(2,1)S(1)}, u32[]{:S(2)}, u32[]{:S(2)}) collective-permute-start(bf16[528,256]{1,0:T(8,128)(2,1)} %copy-done.55), channel_id=1, source_target_pairs={{0,16},{16,0},{1,17},{17,1},{2,18},{18,2},{3,19},{19,3},{4,20},{20... | collective-permute-start | bytes 811016 | tf_op jit(solution)/shard_map/ppermute | solution.py:871
  69.5 27.7 %collective-permute-start.11 = (bf16[256,512]{1,0:T(8,128)(2,1)S(1)}, bf16[256,512]{1,0:T(8,128)(2,1)S(1)}, u32[]{:S(2)}, u32[]{:S(2)}) collective-permute-start(bf16[256,512]{1,0:T(8,128)(2,1)S(1)} %dynamic_slice.42.refs_9_), channel_id=1, source_target_pairs={{0,2},{1,3},{2,0},{3,1},{4,6},{5,7},{6,4},{7,5},{8,10},{9,11},{10,... | collective-permute-start | bytes 786440 | tf_op jit(solution)/shard_map/ppermute | solution.py:871
  71.8 25.3 %collective-permute-start.12 = (bf16[256,512]{1,0:T(8,128)(2,1)S(1)}, bf16[256,512]{1,0:T(8,128)(2,1)S(1)}, u32[]{:S(2)}, u32[]{:S(2)}) collective-permute-start(bf16[256,512]{1,0:T(8,128)(2,1)S(1)} %dynamic_slice.42.refs_9_), channel_id=1, source_target_pairs={{0,16},{16,0},{1,17},{17,1},{2,18},{18,2},{3,19},{19,3},{4,20},{20... | collective-permute-start | bytes 786440 | tf_op jit(solution)/shard_map/ppermute | solution.py:871
  72.4 24.7 %collective-permute-start.8 = (bf16[528,256]{1,0:T(8,128)(2,1)}, bf16[528,256]{1,0:T(8,128)(2,1)S(1)}, u32[]{:S(2)}, u32[]{:S(2)}) collective-permute-start(bf16[528,256]{1,0:T(8,128)(2,1)} %copy-done.54), channel_id=1, source_target_pairs={{0,16},{16,0},{1,17},{17,1},{2,18},{18,2},{3,19},{19,3},{4,20},{20... | collective-permute-start | bytes 811016 | tf_op jit(solution)/shard_map/ppermute | solution.py:871
  102.4 19.6 %collective-permute-start.14 = (bf16[256,512]{1,0:T(8,128)(2,1)}, bf16[256,512]{1,0:T(8,128)(2,1)}, u32[]{:S(2)}, u32[]{:S(2)}) collective-permute-start(bf16[256,512]{1,0:T(8,128)(2,1)} %copy-done.61), channel_id=1, source_target_pairs={{0,1},{1,0},{2,3},{3,2},{4,5},{5,4},{6,7},{7,6},{8,9},{9,8},{10,11... | collective-permute-start | bytes 786440 | tf_op jit(solution)/shard_map/ppermute | solution.py:871
  102.5 19.5 %collective-permute-start.15 = (bf16[256,512]{1,0:T(8,128)(2,1)}, bf16[256,512]{1,0:T(8,128)(2,1)}, u32[]{:S(2)}, u32[]{:S(2)}) collective-permute-start(bf16[256,512]{1,0:T(8,128)(2,1)} %collective-permute-done.10.refs_10_), channel_id=1, source_target_pairs={{0,16},{16,0},{1,17},{17,1},{2,18},{18,2},{3,19},{19,3},{4,20},{20... | collective-permute-start | bytes 786440 | tf_op jit(solution)/shard_map/ppermute | solution.py:871
  104.0 18.5 %collective-permute-start.16 = (bf16[256,512]{1,0:T(8,128)(2,1)}, bf16[256,512]{1,0:T(8,128)(2,1)}, u32[]{:S(2)}, u32[]{:S(2)}) collective-permute-start(bf16[256,512]{1,0:T(8,128)(2,1)} %copy-done.61), channel_id=1, source_target_pairs={{0,16},{16,0},{1,17},{17,1},{2,18},{18,2},{3,19},{19,3},{4,20},{20... | collective-permute-start | bytes 786440 | tf_op jit(solution)/shard_map/ppermute | solution.py:871
  104.7 18.2 %collective-permute-start.13 = (bf16[528,256]{1,0:T(8,128)(2,1)S(1)}, bf16[528,256]{1,0:T(8,128)(2,1)S(1)}, u32[]{:S(2)}, u32[]{:S(2)}) collective-permute-start(bf16[528,256]{1,0:T(8,128)(2,1)S(1)} %collective-permute-done.7.refs_4_), channel_id=1, source_target_pairs={{0,16},{16,0},{1,17},{17,1},{2,18},{18,2},{3,19},{19,3},{4,20},{20... | collective-permute-start | bytes 811016 | tf_op jit(solution)/shard_map/ppermute | solution.py:871
  108.1 28.8 %collective-permute-start.22 = (bf16[384,1024]{1,0:T(8,128)(2,1)}, bf16[384,1024]{1,0:T(8,128)(2,1)}, u32[]{:S(2)}, u32[]{:S(2)}) collective-permute-start(bf16[384,1024]{1,0:T(8,128)(2,1)} %get-tuple-element.257.refs_5_.refs_9_), channel_id=1, source_target_pairs={{0,8},{4,12},{8,0},{12,4},{1,9},{5,13},{9,1},{13,5},{2,10},{6,14},... | collective-permute-start | bytes 2359304 | tf_op jit(solution)/shard_map/ppermute | solution.py:871
  124.3 28.3 %collective-permute-start.20 = (bf16[384,1024]{1,0:T(8,128)(2,1)S(1)}, bf16[384,1024]{1,0:T(8,128)(2,1)S(1)}, u32[]{:S(2)}, u32[]{:S(2)}) collective-permute-start(bf16[384,1024]{1,0:T(8,128)(2,1)S(1)} %get-tuple-element.253.refs_3_.refs_5_), channel_id=1, source_target_pairs={{0,8},{4,12},{8,0},{12,4},{1,9},{5,13},{9,1},{13,5},{2,10},{6,14},... | collective-permute-start | bytes 2359304 | tf_op jit(solution)/shard_map/ppermute | solution.py:871
  172.7 19.8 %collective-permute-start.27 = (bf16[384,1024]{1,0:T(8,128)(2,1)S(1)}, bf16[384,1024]{1,0:T(8,128)(2,1)S(1)}, u32[]{:S(2)}, u32[]{:S(2)}) collective-permute-start(bf16[384,1024]{1,0:T(8,128)(2,1)S(1)} %add_convert_fusion.2), channel_id=1, source_target_pairs={{0,8},{4,12},{8,0},{12,4},{1,9},{5,13},{9,1},{13,5},{2,10},{6,14},... | collective-permute-start | bytes 2359304 | tf_op jit(solution)/shard_map/ppermute | solution.py:871
  174.0 17.6 %collective-permute-start.26 = (bf16[384,1024]{1,0:T(8,128)(2,1)S(1)}, bf16[384,1024]{1,0:T(8,128)(2,1)S(1)}, u32[]{:S(2)}, u32[]{:S(2)}) collective-permute-start(bf16[384,1024]{1,0:T(8,128)(2,1)S(1)} %get-tuple-element.280), channel_id=1, source_target_pairs={{0,4},{4,0},{8,12},{12,8},{1,5},{5,1},{9,13},{13,9},{2,6},{6,2},{1... | collective-permute-start | bytes 2359304 | tf_op jit(solution)/shard_map/ppermute | solution.py:871
  174.0 39.3 %collective-permute-start.28 = (bf16[384,1024]{1,0:T(8,128)(2,1)S(1)}, bf16[384,1024]{1,0:T(8,128)(2,1)}, u32[]{:S(2)}, u32[]{:S(2)}) collective-permute-start(bf16[384,1024]{1,0:T(8,128)(2,1)S(1)} %get-tuple-element.283), channel_id=1, source_target_pairs={{0,4},{4,0},{8,12},{12,8},{1,5},{5,1},{9,13},{13,9},{2,6},{6,2},{1... | collective-permute-start | bytes 2359304 | tf_op jit(solution)/shard_map/ppermute | solution.py:871
  188.8 24.8 %collective-permute-start.29 = (bf16[384,1024]{1,0:T(8,128)(2,1)}, bf16[384,1024]{1,0:T(8,128)(2,1)}, u32[]{:S(2)}, u32[]{:S(2)}) collective-permute-start(bf16[384,1024]{1,0:T(8,128)(2,1)} %get-tuple-element.284), channel_id=1, source_target_pairs={{0,8},{4,12},{8,0},{12,4},{1,9},{5,13},{9,1},{13,5},{2,10},{6,14},... | collective-permute-start | bytes 2359304 | tf_op jit(solution)/shard_map/ppermute | solution.py:871
  190.2 25.7 %collective-permute-start.31 = (bf16[4,4,128,256]{3,2,1,0:T(8,128)(2,1)}, bf16[4,4,128,256]{3,2,1,0:T(8,128)(2,1)}, u32[]{:S(2)}, u32[]{:S(2)}) collective-permute-start(bf16[4,4,128,256]{3,2,1,0:T(8,128)(2,1)} %get-tuple-element.287), channel_id=1, source_target_pairs={{0,16},{16,0},{1,17},{17,1},{2,18},{18,2},{3,19},{19,3},{4,20},{20... | collective-permute-start | bytes 3145736 | tf_op jit(solution)/shard_map/ppermute | solution.py:871
  211.8 45.6 %collective-permute-start.32 = (bf16[4,4,128,256]{3,2,1,0:T(8,128)(2,1)}, bf16[4,4,128,256]{3,2,1,0:T(8,128)(2,1)}, u32[]{:S(2)}, u32[]{:S(2)}) collective-permute-start(bf16[4,4,128,256]{3,2,1,0:T(8,128)(2,1)} %get-tuple-element.301), channel_id=1, source_target_pairs={{0,16},{16,0},{1,17},{17,1},{2,18},{18,2},{3,19},{19,3},{4,20},{20... | collective-permute-start | bytes 3145736 | tf_op jit(solution)/shard_map/ppermute | solution.py:871
  213.4 44.1 %collective-permute-start.34 = (bf16[2,4,256,128]{3,2,1,0:T(8,128)(2,1)S(1)}, bf16[2,4,256,128]{3,2,1,0:T(8,128)(2,1)}, u32[]{:S(2)}, u32[]{:S(2)}) collective-permute-start(bf16[2,4,256,128]{3,2,1,0:T(8,128)(2,1)S(1)} %get-tuple-element.305), channel_id=1, source_target_pairs={{0,4},{4,0},{8,12},{12,8},{1,5},{5,1},{9,13},{13,9},{2,6},{6,2},{1... | collective-permute-start | bytes 1572872 | tf_op jit(solution)/shard_map/ppermute | solution.py:871
  223.9 33.6 %collective-permute-start.33 = (bf16[2,4,128,256]{3,2,1,0:T(8,128)(2,1)}, bf16[2,4,128,256]{3,2,1,0:T(8,128)(2,1)S(1)}, u32[]{:S(2)}, u32[]{:S(2)}) collective-permute-start(bf16[2,4,128,256]{3,2,1,0:T(8,128)(2,1)} %get-tuple-element.303), channel_id=1, source_target_pairs={{0,1},{1,0},{2,3},{3,2},{4,5},{5,4},{6,7},{7,6},{8,9},{9,8},{10,11... | collective-permute-start | bytes 1572872 | tf_op jit(solution)/shard_map/ppermute | solution.py:871
  225.3 32.2 %collective-permute-start.35 = (bf16[2,4,256,128]{3,2,1,0:T(8,128)(2,1)}, bf16[2,4,256,128]{3,2,1,0:T(8,128)(2,1)}, u32[]{:S(2)}, u32[]{:S(2)}) collective-permute-start(bf16[2,4,256,128]{3,2,1,0:T(8,128)(2,1)} %get-tuple-element.306), channel_id=1, source_target_pairs={{0,8},{4,12},{8,0},{12,4},{1,9},{5,13},{9,1},{13,5},{2,10},{6,14},... | collective-permute-start | bytes 1572872 | tf_op jit(solution)/shard_map/ppermute | solution.py:871
  225.8 31.7 %all-to-all-start.4 = ((bf16[8,48,1024]{2,1,0:T(8,128)(2,1)}), bf16[8,48,1024]{2,1,0:T(8,128)(2,1)}, u32[]{:S(2)}, u32[]{:S(2)}) async-start(bf16[8,48,1024]{2,1,0:T(8,128)(2,1)} %bitcast.16), calls=%async_computation.4 | async-start | bytes 1572864 | tf_op jit(solution)/shard_map/all_to_all | solution.py:854
  257.6 29.6 %collective-permute-start.40 = (bf16[384,1024]{1,0:T(8,128)(2,1)}, bf16[384,1024]{1,0:T(8,128)(2,1)S(1)}, u32[]{:S(2)}, u32[]{:S(2)}) collective-permute-start(bf16[384,1024]{1,0:T(8,128)(2,1)} %get-tuple-element.338), channel_id=1, source_target_pairs={{0,4},{4,0},{8,12},{12,8},{1,5},{5,1},{9,13},{13,9},{2,6},{6,2},{1... | collective-permute-start | bytes 2359304 | tf_op jit(solution)/shard_map/ppermute | solution.py:871
  261.3 25.9 %collective-permute-start.41 = (bf16[384,1024]{1,0:T(8,128)(2,1)}, bf16[384,1024]{1,0:T(8,128)(2,1)S(1)}, u32[]{:S(2)}, u32[]{:S(2)}) collective-permute-start(bf16[384,1024]{1,0:T(8,128)(2,1)} %add_convert_fusion.1), channel_id=1, source_target_pairs={{0,8},{4,12},{8,0},{12,4},{1,9},{5,13},{9,1},{13,5},{2,10},{6,14},... | collective-permute-start | bytes 2359304 | tf_op jit(solution)/shard_map/ppermute | solution.py:871
  265.4 19.3 %collective-permute-start.38 = (bf16[2,4,128,256]{3,2,1,0:T(8,128)(2,1)S(1)}, bf16[2,4,128,256]{3,2,1,0:T(8,128)(2,1)S(1)}, u32[]{:S(2)}, u32[]{:S(2)}) collective-permute-start(bf16[2,4,128,256]{3,2,1,0:T(8,128)(2,1)S(1)} %get-tuple-element.320), channel_id=1, source_target_pairs={{0,1},{1,0},{2,3},{3,2},{4,5},{5,4},{6,7},{7,6},{8,9},{9,8},{10,11... | collective-permute-start | bytes 1572872 | tf_op jit(solution)/shard_map/ppermute | solution.py:871
  266.4 16.8 %collective-permute-start.39 = (bf16[1,4,128,256]{3,2,1,0:T(8,128)(2,1)S(1)}, bf16[1,4,128,256]{3,2,1,0:T(8,128)(2,1)S(1)}, u32[]{:S(2)}, u32[]{:S(2)}) collective-permute-start(bf16[1,4,128,256]{3,2,1,0:T(8,128)(2,1)S(1)} %get-tuple-element.331), channel_id=1, source_target_pairs={{0,2},{1,3},{2,0},{3,1},{4,6},{5,7},{6,4},{7,5},{8,10},{9,11},{10,... | collective-permute-start | bytes 786440 | tf_op jit(solution)/shard_map/ppermute | solution.py:871
  279.2 30.9 %collective-permute-start.37 = (bf16[4,4,256,128]{3,2,1,0:T(8,128)(2,1)}, bf16[4,4,256,128]{3,2,1,0:T(8,128)(2,1)}, u32[]{:S(2)}, u32[]{:S(2)}) collective-permute-start(bf16[4,4,256,128]{3,2,1,0:T(8,128)(2,1)} %get-tuple-element.326), channel_id=1, source_target_pairs={{0,16},{16,0},{1,17},{17,1},{2,18},{18,2},{3,19},{19,3},{4,20},{20... | collective-permute-start | bytes 3145736 | tf_op jit(solution)/shard_map/ppermute | solution.py:871
  299.0 33.1 %all-to-all-start.5 = ((bf16[8,48,1024]{2,1,0:T(8,128)(2,1)}), bf16[8,48,1024]{2,1,0:T(8,128)(2,1)}, u32[]{:S(2)}, u32[]{:S(2)}) async-start(bf16[8,48,1024]{2,1,0:T(8,128)(2,1)} %bitcast.20), calls=%async_computation.5 | async-start | bytes 1572864 | tf_op jit(solution)/shard_map/all_to_all | solution.py:854
  313.1 19.0 %collective-permute-start.44 = (bf16[2,4,256,128]{3,2,1,0:T(8,128)(2,1)}, bf16[2,4,256,128]{3,2,1,0:T(8,128)(2,1)}, u32[]{:S(2)}, u32[]{:S(2)}) collective-permute-start(bf16[2,4,256,128]{3,2,1,0:T(8,128)(2,1)} %get-tuple-element.463), channel_id=1, source_target_pairs={{0,1},{1,0},{2,3},{3,2},{4,5},{5,4},{6,7},{7,6},{8,9},{9,8},{10,11... | collective-permute-start | bytes 1572872 | tf_op jit(solution)/shard_map/ppermute | solution.py:871
  (91 other events, 815.8 us)

commit v7 on v6

--- a/solution.py
+++ b/solution.py
@@ -33,7 +33,7 @@
     return lax.dot_general(left, right, (dims, ((), ())), preferred_element_type=F32)
 
 
-def call(name, kernel, operands, specs, outs, scratch=(), limit=LIMIT, out_specs=None):
+def call(name, kernel, operands, specs, outs, scratch=(), limit=LIMIT, out_specs=None, late=None):
     out_specs = out_specs or tuple(HBM if o.size >= 65536 else VMEM for o in outs)
     n_in, n_out, n_scratch = len(specs), len(outs), len(scratch)
     staged_in = [i for i, spec in enumerate(specs) if spec is HBM]
@@ -55,11 +55,27 @@
         for place, i in enumerate(staged_out, len(staged_in)):
             backs.append(pltpu.make_async_copy(held[place], made[i], held[-1].at[place]))
             made[i] = held[place]
-        for copy in copies:
-            copy.wait()
-        kernel(*given, *made, *own)
-        for copy in backs:
-            copy.start()
+        last = [copy for copy, i in zip(copies, staged_in) if i in (late or ())]
+        for copy, i in zip(copies, staged_in):
+            if i not in (late or ()):
+                copy.wait()
+        sent = []
+
+        def wait_late():
+            for copy in last:
+                copy.wait()
+
+        def send(i):
+            backs[staged_out.index(i)].start()
+            sent.append(staged_out.index(i))
+
+        if late:
+            kernel(*given, *made, *own, wait_late=wait_late, send=send)
+        else:
+            kernel(*given, *made, *own)
+        for place, copy in enumerate(backs):
+            if place not in sent:
+                copy.start()
         for copy in backs:
             copy.wait()
 
@@ -601,7 +617,7 @@
 
 
 def middle_back_kernel(
-    dims, middle_ref, branch_ref, up_ref, mod_ref, item_ref, wp_ref, *refs
+    dims, middle_ref, branch_ref, up_ref, mod_ref, item_ref, wp_ref, *refs, wait_late, send
 ):
     parts, items, count, chunk = dims
     me_ref, attn_rows_ref = refs[0], refs[1]
@@ -630,22 +646,24 @@
         add_item_sums(sums_ref, 1, item, grad_in * normed, items)
         add_item_sums(sums_ref, 2, item, grad_in, items)
 
+    send(1)
+    send(2)
+    wait_late()
     attn[...] = dot(gb_ref[...], wp_ref[...], BY_ROW).astype(BF)
     for g in range(group):
         for p in range(parts):
             start = (p * group + g) * sub
             out_ref[g, :, p * sub : (p + 1) * sub] = attn[:, start : start + sub]
+    send(0)
     proj_weights_kernel(
         (group, chunk), me_ref, attn_rows_ref, gb_ref, *proj_refs, left_t, right
     )
 
 
 def output_kernel(dims, middle_ref, up_ref, mod_ref, item_ref, bias_ref, *refs):
-    items, count, proj_count, tile_count = dims
+    items, count, proj_count = dims
     terms, refs = refs[:count], refs[count:]
-    projs, refs = refs[:proj_count], refs[proj_count:]
-    tiles, (out_ref, sums_ref, proj_ref, kept_ref, sent_ref) = refs[:tile_count], refs[tile_count:]
-    add_blocks(tiles, (kept_ref, sent_ref))
+    projs, (out_ref, sums_ref, proj_ref) = refs[:proj_count], refs[proj_count:]
     proj_ref[...] = sum(proj[...].astype(F32) for proj in projs).astype(BF)
     rows, model = middle_ref.shape
     sums_ref[...] = jnp.zeros_like(sums_ref)
@@ -1278,24 +1296,31 @@
             pltpu.VMEM((model, rows), BF),
             pltpu.VMEM((rows, width), BF),
         ],
+        late=(5, 7),
     )
     inbound = over_group(outbound)
     up_terms, down_terms = xor_scatter(up_parts, "yy"), xor_scatter(down_parts, "yy")
     proj_terms, proj_last = to_last(proj_parts)
-    tied = tuple(out_terms) + tuple(proj_last) + tuple(up_terms)
+    tied = tuple(out_terms) + tuple(proj_last)
     half_tiles = shape_of((head_size // 2, group, fine, hidden), BF)
     quarter_tiles = shape_of((head_size // 4, group, fine, hidden), BF)
-    output_rows, output_sums, proj_sent, up_kept, up_sent = call(
+    output_rows, output_sums, proj_sent = call(
         "output",
-        functools.partial(
-            output_kernel, (items, len(out_terms), len(proj_last), len(up_terms))
-        ),
+        functools.partial(output_kernel, (items, len(out_terms), len(proj_last))),
         (middle, upstream, mod, row_item, fc2_bias[None, :], *tied),
         (HBM, HBM, VMEM, VMEM, VMEM) + (HBM,) * len(tied),
-        (rows_bf, shape_of((8, model), F32), shape_of(proj_last[0].shape, BF), half_tiles, half_tiles),
+        (rows_bf, shape_of((8, model), F32), shape_of(proj_last[0].shape, BF)),
+    )
+    up_terms = tie(*up_terms, output_rows)[:-1]
+    up_kept, up_sent = call(
+        "add",
+        functools.partial(add_kernel, (len(up_terms),)),
+        up_terms,
+        (HBM,) * len(up_terms),
+        (half_tiles, half_tiles),
     )
     up_terms = (up_kept, xor_swap(up_sent, "head", 1))
-    inbound, output_rows = tie(inbound, output_rows)
+    inbound, output_rows, _ = tie(inbound, output_rows, up_sent)
     output_back = to_packs(output_rows)
     proj_terms.append(xor_swap(proj_sent, "g", near))
     cols_f32 = pltpu.VMEM((pack_len, 128), F32)

time: 366 us -> 366 us (level)
  Pallas kernels: 145 us -> 149 us
  starting transfers between devices: 87.2 us -> 83.4 us
    pallas_call x26 -> x27, Pallas kernels: 145 us -> 149 us  [call(): pl.pallas_call(body, name=name, out_shape=tuple(outs), in_specs=[ANY if s...]
    unnamed x138 -> x144, local copies, waits for them, and re-layouts: 20.5 us -> 20.9 us
  transfers between devices with their start and end apart: 59 -> 59, of which waited for: 25 -> 22; matrix products, arithmetic and copies ran while one was open for 8% -> 8% of each run, Pallas kernels for 35% -> 36%
where the time goes in v7:
time: 366 us; the launch traced here: 359 us
  Pallas kernels  149 us (41%)
  starting transfers between devices  83.4 us (23%)
  waiting for transfers between devices  70.5 us (19%)
  local copies, waits for them, and re-layouts  32.2 us (9%)
  matrix products  11.9 us (3%)
  other arithmetic  10.6 us (3%)
    pallas_call x27, Pallas kernels, call(): pl.pallas_call(body, name=name, out_shape=tuple(outs), in_specs=[ANY if s...  149 us
    ppermute x49, waiting for transfers between devices, xor_swap(): return lax.ppermute(values, axis, [(i, i ^ step) for i in range(size)])  57.7 us
    ppermute x49, starting transfers between devices, xor_swap(): return lax.ppermute(values, axis, [(i, i ^ step) for i in range(size)])  50.1 us
    all_to_all x4, starting transfers between devices, to_packs(): lax.all_to_all(rows, ('yy', 'head'), split_axis=0, concat_axis=0, tiled=T...  22.9 us
    unnamed x144, local copies, waits for them, and re-layouts  20.9 us
    all_to_all x2, starting transfers between devices, over_group(): return lax.all_to_all(blocks, 'g', split_axis=0, concat_axis=0, tiled=True)  7.86 us
  transfers between devices with their start and end apart: 59, of which 22 were waited for; matrix products, arithmetic and copies ran while one was open for 8% of the time, Pallas kernels for 36%

profile of v7, /device:TPU:0, one launch (start us, length us, event | category | flops | bytes accessed | tf_op | source)
XLA Modules:
  0.0 359.4 jit_solution(3626903735103541106)
XLA Ops:
  2.1 4.4 %sort.1 = (bf16[384,384]{1,0:T(8,128)(2,1)}, bf16[384,1024]{1,0:T(8,128)(2,1)}, bf16[384,1024]{1,0:T(8,128)(2,1)}) custom-call(s32[1,384]{1,0:T(1,128)} %broadcast_in_dim.123.refs_0_, bf16[384,1024]{1,0:T(8,128)(2,1)} %refs_1_.2, bf16[384,1024]{1,0:T(8,128)(2,1)} %refs_2_.2), custom_call_target="tpu_custom_call" | custom-call | flops 2000000000 | bytes 6000001 | tf_op jit(solution)/shard_map/sort/pallas_call | solution.py:83
  6.5 7.3 %all-to-all-start = ((bf16[8,48,1024]{2,1,0:T(8,128)(2,1)}), bf16[8,48,1024]{2,1,0:T(8,128)(2,1)S(1)}, u32[]{:S(2)}, u32[]{:S(2)}) async-start(bf16[8,48,1024]{2,1,0:T(8,128)(2,1)} %bitcast.83), calls=%async_computation | async-start | bytes 1572864 | tf_op jit(solution)/shard_map/all_to_all | solution.py:872
  18.1 6.4 %convolution_add_fusion.refs_1_.refs_4_.refs_3_.refs_2_ = f32[4,6144]{1,0:T(4,128)S(1)} fusion(bf16[1024,6144]{1,0:T(8,128)(2,1)} %param.22, f32[6144]{0:T(1024)S(1)} %convert_element_type.84, f32[32,1024]{1,0:T(8,128)S(1)} %select_convert_fusion, s32[]{:T(128)S(6)} %select_n.97), kind=kOutput, calls=%fused_computation.4 | convolution fusion | flops 50376704 | bytes 12722180 | tf_op jit(solution)/shard_map/dot_general | solution.py:1081
  30.4 4.6 %all-to-all-done = bf16[8,48,1024]{2,1,0:T(8,128)(2,1)S(1)} async-done(((bf16[8,48,1024]{2,1,0:T(8,128)(2,1)}), bf16[8,48,1024]{2,1,0:T(8,128)(2,1)S(1)}, u32[]{:S(2)}, u32[]{:S(2)}) %all-to-all-start) | async-done | bytes 786464 | tf_op jit(solution)/shard_map/all_to_all | solution.py:872
  36.7 4.5 %collective-permute-start.2 = (bf16[384,1024]{1,0:T(8,128)(2,1)S(1)}, bf16[384,1024]{1,0:T(8,128)(2,1)}, u32[]{:S(2)}, u32[]{:S(2)}) collective-permute-start(bf16[384,1024]{1,0:T(8,128)(2,1)S(1)} %first_norm.1.refs_9_.refs_2_), channel_id=1, source_target_pairs={{0,8},{4,12},{8,0},{12,4},{1,9},{5,13},{9,1},{13,5},{2,10},{6,14},... | collective-permute-start | bytes 2359304 | tf_op jit(solution)/shard_map/ppermute | solution.py:889
  43.1 9.2 %collective-permute-done.3.refs_2_ = bf16[528,256]{1,0:T(8,128)(2,1)S(1)} collective-permute-done((bf16[528,256]{1,0:T(8,128)(2,1)S(1)}, bf16[528,256]{1,0:T(8,128)(2,1)S(1)}, u32[]{:S(2)}, u32[]{:S(2)}) %collective-permute-start.3) | collective-permute-done | bytes 270368 | tf_op jit(solution)/shard_map/ppermute | solution.py:889
  59.5 6.4 %all-to-all-start.2 = ((bf16[8,48,1024]{2,1,0:T(8,128)(2,1)}), bf16[8,48,1024]{2,1,0:T(8,128)(2,1)S(1)}, u32[]{:S(2)}, u32[]{:S(2)}) async-start(bf16[8,48,1024]{2,1,0:T(8,128)(2,1)} %bitcast.82), calls=%async_computation.2 | async-start | bytes 1572864 | tf_op jit(solution)/shard_map/all_to_all | solution.py:872
  73.9 22.0 %attend.1 = (bf16[4,384,256]{2,1,0:T(8,128)(2,1)}, f32[256,1536]{1,0:T(8,128)}, f32[8,1536]{1,0:T(8,128)}, bf16[1536,256]{1,0:T(8,128)(2,1)}, bf16[1536,256]{1,0...) custom-call(s32[4]{0:T(128)} %pad_add_fusion.refs_0_.refs_6_, ...), custom_call_target="tpu_custom_call" | custom-call | flops 26000001024 | bytes 78000000 | tf_op jit(solution)/shard_map/attend/pallas_call | solution.py:83
  98.8 3.7 %all-to-all-start.1 = ((bf16[4,384,256]{2,1,0:T(8,128)(2,1)}), bf16[4,384,256]{2,1,0:T(8,128)(2,1)S(1)}, u32[]{:S(2)}, u32[]{:S(2)}) async-start(bf16[4,384,256]{2,1,0:T(8,128)(2,1)} %get-tuple-element.223), calls=%async_computation.1 | async-start | bytes 1572864 | tf_op jit(solution)/shard_map/all_to_all | solution.py:876
  110.1 4.4 %all-to-all-done.1.refs_0_ = bf16[4,384,256]{2,1,0:T(8,128)(2,1)S(1)} async-done(((bf16[4,384,256]{2,1,0:T(8,128)(2,1)}), bf16[4,384,256]{2,1,0:T(8,128)(2,1)S(1)}, u32[]{:S(2)}, u32[]{:S(2)}) %all-to-all-start.1) | async-done | bytes 786464 | tf_op jit(solution)/shard_map/all_to_all | solution.py:876
  116.1 3.9 %project.1 = (bf16[384,1024]{1,0:T(8,128)(2,1)S(1)}, bf16[384,1024]{1,0:T(8,128)(2,1)S(1)}, f32[384,1024]{1,0:T(8,128)S(1)}, bf16[384,1024]{1,0:T(8,128)(2,1)S(1)}) custom-call(bf16[4,384,256]{2,1,0:T(8,128)(2,1)S(1)} %all-to-all-done.1.refs_0_, bf16[1024,1024]{1,0:T(8,128)(2,1)S(1)} %copy-done.2, bf16[1,1024]{1,0:T(2,128)(2,1)S(1)} %broadcast_in_dim.139.refs_2_, ...), custom_call_target="tpu_custom_call" | custom-call | flops 1 | bytes 1 | tf_op jit(solution)/shard_map/project/pallas_call | solution.py:83
  126.0 5.1 %collective-permute-done.17.refs_16_ = bf16[256,512]{1,0:T(8,128)(2,1)S(1)} collective-permute-done((bf16[256,512]{1,0:T(8,128)(2,1)}, bf16[256,512]{1,0:T(8,128)(2,1)S(1)}, u32[]{:S(2)}, u32[]{:S(2)}) %collective-permute-start.17) | collective-permute-done | bytes 262176 | tf_op jit(solution)/shard_map/ppermute | solution.py:889
  131.8 5.0 %weights.1 = (bf16[1024,1024]{1,0:T(8,128)(2,1)}, bf16[1024,1024]{1,0:T(8,128)(2,1)}, f32[1,1024]{1,0:T(1,128)}) custom-call(s32[4]{0:T(128)} %pad_add_fusion.refs_0_.refs_6_, bf16[528,256]{1,0:T(8,128)(2,1)} %copy-done.38, bf16[528,256]{1,0:T(8,128)(2,1)} %copy-done.57, bf16[528,256]{1,0:T(8,128)(2,1)} %copy-done.58, bf16[528,256]{1,0:T(8,128)(2,1)} %copy-done.60, ...), custom_call_target="tpu_custom_call" | custom-call | flops 4000000000 | bytes 12000001 | tf_op jit(solution)/shard_map/weights/pallas_call | solution.py:83
  138.8 13.0 %feed.2 = (bf16[384,1024]{1,0:T(8,128)(2,1)S(1)}, bf16[384,1024]{1,0:T(8,128)(2,1)S(1)}, bf16[384,1024]{1,0:T(8,128)(2,1)S(1)}, bf16[384,1024]{1,0:T(8,128)(2,1)...) custom-call(bf16[1024,1024]{1,0:T(8,128)(2,1)} %get-tuple-element.252.refs_0_, ...), custom_call_target="tpu_custom_call" | custom-call | flops 12000000000 | bytes 36000000 | tf_op jit(solution)/shard_map/feed/pallas_call | solution.py:83
  156.0 13.6 %feed.3 = (bf16[384,1024]{1,0:T(8,128)(2,1)S(1)}, bf16[384,1024]{1,0:T(8,128)(2,1)S(1)}, bf16[384,1024]{1,0:T(8,128)(2,1)S(1)}, bf16[384,1024]{1,0:T(8,128)(2,1)...) custom-call(bf16[1024,1024]{1,0:T(8,128)(2,1)} %get-tuple-element.252.refs_0_, ...), custom_call_target="tpu_custom_call" | custom-call | flops 12000000000 | bytes 36000000 | tf_op jit(solution)/shard_map/feed/pallas_call | solution.py:83
  175.6 13.2 %feed_weights.1 = (bf16[4,4,128,256]{3,2,1,0:T(8,128)(2,1)}, bf16[4,4,128,256]{3,2,1,0:T(8,128)(2,1)}, bf16[4,4,128,256]{3,2,1,0:T(8,128)(2,1)}, bf16[4,4,128,256]{3,2,1,0:T(8,128)(2,1)}, bf16[384,1024]{1,0:T(8,128)(2,1)}) custom-call(s32[4]{0:T(128)} %pad_add_fusion.refs_0_.refs_6_, bf16[768,1024]{1,0:T(8,128)(2,1)} %get-tuple-element.265.refs_1_, ...), custom_call_target="tpu_custom_call" | custom-call | flops 12000000000 | bytes 36000000 | tf_op jit(solution)/shard_map/feed_weights/pallas_call | solution.py:83
  193.5 12.0 %middle_back.1 = (bf16[4,384,256]{2,1,0:T(8,128)(2,1)}, bf16[384,1024]{1,0:T(8,128)(2,1)}, f32[384,1024]{1,0:T(8,128)}, f32[8,3072]{1,0:T(8,128)S(1)}, f32[8,102...) custom-call(f32[384,1024]{1,0:T(8,128)} %copy-done.8, ...), custom_call_target="tpu_custom_call" | custom-call | flops 7000000000 | bytes 21000000 | tf_op jit(solution)/shard_map/middle_back/pallas_call | solution.py:83
  207.9 4.2 %all-to-all-start.3 = ((bf16[4,384,256]{2,1,0:T(8,128)(2,1)}), bf16[4,384,256]{2,1,0:T(8,128)(2,1)}, u32[]{:S(2)}, u32[]{:S(2)}) async-start(bf16[4,384,256]{2,1,0:T(8,128)(2,1)} %get-tuple-element.283), calls=%async_computation.3 | async-start | bytes 1572864 | tf_op jit(solution)/shard_map/all_to_all | solution.py:876
  214.9 4.8 %output.1 = (bf16[384,1024]{1,0:T(8,128)(2,1)}, f32[8,1024]{1,0:T(8,128)S(1)}, bf16[2,4,256,128]{3,2,1,0:T(8,128)(2,1)S(1)}) custom-call(f32[384,1024]{1,0:T(8,128)} %copy-done.8, bf16[384,1024]{1,0:T(8,128)(2,1)S(1)} %bitcast.78, f32[4,6144]{1,0:T(4,128)S(1)} %convolution_add_fusion.refs_1_.refs_4_.refs_3_.refs_2_, ...), custom_call_target="tpu_custom_call" | custom-call | flops 3000000000 | bytes 9000001 | tf_op jit(solution)/shard_map/output/pallas_call | solution.py:83
  226.1 4.4 %all-to-all-start.4 = ((bf16[8,48,1024]{2,1,0:T(8,128)(2,1)}), bf16[8,48,1024]{2,1,0:T(8,128)(2,1)}, u32[]{:S(2)}, u32[]{:S(2)}) async-start(bf16[8,48,1024]{2,1,0:T(8,128)(2,1)} %bitcast.16), calls=%async_computation.4 | async-start | bytes 1572864 | tf_op jit(solution)/shard_map/all_to_all | solution.py:872
  230.5 29.2 %attend_back.1 = (bf16[384,1024]{1,0:T(8,128)(2,1)}, bf16[384,1024]{1,0:T(8,128)(2,1)}, bf16[384,1024]{1,0:T(8,128)(2,1)}, bf16[384,1024]{1,0:T(8,128)(2,1)}, bf...) custom-call(s32[4]{0:T(128)} %pad_add_fusion.refs_0_.refs_6_, f32[1,256]{1,0:T(1,128)} %broadcast_in_dim_reshape.2.refs_5_.refs_1_, ...), custom_call_target="tpu_custom_call" | custom-call | flops 34000001024 | bytes 102000000 | tf_op jit(solution)/shard_map/attend_back/pallas_call | solution.py:83
  268.8 9.5 %qkv_weights.1 = (bf16[4,4,256,128]{3,2,1,0:T(8,128)(2,1)}, bf16[4,4,256,128]{3,2,1,0:T(8,128)(2,1)}) custom-call(s32[4]{0:T(128)} %pad_add_fusion.refs_0_.refs_6_, bf16[1536,768]{1,0:T(8,128)(2,1)} %get-tuple-element.325.refs_1_, bf16[384,1024]{1,0:T(8,128)(2,1)} %copy-done.9, bf16[384,1024]{1,0:T(8,128)(2,1)} %collective-permute-done.1.refs_10_.refs_3_, ...), custom_call_target="tpu_custom_call" | custom-call | flops 8000000000 | bytes 24000000 | tf_op jit(solution)/shard_map/qkv_weights/pallas_call | solution.py:83
  278.4 2.5 collective-permute-start.37
  280.8 2.6 collective-permute-done.39.refs_1_
  287.5 4.4 %tokens_back.1 = (bf16[384,1024]{1,0:T(8,128)(2,1)}, f32[8,2048]{1,0:T(8,128)S(1)}) custom-call(bf16[384,1024]{1,0:T(8,128)(2,1)S(1)} %bitcast.75, f32[384,1024]{1,0:T(8,128)S(1)} %copy-done.24, f32[4,6144]{1,0:T(4,128)S(1)} %convolution_add_fusion.refs_1_.refs_4_.refs_3_.refs_2_, s32[384,1]{1,0:T(8,128)S(1)} %broadcast_in_dim.143.refs_2_.refs_5_.refs_4_.refs_3_, ...), custom_call_target="tpu_custom_call" | custom-call | flops 5000000000 | bytes 15000001 | tf_op jit(solution)/shard_map/tokens_back/pallas_call | solution.py:83
  292.7 7.5 %collective-permute-done.45.refs_3_ = bf16[1,4,128,256]{3,2,1,0:T(8,128)(2,1)S(1)} collective-permute-done((bf16[1,4,128,256]{3,2,1,0:T(8,128)(2,1)S(1)}, bf16[1,4,128,256]{3,2,1,0:T(8,128)(2,1)S(1)}, u32[]{:S(2)}, u32[]{:S(2)}) %collective-permute-start.45) | collective-permute-done | bytes 262176 | tf_op jit(solution)/shard_map/ppermute | solution.py:889
  300.2 4.9 %all-to-all-start.5 = ((bf16[8,48,1024]{2,1,0:T(8,128)(2,1)}), bf16[8,48,1024]{2,1,0:T(8,128)(2,1)}, u32[]{:S(2)}, u32[]{:S(2)}) async-start(bf16[8,48,1024]{2,1,0:T(8,128)(2,1)} %bitcast.20), calls=%async_computation.5 | async-start | bytes 1572864 | tf_op jit(solution)/shard_map/all_to_all | solution.py:872
  306.9 3.4 collective-permute-done.43.refs_1_
  318.3 2.6 convolution_convert_fusion
  324.7 9.0 %collective-permute-done.44 = bf16[2,4,256,128]{3,2,1,0:T(8,128)(2,1)} collective-permute-done((bf16[2,4,256,128]{3,2,1,0:T(8,128)(2,1)}, bf16[2,4,256,128]{3,2,1,0:T(8,128)(2,1)}, u32[]{:S(2)}, u32[]{:S(2)}) %collective-permute-start.44) | collective-permute-done | bytes 524320 | tf_op jit(solution)/shard_map/ppermute | solution.py:889
  338.4 2.9 fusion.22
  345.6 5.6 %collective-permute-done.52 = bf16[1,4,256,128]{3,2,1,0:T(8,128)(2,1)S(1)} collective-permute-done((bf16[1,4,256,128]{3,2,1,0:T(8,128)(2,1)S(1)}, bf16[1,4,256,128]{3,2,1,0:T(8,128)(2,1)S(1)}, u32[]{:S(2)}, u32[]{:S(2)}) %collective-permute-start.52) | collective-permute-done | bytes 262176 | tf_op jit(solution)/shard_map/ppermute | solution.py:889
  (325 shorter events, 121.6 us)
Async XLA Ops:
  6.5 28.6 %all-to-all-start = ((bf16[8,48,1024]{2,1,0:T(8,128)(2,1)}), bf16[8,48,1024]{2,1,0:T(8,128)(2,1)S(1)}, u32[]{:S(2)}, u32[]{:S(2)}) async-start(bf16[8,48,1024]{2,1,0:T(8,128)(2,1)} %bitcast.83), calls=%async_computation | async-start | bytes 1572864 | tf_op jit(solution)/shard_map/all_to_all | solution.py:872
  36.7 19.9 %collective-permute-start.2 = (bf16[384,1024]{1,0:T(8,128)(2,1)S(1)}, bf16[384,1024]{1,0:T(8,128)(2,1)}, u32[]{:S(2)}, u32[]{:S(2)}) collective-permute-start(bf16[384,1024]{1,0:T(8,128)(2,1)S(1)} %first_norm.1.refs_9_.refs_2_), channel_id=1, source_target_pairs={{0,8},{4,12},{8,0},{12,4},{1,9},{5,13},{9,1},{13,5},{2,10},{6,14},... | collective-permute-start | bytes 2359304 | tf_op jit(solution)/shard_map/ppermute | solution.py:889
  42.7 26.8 %collective-permute-start.1 = (bf16[384,1024]{1,0:T(8,128)(2,1)S(1)}, bf16[384,1024]{1,0:T(8,128)(2,1)}, u32[]{:S(2)}, u32[]{:S(2)}) collective-permute-start(bf16[384,1024]{1,0:T(8,128)(2,1)S(1)} %first_norm.1.refs_9_.refs_2_), channel_id=1, source_target_pairs={{0,4},{4,0},{8,12},{12,8},{1,5},{5,1},{9,13},{13,9},{2,6},{6,2},{1... | collective-permute-start | bytes 2359304 | tf_op jit(solution)/shard_map/ppermute | solution.py:889
  59.5 39.2 %all-to-all-start.2 = ((bf16[8,48,1024]{2,1,0:T(8,128)(2,1)}), bf16[8,48,1024]{2,1,0:T(8,128)(2,1)S(1)}, u32[]{:S(2)}, u32[]{:S(2)}) async-start(bf16[8,48,1024]{2,1,0:T(8,128)(2,1)} %bitcast.82), calls=%async_computation.2 | async-start | bytes 1572864 | tf_op jit(solution)/shard_map/all_to_all | solution.py:872
  65.9 31.2 %collective-permute-start.7 = (bf16[528,256]{1,0:T(8,128)(2,1)}, bf16[528,256]{1,0:T(8,128)(2,1)S(1)}, u32[]{:S(2)}, u32[]{:S(2)}) collective-permute-start(bf16[528,256]{1,0:T(8,128)(2,1)} %copy-done.58), channel_id=1, source_target_pairs={{0,1},{1,0},{2,3},{3,2},{4,5},{5,4},{6,7},{7,6},{8,9},{9,8},{10,11... | collective-permute-start | bytes 811016 | tf_op jit(solution)/shard_map/ppermute | solution.py:889
  68.0 29.2 %collective-permute-start.9 = (bf16[528,256]{1,0:T(8,128)(2,1)}, bf16[528,256]{1,0:T(8,128)(2,1)S(1)}, u32[]{:S(2)}, u32[]{:S(2)}) collective-permute-start(bf16[528,256]{1,0:T(8,128)(2,1)} %copy-done.58), channel_id=1, source_target_pairs={{0,16},{16,0},{1,17},{17,1},{2,18},{18,2},{3,19},{19,3},{4,20},{20... | collective-permute-start | bytes 811016 | tf_op jit(solution)/shard_map/ppermute | solution.py:889
  69.5 27.7 %collective-permute-start.11 = (bf16[256,512]{1,0:T(8,128)(2,1)S(1)}, bf16[256,512]{1,0:T(8,128)(2,1)S(1)}, u32[]{:S(2)}, u32[]{:S(2)}) collective-permute-start(bf16[256,512]{1,0:T(8,128)(2,1)S(1)} %dynamic_slice.42.refs_9_), channel_id=1, source_target_pairs={{0,2},{1,3},{2,0},{3,1},{4,6},{5,7},{6,4},{7,5},{8,10},{9,11},{10,... | collective-permute-start | bytes 786440 | tf_op jit(solution)/shard_map/ppermute | solution.py:889
  71.8 25.3 %collective-permute-start.12 = (bf16[256,512]{1,0:T(8,128)(2,1)S(1)}, bf16[256,512]{1,0:T(8,128)(2,1)S(1)}, u32[]{:S(2)}, u32[]{:S(2)}) collective-permute-start(bf16[256,512]{1,0:T(8,128)(2,1)S(1)} %dynamic_slice.42.refs_9_), channel_id=1, source_target_pairs={{0,16},{16,0},{1,17},{17,1},{2,18},{18,2},{3,19},{19,3},{4,20},{20... | collective-permute-start | bytes 786440 | tf_op jit(solution)/shard_map/ppermute | solution.py:889
  72.4 24.7 %collective-permute-start.8 = (bf16[528,256]{1,0:T(8,128)(2,1)}, bf16[528,256]{1,0:T(8,128)(2,1)S(1)}, u32[]{:S(2)}, u32[]{:S(2)}) collective-permute-start(bf16[528,256]{1,0:T(8,128)(2,1)} %copy-done.57), channel_id=1, source_target_pairs={{0,16},{16,0},{1,17},{17,1},{2,18},{18,2},{3,19},{19,3},{4,20},{20... | collective-permute-start | bytes 811016 | tf_op jit(solution)/shard_map/ppermute | solution.py:889
  102.4 19.6 %collective-permute-start.14 = (bf16[256,512]{1,0:T(8,128)(2,1)}, bf16[256,512]{1,0:T(8,128)(2,1)}, u32[]{:S(2)}, u32[]{:S(2)}) collective-permute-start(bf16[256,512]{1,0:T(8,128)(2,1)} %copy-done.64), channel_id=1, source_target_pairs={{0,1},{1,0},{2,3},{3,2},{4,5},{5,4},{6,7},{7,6},{8,9},{9,8},{10,11... | collective-permute-start | bytes 786440 | tf_op jit(solution)/shard_map/ppermute | solution.py:889
  102.5 19.5 %collective-permute-start.15 = (bf16[256,512]{1,0:T(8,128)(2,1)}, bf16[256,512]{1,0:T(8,128)(2,1)}, u32[]{:S(2)}, u32[]{:S(2)}) collective-permute-start(bf16[256,512]{1,0:T(8,128)(2,1)} %collective-permute-done.10.refs_10_), channel_id=1, source_target_pairs={{0,16},{16,0},{1,17},{17,1},{2,18},{18,2},{3,19},{19,3},{4,20},{20... | collective-permute-start | bytes 786440 | tf_op jit(solution)/shard_map/ppermute | solution.py:889
  104.1 18.5 %collective-permute-start.16 = (bf16[256,512]{1,0:T(8,128)(2,1)}, bf16[256,512]{1,0:T(8,128)(2,1)}, u32[]{:S(2)}, u32[]{:S(2)}) collective-permute-start(bf16[256,512]{1,0:T(8,128)(2,1)} %copy-done.64), channel_id=1, source_target_pairs={{0,16},{16,0},{1,17},{17,1},{2,18},{18,2},{3,19},{19,3},{4,20},{20... | collective-permute-start | bytes 786440 | tf_op jit(solution)/shard_map/ppermute | solution.py:889
  104.7 18.2 %collective-permute-start.13 = (bf16[528,256]{1,0:T(8,128)(2,1)S(1)}, bf16[528,256]{1,0:T(8,128)(2,1)S(1)}, u32[]{:S(2)}, u32[]{:S(2)}) collective-permute-start(bf16[528,256]{1,0:T(8,128)(2,1)S(1)} %collective-permute-done.7.refs_4_), channel_id=1, source_target_pairs={{0,16},{16,0},{1,17},{17,1},{2,18},{18,2},{3,19},{19,3},{4,20},{20... | collective-permute-start | bytes 811016 | tf_op jit(solution)/shard_map/ppermute | solution.py:889
  108.1 28.8 %collective-permute-start.22 = (bf16[384,1024]{1,0:T(8,128)(2,1)}, bf16[384,1024]{1,0:T(8,128)(2,1)}, u32[]{:S(2)}, u32[]{:S(2)}) collective-permute-start(bf16[384,1024]{1,0:T(8,128)(2,1)} %get-tuple-element.259.refs_5_.refs_9_), channel_id=1, source_target_pairs={{0,8},{4,12},{8,0},{12,4},{1,9},{5,13},{9,1},{13,5},{2,10},{6,14},... | collective-permute-start | bytes 2359304 | tf_op jit(solution)/shard_map/ppermute | solution.py:889
  124.4 28.3 %collective-permute-start.20 = (bf16[384,1024]{1,0:T(8,128)(2,1)S(1)}, bf16[384,1024]{1,0:T(8,128)(2,1)S(1)}, u32[]{:S(2)}, u32[]{:S(2)}) collective-permute-start(bf16[384,1024]{1,0:T(8,128)(2,1)S(1)} %get-tuple-element.255.refs_3_.refs_5_), channel_id=1, source_target_pairs={{0,8},{4,12},{8,0},{12,4},{1,9},{5,13},{9,1},{13,5},{2,10},{6,14},... | collective-permute-start | bytes 2359304 | tf_op jit(solution)/shard_map/ppermute | solution.py:889
  172.7 19.9 %collective-permute-start.27 = (bf16[384,1024]{1,0:T(8,128)(2,1)S(1)}, bf16[384,1024]{1,0:T(8,128)(2,1)S(1)}, u32[]{:S(2)}, u32[]{:S(2)}) collective-permute-start(bf16[384,1024]{1,0:T(8,128)(2,1)S(1)} %add_convert_fusion.2), channel_id=1, source_target_pairs={{0,8},{4,12},{8,0},{12,4},{1,9},{5,13},{9,1},{13,5},{2,10},{6,14},... | collective-permute-start | bytes 2359304 | tf_op jit(solution)/shard_map/ppermute | solution.py:889
  174.0 17.6 %collective-permute-start.26 = (bf16[384,1024]{1,0:T(8,128)(2,1)S(1)}, bf16[384,1024]{1,0:T(8,128)(2,1)S(1)}, u32[]{:S(2)}, u32[]{:S(2)}) collective-permute-start(bf16[384,1024]{1,0:T(8,128)(2,1)S(1)} %get-tuple-element.282), channel_id=1, source_target_pairs={{0,4},{4,0},{8,12},{12,8},{1,5},{5,1},{9,13},{13,9},{2,6},{6,2},{1... | collective-permute-start | bytes 2359304 | tf_op jit(solution)/shard_map/ppermute | solution.py:889
  174.0 39.6 %collective-permute-start.28 = (bf16[384,1024]{1,0:T(8,128)(2,1)S(1)}, bf16[384,1024]{1,0:T(8,128)(2,1)}, u32[]{:S(2)}, u32[]{:S(2)}) collective-permute-start(bf16[384,1024]{1,0:T(8,128)(2,1)S(1)} %get-tuple-element.285), channel_id=1, source_target_pairs={{0,4},{4,0},{8,12},{12,8},{1,5},{5,1},{9,13},{13,9},{2,6},{6,2},{1... | collective-permute-start | bytes 2359304 | tf_op jit(solution)/shard_map/ppermute | solution.py:889
  188.7 25.1 %collective-permute-start.29 = (bf16[384,1024]{1,0:T(8,128)(2,1)}, bf16[384,1024]{1,0:T(8,128)(2,1)}, u32[]{:S(2)}, u32[]{:S(2)}) collective-permute-start(bf16[384,1024]{1,0:T(8,128)(2,1)} %get-tuple-element.286), channel_id=1, source_target_pairs={{0,8},{4,12},{8,0},{12,4},{1,9},{5,13},{9,1},{13,5},{2,10},{6,14},... | collective-permute-start | bytes 2359304 | tf_op jit(solution)/shard_map/ppermute | solution.py:889
  190.1 31.4 %collective-permute-start.31 = (bf16[4,4,128,256]{3,2,1,0:T(8,128)(2,1)}, bf16[4,4,128,256]{3,2,1,0:T(8,128)(2,1)}, u32[]{:S(2)}, u32[]{:S(2)}) collective-permute-start(bf16[4,4,128,256]{3,2,1,0:T(8,128)(2,1)} %get-tuple-element.290), channel_id=1, source_target_pairs={{0,16},{16,0},{1,17},{17,1},{2,18},{18,2},{3,19},{19,3},{4,20},{20... | collective-permute-start | bytes 3145736 | tf_op jit(solution)/shard_map/ppermute | solution.py:889
  207.9 18.2 %all-to-all-start.3 = ((bf16[4,384,256]{2,1,0:T(8,128)(2,1)}), bf16[4,384,256]{2,1,0:T(8,128)(2,1)}, u32[]{:S(2)}, u32[]{:S(2)}) async-start(bf16[4,384,256]{2,1,0:T(8,128)(2,1)} %get-tuple-element.283), calls=%async_computation.3 | async-start | bytes 1572864 | tf_op jit(solution)/shard_map/all_to_all | solution.py:876
  212.1 47.6 %collective-permute-start.32 = (bf16[4,4,128,256]{3,2,1,0:T(8,128)(2,1)}, bf16[4,4,128,256]{3,2,1,0:T(8,128)(2,1)}, u32[]{:S(2)}, u32[]{:S(2)}) collective-permute-start(bf16[4,4,128,256]{3,2,1,0:T(8,128)(2,1)} %get-tuple-element.306), channel_id=1, source_target_pairs={{0,16},{16,0},{1,17},{17,1},{2,18},{18,2},{3,19},{19,3},{4,20},{20... | collective-permute-start | bytes 3145736 | tf_op jit(solution)/shard_map/ppermute | solution.py:889
  213.7 46.1 %collective-permute-start.34 = (bf16[2,4,256,128]{3,2,1,0:T(8,128)(2,1)}, bf16[2,4,256,128]{3,2,1,0:T(8,128)(2,1)}, u32[]{:S(2)}, u32[]{:S(2)}) collective-permute-start(bf16[2,4,256,128]{3,2,1,0:T(8,128)(2,1)} %copy-done.14), channel_id=1, source_target_pairs={{0,4},{4,0},{8,12},{12,8},{1,5},{5,1},{9,13},{13,9},{2,6},{6,2},{1... | collective-permute-start | bytes 1572872 | tf_op jit(solution)/shard_map/ppermute | solution.py:889
  219.7 40.1 %collective-permute-start.35 = (bf16[2,4,256,128]{3,2,1,0:T(8,128)(2,1)S(1)}, bf16[2,4,256,128]{3,2,1,0:T(8,128)(2,1)}, u32[]{:S(2)}, u32[]{:S(2)}) collective-permute-start(bf16[2,4,256,128]{3,2,1,0:T(8,128)(2,1)S(1)} %get-tuple-element.310), channel_id=1, source_target_pairs={{0,8},{4,12},{8,0},{12,4},{1,9},{5,13},{9,1},{13,5},{2,10},{6,14},... | collective-permute-start | bytes 1572872 | tf_op jit(solution)/shard_map/ppermute | solution.py:889
  224.8 35.0 %collective-permute-start.33 = (bf16[2,4,128,256]{3,2,1,0:T(8,128)(2,1)}, bf16[2,4,128,256]{3,2,1,0:T(8,128)(2,1)S(1)}, u32[]{:S(2)}, u32[]{:S(2)}) collective-permute-start(bf16[2,4,128,256]{3,2,1,0:T(8,128)(2,1)} %get-tuple-element.293), channel_id=1, source_target_pairs={{0,1},{1,0},{2,3},{3,2},{4,5},{5,4},{6,7},{7,6},{8,9},{9,8},{10,11... | collective-permute-start | bytes 1572872 | tf_op jit(solution)/shard_map/ppermute | solution.py:889
  226.1 33.7 %all-to-all-start.4 = ((bf16[8,48,1024]{2,1,0:T(8,128)(2,1)}), bf16[8,48,1024]{2,1,0:T(8,128)(2,1)}, u32[]{:S(2)}, u32[]{:S(2)}) async-start(bf16[8,48,1024]{2,1,0:T(8,128)(2,1)} %bitcast.16), calls=%async_computation.4 | async-start | bytes 1572864 | tf_op jit(solution)/shard_map/all_to_all | solution.py:872
  259.9 27.6 %collective-permute-start.40 = (bf16[384,1024]{1,0:T(8,128)(2,1)}, bf16[384,1024]{1,0:T(8,128)(2,1)S(1)}, u32[]{:S(2)}, u32[]{:S(2)}) collective-permute-start(bf16[384,1024]{1,0:T(8,128)(2,1)} %get-tuple-element.342), channel_id=1, source_target_pairs={{0,4},{4,0},{8,12},{12,8},{1,5},{5,1},{9,13},{13,9},{2,6},{6,2},{1... | collective-permute-start | bytes 2359304 | tf_op jit(solution)/shard_map/ppermute | solution.py:889
  263.5 23.9 %collective-permute-start.41 = (bf16[384,1024]{1,0:T(8,128)(2,1)}, bf16[384,1024]{1,0:T(8,128)(2,1)S(1)}, u32[]{:S(2)}, u32[]{:S(2)}) collective-permute-start(bf16[384,1024]{1,0:T(8,128)(2,1)} %add_convert_fusion.1), channel_id=1, source_target_pairs={{0,8},{4,12},{8,0},{12,4},{1,9},{5,13},{9,1},{13,5},{2,10},{6,14},... | collective-permute-start | bytes 2359304 | tf_op jit(solution)/shard_map/ppermute | solution.py:889
  266.3 19.4 %collective-permute-start.38 = (bf16[2,4,128,256]{3,2,1,0:T(8,128)(2,1)S(1)}, bf16[2,4,128,256]{3,2,1,0:T(8,128)(2,1)S(1)}, u32[]{:S(2)}, u32[]{:S(2)}) collective-permute-start(bf16[2,4,128,256]{3,2,1,0:T(8,128)(2,1)S(1)} %get-tuple-element.324), channel_id=1, source_target_pairs={{0,1},{1,0},{2,3},{3,2},{4,5},{5,4},{6,7},{7,6},{8,9},{9,8},{10,11... | collective-permute-start | bytes 1572872 | tf_op jit(solution)/shard_map/ppermute | solution.py:889
  278.4 32.0 %collective-permute-start.37 = (bf16[4,4,256,128]{3,2,1,0:T(8,128)(2,1)}, bf16[4,4,256,128]{3,2,1,0:T(8,128)(2,1)}, u32[]{:S(2)}, u32[]{:S(2)}) collective-permute-start(bf16[4,4,256,128]{3,2,1,0:T(8,128)(2,1)} %get-tuple-element.330), channel_id=1, source_target_pairs={{0,16},{16,0},{1,17},{17,1},{2,18},{18,2},{3,19},{19,3},{4,20},{20... | collective-permute-start | bytes 3145736 | tf_op jit(solution)/shard_map/ppermute | solution.py:889
  300.2 33.5 %all-to-all-start.5 = ((bf16[8,48,1024]{2,1,0:T(8,128)(2,1)}), bf16[8,48,1024]{2,1,0:T(8,128)(2,1)}, u32[]{:S(2)}, u32[]{:S(2)}) async-start(bf16[8,48,1024]{2,1,0:T(8,128)(2,1)} %bitcast.20), calls=%async_computation.5 | async-start | bytes 1572864 | tf_op jit(solution)/shard_map/all_to_all | solution.py:872
  313.3 20.4 %collective-permute-start.44 = (bf16[2,4,256,128]{3,2,1,0:T(8,128)(2,1)}, bf16[2,4,256,128]{3,2,1,0:T(8,128)(2,1)}, u32[]{:S(2)}, u32[]{:S(2)}) collective-permute-start(bf16[2,4,256,128]{3,2,1,0:T(8,128)(2,1)} %get-tuple-element.467), channel_id=1, source_target_pairs={{0,1},{1,0},{2,3},{3,2},{4,5},{5,4},{6,7},{7,6},{8,9},{9,8},{10,11... | collective-permute-start | bytes 1572872 | tf_op jit(solution)/shard_map/ppermute | solution.py:889
  (94 other events, 840.2 us)
